TPU v7x, 32 devices: a whole 2x2x4 slice. The times are simulated.
32 devices in a mesh: parts: 2 (over y), row: 8 (over z, x), col: 2 (over core).
Axes of the slice: x: 2, y: 2, z: 4, core: 2. Of those that a mesh axis runs over, the one named last changes fastest.
Arguments:
- values: bfloat16 [16, 46, 128, 128], P(('parts', 'row'), 'col'), parts along dimension 0, as said below
- block_rows: int32 [16, 46], P(('parts', 'row'), 'col'), parts along dimension 0, may hold values from 0 to 23, as said below
- block_cols: int32 [16, 46], P(('parts', 'row'), 'col'), parts along dimension 0, may hold values from 0 to 23, as said below
- counts: int32 [16, 2], P(('parts', 'row'), 'col'), parts along dimension 0, may hold values from 1 to 23, as said below
Outputs:
- product: float32 [16, 46, 128, 128], P(('parts', 'row'), 'col'), parts along dimension 0
There are 2 independent parts, one for each index of `parts`. A program takes and returns all parts, laid end to end along the dimension named above; each array names one. Nothing has to cross between parts.
Inputs may be any that keep to these rules, and one draw needn't show every extreme that they name: `block_rows`: slots below a device's count hold global block rows of that device's panel, rows 3 r to 3 r + 2; later slots hold 0. `block_cols`: slots below a device's count hold block columns whose parity is the device's col index and whose cyclic distance from the slot's row is at most 7; no position appears twice; the stored pattern and X are symmetric (block (J, I) is the transpose of block (I, J)); later slots hold 0. `counts`: the number of used slots of each device; some device is full. `values`: blocks in unused slots are zero.
All inputs are finite; a program needn't handle non-finite values.
Results may differ from a plain program's by a relative error of at most 0.0003.
Values may be sent and summed in bfloat16 or wider, within the bound.
No kernel may reach another device: no remote copies, remote signals or barrier semaphores. Data moves between devices by JAX's collectives and lax.ppermute only.
A program may use at most 128 MiB of HBM per device.

v0:
```python
import jax
import jax.numpy as jnp
from jax import lax
from jax.sharding import PartitionSpec as P

BR = 3
HB = 7


def shifted(block, axis, distance):
    devices = range(lax.axis_size(axis))
    route = [((i - distance) % len(devices), i) for i in devices]
    return lax.ppermute(block, axis, route)


def build_table(local_rows, global_cols, valid, row_width, nblocks):
    slot_count = local_rows.shape[0]
    target_ids = jnp.where(valid, local_rows * nblocks + global_cols, row_width * nblocks)
    table_flat = jnp.full((row_width * nblocks,), -1, jnp.int32)
    table_flat = table_flat.at[target_ids].set(jnp.arange(slot_count, dtype=jnp.int32), mode="drop")
    return table_flat.reshape(row_width, nblocks)


def with_zero(blocks):
    return jnp.concatenate([blocks, jnp.zeros((1,) + blocks.shape[1:], blocks.dtype)], axis=0)


def local(values, block_rows, block_cols, counts):
    slot_count = values.shape[1]
    row_count = lax.axis_size("row")
    nblocks = BR * row_count
    own_index = lax.axis_index("row")
    full_vals, full_rows, full_cols, full_counts = (
        lax.all_gather(values, "col", axis=1, tiled=True),
        lax.all_gather(block_rows, "col", axis=1, tiled=True),
        lax.all_gather(block_cols, "col", axis=1, tiled=True),
        lax.all_gather(counts, "col", axis=1, tiled=True),
    )
    slot_ids = jnp.arange(2 * slot_count, dtype=jnp.int32)
    half_ids = slot_ids // slot_count
    own_valid = slot_ids % slot_count < full_counts[0][half_ids]
    own_table = build_table(full_rows[0] - own_index * BR, full_cols[0], own_valid, BR, nblocks)
    own_blocks = with_zero(full_vals[0])
    own_zero = own_blocks.shape[0] - 1
    local_ids = jnp.arange(slot_count, dtype=jnp.int32)
    local_valid = local_ids < counts[0, 0]
    safe_rows = jnp.clip(block_rows[0] - own_index * BR, 0, BR - 1)
    local_cols = block_cols[0]
    panel_rows = jnp.arange(BR, dtype=jnp.int32)

    def accumulate(running, remote, offset):
        rem_vals, rem_rows, rem_cols, rem_counts = remote
        source = (own_index + offset) % row_count
        rem_valid = jnp.arange(rem_rows.shape[1], dtype=jnp.int32) < rem_counts[0, 0]
        rem_table = build_table(rem_rows[0] - source * BR, rem_cols[0], rem_valid, BR, nblocks)
        rem_blocks = with_zero(rem_vals[0])
        rem_zero = rem_blocks.shape[0] - 1
        block_k = source * BR + panel_rows
        left_idx = own_table[safe_rows[:, None], block_k[None, :]]
        right_idx = rem_table[panel_rows[None, :], local_cols[:, None]]
        keep_mask = (left_idx >= 0) & (right_idx >= 0) & local_valid[:, None]
        left_blocks = own_blocks[jnp.where(keep_mask, left_idx, own_zero)]
        right_blocks = rem_blocks[jnp.where(keep_mask, right_idx, rem_zero)]
        return running + jnp.einsum(
            "skab,skbc->sac", left_blocks, right_blocks, preferred_element_type=jnp.float32
        )

    reach_max = (HB + BR - 1) // BR
    local_panel = (values, block_rows, block_cols, counts)
    running = jnp.zeros((slot_count, values.shape[2], values.shape[3]), jnp.float32)
    running = accumulate(running, local_panel, 0)
    upper_panel = local_panel
    lower_panel = local_panel
    for shift_step in range(1, reach_max + 1):
        upper_panel = shifted(
            (upper_panel[0], upper_panel[1], upper_panel[2], upper_panel[3]), "row", -1
        )
        running = accumulate(running, upper_panel, shift_step)
        lower_panel = shifted(
            (lower_panel[0], lower_panel[1], lower_panel[2], lower_panel[3]), "row", 1
        )
        running = accumulate(running, lower_panel, -shift_step)
    running = jnp.where(local_valid[:, None, None], running, 0.0)
    return running[None]


def solution(mesh):
    return jax.shard_map(
        local,
        mesh=mesh,
        in_specs=(
            P(("parts", "row"), "col", None, None),
            P(("parts", "row"), "col"),
            P(("parts", "row"), "col"),
            P(("parts", "row"), "col"),
        ),
        out_specs=P(("parts", "row"), "col", None, None),
        check_vma=False,
    )
```

profile of v0, /device:TPU:0, one launch (start us, length us, event | category | flops | bytes accessed | tf_op | source)
XLA Modules:
  0.0 241.7 jit_solution(12856757389620151776)
XLA Ops:
  6.5 6.0 %collective-permute-start = (s32[1,1]{1,0:T(1,128)}, s32[1,1]{1,0:T(1,128)}, u32[]{:S(2)}, u32[]{:S(2)}) collective-permute-start(s32[1,1]{1,0:T(1,128)} %param.7), channel_id=1, source_target_pairs={{2,0},{4,2},{6,4},{8,6},{10,8},{12,10},{14,12},{0,14},{3,1},{5,3},... | collective-permute-start | bytes 20 | tf_op jit(solution)/shard_map/ppermute | solution.py:13
  12.5 4.7 %collective-permute-start.1 = (s32[1,23]{1,0:T(1,128)}, s32[1,23]{1,0:T(1,128)S(1)}, u32[]{:S(2)}, u32[]{:S(2)}) collective-permute-start(s32[1,23]{1,0:T(1,128)} %param.5), channel_id=1, source_target_pairs={{2,0},{4,2},{6,4},{8,6},{10,8},{12,10},{14,12},{0,14},{3,1},{5,3},... | collective-permute-start | bytes 284 | tf_op jit(solution)/shard_map/ppermute | solution.py:13
  17.2 4.7 %collective-permute-start.2 = (s32[1,23]{1,0:T(1,128)}, s32[1,23]{1,0:T(1,128)S(1)}, u32[]{:S(2)}, u32[]{:S(2)}) collective-permute-start(s32[1,23]{1,0:T(1,128)} %param.6), channel_id=1, source_target_pairs={{2,0},{4,2},{6,4},{8,6},{10,8},{12,10},{14,12},{0,14},{3,1},{5,3},... | collective-permute-start | bytes 284 | tf_op jit(solution)/shard_map/ppermute | solution.py:13
  50.3 4.7 %collective-permute-start.3 = (bf16[1,23,128,128]{3,2,1,0:T(8,128)(2,1)S(1)}, bf16[1,23,128,128]{3,2,1,0:T(8,128)(2,1)S(1)}, u32[]{:S(2)}, u32[]{:S(2)}) collective-permute-start(bf16[1,23,128,128]{3,2,1,0:T(8,128)(2,1)S(1)} %copy-done.7), channel_id=1, source_target_pairs={{2,0},{4,2},{6,4},{8,6},{10,8},{12,10},{14,12},{0,14},{3,1},{5,3},... | collective-permute-start | bytes 2261000 | tf_op jit(solution)/shard_map/ppermute | solution.py:13
  58.6 4.8 %collective-permute-start.8 = (s32[1,1]{1,0:T(1,128)}, s32[1,1]{1,0:T(1,128)}, u32[]{:S(2)}, u32[]{:S(2)}) collective-permute-start(s32[1,1]{1,0:T(1,128)} %collective-permute-done), channel_id=1, source_target_pairs={{2,0},{4,2},{6,4},{8,6},{10,8},{12,10},{14,12},{0,14},{3,1},{5,3},... | collective-permute-start | bytes 20 | tf_op jit(solution)/shard_map/ppermute | solution.py:13
  67.0 4.8 %collective-permute-start.9 = (s32[1,23]{1,0:T(1,128)S(1)}, s32[1,23]{1,0:T(1,128)S(1)}, u32[]{:S(2)}, u32[]{:S(2)}) collective-permute-start(s32[1,23]{1,0:T(1,128)S(1)} %collective-permute-done.1), channel_id=1, source_target_pairs={{2,0},{4,2},{6,4},{8,6},{10,8},{12,10},{14,12},{0,14},{3,1},{5,3},... | collective-permute-start | bytes 284 | tf_op jit(solution)/shard_map/ppermute | solution.py:13
  71.8 13.7 %collective-permute-done.8 = s32[1,1]{1,0:T(1,128)} collective-permute-done((s32[1,1]{1,0:T(1,128)}, s32[1,1]{1,0:T(1,128)}, u32[]{:S(2)}, u32[]{:S(2)}) %collective-permute-start.8) | collective-permute-done | bytes 36 | tf_op jit(solution)/shard_map/ppermute | solution.py:13
  85.7 2.4 %collective-permute-start.16 = (s32[1,1]{1,0:T(1,128)}, s32[1,1]{1,0:T(1,128)}, u32[]{:S(2)}, u32[]{:S(2)}) collective-permute-start(s32[1,1]{1,0:T(1,128)} %collective-permute-done.8), channel_id=1, source_target_pairs={{2,0},{4,2},{6,4},{8,6},{10,8},{12,10},{14,12},{0,14},{3,1},{5,3},... | collective-permute-start | bytes 20 | tf_op jit(solution)/shard_map/ppermute | solution.py:13
  95.3 4.2 %collective-permute-done.14 = s32[1,23]{1,0:T(1,128)S(1)} collective-permute-done((s32[1,23]{1,0:T(1,128)S(1)}, s32[1,23]{1,0:T(1,128)S(1)}, u32[]{:S(2)}, u32[]{:S(2)}) %collective-permute-start.14) | collective-permute-done | bytes 124 | tf_op jit(solution)/shard_map/ppermute | solution.py:13
  119.4 2.4 %gather_fusion.3 = bf16[69,128,128]{2,1,0:T(8,128)(2,1)} fusion(bf16[24,128,128]{2,1,0:T(8,128)(2,1)S(1)} %concatenate.57, s32[1024]{0:T(1024)S(1)} %pad_clamp_fusion.12), kind=kCustom, calls=%fused_computation.3 | custom fusion | bytes 4522260 | tf_op jit(solution)/shard_map/gather | solution.py:63
  127.8 2.5 %gather_fusion.11 = bf16[69,128,128]{2,1,0:T(8,128)(2,1)} fusion(bf16[24,128,128]{2,1,0:T(8,128)(2,1)S(1)} %concatenate.61, s32[1024]{0:T(1024)S(1)} %pad_clamp_fusion.8), kind=kCustom, calls=%fused_computation.11 | custom fusion | bytes 4522260 | tf_op jit(solution)/shard_map/gather | solution.py:63
  130.3 21.2 %collective-permute-done.11 = bf16[1,23,128,128]{3,2,1,0:T(8,128)(2,1)} collective-permute-done((bf16[1,23,128,128]{3,2,1,0:T(8,128)(2,1)S(1)}, bf16[1,23,128,128]{3,2,1,0:T(8,128)(2,1)}, u32[]{:S(2)}, u32[]{:S(2)}) %collective-permute-start.11) | collective-permute-done | bytes 753696 | tf_op jit(solution)/shard_map/ppermute | solution.py:13
  155.5 2.4 gather_fusion.14
  165.0 2.5 %gather_fusion.2 = bf16[69,128,128]{2,1,0:T(8,128)(2,1)} fusion(bf16[47,128,128]{2,1,0:T(8,128)(2,1)S(1)} %concatenate.54, s32[1024]{0:T(1024)S(1)} %pad_clamp_fusion.13), kind=kCustom, calls=%fused_computation.2 | custom fusion | bytes 4522260 | tf_op jit(solution)/shard_map/gather | solution.py:62
  167.6 2.4 %gather_fusion.22 = bf16[69,128,128]{2,1,0:T(8,128)(2,1)} fusion(bf16[47,128,128]{2,1,0:T(8,128)(2,1)S(1)} %concatenate.54, s32[1024]{0:T(1024)S(1)} %pad_clamp_fusion.3), kind=kCustom, calls=%fused_computation.22 | custom fusion | bytes 4522260 | tf_op jit(solution)/shard_map/gather | solution.py:62
  170.0 2.4 gather_fusion.26
  172.4 2.4 %gather_fusion.15 = bf16[69,128,128]{2,1,0:T(8,128)(2,1)} fusion(bf16[24,128,128]{2,1,0:T(8,128)(2,1)S(1)} %concatenate.63, s32[1024]{0:T(1024)S(1)} %pad_clamp_fusion.6), kind=kCustom, calls=%fused_computation.15 | custom fusion | bytes 4522260 | tf_op jit(solution)/shard_map/gather | solution.py:63
  174.8 4.3 %fusion.48 = f32[23,128,128,1]{2,1,3,0:T(8,128)} fusion(bf16[23,3,128,128]{3,2,1,0:T(8,128)(2,1)} %bitcast.199, bf16[23,3,128,128]{3,2,1,0:T(8,128)(2,1)} %bitcast.200), kind=kOutput, calls=%fused_computation.168 | convolution fusion | flops 289406976 | bytes 6029312 | tf_op jit(solution)/shard_map/skab,skbc->sac/dot_general | solution.py:64
  181.5 4.4 %fusion.49 = f32[23,128,128,1]{2,1,3,0:T(8,128)} fusion(bf16[23,3,128,128]{3,2,1,0:T(8,128)(2,1)} %bitcast.198, bf16[23,3,128,128]{3,2,1,0:T(8,128)(2,1)} %bitcast.201), kind=kOutput, calls=%fused_computation.169 | convolution fusion | flops 289406976 | bytes 6029312 | tf_op jit(solution)/shard_map/skab,skbc->sac/dot_general | solution.py:64
  194.6 24.5 %collective-permute-done.19 = bf16[1,23,128,128]{3,2,1,0:T(8,128)(2,1)S(1)} collective-permute-done((bf16[1,23,128,128]{3,2,1,0:T(8,128)(2,1)}, bf16[1,23,128,128]{3,2,1,0:T(8,128)(2,1)S(1)}, u32[]{:S(2)}, u32[]{:S(2)}) %collective-permute-start.19) | collective-permute-done | bytes 753696 | tf_op jit(solution)/shard_map/ppermute | solution.py:13
  219.4 2.4 %gather_fusion.23 = bf16[69,128,128]{2,1,0:T(8,128)(2,1)} fusion(bf16[24,128,128]{2,1,0:T(8,128)(2,1)S(1)} %concatenate.67, s32[1024]{0:T(1024)S(1)} %pad_clamp_fusion.2), kind=kCustom, calls=%fused_computation.23 | custom fusion | bytes 4522260 | tf_op jit(solution)/shard_map/gather | solution.py:63
  221.8 4.2 %fusion.50 = f32[23,128,128,1]{2,1,3,0:T(8,128)} fusion(bf16[23,3,128,128]{3,2,1,0:T(8,128)(2,1)} %bitcast.193, bf16[23,3,128,128]{3,2,1,0:T(8,128)(2,1)} %bitcast.202), kind=kOutput, calls=%fused_computation.170 | convolution fusion | flops 289406976 | bytes 6029312 | tf_op jit(solution)/shard_map/skab,skbc->sac/dot_general | solution.py:64
  226.0 2.4 %gather_fusion.27 = bf16[69,128,128]{2,1,0:T(8,128)(2,1)} fusion(bf16[24,128,128]{2,1,0:T(8,128)(2,1)S(1)} %concatenate.69, s32[1024]{0:T(1024)S(1)} %pad_clamp_fusion), kind=kCustom, calls=%fused_computation.27 | custom fusion | bytes 4522260 | tf_op jit(solution)/shard_map/gather | solution.py:63
  228.5 6.4 %fusion.1 = f32[1,23,128,128]{3,2,1,0:T(8,128)} fusion(f32[23,128,128,1]{2,1,3,0:T(8,128)} %fusion.50, f32[23,128,128,1]{2,1,3,0:T(8,128)} %fusion.49, f32[23,128,128,1]{2,1,3,0:T(8,128)} %fusion.48, f32[23,128,128,1]{2,1,3,0:T(8,128)} %fusion.47, f32[23,128,128,1]{2,1,3,0:T(8,128)} %fusion.46, f32[23,128,128,1]{2,1,3,0:T(8,128)} %fusion.45, ...), kind=kOutput, calls=%fused_computation.38 | convolution fusion | flops 292044800 | bytes 15073303 | tf_op jit(solution)/shard_map/skab,skbc->sac/dot_general | solution.py:64
  (189 shorter events, 89.2 us)
Async XLA Ops:
  6.5 146.2 %all-gather.2.cloned.1.call-start = ((), (), s32[]{:S(2)}) async-start(), calls=%async_computation | async-start | bytes 2260992 | tf_op jit(solution)/shard_map/all_gather | solution.py:34
  6.5 43.7 %collective-permute-start = (s32[1,1]{1,0:T(1,128)}, s32[1,1]{1,0:T(1,128)}, u32[]{:S(2)}, u32[]{:S(2)}) collective-permute-start(s32[1,1]{1,0:T(1,128)} %param.7), channel_id=1, source_target_pairs={{2,0},{4,2},{6,4},{8,6},{10,8},{12,10},{14,12},{0,14},{3,1},{5,3},... | collective-permute-start | bytes 20 | tf_op jit(solution)/shard_map/ppermute | solution.py:13
  12.5 46.1 %collective-permute-start.4 = (s32[1,1]{1,0:T(1,128)}, s32[1,1]{1,0:T(1,128)}, u32[]{:S(2)}, u32[]{:S(2)}) collective-permute-start(s32[1,1]{1,0:T(1,128)} %param.7), channel_id=1, source_target_pairs={{14,0},{0,2},{2,4},{4,6},{6,8},{8,10},{10,12},{12,14},{15,1},{1,3}... | collective-permute-start | bytes 20 | tf_op jit(solution)/shard_map/ppermute | solution.py:13
  12.5 37.8 %collective-permute-start.1 = (s32[1,23]{1,0:T(1,128)}, s32[1,23]{1,0:T(1,128)S(1)}, u32[]{:S(2)}, u32[]{:S(2)}) collective-permute-start(s32[1,23]{1,0:T(1,128)} %param.5), channel_id=1, source_target_pairs={{2,0},{4,2},{6,4},{8,6},{10,8},{12,10},{14,12},{0,14},{3,1},{5,3},... | collective-permute-start | bytes 284 | tf_op jit(solution)/shard_map/ppermute | solution.py:13
  17.2 46.2 %collective-permute-start.5 = (s32[1,23]{1,0:T(1,128)}, s32[1,23]{1,0:T(1,128)S(1)}, u32[]{:S(2)}, u32[]{:S(2)}) collective-permute-start(s32[1,23]{1,0:T(1,128)} %param.5), channel_id=1, source_target_pairs={{14,0},{0,2},{2,4},{4,6},{6,8},{8,10},{10,12},{12,14},{15,1},{1,3}... | collective-permute-start | bytes 284 | tf_op jit(solution)/shard_map/ppermute | solution.py:13
  17.2 37.8 %collective-permute-start.2 = (s32[1,23]{1,0:T(1,128)}, s32[1,23]{1,0:T(1,128)S(1)}, u32[]{:S(2)}, u32[]{:S(2)}) collective-permute-start(s32[1,23]{1,0:T(1,128)} %param.6), channel_id=1, source_target_pairs={{2,0},{4,2},{6,4},{8,6},{10,8},{12,10},{14,12},{0,14},{3,1},{5,3},... | collective-permute-start | bytes 284 | tf_op jit(solution)/shard_map/ppermute | solution.py:13
  50.3 13.1 %collective-permute-start.6 = (s32[1,23]{1,0:T(1,128)S(1)}, s32[1,23]{1,0:T(1,128)S(1)}, u32[]{:S(2)}, u32[]{:S(2)}) collective-permute-start(s32[1,23]{1,0:T(1,128)S(1)} %copy-done.9), channel_id=1, source_target_pairs={{14,0},{0,2},{2,4},{4,6},{6,8},{8,10},{10,12},{12,14},{15,1},{1,3}... | collective-permute-start | bytes 284 | tf_op jit(solution)/shard_map/ppermute | solution.py:13
  50.3 71.6 %collective-permute-start.3 = (bf16[1,23,128,128]{3,2,1,0:T(8,128)(2,1)S(1)}, bf16[1,23,128,128]{3,2,1,0:T(8,128)(2,1)S(1)}, u32[]{:S(2)}, u32[]{:S(2)}) collective-permute-start(bf16[1,23,128,128]{3,2,1,0:T(8,128)(2,1)S(1)} %copy-done.7), channel_id=1, source_target_pairs={{2,0},{4,2},{6,4},{8,6},{10,8},{12,10},{14,12},{0,14},{3,1},{5,3},... | collective-permute-start | bytes 2261000 | tf_op jit(solution)/shard_map/ppermute | solution.py:13
  55.1 69.0 %collective-permute-start.7 = (bf16[1,23,128,128]{3,2,1,0:T(8,128)(2,1)S(1)}, bf16[1,23,128,128]{3,2,1,0:T(8,128)(2,1)}, u32[]{:S(2)}, u32[]{:S(2)}) collective-permute-start(bf16[1,23,128,128]{3,2,1,0:T(8,128)(2,1)S(1)} %copy-done.7), channel_id=1, source_target_pairs={{14,0},{0,2},{2,4},{4,6},{6,8},{8,10},{10,12},{12,14},{15,1},{1,3}... | collective-permute-start | bytes 2261000 | tf_op jit(solution)/shard_map/ppermute | solution.py:13
  58.6 26.9 %collective-permute-start.8 = (s32[1,1]{1,0:T(1,128)}, s32[1,1]{1,0:T(1,128)}, u32[]{:S(2)}, u32[]{:S(2)}) collective-permute-start(s32[1,1]{1,0:T(1,128)} %collective-permute-done), channel_id=1, source_target_pairs={{2,0},{4,2},{6,4},{8,6},{10,8},{12,10},{14,12},{0,14},{3,1},{5,3},... | collective-permute-start | bytes 20 | tf_op jit(solution)/shard_map/ppermute | solution.py:13
  63.4 29.8 %collective-permute-start.12 = (s32[1,1]{1,0:T(1,128)}, s32[1,1]{1,0:T(1,128)}, u32[]{:S(2)}, u32[]{:S(2)}) collective-permute-start(s32[1,1]{1,0:T(1,128)} %collective-permute-done.4), channel_id=1, source_target_pairs={{14,0},{0,2},{2,4},{4,6},{6,8},{8,10},{10,12},{12,14},{15,1},{1,3}... | collective-permute-start | bytes 20 | tf_op jit(solution)/shard_map/ppermute | solution.py:13
  67.0 18.7 %collective-permute-start.9 = (s32[1,23]{1,0:T(1,128)S(1)}, s32[1,23]{1,0:T(1,128)S(1)}, u32[]{:S(2)}, u32[]{:S(2)}) collective-permute-start(s32[1,23]{1,0:T(1,128)S(1)} %collective-permute-done.1), channel_id=1, source_target_pairs={{2,0},{4,2},{6,4},{8,6},{10,8},{12,10},{14,12},{0,14},{3,1},{5,3},... | collective-permute-start | bytes 284 | tf_op jit(solution)/shard_map/ppermute | solution.py:13
  85.7 18.9 %collective-permute-start.16 = (s32[1,1]{1,0:T(1,128)}, s32[1,1]{1,0:T(1,128)}, u32[]{:S(2)}, u32[]{:S(2)}) collective-permute-start(s32[1,1]{1,0:T(1,128)} %collective-permute-done.8), channel_id=1, source_target_pairs={{2,0},{4,2},{6,4},{8,6},{10,8},{12,10},{14,12},{0,14},{3,1},{5,3},... | collective-permute-start | bytes 20 | tf_op jit(solution)/shard_map/ppermute | solution.py:13
  89.0 6.2 %collective-permute-start.13 = (s32[1,23]{1,0:T(1,128)S(1)}, s32[1,23]{1,0:T(1,128)S(1)}, u32[]{:S(2)}, u32[]{:S(2)}) collective-permute-start(s32[1,23]{1,0:T(1,128)S(1)} %collective-permute-done.5), channel_id=1, source_target_pairs={{14,0},{0,2},{2,4},{4,6},{6,8},{8,10},{10,12},{12,14},{15,1},{1,3}... | collective-permute-start | bytes 284 | tf_op jit(solution)/shard_map/ppermute | solution.py:13
  93.2 6.3 %collective-permute-start.14 = (s32[1,23]{1,0:T(1,128)S(1)}, s32[1,23]{1,0:T(1,128)S(1)}, u32[]{:S(2)}, u32[]{:S(2)}) collective-permute-start(s32[1,23]{1,0:T(1,128)S(1)} %collective-permute-done.6), channel_id=1, source_target_pairs={{14,0},{0,2},{2,4},{4,6},{6,8},{8,10},{10,12},{12,14},{15,1},{1,3}... | collective-permute-start | bytes 284 | tf_op jit(solution)/shard_map/ppermute | solution.py:13
  95.3 17.8 %collective-permute-start.20 = (s32[1,1]{1,0:T(1,128)}, s32[1,1]{1,0:T(1,128)}, u32[]{:S(2)}, u32[]{:S(2)}) collective-permute-start(s32[1,1]{1,0:T(1,128)} %collective-permute-done.12), channel_id=1, source_target_pairs={{14,0},{0,2},{2,4},{4,6},{6,8},{8,10},{10,12},{12,14},{15,1},{1,3}... | collective-permute-start | bytes 20 | tf_op jit(solution)/shard_map/ppermute | solution.py:13
  103.0 3.6 %collective-permute-start.17 = (s32[1,23]{1,0:T(1,128)S(1)}, s32[1,23]{1,0:T(1,128)S(1)}, u32[]{:S(2)}, u32[]{:S(2)}) collective-permute-start(s32[1,23]{1,0:T(1,128)S(1)} %collective-permute-done.9), channel_id=1, source_target_pairs={{2,0},{4,2},{6,4},{8,6},{10,8},{12,10},{14,12},{0,14},{3,1},{5,3},... | collective-permute-start | bytes 284 | tf_op jit(solution)/shard_map/ppermute | solution.py:13
  104.6 3.5 %collective-permute-start.18 = (s32[1,23]{1,0:T(1,128)S(1)}, s32[1,23]{1,0:T(1,128)S(1)}, u32[]{:S(2)}, u32[]{:S(2)}) collective-permute-start(s32[1,23]{1,0:T(1,128)S(1)} %collective-permute-done.10), channel_id=1, source_target_pairs={{2,0},{4,2},{6,4},{8,6},{10,8},{12,10},{14,12},{0,14},{3,1},{5,3},... | collective-permute-start | bytes 284 | tf_op jit(solution)/shard_map/ppermute | solution.py:13
  106.6 6.5 %collective-permute-start.21 = (s32[1,23]{1,0:T(1,128)S(1)}, s32[1,23]{1,0:T(1,128)S(1)}, u32[]{:S(2)}, u32[]{:S(2)}) collective-permute-start(s32[1,23]{1,0:T(1,128)S(1)} %collective-permute-done.13), channel_id=1, source_target_pairs={{14,0},{0,2},{2,4},{4,6},{6,8},{8,10},{10,12},{12,14},{15,1},{1,3}... | collective-permute-start | bytes 284 | tf_op jit(solution)/shard_map/ppermute | solution.py:13
  108.1 6.2 %collective-permute-start.22 = (s32[1,23]{1,0:T(1,128)S(1)}, s32[1,23]{1,0:T(1,128)S(1)}, u32[]{:S(2)}, u32[]{:S(2)}) collective-permute-start(s32[1,23]{1,0:T(1,128)S(1)} %collective-permute-done.14), channel_id=1, source_target_pairs={{14,0},{0,2},{2,4},{4,6},{6,8},{8,10},{10,12},{12,14},{15,1},{1,3}... | collective-permute-start | bytes 284 | tf_op jit(solution)/shard_map/ppermute | solution.py:13
  121.9 29.6 %collective-permute-start.11 = (bf16[1,23,128,128]{3,2,1,0:T(8,128)(2,1)S(1)}, bf16[1,23,128,128]{3,2,1,0:T(8,128)(2,1)}, u32[]{:S(2)}, u32[]{:S(2)}) collective-permute-start(bf16[1,23,128,128]{3,2,1,0:T(8,128)(2,1)S(1)} %collective-permute-done.3), channel_id=1, source_target_pairs={{2,0},{4,2},{6,4},{8,6},{10,8},{12,10},{14,12},{0,14},{3,1},{5,3},... | collective-permute-start | bytes 2261000 | tf_op jit(solution)/shard_map/ppermute | solution.py:13
  124.1 30.2 %collective-permute-start.15 = (bf16[1,23,128,128]{3,2,1,0:T(8,128)(2,1)}, bf16[1,23,128,128]{3,2,1,0:T(8,128)(2,1)}, u32[]{:S(2)}, u32[]{:S(2)}) collective-permute-start(bf16[1,23,128,128]{3,2,1,0:T(8,128)(2,1)} %collective-permute-done.7), channel_id=1, source_target_pairs={{14,0},{0,2},{2,4},{4,6},{6,8},{8,10},{10,12},{12,14},{15,1},{1,3}... | collective-permute-start | bytes 2261000 | tf_op jit(solution)/shard_map/ppermute | solution.py:13
  187.8 31.2 %collective-permute-start.19 = (bf16[1,23,128,128]{3,2,1,0:T(8,128)(2,1)}, bf16[1,23,128,128]{3,2,1,0:T(8,128)(2,1)S(1)}, u32[]{:S(2)}, u32[]{:S(2)}) collective-permute-start(bf16[1,23,128,128]{3,2,1,0:T(8,128)(2,1)} %collective-permute-done.11), channel_id=1, source_target_pairs={{2,0},{4,2},{6,4},{8,6},{10,8},{12,10},{14,12},{0,14},{3,1},{5,3},... | collective-permute-start | bytes 2261000 | tf_op jit(solution)/shard_map/ppermute | solution.py:13
  189.6 29.7 %collective-permute-start.23 = (bf16[1,23,128,128]{3,2,1,0:T(8,128)(2,1)}, bf16[1,23,128,128]{3,2,1,0:T(8,128)(2,1)S(1)}, u32[]{:S(2)}, u32[]{:S(2)}) collective-permute-start(bf16[1,23,128,128]{3,2,1,0:T(8,128)(2,1)} %collective-permute-done.15), channel_id=1, source_target_pairs={{14,0},{0,2},{2,4},{4,6},{6,8},{8,10},{10,12},{12,14},{15,1},{1,3}... | collective-permute-start | bytes 2261000 | tf_op jit(solution)/shard_map/ppermute | solution.py:13
  (11 other events, 34.2 us)
Sparse Core Ops, SparseCore 0:
  22.1 6.9 all-gather.1
where the time goes:
time: 243 us; the launch traced here: 242 us
  local copies, waits for them, and re-layouts  80.4 us (33%)
  waiting for transfers between devices  69.6 us (29%)
  starting transfers between devices  42.1 us (17%)
  matrix products  25 us (10%)
  between operations  15.6 us (6%)
  other arithmetic  7.19 us (3%)
    ppermute x24, waiting for transfers between devices, shifted(): return lax.ppermute(block, axis, route)  69.5 us
    ppermute x24, starting transfers between devices, shifted(): return lax.ppermute(block, axis, route)  42.1 us
    dot_general x7, matrix products, accumulate(): jnp.einsum('skab,skbc->sac', left_blocks, right_blocks, preferred_element...  25 us
    gather x7, local copies, waits for them, and re-layouts, accumulate(): right_blocks = rem_blocks[jnp.where(keep_mask, right_idx, rem_zero)]  16.9 us
    gather x7, local copies, waits for them, and re-layouts, accumulate(): left_blocks = own_blocks[jnp.where(keep_mask, left_idx, own_zero)]  16.9 us
    gather x14, local copies, waits for them, and re-layouts, accumulate(): left_idx = own_table[safe_rows[:, None], block_k[None, :]]  14.7 us
    gather x14, local copies, waits for them, and re-layouts, accumulate(): right_idx = rem_table[panel_rows[None, :], local_cols[:, None]]  14.7 us
    concatenate x8, local copies, waits for them, and re-layouts, with_zero(): jnp.concatenate([blocks, jnp.zeros((1,) + blocks.shape[1:], blocks.dtype)...  5.45 us
  transfers between devices with their start and end apart: 25, of which 10 were waited for; matrix products, arithmetic and copies ran while one was open for 26% of the time, Pallas kernels for 0%

commit v1 on v0

v1 whole, which is shorter than its diff:
```python
import functools

import jax
import jax.numpy as jnp
from jax import lax
from jax.experimental import pallas as pl
from jax.experimental.pallas import tpu as pltpu
from jax.sharding import PartitionSpec as P

BLK = 128
BR = 3
HB = 7
WIDTH = 2 * HB + 1
LOW, HIGH = -HB, BR - 1 + HB
NCOL = 9

CROSS = {
    (1, 0): [(3, -4), (3, -2), (5, -2), (4, -2)],
    (1, 1): [(3, -3)],
    (-1, 0): [(-1, 6), (-1, 4), (-3, 4)],
    (-1, 1): [(-1, 5), (-1, 3)],
}
SIZES = {1: 12, -1: 12, 2: 5, -2: 5, 3: 1, -3: 1}


def sent_positions(distance, parity):
    rows = [3 * distance + i for i in range(BR)]
    found = []
    for k in rows:
        for j in range(LOW, HIGH + 1):
            if j % 2 != parity or not LOW <= k <= HIGH:
                continue
            if (distance > 0 and j >= k) or (distance < 0 and j <= k):
                found.append((k, j))
    found += CROSS.get((distance, parity), [])
    return found


def own_parity():
    return (lax.axis_index("row") + lax.axis_index("col")) % 2


def first_column(parity):
    return LOW if parity == 1 else LOW + 1


def slot_position(rows_ref, cols_ref, slot, panel, nblocks):
    row = rows_ref[0, slot] - panel * BR
    band = cols_ref[0, slot] - rows_ref[0, slot] + HB
    band = jnp.where(band < 0, band + nblocks, band)
    band = jnp.where(band >= nblocks, band - nblocks, band)
    return row, band


def pack_kernel(nblocks, slots, rows_ref, cols_ref, counts_ref, values_ref, *rest):
    out_refs = dict(zip((1, -1, 2, -2, 3, -3), rest[:6]))
    left_ref, held, table, sem = rest[6:]
    panel = lax.axis_index("row")
    parity = own_parity()
    load = pltpu.make_async_copy(values_ref.at[0], held.at[pl.ds(0, slots)], sem)
    load.start()
    held[slots] = jnp.zeros((BLK, BLK), held.dtype)
    for i in range(BR * WIDTH + 1):
        table[i] = slots
    count = counts_ref[0, 0]
    for m in range(slots):
        row, band = slot_position(rows_ref, cols_ref, m, panel, nblocks)
        table[jnp.where(m < count, row * WIDTH + band, BR * WIDTH)] = m
    load.wait()

    for mine in (0, 1):

        @pl.when(parity == mine)
        def _(mine=mine):
            for distance, ref in out_refs.items():
                wanted = sent_positions(distance, (mine + distance) % 2)
                for n in range(SIZES[distance]):
                    if n < len(wanted):
                        k, j = wanted[n]
                        at = (k - 3 * distance) * WIDTH + j - k + HB
                        ref[n] = held[table[at]]
                    else:
                        ref[n] = jnp.zeros((BLK, BLK), ref.dtype)
            for i in range(BR):
                for n in range(NCOL):
                    j = first_column(mine) + 2 * n
                    rows, cols = pl.ds(i * BLK, BLK), pl.ds(n * BLK, BLK)
                    if abs(j - i) <= HB:
                        left_ref[rows, cols] = held[table[i * WIDTH + j - i + HB]]
                    else:
                        left_ref[rows, cols] = jnp.zeros((BLK, BLK), left_ref.dtype)


def find_block(parity, k, j):
    if abs(k - j) > HB:
        return None
    if 0 <= k < BR:
        return ("left", parity == j % 2), (k, (j - first_column(j % 2)) // 2), False
    if 0 <= j < BR:
        return ("left", parity == k % 2), (j, (k - first_column(k % 2)) // 2), True
    for a, b, flip in ((k, j, False), (j, k, True)):
        for distance in SIZES:
            wanted = sent_positions(distance, b % 2)
            if (a, b) in wanted:
                return (distance, parity == b % 2), wanted.index((a, b)), flip
    raise AssertionError((k, j))


def multiply_kernel(nblocks, slots, rows_ref, cols_ref, counts_ref, *rest):
    names = [("left", True), ("left", False)]
    names += [(d, own) for own in (True, False) for d in (1, -1, 2, -2)]
    names += [(3, True), (-3, True)]
    refs = dict(zip(names, rest[: len(names)]))
    out_ref, right, made, sems = rest[len(names) :]
    panel = lax.axis_index("row")
    parity = own_parity()
    zero = jnp.zeros((BLK, BLK), right.dtype)
    made[BR * NCOL] = jnp.zeros((BLK, BLK), made.dtype)

    def read(source, place):
        if source[0] == "left":
            i, n = place
            return refs[source][pl.ds(i * BLK, BLK), pl.ds(n * BLK, BLK)]
        return refs[source][place]

    def one_parity(mine):
        columns = [j for j in range(LOW, HIGH + 1) if j % 2 == mine]
        for pair in range(0, len(columns), 2):
            js = columns[pair : pair + 2]
            total = None
            for own in (True, False):
                kind = mine if own else 1 - mine
                ks = [
                    k
                    for k in range(max(LOW, js[0] - HB), min(HIGH, js[-1] + HB) + 1)
                    if k % 2 == kind
                ]
                side = 0 if own else 1
                for x, k in enumerate(ks):
                    for y, j in enumerate(js):
                        found = find_block(mine, k, j)
                        if found is None:
                            block = zero
                        else:
                            source, place, flip = found
                            block = read(source, place)
                            block = block.T if flip else block
                        right[pair // 2, side, pl.ds(x * BLK, BLK), pl.ds(y * BLK, BLK)] = block
                n0 = (ks[0] - first_column(kind)) // 2
                part = jnp.dot(
                    refs[("left", own)][:, pl.ds(n0 * BLK, len(ks) * BLK)],
                    right[pair // 2, side, pl.ds(0, len(ks) * BLK), pl.ds(0, len(js) * BLK)],
                    preferred_element_type=jnp.float32,
                )
                total = part if total is None else total + part
            for i in range(BR):
                for y in range(len(js)):
                    made[i * NCOL + pair + y] = total[i * BLK : (i + 1) * BLK, y * BLK : (y + 1) * BLK]

    for mine in (0, 1):
        pl.when(parity == mine)(functools.partial(one_parity, mine))

    count = counts_ref[0, 0]
    copies = []
    for m in range(slots):
        row, band = slot_position(rows_ref, cols_ref, m, panel, nblocks)
        at = jnp.where(m < count, row * NCOL + (row + band) // 2, BR * NCOL)
        copy = pltpu.make_async_copy(made.at[at], out_ref.at[0, m], sems.at[m])
        copy.start()
        copies.append(copy)
    for copy in copies:
        copy.wait()


def local(values, block_rows, block_cols, counts):
    slots = values.shape[1]
    row_count, col_count = lax.axis_size("row"), lax.axis_size("col")
    nblocks = BR * row_count
    smem = pl.BlockSpec(memory_space=pltpu.SMEM)
    vmem = pl.BlockSpec(memory_space=pltpu.VMEM)
    hbm = pl.BlockSpec(memory_space=pl.ANY)
    order = (1, -1, 2, -2, 3, -3)
    packed = pl.pallas_call(
        functools.partial(pack_kernel, nblocks, slots),
        out_shape=[jax.ShapeDtypeStruct((SIZES[d], BLK, BLK), values.dtype) for d in order]
        + [jax.ShapeDtypeStruct((BR * BLK, NCOL * BLK), values.dtype)],
        in_specs=[smem, smem, smem, hbm],
        out_specs=[vmem] * 7,
        scratch_shapes=[
            pltpu.VMEM((slots + 1, BLK, BLK), values.dtype),
            pltpu.SMEM((BR * WIDTH + 1,), jnp.int32),
            pltpu.SemaphoreType.DMA,
        ],
        name="pack",
    )(block_rows, block_cols, counts, values)
    messages, left = dict(zip(order, packed[:6])), packed[6]

    def towards(distance):
        pairs = []
        for r in range(row_count):
            for c in range(col_count):
                if abs(distance) == 3 and (r + c) % 2 == 0:
                    continue
                pairs.append((((r + distance) % row_count) * col_count + c, r * col_count + c))
        return lax.ppermute(messages[distance], ("row", "col"), pairs)

    def swapped(block):
        return lax.ppermute(block, "col", [(0, 1), (1, 0)])

    got = {d: towards(d) for d in order}
    other = {d: swapped(got[d]) for d in (1, -1, 2, -2)}
    left_other = swapped(left)
    return pl.pallas_call(
        functools.partial(multiply_kernel, nblocks, slots),
        out_shape=jax.ShapeDtypeStruct(values.shape, jnp.float32),
        in_specs=[smem, smem, smem] + [vmem] * 12,
        out_specs=hbm,
        scratch_shapes=[
            pltpu.VMEM((5, 2, 8 * BLK, 2 * BLK), values.dtype),
            pltpu.VMEM((BR * NCOL + 1, BLK, BLK), jnp.float32),
            pltpu.SemaphoreType.DMA((slots,)),
        ],
        compiler_params=pltpu.CompilerParams(vmem_limit_bytes=32 * 2**20),
        name="multiply",
    )(
        block_rows, block_cols, counts, left, left_other,
        *[got[d] for d in (1, -1, 2, -2)], *[other[d] for d in (1, -1, 2, -2)], got[3], got[-3],
    )


def solution(mesh):
    return jax.shard_map(
        local,
        mesh=mesh,
        in_specs=(
            P(("parts", "row"), "col", None, None),
            P(("parts", "row"), "col"),
            P(("parts", "row"), "col"),
            P(("parts", "row"), "col"),
        ),
        out_specs=P(("parts", "row"), "col", None, None),
        check_vma=False,
    )
```

time: 243 us -> 52.1 us (0.21)
  local copies, waits for them, and re-layouts: 80.4 us -> 2.47 us
  waiting for transfers between devices: 69.6 us -> 22.2 us
  matrix products: 25 us -> 0 us
  starting transfers between devices: 42.1 us -> 19.2 us
  between operations: 15.6 us -> 0.7 us
  other arithmetic: 7.19 us -> 0 us
  Pallas kernels: 0 us -> 7.05 us
    gather x43 -> x0, local copies, waits for them, and re-layouts: 63.9 us -> none  [the longest x7 16.9 us: accumulate(): right_blocks = rem_blocks[jnp.where(keep_mask, right_idx, rem_zero)]]
    ppermute x24 -> x11, waiting for transfers between devices: 69.5 us -> 22.2 us  [the longest x6 21.2 us: towards(): return lax.ppermute(messages[distance], ('row', 'col'), pairs)]
    dot_general x7 -> x0, matrix products: 25 us -> none  [accumulate(): jnp.einsum('skab,skbc->sac', left_blocks, right_blocks, preferred_element...]
    ppermute x24 -> x11, starting transfers between devices: 42.1 us -> 19.2 us  [the longest x6 15.2 us: towards(): return lax.ppermute(messages[distance], ('row', 'col'), pairs)]
    pallas_call x0 -> x2, Pallas kernels: none -> 7.05 us  [the longest x1 3.72 us: local(): pl.pallas_call(functools.partial(multiply_kernel, nblocks, slots), out_sh...]
    concatenate x16 -> x0, local copies, waits for them, and re-layouts: 6.22 us -> none  [the longest x8 5.45 us: with_zero(): jnp.concatenate([blocks, jnp.zeros((1,) + blocks.shape[1:], blocks.dtype)...]
    select_n x9 -> x0, other arithmetic: 5.42 us -> none  [the longest x8 5.31 us: build_table(): table_flat.at[target_ids]]
    scatter x8 -> x0, local copies, waits for them, and re-layouts: 5.41 us -> none  [build_table(): table_flat.at[target_ids]]
  transfers between devices with their start and end apart: 25 -> 11, of which waited for: 10 -> 6; matrix products, arithmetic and copies ran while one was open for 26% -> 0% of each run, Pallas kernels for 0% -> 0%
where the time goes in v1:
time: 52.1 us; the launch traced here: 51.6 us
  waiting for transfers between devices  22.2 us (43%)
  starting transfers between devices  19.2 us (37%)
  Pallas kernels  7.05 us (14%)
  local copies, waits for them, and re-layouts  2.47 us (5%)
  between operations  0.7 us (1%)
    ppermute x6, waiting for transfers between devices, towards(): return lax.ppermute(messages[distance], ('row', 'col'), pairs)  21.2 us
    ppermute x6, starting transfers between devices, towards(): return lax.ppermute(messages[distance], ('row', 'col'), pairs)  15.2 us
    ppermute x5, starting transfers between devices, swapped(): return lax.ppermute(block, 'col', [(0, 1), (1, 0)])  4 us
    pallas_call x1, Pallas kernels, local(): pl.pallas_call(functools.partial(multiply_kernel, nblocks, slots), out_sh...  3.72 us
    pallas_call x1, Pallas kernels, local(): pl.pallas_call(functools.partial(pack_kernel, nblocks, slots), out_shape=...  3.33 us
    unnamed x6, local copies, waits for them, and re-layouts  2.47 us
  transfers between devices with their start and end apart: 11, of which 6 were waited for; matrix products, arithmetic and copies ran while one was open for 0% of the time, Pallas kernels for 0%

profile of v1, /device:TPU:0, one launch (start us, length us, event | category | flops | bytes accessed | tf_op | source)
XLA Modules:
  0.0 51.6 jit_solution(8543000674705152247)
XLA Ops:
  0.7 3.3 %pack.1 = (bf16[12,128,128]{2,1,0:T(8,128)(2,1)}, bf16[12,128,128]{2,1,0:T(8,128)(2,1)}, bf16[5,128,128]{2,1,0:T(8,128)(2,1)}, bf16[5,128,128]{2,1,0:T(8,128)(2,...) custom-call(s32[1,23]{1,0:T(1,128)} %rows_ref.3, s32[1,23]{1,0:T(1,128)} %cols_ref.3, ...), custom_call_target="tpu_custom_call" | custom-call | tf_op jit(solution)/shard_map/pack/pallas_call | solution.py:183
  4.0 0.5 %collective-permute-start = (bf16[384,1152]{1,0:T(8,128)(2,1)}, bf16[384,1152]{1,0:T(8,128)(2,1)S(1)}, u32[]{:S(2)}, u32[]{:S(2)}) collective-permute-start(bf16[384,1152]{1,0:T(8,128)(2,1)} %get-tuple-element.12.rest_0_), channel_id=1, source_target_pairs={{0,1},{1,0},{2,3},{3,2},{4,5},{5,4},{6,7},{7,6},{8,9},{9,8},{10,11... | collective-permute-start | bytes 2654216 | tf_op jit(solution)/shard_map/ppermute | solution.py:208
  4.5 5.6 %collective-permute-start.1 = (bf16[12,128,128]{2,1,0:T(8,128)(2,1)}, bf16[12,128,128]{2,1,0:T(8,128)(2,1)S(1)}, u32[]{:S(2)}, u32[]{:S(2)}) collective-permute-start(bf16[12,128,128]{2,1,0:T(8,128)(2,1)} %get-tuple-element.13), channel_id=1, source_target_pairs={{2,0},{3,1},{4,2},{5,3},{6,4},{7,5},{8,6},{9,7},{10,8},{11,9},{12,... | collective-permute-start | bytes 1179656 | tf_op jit(solution)/shard_map/ppermute | solution.py:205
  10.1 0.0 collective-permute-start.2
  10.1 15.3 %collective-permute-done.1.rest_2_ = bf16[12,128,128]{2,1,0:T(8,128)(2,1)S(1)} collective-permute-done((bf16[12,128,128]{2,1,0:T(8,128)(2,1)}, bf16[12,128,128]{2,1,0:T(8,128)(2,1)S(1)}, u32[]{:S(2)}, u32[]{:S(2)}) %collective-permute-start.1) | collective-permute-done | bytes 393248 | tf_op jit(solution)/shard_map/ppermute | solution.py:205
  25.4 0.3 collective-permute-done.2.rest_3_
  25.7 0.2 collective-permute-start.6
  25.9 5.4 %collective-permute-start.9 = (bf16[1,128,128]{2,1,0:T(8,128)(2,1)}, bf16[1,128,128]{2,1,0:T(8,128)(2,1)S(1)}, u32[]{:S(2)}, u32[]{:S(2)}) collective-permute-start(bf16[1,128,128]{2,1,0:T(8,128)(2,1)} %get-tuple-element.17), channel_id=1, source_target_pairs={{7,1},{8,2},{11,5},{12,6},{15,9},{0,10},{3,13},{4,14},{23,17},{24,... | collective-permute-start | bytes 98312 | tf_op jit(solution)/shard_map/ppermute | solution.py:205
  31.3 1.3 %collective-permute-start.10 = (bf16[1,128,128]{2,1,0:T(8,128)(2,1)}, bf16[1,128,128]{2,1,0:T(8,128)(2,1)S(1)}, u32[]{:S(2)}, u32[]{:S(2)}) collective-permute-start(bf16[1,128,128]{2,1,0:T(8,128)(2,1)} %get-tuple-element.18), channel_id=1, source_target_pairs={{11,1},{12,2},{15,5},{0,6},{3,9},{4,10},{7,13},{8,14},{27,17},{28,... | collective-permute-start | bytes 98312 | tf_op jit(solution)/shard_map/ppermute | solution.py:205
  32.6 0.6 %collective-permute-done.9.rest_10_ = bf16[1,128,128]{2,1,0:T(8,128)(2,1)S(1)} collective-permute-done((bf16[1,128,128]{2,1,0:T(8,128)(2,1)}, bf16[1,128,128]{2,1,0:T(8,128)(2,1)S(1)}, u32[]{:S(2)}, u32[]{:S(2)}) %collective-permute-start.9) | collective-permute-done | bytes 32800 | tf_op jit(solution)/shard_map/ppermute | solution.py:205
  33.2 1.4 %collective-permute-start.3 = (bf16[5,128,128]{2,1,0:T(8,128)(2,1)}, bf16[5,128,128]{2,1,0:T(8,128)(2,1)S(1)}, u32[]{:S(2)}, u32[]{:S(2)}) collective-permute-start(bf16[5,128,128]{2,1,0:T(8,128)(2,1)} %get-tuple-element.15), channel_id=1, source_target_pairs={{4,0},{5,1},{6,2},{7,3},{8,4},{9,5},{10,6},{11,7},{12,8},{13,9},{1... | collective-permute-start | bytes 491528 | tf_op jit(solution)/shard_map/ppermute | solution.py:205
  34.7 1.5 %collective-permute-start.4 = (bf16[5,128,128]{2,1,0:T(8,128)(2,1)}, bf16[5,128,128]{2,1,0:T(8,128)(2,1)S(1)}, u32[]{:S(2)}, u32[]{:S(2)}) collective-permute-start(bf16[5,128,128]{2,1,0:T(8,128)(2,1)} %get-tuple-element.16), channel_id=1, source_target_pairs={{12,0},{13,1},{14,2},{15,3},{0,4},{1,5},{2,6},{3,7},{4,8},{5,9},{6... | collective-permute-start | bytes 491528 | tf_op jit(solution)/shard_map/ppermute | solution.py:205
  36.1 2.7 %collective-permute-done.3.rest_4_ = bf16[5,128,128]{2,1,0:T(8,128)(2,1)S(1)} collective-permute-done((bf16[5,128,128]{2,1,0:T(8,128)(2,1)}, bf16[5,128,128]{2,1,0:T(8,128)(2,1)S(1)}, u32[]{:S(2)}, u32[]{:S(2)}) %collective-permute-start.3) | collective-permute-done | bytes 163872 | tf_op jit(solution)/shard_map/ppermute | solution.py:205
  38.8 2.7 %collective-permute-start.7 = (bf16[5,128,128]{2,1,0:T(8,128)(2,1)S(1)}, bf16[5,128,128]{2,1,0:T(8,128)(2,1)S(1)}, u32[]{:S(2)}, u32[]{:S(2)}) collective-permute-start(bf16[5,128,128]{2,1,0:T(8,128)(2,1)S(1)} %collective-permute-done.3.rest_4_), channel_id=1, source_target_pairs={{0,1},{1,0},{2,3},{3,2},{4,5},{5,4},{6,7},{7,6},{8,9},{9,8},{10,11... | collective-permute-start | bytes 491528 | tf_op jit(solution)/shard_map/ppermute | solution.py:208
  41.5 2.3 %collective-permute-done.4.rest_5_ = bf16[5,128,128]{2,1,0:T(8,128)(2,1)S(1)} collective-permute-done((bf16[5,128,128]{2,1,0:T(8,128)(2,1)}, bf16[5,128,128]{2,1,0:T(8,128)(2,1)S(1)}, u32[]{:S(2)}, u32[]{:S(2)}) %collective-permute-start.4) | collective-permute-done | bytes 163872 | tf_op jit(solution)/shard_map/ppermute | solution.py:205
  43.8 0.5 %collective-permute-start.8 = (bf16[5,128,128]{2,1,0:T(8,128)(2,1)S(1)}, bf16[5,128,128]{2,1,0:T(8,128)(2,1)S(1)}, u32[]{:S(2)}, u32[]{:S(2)}) collective-permute-start(bf16[5,128,128]{2,1,0:T(8,128)(2,1)S(1)} %collective-permute-done.4.rest_5_), channel_id=1, source_target_pairs={{0,1},{1,0},{2,3},{3,2},{4,5},{5,4},{6,7},{7,6},{8,9},{9,8},{10,11... | collective-permute-start | bytes 491528 | tf_op jit(solution)/shard_map/ppermute | solution.py:208
  44.3 1.0 %collective-permute-done.8.rest_9_ = bf16[5,128,128]{2,1,0:T(8,128)(2,1)S(1)} collective-permute-done((bf16[5,128,128]{2,1,0:T(8,128)(2,1)S(1)}, bf16[5,128,128]{2,1,0:T(8,128)(2,1)S(1)}, u32[]{:S(2)}, u32[]{:S(2)}) %collective-permute-start.8) | collective-permute-done | bytes 163872 | tf_op jit(solution)/shard_map/ppermute | solution.py:208
  45.4 0.0 collective-permute-done.5.rest_6_
  45.4 0.0 collective-permute-done.6.rest_7_
  45.4 0.0 copy-start
  45.4 1.2 %copy-done = bf16[384,1152]{1,0:T(8,128)(2,1)S(1)} copy-done((bf16[384,1152]{1,0:T(8,128)(2,1)S(1)}, bf16[384,1152]{1,0:T(8,128)(2,1)}, u32[]{:S(2)}) %copy-start) | copy-done | bytes 884760
  46.6 0.7 %copy-done.1 = s32[1,23]{1,0:T(1,128)S(1)} copy-done((s32[1,23]{1,0:T(1,128)S(1)}, s32[1,23]{1,0:T(1,128)}, u32[]{:S(2)}) %copy-start.1) | copy-done | bytes 116
  47.2 0.7 %copy-done.2 = s32[1,23]{1,0:T(1,128)S(1)} copy-done((s32[1,23]{1,0:T(1,128)S(1)}, s32[1,23]{1,0:T(1,128)}, u32[]{:S(2)}) %copy-start.2) | copy-done | bytes 116
  47.9 3.7 %multiply.1 = f32[1,23,128,128]{3,2,1,0:T(8,128)} custom-call(s32[1,23]{1,0:T(1,128)S(1)} %copy-done.1, s32[1,23]{1,0:T(1,128)S(1)} %copy-done.2, s32[1,1]{1,0:T(1,128)S(6)} %copy.5.counts_ref, bf16[384,1152]{1,0:T(8,128)(2,1)S(1)} %copy-done, bf16[384,1152]{1,0:T(8,128)(2,1)S(1)} %collective-permute-done.rest_1_, ...), custom_call_target="tpu_custom_call" | custom-call | tf_op jit(solution)/shard_map/multiply/pallas_call | solution.py:213
  (6 shorter events, 0.0 us)
Async XLA Ops:
  4.0 41.4 %collective-permute-start = (bf16[384,1152]{1,0:T(8,128)(2,1)}, bf16[384,1152]{1,0:T(8,128)(2,1)S(1)}, u32[]{:S(2)}, u32[]{:S(2)}) collective-permute-start(bf16[384,1152]{1,0:T(8,128)(2,1)} %get-tuple-element.12.rest_0_), channel_id=1, source_target_pairs={{0,1},{1,0},{2,3},{3,2},{4,5},{5,4},{6,7},{7,6},{8,9},{9,8},{10,11... | collective-permute-start | bytes 2654216 | tf_op jit(solution)/shard_map/ppermute | solution.py:208
  4.5 20.9 %collective-permute-start.1 = (bf16[12,128,128]{2,1,0:T(8,128)(2,1)}, bf16[12,128,128]{2,1,0:T(8,128)(2,1)S(1)}, u32[]{:S(2)}, u32[]{:S(2)}) collective-permute-start(bf16[12,128,128]{2,1,0:T(8,128)(2,1)} %get-tuple-element.13), channel_id=1, source_target_pairs={{2,0},{3,1},{4,2},{5,3},{6,4},{7,5},{8,6},{9,7},{10,8},{11,9},{12,... | collective-permute-start | bytes 1179656 | tf_op jit(solution)/shard_map/ppermute | solution.py:205
  10.1 15.6 %collective-permute-start.2 = (bf16[12,128,128]{2,1,0:T(8,128)(2,1)}, bf16[12,128,128]{2,1,0:T(8,128)(2,1)S(1)}, u32[]{:S(2)}, u32[]{:S(2)}) collective-permute-start(bf16[12,128,128]{2,1,0:T(8,128)(2,1)} %get-tuple-element.14), channel_id=1, source_target_pairs={{14,0},{15,1},{0,2},{1,3},{2,4},{3,5},{4,6},{5,7},{6,8},{7,9},{8,1... | collective-permute-start | bytes 1179656 | tf_op jit(solution)/shard_map/ppermute | solution.py:205
  25.4 20.0 %collective-permute-start.5 = (bf16[12,128,128]{2,1,0:T(8,128)(2,1)S(1)}, bf16[12,128,128]{2,1,0:T(8,128)(2,1)S(1)}, u32[]{:S(2)}, u32[]{:S(2)}) collective-permute-start(bf16[12,128,128]{2,1,0:T(8,128)(2,1)S(1)} %collective-permute-done.1.rest_2_), channel_id=1, source_target_pairs={{0,1},{1,0},{2,3},{3,2},{4,5},{5,4},{6,7},{7,6},{8,9},{9,8},{10,11... | collective-permute-start | bytes 1179656 | tf_op jit(solution)/shard_map/ppermute | solution.py:208
  25.7 19.7 %collective-permute-start.6 = (bf16[12,128,128]{2,1,0:T(8,128)(2,1)S(1)}, bf16[12,128,128]{2,1,0:T(8,128)(2,1)S(1)}, u32[]{:S(2)}, u32[]{:S(2)}) collective-permute-start(bf16[12,128,128]{2,1,0:T(8,128)(2,1)S(1)} %collective-permute-done.2.rest_3_), channel_id=1, source_target_pairs={{0,1},{1,0},{2,3},{3,2},{4,5},{5,4},{6,7},{7,6},{8,9},{9,8},{10,11... | collective-permute-start | bytes 1179656 | tf_op jit(solution)/shard_map/ppermute | solution.py:208
  25.9 7.3 %collective-permute-start.9 = (bf16[1,128,128]{2,1,0:T(8,128)(2,1)}, bf16[1,128,128]{2,1,0:T(8,128)(2,1)S(1)}, u32[]{:S(2)}, u32[]{:S(2)}) collective-permute-start(bf16[1,128,128]{2,1,0:T(8,128)(2,1)} %get-tuple-element.17), channel_id=1, source_target_pairs={{7,1},{8,2},{11,5},{12,6},{15,9},{0,10},{3,13},{4,14},{23,17},{24,... | collective-permute-start | bytes 98312 | tf_op jit(solution)/shard_map/ppermute | solution.py:205
  31.3 3.3 %collective-permute-start.10 = (bf16[1,128,128]{2,1,0:T(8,128)(2,1)}, bf16[1,128,128]{2,1,0:T(8,128)(2,1)S(1)}, u32[]{:S(2)}, u32[]{:S(2)}) collective-permute-start(bf16[1,128,128]{2,1,0:T(8,128)(2,1)} %get-tuple-element.18), channel_id=1, source_target_pairs={{11,1},{12,2},{15,5},{0,6},{3,9},{4,10},{7,13},{8,14},{27,17},{28,... | collective-permute-start | bytes 98312 | tf_op jit(solution)/shard_map/ppermute | solution.py:205
  33.2 5.5 %collective-permute-start.3 = (bf16[5,128,128]{2,1,0:T(8,128)(2,1)}, bf16[5,128,128]{2,1,0:T(8,128)(2,1)S(1)}, u32[]{:S(2)}, u32[]{:S(2)}) collective-permute-start(bf16[5,128,128]{2,1,0:T(8,128)(2,1)} %get-tuple-element.15), channel_id=1, source_target_pairs={{4,0},{5,1},{6,2},{7,3},{8,4},{9,5},{10,6},{11,7},{12,8},{13,9},{1... | collective-permute-start | bytes 491528 | tf_op jit(solution)/shard_map/ppermute | solution.py:205
  34.7 9.1 %collective-permute-start.4 = (bf16[5,128,128]{2,1,0:T(8,128)(2,1)}, bf16[5,128,128]{2,1,0:T(8,128)(2,1)S(1)}, u32[]{:S(2)}, u32[]{:S(2)}) collective-permute-start(bf16[5,128,128]{2,1,0:T(8,128)(2,1)} %get-tuple-element.16), channel_id=1, source_target_pairs={{12,0},{13,1},{14,2},{15,3},{0,4},{1,5},{2,6},{3,7},{4,8},{5,9},{6... | collective-permute-start | bytes 491528 | tf_op jit(solution)/shard_map/ppermute | solution.py:205
  38.8 5.6 %collective-permute-start.7 = (bf16[5,128,128]{2,1,0:T(8,128)(2,1)S(1)}, bf16[5,128,128]{2,1,0:T(8,128)(2,1)S(1)}, u32[]{:S(2)}, u32[]{:S(2)}) collective-permute-start(bf16[5,128,128]{2,1,0:T(8,128)(2,1)S(1)} %collective-permute-done.3.rest_4_), channel_id=1, source_target_pairs={{0,1},{1,0},{2,3},{3,2},{4,5},{5,4},{6,7},{7,6},{8,9},{9,8},{10,11... | collective-permute-start | bytes 491528 | tf_op jit(solution)/shard_map/ppermute | solution.py:208
  43.8 1.6 %collective-permute-start.8 = (bf16[5,128,128]{2,1,0:T(8,128)(2,1)S(1)}, bf16[5,128,128]{2,1,0:T(8,128)(2,1)S(1)}, u32[]{:S(2)}, u32[]{:S(2)}) collective-permute-start(bf16[5,128,128]{2,1,0:T(8,128)(2,1)S(1)} %collective-permute-done.4.rest_5_), channel_id=1, source_target_pairs={{0,1},{1,0},{2,3},{3,2},{4,5},{5,4},{6,7},{7,6},{8,9},{9,8},{10,11... | collective-permute-start | bytes 491528 | tf_op jit(solution)/shard_map/ppermute | solution.py:208
  45.4 1.2 %copy-start = (bf16[384,1152]{1,0:T(8,128)(2,1)S(1)}, bf16[384,1152]{1,0:T(8,128)(2,1)}, u32[]{:S(2)}) copy-start(bf16[384,1152]{1,0:T(8,128)(2,1)} %get-tuple-element.12.rest_0_) | copy-start | bytes 2654212
  46.6 0.7 %copy-start.1 = (s32[1,23]{1,0:T(1,128)S(1)}, s32[1,23]{1,0:T(1,128)}, u32[]{:S(2)}) copy-start(s32[1,23]{1,0:T(1,128)} %rows_ref.3) | copy-start | bytes 280
  47.2 0.7 %copy-start.2 = (s32[1,23]{1,0:T(1,128)S(1)}, s32[1,23]{1,0:T(1,128)}, u32[]{:S(2)}) copy-start(s32[1,23]{1,0:T(1,128)} %cols_ref.3) | copy-start | bytes 280

commit v2 on v1

v2 whole, which is shorter than its diff:
```python
import functools

import jax
import jax.numpy as jnp
from jax import lax
from jax.experimental import pallas as pl
from jax.experimental.pallas import tpu as pltpu
from jax.sharding import PartitionSpec as P

BLK = 128
BR = 3
HB = 7
WIDTH = 2 * HB + 1
LOW, HIGH = -HB, BR - 1 + HB
NCOL = 9
INNER = 6

CROSS = {
    (1, 0): [(3, -4), (3, -2), (5, -2), (4, -2)],
    (1, 1): [(3, -3), (4, -3)],
    (-1, 0): [(-1, 6), (-1, 4)],
    (-1, 1): [(-1, 5), (-1, 3)],
}
SIZES = {-1: 12, 1: 12, -2: 5, 2: 5, -3: 1, 3: 1}
STAGED = 17
VMEM_LIMIT = 12 * 2**20


def sent_positions(distance, parity):
    rows = [3 * distance + i for i in range(BR)]
    found = []
    for k in rows:
        for j in range(LOW, HIGH + 1):
            if j % 2 != parity or not LOW <= k <= HIGH:
                continue
            if (distance > 0 and j >= k) or (distance < 0 and j <= k):
                found.append((k, j))
    found += CROSS.get((distance, parity), [])
    assert len(found) <= SIZES[distance]
    return found


def staged_positions(parity):
    found = []
    for distance in SIZES:
        for n, (k, j) in enumerate(sent_positions(distance, parity)):
            if k % 2 != parity:
                found.append((distance, n, (k, j)))
    assert len(found) <= STAGED
    return found


def columns_of(parity):
    return [j for j in range(LOW, HIGH + 1) if j % 2 == parity]


def own_parity():
    return (lax.axis_index("row") + lax.axis_index("col")) % 2


def for_own_parity(body):
    parity = own_parity()
    for mine in (0, 1):
        pl.when(parity == mine)(functools.partial(body, mine))


def slot_position(rows_ref, cols_ref, slot, panel, nblocks):
    row = rows_ref[0, slot] - panel * BR
    band = cols_ref[0, slot] - rows_ref[0, slot] + HB
    band = jnp.where(band < 0, band + nblocks, band)
    band = jnp.where(band >= nblocks, band - nblocks, band)
    return row, band


def index_copies(hbm_refs, smem_refs, sems):
    return [pltpu.make_async_copy(a, b, sems.at[i]) for i, (a, b) in enumerate(zip(hbm_refs, smem_refs))]


def load_slots(nblocks, slots, index_refs, values_ref, held, table, index, sems, value_sem):
    load = pltpu.make_async_copy(values_ref.at[0], held.at[pl.ds(0, slots)], value_sem)
    load.start()
    copies = index_copies(index_refs, index, sems)
    for copy in copies:
        copy.start()
    held[slots] = jnp.zeros((BLK, BLK), held.dtype)
    for i in range(BR * WIDTH + 1):
        table[i] = slots
    for copy in copies:
        copy.wait()
    panel = lax.axis_index("row")
    for m in reversed(range(slots)):
        row, band = slot_position(*index, m, panel, nblocks)
        table[jnp.where(row >= 0, row * WIDTH + band, BR * WIDTH)] = m
    load.wait()


def pack_kernel(nblocks, slots, rows_ref, cols_ref, values_ref, *rest):
    out_refs = dict(zip(SIZES, rest[:6]))
    left_ref, held, table, *index, sems, value_sem = rest[6:]
    load_slots(nblocks, slots, (rows_ref, cols_ref), values_ref, held, table, index, sems, value_sem)

    @for_own_parity
    def _(mine):
        for distance, ref in out_refs.items():
            wanted = sent_positions(distance, (mine + distance) % 2)
            for n in range(SIZES[distance]):
                if n < len(wanted):
                    k, j = wanted[n]
                    ref[n] = held[table[(k - 3 * distance) * WIDTH + j - k + HB]]
                else:
                    ref[n] = jnp.zeros((BLK, BLK), ref.dtype)
        columns = columns_of(mine)
        for i in range(BR):
            for n in range(NCOL):
                rows, cols = pl.ds(i * BLK, BLK), pl.ds(n * BLK, BLK)
                if n < len(columns) and abs(columns[n] - i) <= HB:
                    left_ref[rows, cols] = held[table[i * WIDTH + columns[n] - i + HB]]
                else:
                    left_ref[rows, cols] = jnp.zeros((BLK, BLK), left_ref.dtype)


def find_block(parity, k, j):
    if abs(k - j) > HB:
        return None
    if 0 <= k < BR:
        return ("left", parity == j % 2), (k, columns_of(j % 2).index(j)), False
    if 0 <= j < BR:
        return ("left", parity == k % 2), (j, columns_of(k % 2).index(k)), True
    for a, b, flip in ((k, j, False), (j, k, True)):
        for distance in SIZES:
            wanted = sent_positions(distance, b % 2)
            if (a, b) in wanted:
                if b % 2 == parity:
                    return distance, wanted.index((a, b)), flip
                staged = [position for _, _, position in staged_positions(1 - parity)]
                return "staged", staged.index((a, b)), flip
    raise AssertionError((k, j))


def columns_product(refs, right, parity, js):
    total = None
    for own in (True, False):
        kind = parity if own else 1 - parity
        ks = [k for k in columns_of(kind) if js[0] - HB <= k <= js[-1] + HB]
        for x, k in enumerate(ks):
            for y, j in enumerate(js):
                found = find_block(parity, k, j)
                if found is None:
                    block = jnp.zeros((BLK, BLK), right.dtype)
                else:
                    source, place, flip = found
                    if isinstance(place, tuple):
                        block = refs[source][pl.ds(place[0] * BLK, BLK), pl.ds(place[1] * BLK, BLK)]
                    else:
                        block = refs[source][place]
                    block = block.T if flip else block
                right[0 if own else 1, pl.ds(x * BLK, BLK), pl.ds(y * BLK, BLK)] = block
        start = columns_of(kind).index(ks[0])
        part = jnp.dot(
            refs[("left", own)][:, pl.ds(start * BLK, len(ks) * BLK)],
            right[0 if own else 1, pl.ds(0, len(ks) * BLK), pl.ds(0, len(js) * BLK)],
            preferred_element_type=jnp.float32,
        )
        total = part if total is None else total + part
    return total


def inner_kernel(left_ref, left_other_ref, made_ref, right):
    refs = {("left", True): left_ref, ("left", False): left_other_ref}

    @for_own_parity
    def _(mine):
        js = [j for j in columns_of(mine) if 0 <= j < BR]
        total = columns_product(refs, right, mine, js)
        for i in range(BR):
            for y in range(len(js)):
                made_ref[i * 2 + y] = total[i * BLK : (i + 1) * BLK, y * BLK : (y + 1) * BLK]
        if len(js) == 1:
            for i in range(BR):
                made_ref[i * 2 + 1] = jnp.zeros((BLK, BLK), made_ref.dtype)


def stage_kernel(*refs):
    got = dict(zip(SIZES, refs[:4]))
    out_ref = refs[4]

    @for_own_parity
    def _(mine):
        staged = staged_positions(mine)
        for n in range(STAGED):
            if n < len(staged):
                distance, place, _ = staged[n]
                out_ref[n] = got[distance][place]
            else:
                out_ref[n] = jnp.zeros((BLK, BLK), out_ref.dtype)


def multiply_kernel(nblocks, slots, rows_ref, cols_ref, counts_ref, *rest):
    names = [("left", True), ("left", False), *SIZES, "staged"]
    refs = dict(zip(names, rest[: len(names)]))
    inner_ref, out_ref, right, made, zero, slot_of, *index, sems, out_sems = rest[len(names) :]
    copies = index_copies((rows_ref, cols_ref), index, sems)
    for copy in copies:
        copy.start()
    zero[...] = jnp.zeros((BLK, BLK), zero.dtype)
    for i in range(BR * NCOL + 1):
        slot_of[i] = -1
    for copy in copies:
        copy.wait()
    panel = lax.axis_index("row")
    count = counts_ref[0, 0]
    for m in range(slots):
        row, band = slot_position(*index, m, panel, nblocks)
        slot_of[jnp.where(m < count, row * NCOL + (row + band) // 2, BR * NCOL)] = m

        @pl.when(m >= count)
        def _(m=m):
            pltpu.make_async_copy(zero, out_ref.at[0, m], out_sems.at[m]).start()

    def store(block, place):
        slot = slot_of[place]

        @pl.when(slot >= 0)
        def _():
            pltpu.make_async_copy(block, out_ref.at[0, slot], out_sems.at[slot]).start()

    @for_own_parity
    def _(mine):
        columns = columns_of(mine)
        inner = [j for j in columns if 0 <= j < BR]
        for i in range(BR):
            for y, j in enumerate(inner):
                store(inner_ref.at[i * 2 + y], i * NCOL + columns.index(j))
        outer = [j for j in columns if j not in inner]
        for pair in range(0, len(outer), 2):
            js = outer[pair : pair + 2]
            total = columns_product(refs, right.at[pair // 2], mine, js)
            for i in range(BR):
                for y, j in enumerate(js):
                    if abs(i - j) <= HB:
                        place = i * NCOL + columns.index(j)
                        made[place] = total[i * BLK : (i + 1) * BLK, y * BLK : (y + 1) * BLK]
                        store(made.at[place], place)

    for m in range(slots):
        pltpu.make_async_copy(zero, out_ref.at[0, m], out_sems.at[m]).wait()


def local(values, block_rows, block_cols, counts):
    slots = values.shape[1]
    row_count, col_count = lax.axis_size("row"), lax.axis_size("col")
    nblocks = BR * row_count
    smem = pl.BlockSpec(memory_space=pltpu.SMEM)
    vmem = pl.BlockSpec(memory_space=pltpu.VMEM)
    hbm = pl.BlockSpec(memory_space=pltpu.HBM)
    params = pltpu.CompilerParams(vmem_limit_bytes=VMEM_LIMIT)
    values, *places = (pltpu.with_memory_space_constraint(x, pltpu.HBM) for x in (values, block_rows, block_cols))
    index_scratch = [
        pltpu.SMEM((1, slots), jnp.int32),
        pltpu.SMEM((1, slots), jnp.int32),
        pltpu.SemaphoreType.DMA((2,)),
    ]
    def blocks(count, dtype=values.dtype):
        return jax.ShapeDtypeStruct((count, BLK, BLK), dtype)

    def cost(flops, nbytes):
        return pl.CostEstimate(flops=flops, bytes_accessed=nbytes, transcendentals=0)

    *packed, left = pl.pallas_call(
        functools.partial(pack_kernel, nblocks, slots),
        out_shape=[blocks(n) for n in SIZES.values()]
        + [jax.ShapeDtypeStruct((BR * BLK, NCOL * BLK), values.dtype)],
        in_specs=[hbm] * 3,
        out_specs=[vmem] * 7,
        scratch_shapes=[
            pltpu.VMEM((slots + 1, BLK, BLK), values.dtype),
            pltpu.SMEM((BR * WIDTH + 1,), jnp.int32),
            *index_scratch,
            pltpu.SemaphoreType.DMA,
        ],
        compiler_params=params,
        name="pack",
    )(*places, values)
    def towards(distance, message):
        pairs = []
        for r in range(row_count):
            for c in range(col_count):
                if abs(distance) == 3 and (r + c) % 2 == 0:
                    continue
                pairs.append((((r + distance) % row_count) * col_count + c, r * col_count + c))
        return lax.ppermute(message, ("row", "col"), pairs)

    def swapped(block):
        return lax.ppermute(block, "col", [(0, 1), (1, 0)])

    got = [towards(distance, message) for distance, message in zip(SIZES, packed)]
    left_other = swapped(left)
    inner = pl.pallas_call(
        inner_kernel,
        out_shape=blocks(INNER, jnp.float32),
        in_specs=[vmem] * 2,
        out_specs=vmem,
        scratch_shapes=[pltpu.VMEM((2, 9 * BLK, 2 * BLK), values.dtype)],
        compiler_params=params,
        cost_estimate=cost(2 * 3 * 2 * 17 * BLK**3, 4 * values.size * 2),
        name="inner",
    )(left, left_other)
    got = list(lax.optimization_barrier((*got, inner)))
    inner = got.pop()
    staged = swapped(
        pl.pallas_call(
            stage_kernel,
            out_shape=blocks(STAGED),
            in_specs=[vmem] * 4,
            out_specs=vmem,
            compiler_params=params,
            name="stage",
        )(*got[:4])
    )
    return pl.pallas_call(
        functools.partial(multiply_kernel, nblocks, slots),
        out_shape=jax.ShapeDtypeStruct(values.shape, jnp.float32),
        in_specs=[hbm] * 2 + [smem] + [vmem] * 10,
        out_specs=hbm,
        scratch_shapes=[
            pltpu.VMEM((4, 2, 9 * BLK, 2 * BLK), values.dtype),
            pltpu.VMEM((BR * NCOL, BLK, BLK), jnp.float32),
            pltpu.VMEM((BLK, BLK), jnp.float32),
            pltpu.SMEM((BR * NCOL + 1,), jnp.int32),
            *index_scratch,
            pltpu.SemaphoreType.DMA((slots,)),
        ],
        compiler_params=params,
        name="multiply",
    )(*places, counts, left, left_other, *got, staged, inner)


def solution(mesh):
    return jax.shard_map(
        local,
        mesh=mesh,
        in_specs=(
            P(("parts", "row"), "col", None, None),
            P(("parts", "row"), "col"),
            P(("parts", "row"), "col"),
            P(("parts", "row"), "col"),
        ),
        out_specs=P(("parts", "row"), "col", None, None),
        check_vma=False,
    )
```

time: 52.1 us -> 34.1 us (0.65)
  the two profiles are of different devices: /device:TPU:0 before, /device:TPU:3 now
where the time goes in v2:
time: 34.1 us; the launch traced here: 33.9 us
  starting transfers between devices  22.9 us (67%)
  Pallas kernels  5.54 us (16%)
  waiting for transfers between devices  4.77 us (14%)
  between operations  0.7 us (2%)
    ppermute x6, starting transfers between devices, towards(): return lax.ppermute(message, ('row', 'col'), pairs)  14.9 us
    ppermute x2, starting transfers between devices, swapped(): return lax.ppermute(block, 'col', [(0, 1), (1, 0)])  8.03 us
    ppermute x6, waiting for transfers between devices, towards(): return lax.ppermute(message, ('row', 'col'), pairs)  3.83 us
    pallas_call x1, Pallas kernels, local(): pl.pallas_call(functools.partial(multiply_kernel, nblocks, slots), out_sh...  3.39 us
    pallas_call x1, Pallas kernels, local(): pl.pallas_call(functools.partial(pack_kernel, nblocks, slots), out_shape=...  1.37 us
    ppermute x2, waiting for transfers between devices, swapped(): return lax.ppermute(block, 'col', [(0, 1), (1, 0)])  0.94 us
    pallas_call x1, Pallas kernels, local(): pl.pallas_call(inner_kernel, out_shape=blocks(INNER, jnp.float32), in_spe...  0.74 us
  transfers between devices with their start and end apart: 8, of which 5 were waited for; matrix products, arithmetic and copies ran while one was open for 0% of the time, Pallas kernels for 2%

profile of v2, /device:TPU:3, one launch (start us, length us, event | category | flops | bytes accessed | tf_op | source)
XLA Modules:
  0.0 33.9 jit_solution(17981269849452906624)
XLA Ops:
  0.0 1.4 %pack.1 = (bf16[12,128,128]{2,1,0:T(8,128)(2,1)S(1)}, bf16[12,128,128]{2,1,0:T(8,128)(2,1)S(1)}, bf16[5,128,128]{2,1,0:T(8,128)(2,1)S(1)}, bf16[5,128,128]{2,1,0...) custom-call(s32[1,23]{1,0:T(1,128)} %rows_ref.3, ...), custom_call_target="tpu_custom_call" | custom-call | tf_op jit(solution)/shard_map/pack/pallas_call | solution.py:269
  1.4 0.7 %collective-permute-start = (bf16[384,1152]{1,0:T(8,128)(2,1)S(1)}, bf16[384,1152]{1,0:T(8,128)(2,1)S(1)}, u32[]{:S(2)}, u32[]{:S(2)}) collective-permute-start(bf16[384,1152]{1,0:T(8,128)(2,1)S(1)} %get-tuple-element.19.left_ref.rest_0_), channel_id=1, source_target_pairs={{0,1},{1,0},{2,3},{3,2},{4,5},{5,4},{6,7},{7,6},{8,9},{9,8},{10,11... | collective-permute-start | bytes 2654216 | tf_op jit(solution)/shard_map/ppermute | solution.py:294
  2.1 1.3 %collective-permute-start.1 = (bf16[12,128,128]{2,1,0:T(8,128)(2,1)S(1)}, bf16[12,128,128]{2,1,0:T(8,128)(2,1)S(1)}, u32[]{:S(2)}, u32[]{:S(2)}) collective-permute-start(bf16[12,128,128]{2,1,0:T(8,128)(2,1)S(1)} %get-tuple-element.20), channel_id=1, source_target_pairs={{14,0},{15,1},{0,2},{1,3},{2,4},{3,5},{4,6},{5,7},{6,8},{7,9},{8,1... | collective-permute-start | bytes 1179656 | tf_op jit(solution)/shard_map/ppermute | solution.py:291
  3.4 0.2 collective-permute-start.2
  3.6 5.1 %collective-permute-start.5 = (bf16[1,128,128]{2,1,0:T(8,128)(2,1)S(1)}, bf16[1,128,128]{2,1,0:T(8,128)(2,1)S(1)}, u32[]{:S(2)}, u32[]{:S(2)}) collective-permute-start(bf16[1,128,128]{2,1,0:T(8,128)(2,1)S(1)} %get-tuple-element.24), channel_id=1, source_target_pairs={{11,1},{12,2},{15,5},{0,6},{3,9},{4,10},{7,13},{8,14},{27,17},{28,... | collective-permute-start | bytes 98312 | tf_op jit(solution)/shard_map/ppermute | solution.py:291
  8.7 1.3 %collective-permute-start.3 = (bf16[5,128,128]{2,1,0:T(8,128)(2,1)S(1)}, bf16[5,128,128]{2,1,0:T(8,128)(2,1)S(1)}, u32[]{:S(2)}, u32[]{:S(2)}) collective-permute-start(bf16[5,128,128]{2,1,0:T(8,128)(2,1)S(1)} %get-tuple-element.22), channel_id=1, source_target_pairs={{12,0},{13,1},{14,2},{15,3},{0,4},{1,5},{2,6},{3,7},{4,8},{5,9},{6... | collective-permute-start | bytes 491528 | tf_op jit(solution)/shard_map/ppermute | solution.py:291
  10.0 2.6 %collective-permute-done.5.rest_6_ = bf16[1,128,128]{2,1,0:T(8,128)(2,1)S(1)} collective-permute-done((bf16[1,128,128]{2,1,0:T(8,128)(2,1)S(1)}, bf16[1,128,128]{2,1,0:T(8,128)(2,1)S(1)}, u32[]{:S(2)}, u32[]{:S(2)}) %collective-permute-start.5) | collective-permute-done | bytes 32800 | tf_op jit(solution)/shard_map/ppermute | solution.py:291
  12.6 2.3 %collective-permute-start.4 = (bf16[5,128,128]{2,1,0:T(8,128)(2,1)S(1)}, bf16[5,128,128]{2,1,0:T(8,128)(2,1)S(1)}, u32[]{:S(2)}, u32[]{:S(2)}) collective-permute-start(bf16[5,128,128]{2,1,0:T(8,128)(2,1)S(1)} %get-tuple-element.23), channel_id=1, source_target_pairs={{4,0},{5,1},{6,2},{7,3},{8,4},{9,5},{10,6},{11,7},{12,8},{13,9},{1... | collective-permute-start | bytes 491528 | tf_op jit(solution)/shard_map/ppermute | solution.py:291
  14.9 0.0 collective-permute-done.left_other_ref.rest_1_
  14.9 4.7 %collective-permute-start.6 = (bf16[1,128,128]{2,1,0:T(8,128)(2,1)S(1)}, bf16[1,128,128]{2,1,0:T(8,128)(2,1)S(1)}, u32[]{:S(2)}, u32[]{:S(2)}) collective-permute-start(bf16[1,128,128]{2,1,0:T(8,128)(2,1)S(1)} %get-tuple-element.25), channel_id=1, source_target_pairs={{7,1},{8,2},{11,5},{12,6},{15,9},{0,10},{3,13},{4,14},{23,17},{24,... | collective-permute-start | bytes 98312 | tf_op jit(solution)/shard_map/ppermute | solution.py:291
  19.6 0.7 %inner.1.rest_9_ = f32[6,128,128]{2,1,0:T(8,128)S(1)} custom-call(bf16[384,1152]{1,0:T(8,128)(2,1)S(1)} %get-tuple-element.19.left_ref.rest_0_, bf16[384,1152]{1,0:T(8,128)(2,1)S(1)} %collective-permute-done.left_other_ref.rest_1_), custom_call_target="tpu_custom_call" | custom-call | flops 427819008 | bytes 3014656 | tf_op jit(solution)/shard_map/inner/pallas_call | solution.py:298
  20.3 0.3 collective-permute-done.6.rest_7_
  20.6 0.0 collective-permute-done.3.refs_2_.rest_4_
  20.6 0.3 collective-permute-done.4.refs_3_.rest_5_
  20.9 0.6 %collective-permute-done.1.refs_0_.rest_2_ = bf16[12,128,128]{2,1,0:T(8,128)(2,1)S(1)} collective-permute-done((bf16[12,128,128]{2,1,0:T(8,128)(2,1)S(1)}, bf16[12,128,128]{2,1,0:T(8,128)(2,1)S(1)}, u32[]{:S(2)}, u32[]{:S(2)}) %collective-permute-start.1) | collective-permute-done | bytes 393248 | tf_op jit(solution)/shard_map/ppermute | solution.py:291
  21.6 0.0 collective-permute-done.2.refs_1_.rest_3_
  21.6 7.3 %collective-permute-start.7 = (bf16[17,128,128]{2,1,0:T(8,128)(2,1)S(1)}, bf16[17,128,128]{2,1,0:T(8,128)(2,1)S(1)}, u32[]{:S(2)}, u32[]{:S(2)}) collective-permute-start(bf16[17,128,128]{2,1,0:T(8,128)(2,1)S(1)} %stage.1), channel_id=1, source_target_pairs={{0,1},{1,0},{2,3},{3,2},{4,5},{5,4},{6,7},{7,6},{8,9},{9,8},{10,11... | collective-permute-start | bytes 1671176 | tf_op jit(solution)/shard_map/ppermute | solution.py:294
  29.6 0.9 %collective-permute-done.7.rest_8_ = bf16[17,128,128]{2,1,0:T(8,128)(2,1)S(1)} collective-permute-done((bf16[17,128,128]{2,1,0:T(8,128)(2,1)S(1)}, bf16[17,128,128]{2,1,0:T(8,128)(2,1)S(1)}, u32[]{:S(2)}, u32[]{:S(2)}) %collective-permute-start.7) | collective-permute-done | bytes 557088 | tf_op jit(solution)/shard_map/ppermute | solution.py:294
  30.5 3.4 %multiply.1 = f32[1,23,128,128]{3,2,1,0:T(8,128)} custom-call(s32[1,23]{1,0:T(1,128)} %rows_ref.3, s32[1,23]{1,0:T(1,128)} %cols_ref.3, s32[1,1]{1,0:T(1,128)S(6)} %copy.5.counts_ref, bf16[384,1152]{1,0:T(8,128)(2,1)S(1)} %get-tuple-element.19.left_ref.rest_0_, bf16[384,1152]{1,0:T(8,128)(2,1)S(1)} %collective-permute-done.left_other_ref.rest_1_, ...), custom_call_target="tpu_custom_call" | custom-call | tf_op jit(solution)/shard_map/multiply/pallas_call | solution.py:320
  (1 shorter events, 0.0 us)
Async XLA Ops:
  1.4 13.5 %collective-permute-start = (bf16[384,1152]{1,0:T(8,128)(2,1)S(1)}, bf16[384,1152]{1,0:T(8,128)(2,1)S(1)}, u32[]{:S(2)}, u32[]{:S(2)}) collective-permute-start(bf16[384,1152]{1,0:T(8,128)(2,1)S(1)} %get-tuple-element.19.left_ref.rest_0_), channel_id=1, source_target_pairs={{0,1},{1,0},{2,3},{3,2},{4,5},{5,4},{6,7},{7,6},{8,9},{9,8},{10,11... | collective-permute-start | bytes 2654216 | tf_op jit(solution)/shard_map/ppermute | solution.py:294
  2.1 19.5 %collective-permute-start.1 = (bf16[12,128,128]{2,1,0:T(8,128)(2,1)S(1)}, bf16[12,128,128]{2,1,0:T(8,128)(2,1)S(1)}, u32[]{:S(2)}, u32[]{:S(2)}) collective-permute-start(bf16[12,128,128]{2,1,0:T(8,128)(2,1)S(1)} %get-tuple-element.20), channel_id=1, source_target_pairs={{14,0},{15,1},{0,2},{1,3},{2,4},{3,5},{4,6},{5,7},{6,8},{7,9},{8,1... | collective-permute-start | bytes 1179656 | tf_op jit(solution)/shard_map/ppermute | solution.py:291
  3.4 18.2 %collective-permute-start.2 = (bf16[12,128,128]{2,1,0:T(8,128)(2,1)S(1)}, bf16[12,128,128]{2,1,0:T(8,128)(2,1)S(1)}, u32[]{:S(2)}, u32[]{:S(2)}) collective-permute-start(bf16[12,128,128]{2,1,0:T(8,128)(2,1)S(1)} %get-tuple-element.21), channel_id=1, source_target_pairs={{2,0},{3,1},{4,2},{5,3},{6,4},{7,5},{8,6},{9,7},{10,8},{11,9},{12,... | collective-permute-start | bytes 1179656 | tf_op jit(solution)/shard_map/ppermute | solution.py:291
  3.6 9.0 %collective-permute-start.5 = (bf16[1,128,128]{2,1,0:T(8,128)(2,1)S(1)}, bf16[1,128,128]{2,1,0:T(8,128)(2,1)S(1)}, u32[]{:S(2)}, u32[]{:S(2)}) collective-permute-start(bf16[1,128,128]{2,1,0:T(8,128)(2,1)S(1)} %get-tuple-element.24), channel_id=1, source_target_pairs={{11,1},{12,2},{15,5},{0,6},{3,9},{4,10},{7,13},{8,14},{27,17},{28,... | collective-permute-start | bytes 98312 | tf_op jit(solution)/shard_map/ppermute | solution.py:291
  8.7 11.9 %collective-permute-start.3 = (bf16[5,128,128]{2,1,0:T(8,128)(2,1)S(1)}, bf16[5,128,128]{2,1,0:T(8,128)(2,1)S(1)}, u32[]{:S(2)}, u32[]{:S(2)}) collective-permute-start(bf16[5,128,128]{2,1,0:T(8,128)(2,1)S(1)} %get-tuple-element.22), channel_id=1, source_target_pairs={{12,0},{13,1},{14,2},{15,3},{0,4},{1,5},{2,6},{3,7},{4,8},{5,9},{6... | collective-permute-start | bytes 491528 | tf_op jit(solution)/shard_map/ppermute | solution.py:291
  12.6 8.3 %collective-permute-start.4 = (bf16[5,128,128]{2,1,0:T(8,128)(2,1)S(1)}, bf16[5,128,128]{2,1,0:T(8,128)(2,1)S(1)}, u32[]{:S(2)}, u32[]{:S(2)}) collective-permute-start(bf16[5,128,128]{2,1,0:T(8,128)(2,1)S(1)} %get-tuple-element.23), channel_id=1, source_target_pairs={{4,0},{5,1},{6,2},{7,3},{8,4},{9,5},{10,6},{11,7},{12,8},{13,9},{1... | collective-permute-start | bytes 491528 | tf_op jit(solution)/shard_map/ppermute | solution.py:291
  14.9 5.7 %collective-permute-start.6 = (bf16[1,128,128]{2,1,0:T(8,128)(2,1)S(1)}, bf16[1,128,128]{2,1,0:T(8,128)(2,1)S(1)}, u32[]{:S(2)}, u32[]{:S(2)}) collective-permute-start(bf16[1,128,128]{2,1,0:T(8,128)(2,1)S(1)} %get-tuple-element.25), channel_id=1, source_target_pairs={{7,1},{8,2},{11,5},{12,6},{15,9},{0,10},{3,13},{4,14},{23,17},{24,... | collective-permute-start | bytes 98312 | tf_op jit(solution)/shard_map/ppermute | solution.py:291
  21.6 8.9 %collective-permute-start.7 = (bf16[17,128,128]{2,1,0:T(8,128)(2,1)S(1)}, bf16[17,128,128]{2,1,0:T(8,128)(2,1)S(1)}, u32[]{:S(2)}, u32[]{:S(2)}) collective-permute-start(bf16[17,128,128]{2,1,0:T(8,128)(2,1)S(1)} %stage.1), channel_id=1, source_target_pairs={{0,1},{1,0},{2,3},{3,2},{4,5},{5,4},{6,7},{7,6},{8,9},{9,8},{10,11... | collective-permute-start | bytes 1671176 | tf_op jit(solution)/shard_map/ppermute | solution.py:294

commit v3 on v2

v3 whole, which is shorter than its diff:
```python
import functools

import jax
import jax.numpy as jnp
from jax import lax
from jax.experimental import pallas as pl
from jax.experimental.pallas import tpu as pltpu
from jax.sharding import PartitionSpec as P

BLK = 128
BR = 3
HB = 7
WIDTH = 2 * HB + 1
LOW, HIGH = -HB, BR - 1 + HB
NCOL = 9
INNER = 6
PLACES = 32
VMEM_LIMIT = 12 * 2**20

DISTANCES = {"a": 1, "b": -1, "c": -2, "d": 2, "e": None}
SENT = {
    ("a", 1): [(3, 3), (5, 5), (3, 5), (3, 7), (4, 7), (5, 7), (3, 9), (4, 9), (5, 9), (3, -3), (3, -1), (4, -3), (5, -1)],
    ("a", 0): [(4, 4), (3, 4), (5, 4), (3, 6), (4, 6), (5, 6), (3, 8), (4, 8), (5, 8), (3, -2), (4, -2), (5, -2), (3, -4)],
    ("b", 1): [(-1, -1), (-3, -3), (-1, -3), (-1, -7), (-2, -7), (-3, -7)],
    ("b", 0): [(-2, -2), (-1, -2), (-3, -2), (-1, 4), (-1, -4), (-1, -6)],
    ("c", 1): [(-5, -5), (-4, -7), (-5, -7), (-6, -7), (-4, -3), (-5, -1), (-5, -3), (-6, -3)],
    ("c", 0): [(-4, -4), (-6, -6), (-4, -6), (-4, -2), (-5, -2), (-6, -2), (-5, -4), (-5, -6)],
    ("d", 1): [(6, 9), (7, 7), (7, 9), (8, 9), (6, -1)],
    ("d", 0): [(6, 6), (6, 8), (8, 8), (7, 6), (7, 8)],
    ("e", 1): [(9, 9)],
    ("e", 0): [(-7, -7)],
}
SIZES = {name: len(SENT[name, 1]) for name in DISTANCES}
STAGED = {
    parity: [
        (name, n, (k, j))
        for name in DISTANCES
        for n, (k, j) in enumerate(SENT[name, parity])
        if k % 2 != j % 2 or (k, j) == (-7, -7)
    ]
    for parity in (0, 1)
}
STAGED_SIZE = max(len(found) for found in STAGED.values())


def columns_of(parity):
    return [j for j in range(LOW, HIGH + 1) if j % 2 == parity]


def own_parity():
    return (lax.axis_index("row") + lax.axis_index("col")) % 2


def for_own_parity(body):
    parity = own_parity()
    for mine in (0, 1):
        pl.when(parity == mine)(functools.partial(body, mine))


def slot_position(rows_ref, cols_ref, slot, nblocks):
    panel = lax.axis_index("row")
    row = rows_ref[0, slot] - panel * BR
    band = cols_ref[0, slot] - rows_ref[0, slot] + HB
    band = jnp.where(band < 0, band + nblocks, band)
    band = jnp.where(band >= nblocks, band - nblocks, band)
    odd = panel % 2 == 1
    return row, jnp.where(odd, BR - 1 - row, row), jnp.where(odd, WIDTH - 1 - band, band)


def index_copies(hbm_refs, smem_refs, sems):
    return [pltpu.make_async_copy(a, b, sems.at[i]) for i, (a, b) in enumerate(zip(hbm_refs, smem_refs))]


def pack_kernel(nblocks, slots, rows_ref, cols_ref, values_ref, *rest):
    out_refs = dict(zip("abcd", rest[:4]))
    left_ref, held, table, *index, sems, value_sem = rest[4:]
    load = pltpu.make_async_copy(values_ref.at[0], held.at[pl.ds(0, slots)], value_sem)
    load.start()
    copies = index_copies((rows_ref, cols_ref), index, sems)
    for copy in copies:
        copy.start()
    held[slots] = jnp.zeros((BLK, BLK), held.dtype)
    for i in range(BR * WIDTH + 1):
        table[i] = slots
    for copy in copies:
        copy.wait()
    for m in reversed(range(slots)):
        real_row, row, band = slot_position(*index, m, nblocks)
        table[jnp.where(real_row >= 0, row * WIDTH + band, BR * WIDTH)] = m
    load.wait()

    @for_own_parity
    def _(mine):
        for name, ref in out_refs.items():
            distance = DISTANCES[name]
            for n, (k, j) in enumerate(SENT[name, (mine + distance) % 2]):
                at = (k - BR * distance) * WIDTH + j - k + HB
                if distance % 2 == 1:
                    at = BR * WIDTH - 1 - at
                ref[n] = held[table[at]]
        columns = columns_of(mine)
        for i in range(BR):
            for n in range(NCOL):
                rows, cols = pl.ds(i * BLK, BLK), pl.ds(n * BLK, BLK)
                if n < len(columns) and abs(columns[n] - i) <= HB:
                    left_ref[rows, cols] = held[table[i * WIDTH + columns[n] - i + HB]]
                else:
                    left_ref[rows, cols] = jnp.zeros((BLK, BLK), left_ref.dtype)


def find_block(parity, k, j):
    if abs(k - j) > HB:
        return None
    if 0 <= k < BR:
        return ("left", parity == j % 2), (k, columns_of(j % 2).index(j)), False
    if 0 <= j < BR:
        return ("left", parity == k % 2), (j, columns_of(k % 2).index(k)), True
    for a, b, flip in ((k, j, False), (j, k, True)):
        for name in DISTANCES:
            if (a, b) in SENT[name, parity]:
                return name, SENT[name, parity].index((a, b)), flip
        staged = [position for _, _, position in STAGED[1 - parity]]
        if (a, b) in staged:
            return "staged", staged.index((a, b)), flip
    raise AssertionError((k, j))


def columns_product(refs, right, parity, js, wanted):
    total = None
    for own in (True, False):
        kind = parity if own else 1 - parity
        found = {}
        for k in columns_of(kind):
            for j in js:
                place = find_block(parity, k, j)
                if place is not None and wanted(place[0]):
                    found[k, j] = place
        if not found:
            continue
        first, last = min(k for k, _ in found), max(k for k, _ in found)
        ks = [k for k in columns_of(kind) if first <= k <= last]
        side = right.at[0 if own else 1]
        for x, k in enumerate(ks):
            for y, j in enumerate(js):
                if (k, j) in found:
                    source, place, flip = found[k, j]
                    if isinstance(place, tuple):
                        block = refs[source][pl.ds(place[0] * BLK, BLK), pl.ds(place[1] * BLK, BLK)]
                    else:
                        block = refs[source][place]
                    block = block.T if flip else block
                else:
                    block = jnp.zeros((BLK, BLK), right.dtype)
                side[pl.ds(x * BLK, BLK), pl.ds(y * BLK, BLK)] = block
        start = columns_of(kind).index(first)
        part = jnp.dot(
            refs["left", own][:, pl.ds(start * BLK, len(ks) * BLK)],
            side[pl.ds(0, len(ks) * BLK), pl.ds(0, len(js) * BLK)],
            preferred_element_type=jnp.float32,
        )
        total = part if total is None else total + part
    return total


def block_of(total, i, y):
    return total[i * BLK : (i + 1) * BLK, y * BLK : (y + 1) * BLK]


def outer_pairs(parity):
    outer = [j for j in columns_of(parity) if not 0 <= j < BR]
    return [outer[n : n + 2] for n in range(0, len(outer), 2)]


def inner_kernel(nblocks, slots, rows_ref, cols_ref, counts_ref, left_ref, left_other_ref, *rest):
    made_ref, message_ref, table_ref, right, table, *index, sems, table_sem = rest
    copies = index_copies((rows_ref, cols_ref), index, sems)
    for copy in copies:
        copy.start()
    refs = {("left", True): left_ref, ("left", False): left_other_ref}

    @for_own_parity
    def _(mine):
        js = [j for j in columns_of(mine) if 0 <= j < BR]
        total = columns_product(refs, right, mine, js, lambda source: True)
        for i in range(BR):
            for y in range(2):
                made_ref[i * 2 + y] = block_of(total, i, y) if y < len(js) else jnp.zeros((BLK, BLK), made_ref.dtype)
        i = 2 if mine == 0 else 0
        n = columns_of(0).index(i)
        message_ref[0] = refs["left", mine == 0][pl.ds(i * BLK, BLK), pl.ds(n * BLK, BLK)]

    for i in range(BR * NCOL + 1):
        table[0, i] = -1
    for copy in copies:
        copy.wait()
    count = counts_ref[0, 0]
    for m in range(slots):
        _, row, band = slot_position(*index, m, nblocks)
        place = jnp.where(m < count, row * NCOL + (row + band) // 2, BR * NCOL)
        table[0, place] = m
        table[0, PLACES + m] = place
    copy = pltpu.make_async_copy(table, table_ref, table_sem)
    copy.start()
    copy.wait()


def stage_kernel(*refs):
    got = dict(zip(DISTANCES, refs))
    out_ref = refs[-1]

    @for_own_parity
    def _(mine):
        for n, (name, place, _) in enumerate(STAGED[mine]):
            out_ref[n] = got[name][place]
        for n in range(len(STAGED[mine]), STAGED_SIZE):
            out_ref[n] = jnp.zeros((BLK, BLK), out_ref.dtype)


def outer_kernel(left_ref, left_other_ref, *rest):
    refs = {("left", True): left_ref, ("left", False): left_other_ref, **dict(zip(DISTANCES, rest))}
    out_ref, right = rest[len(DISTANCES) :]

    @for_own_parity
    def _(mine):
        for pair, js in enumerate(outer_pairs(mine)):
            total = columns_product(refs, right.at[pair], mine, js, lambda source: source != "staged")
            for i in range(BR):
                for y, j in enumerate(js):
                    if abs(i - j) <= HB:
                        out_ref[i * NCOL + columns_of(mine).index(j)] = block_of(total, i, y)


def multiply_kernel(slots, left_ref, left_other_ref, staged_ref, outer_ref, inner_ref, table_ref, out_ref, *rest):
    right, made, zero, table, table_sem, out_sems = rest
    refs = {("left", True): left_ref, ("left", False): left_other_ref, "staged": staged_ref}
    load = pltpu.make_async_copy(table_ref, table, table_sem)
    load.start()
    zero[...] = jnp.zeros((BLK, BLK), zero.dtype)
    load.wait()

    def store(block, place):
        slot = table[0, place]

        @pl.when(slot >= 0)
        def _():
            pltpu.make_async_copy(block, out_ref.at[0, slot], out_sems.at[slot]).start()

    @for_own_parity
    def _(mine):
        columns = columns_of(mine)
        for pair, js in enumerate(outer_pairs(mine)):
            total = columns_product(refs, right.at[pair], mine, js, lambda source: source == "staged")
            for i in range(BR):
                for y, j in enumerate(js):
                    if abs(i - j) <= HB:
                        place = i * NCOL + columns.index(j)
                        made[place] = outer_ref[place] + block_of(total, i, y)
                        store(made.at[place], place)
        for i in range(BR):
            for y, j in enumerate(j for j in columns if 0 <= j < BR):
                store(inner_ref.at[i * 2 + y], i * NCOL + columns.index(j))

    for m in range(slots):

        @pl.when(table[0, PLACES + m] == BR * NCOL)
        def _(m=m):
            pltpu.make_async_copy(zero, out_ref.at[0, m], out_sems.at[m]).start()

    for m in range(slots):
        pltpu.make_async_copy(zero, out_ref.at[0, m], out_sems.at[m]).wait()


def local(values, block_rows, block_cols, counts):
    slots = values.shape[1]
    row_count, col_count = lax.axis_size("row"), lax.axis_size("col")
    nblocks = BR * row_count
    smem = pl.BlockSpec(memory_space=pltpu.SMEM)
    vmem = pl.BlockSpec(memory_space=pltpu.VMEM)
    hbm = pl.BlockSpec(memory_space=pltpu.HBM)
    params = pltpu.CompilerParams(vmem_limit_bytes=VMEM_LIMIT)
    values, *places = (pltpu.with_memory_space_constraint(x, pltpu.HBM) for x in (values, block_rows, block_cols))
    index_scratch = [
        pltpu.SMEM((1, slots), jnp.int32),
        pltpu.SMEM((1, slots), jnp.int32),
        pltpu.SemaphoreType.DMA((2,)),
    ]
    table_shape = (1, BLK)

    def blocks(count, dtype=values.dtype):
        return jax.ShapeDtypeStruct((count, BLK, BLK), dtype)

    def cost(products, nbytes):
        return pl.CostEstimate(flops=2 * products * BLK**3, bytes_accessed=nbytes, transcendentals=0)

    def right_scratch(pairs):
        return pltpu.VMEM((pairs, 2, NCOL * BLK, 2 * BLK), values.dtype)

    *packed, left = pl.pallas_call(
        functools.partial(pack_kernel, nblocks, slots),
        out_shape=[blocks(SIZES[name]) for name in "abcd"]
        + [jax.ShapeDtypeStruct((BR * BLK, NCOL * BLK), values.dtype)],
        in_specs=[hbm] * 3,
        out_specs=[vmem] * 5,
        scratch_shapes=[
            pltpu.VMEM((slots + 1, BLK, BLK), values.dtype),
            pltpu.SMEM((BR * WIDTH + 1,), jnp.int32),
            *index_scratch,
            pltpu.SemaphoreType.DMA,
        ],
        compiler_params=params,
        name="pack",
    )(*places, values)

    def towards(name, message):
        pairs = []
        for r in range(row_count):
            for c in range(col_count):
                distance = DISTANCES[name] or (3 if (r + c) % 2 == 1 else -3)
                source = (r - distance if r % 2 == 1 else r + distance) % row_count
                pairs.append((source * col_count + c, r * col_count + c))
        return lax.ppermute(message, ("row", "col"), pairs)

    def swapped(block):
        return lax.ppermute(block, "col", [(0, 1), (1, 0)])

    left_other = swapped(left)
    got = [towards(name, message) for name, message in zip("abcd", packed)]
    inner, message, table = pl.pallas_call(
        functools.partial(inner_kernel, nblocks, slots),
        out_shape=[blocks(INNER, jnp.float32), blocks(1), jax.ShapeDtypeStruct(table_shape, jnp.int32)],
        in_specs=[hbm] * 2 + [smem] + [vmem] * 2,
        out_specs=[vmem] * 3,
        scratch_shapes=[
            pltpu.VMEM((2, NCOL * BLK, 2 * BLK), values.dtype),
            pltpu.SMEM(table_shape, jnp.int32),
            *index_scratch,
            pltpu.SemaphoreType.DMA,
        ],
        compiler_params=params,
        cost_estimate=cost(3 * 2 * 17, 4 * values.size),
        name="inner",
    )(*places, counts, left, left_other)
    got.append(towards("e", message))
    staged = swapped(
        pl.pallas_call(
            stage_kernel,
            out_shape=blocks(STAGED_SIZE),
            in_specs=[vmem] * 5,
            out_specs=vmem,
            compiler_params=params,
            name="stage",
        )(*got)
    )
    outer = pl.pallas_call(
        outer_kernel,
        out_shape=blocks(BR * NCOL, jnp.float32),
        in_specs=[vmem] * 7,
        out_specs=vmem,
        scratch_shapes=[right_scratch(4)],
        compiler_params=params,
        cost_estimate=cost(3 * 2 * 56, 10 * values.size),
        name="outer",
    )(left, left_other, *got)
    return pl.pallas_call(
        functools.partial(multiply_kernel, slots),
        out_shape=jax.ShapeDtypeStruct(values.shape, jnp.float32),
        in_specs=[vmem] * 6,
        out_specs=hbm,
        scratch_shapes=[
            right_scratch(4),
            pltpu.VMEM((BR * NCOL, BLK, BLK), jnp.float32),
            pltpu.VMEM((BLK, BLK), jnp.float32),
            pltpu.SMEM(table_shape, jnp.int32),
            pltpu.SemaphoreType.DMA,
            pltpu.SemaphoreType.DMA((slots,)),
        ],
        compiler_params=params,
        name="multiply",
    )(left, left_other, staged, outer, inner, table)


def solution(mesh):
    return jax.shard_map(
        local,
        mesh=mesh,
        in_specs=(
            P(("parts", "row"), "col", None, None),
            P(("parts", "row"), "col"),
            P(("parts", "row"), "col"),
            P(("parts", "row"), "col"),
        ),
        out_specs=P(("parts", "row"), "col", None, None),
        check_vma=False,
    )
```

time: 34.1 us -> 28.2 us (0.83)
  the two profiles are of different devices: /device:TPU:3 before, /device:TPU:0 now
where the time goes in v3:
time: 28.2 us; the launch traced here: 28.1 us
  waiting for transfers between devices  11.5 us (41%)
  starting transfers between devices  8.97 us (32%)
  Pallas kernels  6.86 us (24%)
  between operations  0.71 us (3%)
    ppermute x5, waiting for transfers between devices, towards(): return lax.ppermute(message, ('row', 'col'), pairs)  10.7 us
    ppermute x5, starting transfers between devices, towards(): return lax.ppermute(message, ('row', 'col'), pairs)  8.38 us
    pallas_call x1, Pallas kernels, local(): pl.pallas_call(functools.partial(multiply_kernel, slots), out_shape=jax.S...  2.55 us
    pallas_call x1, Pallas kernels, local(): pl.pallas_call(functools.partial(inner_kernel, nblocks, slots), out_shape...  1.64 us
    pallas_call x1, Pallas kernels, local(): pl.pallas_call(functools.partial(pack_kernel, nblocks, slots), out_shape=...  1.36 us
    pallas_call x1, Pallas kernels, local(): pl.pallas_call(outer_kernel, out_shape=blocks(BR * NCOL, jnp.float32), in...  1.26 us
    ppermute x2, waiting for transfers between devices, swapped(): return lax.ppermute(block, 'col', [(0, 1), (1, 0)])  0.82 us
    ppermute x2, starting transfers between devices, swapped(): return lax.ppermute(block, 'col', [(0, 1), (1, 0)])  0.59 us
  transfers between devices with their start and end apart: 7, of which 3 were waited for; matrix products, arithmetic and copies ran while one was open for 0% of the time, Pallas kernels for 10%

profile of v3, /device:TPU:0, one launch (start us, length us, event | category | flops | bytes accessed | tf_op | source)
XLA Modules:
  0.0 28.1 jit_solution(762002791402898120)
XLA Ops:
  0.0 1.4 %pack.1 = (bf16[13,128,128]{2,1,0:T(8,128)(2,1)S(1)}, bf16[6,128,128]{2,1,0:T(8,128)(2,1)S(1)}, bf16[8,128,128]{2,1,0:T(8,128)(2,1)S(1)}, bf16[5,128,128]{2,1,0:T(8,128)(2,1)S(1)}, bf16[384,1152]{1,0:T(8,128)(2,1)S(1)}) custom-call(s32[1,23]{1,0:T(1,128)} %rows_ref.3, s32[1,23]{1,0:T(1,128)} %cols_ref.3, bf16[1,23,128,128]{3,2,1,0:T(8,128)(2,1)} %values_ref.1), custom_call_target="tpu_custom_call" | custom-call | tf_op jit(solution)/shard_map/pack/pallas_call | solution.py:298
  1.4 0.5 %collective-permute-start = (bf16[384,1152]{1,0:T(8,128)(2,1)S(1)}, bf16[384,1152]{1,0:T(8,128)(2,1)S(1)}, u32[]{:S(2)}, u32[]{:S(2)}) collective-permute-start(bf16[384,1152]{1,0:T(8,128)(2,1)S(1)} %get-tuple-element.13.left_ref), channel_id=1, source_target_pairs={{0,1},{1,0},{2,3},{3,2},{4,5},{5,4},{6,7},{7,6},{8,9},{9,8},{10,11... | collective-permute-start | bytes 2654216 | tf_op jit(solution)/shard_map/ppermute | solution.py:324
  1.9 2.6 %collective-permute-start.1 = (bf16[13,128,128]{2,1,0:T(8,128)(2,1)S(1)}, bf16[13,128,128]{2,1,0:T(8,128)(2,1)S(1)}, u32[]{:S(2)}, u32[]{:S(2)}) collective-permute-start(bf16[13,128,128]{2,1,0:T(8,128)(2,1)S(1)} %get-tuple-element.14), channel_id=1, source_target_pairs={{2,0},{3,1},{0,2},{1,3},{6,4},{7,5},{4,6},{5,7},{10,8},{11,9},{8,1... | collective-permute-start | bytes 1277960 | tf_op jit(solution)/shard_map/ppermute | solution.py:321
  4.4 1.6 %collective-permute-start.3 = (bf16[8,128,128]{2,1,0:T(8,128)(2,1)S(1)}, bf16[8,128,128]{2,1,0:T(8,128)(2,1)S(1)}, u32[]{:S(2)}, u32[]{:S(2)}) collective-permute-start(bf16[8,128,128]{2,1,0:T(8,128)(2,1)S(1)} %get-tuple-element.16), channel_id=1, source_target_pairs={{12,0},{13,1},{6,2},{7,3},{0,4},{1,5},{10,6},{11,7},{4,8},{5,9},{1... | collective-permute-start | bytes 786440 | tf_op jit(solution)/shard_map/ppermute | solution.py:321
  6.0 2.4 %collective-permute-start.2 = (bf16[6,128,128]{2,1,0:T(8,128)(2,1)S(1)}, bf16[6,128,128]{2,1,0:T(8,128)(2,1)S(1)}, u32[]{:S(2)}, u32[]{:S(2)}) collective-permute-start(bf16[6,128,128]{2,1,0:T(8,128)(2,1)S(1)} %get-tuple-element.15), channel_id=1, source_target_pairs={{14,0},{15,1},{4,2},{5,3},{2,4},{3,5},{8,6},{9,7},{6,8},{7,9},{12,... | collective-permute-start | bytes 589832 | tf_op jit(solution)/shard_map/ppermute | solution.py:321
  8.5 0.4 %collective-permute-start.4 = (bf16[5,128,128]{2,1,0:T(8,128)(2,1)S(1)}, bf16[5,128,128]{2,1,0:T(8,128)(2,1)S(1)}, u32[]{:S(2)}, u32[]{:S(2)}) collective-permute-start(bf16[5,128,128]{2,1,0:T(8,128)(2,1)S(1)} %get-tuple-element.17), channel_id=1, source_target_pairs={{4,0},{5,1},{14,2},{15,3},{8,4},{9,5},{2,6},{3,7},{12,8},{13,9},{6... | collective-permute-start | bytes 491528 | tf_op jit(solution)/shard_map/ppermute | solution.py:321
  9.6 0.0 collective-permute-done.left_other_ref
  9.6 1.6 %inner.1 = (f32[6,128,128]{2,1,0:T(8,128)S(1)}, bf16[1,128,128]{2,1,0:T(8,128)(2,1)S(1)}, s32[1,128]{1,0:T(1,128)S(1)}) custom-call(s32[1,23]{1,0:T(1,128)} %rows_ref.3, s32[1,23]{1,0:T(1,128)} %cols_ref.3, s32[1,1]{1,0:T(1,128)S(6)} %copy.5.counts_ref, bf16[384,1152]{1,0:T(8,128)(2,1)S(1)} %get-tuple-element.13.left_ref, ...), custom_call_target="tpu_custom_call" | custom-call | flops 427819008 | bytes 1507328 | tf_op jit(solution)/shard_map/inner/pallas_call | solution.py:328
  11.2 1.3 %collective-permute-start.5 = (bf16[1,128,128]{2,1,0:T(8,128)(2,1)S(1)}, bf16[1,128,128]{2,1,0:T(8,128)(2,1)S(1)}, u32[]{:S(2)}, u32[]{:S(2)}) collective-permute-start(bf16[1,128,128]{2,1,0:T(8,128)(2,1)S(1)} %get-tuple-element.18), channel_id=1, source_target_pairs={{10,0},{7,1},{12,2},{9,3},{14,4},{11,5},{0,6},{13,7},{2,8},{15,9},... | collective-permute-start | bytes 98312 | tf_op jit(solution)/shard_map/ppermute | solution.py:321
  12.6 10.0 %collective-permute-done.4.refs_3_.rest_3_ = bf16[5,128,128]{2,1,0:T(8,128)(2,1)S(1)} collective-permute-done((bf16[5,128,128]{2,1,0:T(8,128)(2,1)S(1)}, bf16[5,128,128]{2,1,0:T(8,128)(2,1)S(1)}, u32[]{:S(2)}, u32[]{:S(2)}) %collective-permute-start.4) | collective-permute-done | bytes 163872 | tf_op jit(solution)/shard_map/ppermute | solution.py:321
  22.6 0.0 collective-permute-done.2.refs_1_.rest_1_
  22.6 0.0 collective-permute-done.3.refs_2_.rest_2_
  22.6 0.0 collective-permute-done.1.refs_0_.rest_0_
  22.6 0.8 %collective-permute-done.5.refs_4_.rest_4_ = bf16[1,128,128]{2,1,0:T(8,128)(2,1)S(1)} collective-permute-done((bf16[1,128,128]{2,1,0:T(8,128)(2,1)S(1)}, bf16[1,128,128]{2,1,0:T(8,128)(2,1)S(1)}, u32[]{:S(2)}, u32[]{:S(2)}) %collective-permute-start.5) | collective-permute-done | bytes 32800 | tf_op jit(solution)/shard_map/ppermute | solution.py:321
  23.4 0.1 collective-permute-start.6
  23.5 1.3 %outer.1.outer_ref = f32[27,128,128]{2,1,0:T(8,128)S(1)} custom-call(bf16[384,1152]{1,0:T(8,128)(2,1)S(1)} %get-tuple-element.13.left_ref, bf16[384,1152]{1,0:T(8,128)(2,1)S(1)} %collective-permute-done.left_other_ref, bf16[13,128,128]{2,1,0:T(8,128)(2,1)S(1)} %collective-permute-done.1.refs_0_.rest_0_, ...), custom_call_target="tpu_custom_call" | custom-call | flops 1409286144 | bytes 3768320 | tf_op jit(solution)/shard_map/outer/pallas_call | solution.py:354
  24.7 0.8 %collective-permute-done.6.staged_ref = bf16[20,128,128]{2,1,0:T(8,128)(2,1)S(1)} collective-permute-done((bf16[20,128,128]{2,1,0:T(8,128)(2,1)S(1)}, bf16[20,128,128]{2,1,0:T(8,128)(2,1)S(1)}, u32[]{:S(2)}, u32[]{:S(2)}) %collective-permute-start.6) | collective-permute-done | bytes 655392 | tf_op jit(solution)/shard_map/ppermute | solution.py:324
  25.5 2.5 %multiply.1 = f32[1,23,128,128]{3,2,1,0:T(8,128)} custom-call(bf16[384,1152]{1,0:T(8,128)(2,1)S(1)} %get-tuple-element.13.left_ref, bf16[384,1152]{1,0:T(8,128)(2,1)S(1)} %collective-permute-done.left_other_ref, bf16[20,128,128]{2,1,0:T(8,128)(2,1)S(1)} %collective-permute-done.6.staged_ref, f32[27,128,128]{2,1,0:T(8,128)S(1)} %outer.1.outer_ref, ...), custom_call_target="tpu_custom_call" | custom-call | tf_op jit(solution)/shard_map/multiply/pallas_call | solution.py:364
  (1 shorter events, 0.0 us)
Async XLA Ops:
  1.4 8.2 %collective-permute-start = (bf16[384,1152]{1,0:T(8,128)(2,1)S(1)}, bf16[384,1152]{1,0:T(8,128)(2,1)S(1)}, u32[]{:S(2)}, u32[]{:S(2)}) collective-permute-start(bf16[384,1152]{1,0:T(8,128)(2,1)S(1)} %get-tuple-element.13.left_ref), channel_id=1, source_target_pairs={{0,1},{1,0},{2,3},{3,2},{4,5},{5,4},{6,7},{7,6},{8,9},{9,8},{10,11... | collective-permute-start | bytes 2654216 | tf_op jit(solution)/shard_map/ppermute | solution.py:324
  1.9 20.7 %collective-permute-start.1 = (bf16[13,128,128]{2,1,0:T(8,128)(2,1)S(1)}, bf16[13,128,128]{2,1,0:T(8,128)(2,1)S(1)}, u32[]{:S(2)}, u32[]{:S(2)}) collective-permute-start(bf16[13,128,128]{2,1,0:T(8,128)(2,1)S(1)} %get-tuple-element.14), channel_id=1, source_target_pairs={{2,0},{3,1},{0,2},{1,3},{6,4},{7,5},{4,6},{5,7},{10,8},{11,9},{8,1... | collective-permute-start | bytes 1277960 | tf_op jit(solution)/shard_map/ppermute | solution.py:321
  4.4 18.1 %collective-permute-start.3 = (bf16[8,128,128]{2,1,0:T(8,128)(2,1)S(1)}, bf16[8,128,128]{2,1,0:T(8,128)(2,1)S(1)}, u32[]{:S(2)}, u32[]{:S(2)}) collective-permute-start(bf16[8,128,128]{2,1,0:T(8,128)(2,1)S(1)} %get-tuple-element.16), channel_id=1, source_target_pairs={{12,0},{13,1},{6,2},{7,3},{0,4},{1,5},{10,6},{11,7},{4,8},{5,9},{1... | collective-permute-start | bytes 786440 | tf_op jit(solution)/shard_map/ppermute | solution.py:321
  6.0 16.5 %collective-permute-start.2 = (bf16[6,128,128]{2,1,0:T(8,128)(2,1)S(1)}, bf16[6,128,128]{2,1,0:T(8,128)(2,1)S(1)}, u32[]{:S(2)}, u32[]{:S(2)}) collective-permute-start(bf16[6,128,128]{2,1,0:T(8,128)(2,1)S(1)} %get-tuple-element.15), channel_id=1, source_target_pairs={{14,0},{15,1},{4,2},{5,3},{2,4},{3,5},{8,6},{9,7},{6,8},{7,9},{12,... | collective-permute-start | bytes 589832 | tf_op jit(solution)/shard_map/ppermute | solution.py:321
  8.5 14.1 %collective-permute-start.4 = (bf16[5,128,128]{2,1,0:T(8,128)(2,1)S(1)}, bf16[5,128,128]{2,1,0:T(8,128)(2,1)S(1)}, u32[]{:S(2)}, u32[]{:S(2)}) collective-permute-start(bf16[5,128,128]{2,1,0:T(8,128)(2,1)S(1)} %get-tuple-element.17), channel_id=1, source_target_pairs={{4,0},{5,1},{14,2},{15,3},{8,4},{9,5},{2,6},{3,7},{12,8},{13,9},{6... | collective-permute-start | bytes 491528 | tf_op jit(solution)/shard_map/ppermute | solution.py:321
  11.2 12.1 %collective-permute-start.5 = (bf16[1,128,128]{2,1,0:T(8,128)(2,1)S(1)}, bf16[1,128,128]{2,1,0:T(8,128)(2,1)S(1)}, u32[]{:S(2)}, u32[]{:S(2)}) collective-permute-start(bf16[1,128,128]{2,1,0:T(8,128)(2,1)S(1)} %get-tuple-element.18), channel_id=1, source_target_pairs={{10,0},{7,1},{12,2},{9,3},{14,4},{11,5},{0,6},{13,7},{2,8},{15,9},... | collective-permute-start | bytes 98312 | tf_op jit(solution)/shard_map/ppermute | solution.py:321
  23.4 2.2 %collective-permute-start.6 = (bf16[20,128,128]{2,1,0:T(8,128)(2,1)S(1)}, bf16[20,128,128]{2,1,0:T(8,128)(2,1)S(1)}, u32[]{:S(2)}, u32[]{:S(2)}) collective-permute-start(bf16[20,128,128]{2,1,0:T(8,128)(2,1)S(1)} %stage.1), channel_id=1, source_target_pairs={{0,1},{1,0},{2,3},{3,2},{4,5},{5,4},{6,7},{7,6},{8,9},{9,8},{10,11... | collective-permute-start | bytes 1966088 | tf_op jit(solution)/shard_map/ppermute | solution.py:324

commit v4 on v3

--- a/solution.py
+++ b/solution.py
@@ -19,18 +19,20 @@
 
 DISTANCES = {"a": 1, "b": -1, "c": -2, "d": 2, "e": None}
 SENT = {
-    ("a", 1): [(3, 3), (5, 5), (3, 5), (3, 7), (4, 7), (5, 7), (3, 9), (4, 9), (5, 9), (3, -3), (3, -1), (4, -3), (5, -1)],
-    ("a", 0): [(4, 4), (3, 4), (5, 4), (3, 6), (4, 6), (5, 6), (3, 8), (4, 8), (5, 8), (3, -2), (4, -2), (5, -2), (3, -4)],
-    ("b", 1): [(-1, -1), (-3, -3), (-1, -3), (-1, -7), (-2, -7), (-3, -7)],
-    ("b", 0): [(-2, -2), (-1, -2), (-3, -2), (-1, 4), (-1, -4), (-1, -6)],
-    ("c", 1): [(-5, -5), (-4, -7), (-5, -7), (-6, -7), (-4, -3), (-5, -1), (-5, -3), (-6, -3)],
-    ("c", 0): [(-4, -4), (-6, -6), (-4, -6), (-4, -2), (-5, -2), (-6, -2), (-5, -4), (-5, -6)],
-    ("d", 1): [(6, 9), (7, 7), (7, 9), (8, 9), (6, -1)],
-    ("d", 0): [(6, 6), (6, 8), (8, 8), (7, 6), (7, 8)],
+    ("a", 1): [(3, 3), (5, 5), (3, 5), (3, 9), (4, 9), (5, 9), (3, -3), (3, -1), (4, -3), (4, -1), (5, -1)],
+    ("a", 0): [(4, 4), (3, 4), (5, 4), (3, 6), (4, 6), (5, 6), (3, 8), (5, 8), (3, -2), (5, -2), (3, -4)],
+    ("b", 1): [(-1, -1), (-3, -3), (-1, -3), (-1, -7), (-2, -7), (-3, -7), (-2, -5)],
+    ("b", 0): [(-2, -2), (-1, -2), (-3, -2), (-2, 4), (-1, -4), (-1, -6), (-3, -6)],
+    ("c", 1): [(-5, -5), (-4, -7), (-5, -7), (-6, -7), (-5, -1), (-5, -3), (-4, -3)],
+    ("c", 0): [(-4, -4), (-6, -6), (-4, -6), (-5, -4), (-5, -6), (-4, -2), (-6, -2)],
+    ("d", 1): [(7, 7), (6, 9), (7, 9), (8, 9), (6, -1), (7, 3), (7, 5)],
+    ("d", 0): [(6, 6), (8, 8), (6, 8), (7, 6), (7, 8), (7, 4), (8, 4)],
     ("e", 1): [(9, 9)],
     ("e", 0): [(-7, -7)],
 }
+PERMUTES = ("a", "f", "g", "b", "e")
 SIZES = {name: len(SENT[name, 1]) for name in DISTANCES}
+SIZES["f"] = SIZES["g"] = SIZES["c"]
 STAGED = {
     parity: [
         (name, n, (k, j))
@@ -57,6 +59,11 @@
         pl.when(parity == mine)(functools.partial(body, mine))
 
 
+def received_c_first():
+    place = lax.axis_index("row") % 4
+    return (place == 1) | (place == 2)
+
+
 def slot_position(rows_ref, cols_ref, slot, nblocks):
     panel = lax.axis_index("row")
     row = rows_ref[0, slot] - panel * BR
@@ -71,9 +78,14 @@
     return [pltpu.make_async_copy(a, b, sems.at[i]) for i, (a, b) in enumerate(zip(hbm_refs, smem_refs))]
 
 
+def position_at_sender(name, k, j):
+    distance = DISTANCES[name]
+    row, col = k - BR * distance, j - BR * distance
+    return (BR - 1 - row, BR - 1 - col) if distance % 2 == 1 else (row, col)
+
+
 def pack_kernel(nblocks, slots, rows_ref, cols_ref, values_ref, *rest):
-    out_refs = dict(zip("abcd", rest[:4]))
-    left_ref, held, table, *index, sems, value_sem = rest[4:]
+    a_ref, f_ref, g_ref, b_ref, left_ref, held, table, *index, sems, value_sem = rest
     load = pltpu.make_async_copy(values_ref.at[0], held.at[pl.ds(0, slots)], value_sem)
     load.start()
     copies = index_copies((rows_ref, cols_ref), index, sems)
@@ -88,16 +100,21 @@
         real_row, row, band = slot_position(*index, m, nblocks)
         table[jnp.where(real_row >= 0, row * WIDTH + band, BR * WIDTH)] = m
     load.wait()
-
-    @for_own_parity
-    def _(mine):
-        for name, ref in out_refs.items():
-            distance = DISTANCES[name]
-            for n, (k, j) in enumerate(SENT[name, (mine + distance) % 2]):
-                at = (k - BR * distance) * WIDTH + j - k + HB
-                if distance % 2 == 1:
-                    at = BR * WIDTH - 1 - at
-                ref[n] = held[table[at]]
+    sends_c_in_f = ~received_c_first()
+
+    def table_place(name, k, j):
+        row, col = position_at_sender(name, k, j)
+        return row * WIDTH + col - row + HB
+
+    @for_own_parity
+    def _(mine):
+        for name, ref in (("a", a_ref), ("b", b_ref)):
+            for n, (k, j) in enumerate(SENT[name, 1 - mine]):
+                ref[n] = held[table[table_place(name, k, j)]]
+        for n in range(SIZES["f"]):
+            c, d = (table_place(name, *SENT[name, mine][n]) for name in "cd")
+            f_ref[n] = held[table[jnp.where(sends_c_in_f, c, d)]]
+            g_ref[n] = held[table[jnp.where(sends_c_in_f, d, c)]]
         columns = columns_of(mine)
         for i in range(BR):
             for n in range(NCOL):
@@ -106,6 +123,14 @@
                     left_ref[rows, cols] = held[table[i * WIDTH + columns[n] - i + HB]]
                 else:
                     left_ref[rows, cols] = jnp.zeros((BLK, BLK), left_ref.dtype)
+
+
+def pack_e_kernel(left_ref, left_other_ref, e_ref):
+    @for_own_parity
+    def _(mine):
+        i = 2 if mine == 0 else 0
+        n = columns_of(0).index(i)
+        e_ref[0] = (left_ref if mine == 0 else left_other_ref)[pl.ds(i * BLK, BLK), pl.ds(n * BLK, BLK)]
 
 
 def find_block(parity, k, j):
@@ -123,6 +148,15 @@
         if (a, b) in staged:
             return "staged", staged.index((a, b)), flip
     raise AssertionError((k, j))
+
+
+def read_block(refs, source, place):
+    if isinstance(place, tuple):
+        return refs[source][pl.ds(place[0] * BLK, BLK), pl.ds(place[1] * BLK, BLK)]
+    if source in ("c", "d"):
+        f, g = refs["f"][place], refs["g"][place]
+        return jnp.where(received_c_first(), *((f, g) if source == "c" else (g, f)))
+    return refs[source][place]
 
 
 def columns_product(refs, right, parity, js, wanted):
@@ -144,10 +178,7 @@
             for y, j in enumerate(js):
                 if (k, j) in found:
                     source, place, flip = found[k, j]
-                    if isinstance(place, tuple):
-                        block = refs[source][pl.ds(place[0] * BLK, BLK), pl.ds(place[1] * BLK, BLK)]
-                    else:
-                        block = refs[source][place]
+                    block = read_block(refs, source, place)
                     block = block.T if flip else block
                 else:
                     block = jnp.zeros((BLK, BLK), right.dtype)
@@ -172,7 +203,7 @@
 
 
 def inner_kernel(nblocks, slots, rows_ref, cols_ref, counts_ref, left_ref, left_other_ref, *rest):
-    made_ref, message_ref, table_ref, right, table, *index, sems, table_sem = rest
+    made_ref, table_ref, right, table, *index, sems, table_sem = rest
     copies = index_copies((rows_ref, cols_ref), index, sems)
     for copy in copies:
         copy.start()
@@ -185,9 +216,6 @@
         for i in range(BR):
             for y in range(2):
                 made_ref[i * 2 + y] = block_of(total, i, y) if y < len(js) else jnp.zeros((BLK, BLK), made_ref.dtype)
-        i = 2 if mine == 0 else 0
-        n = columns_of(0).index(i)
-        message_ref[0] = refs["left", mine == 0][pl.ds(i * BLK, BLK), pl.ds(n * BLK, BLK)]
 
     for i in range(BR * NCOL + 1):
         table[0, i] = -1
@@ -205,20 +233,20 @@
 
 
 def stage_kernel(*refs):
-    got = dict(zip(DISTANCES, refs))
+    got = dict(zip(PERMUTES, refs))
     out_ref = refs[-1]
 
     @for_own_parity
     def _(mine):
         for n, (name, place, _) in enumerate(STAGED[mine]):
-            out_ref[n] = got[name][place]
+            out_ref[n] = read_block(got, name, place)
         for n in range(len(STAGED[mine]), STAGED_SIZE):
             out_ref[n] = jnp.zeros((BLK, BLK), out_ref.dtype)
 
 
 def outer_kernel(left_ref, left_other_ref, *rest):
-    refs = {("left", True): left_ref, ("left", False): left_other_ref, **dict(zip(DISTANCES, rest))}
-    out_ref, right = rest[len(DISTANCES) :]
+    refs = {("left", True): left_ref, ("left", False): left_other_ref, **dict(zip(PERMUTES, rest))}
+    out_ref, right = rest[len(PERMUTES) :]
 
     @for_own_parity
     def _(mine):
@@ -297,7 +325,7 @@
 
     *packed, left = pl.pallas_call(
         functools.partial(pack_kernel, nblocks, slots),
-        out_shape=[blocks(SIZES[name]) for name in "abcd"]
+        out_shape=[blocks(SIZES[name]) for name in "afgb"]
         + [jax.ShapeDtypeStruct((BR * BLK, NCOL * BLK), values.dtype)],
         in_specs=[hbm] * 3,
         out_specs=[vmem] * 5,
@@ -315,21 +343,34 @@
         pairs = []
         for r in range(row_count):
             for c in range(col_count):
-                distance = DISTANCES[name] or (3 if (r + c) % 2 == 1 else -3)
-                source = (r - distance if r % 2 == 1 else r + distance) % row_count
-                pairs.append((source * col_count + c, r * col_count + c))
+                if name == "f":
+                    distance = 2 if r % 4 < 2 else -2
+                elif name == "g":
+                    distance = -2 if r % 4 < 2 else 2
+                else:
+                    distance = DISTANCES[name] or (3 if (r + c) % 2 == 1 else -3)
+                    distance = -distance if r % 2 == 1 else distance
+                pairs.append(((r + distance) % row_count * col_count + c, r * col_count + c))
         return lax.ppermute(message, ("row", "col"), pairs)
 
     def swapped(block):
         return lax.ppermute(block, "col", [(0, 1), (1, 0)])
 
     left_other = swapped(left)
-    got = [towards(name, message) for name, message in zip("abcd", packed)]
-    inner, message, table = pl.pallas_call(
+    message_e = pl.pallas_call(
+        pack_e_kernel,
+        out_shape=blocks(SIZES["e"]),
+        in_specs=[vmem] * 2,
+        out_specs=vmem,
+        compiler_params=params,
+        name="pack_e",
+    )(left, left_other)
+    got = [towards(name, message) for name, message in zip(PERMUTES, (*packed, message_e))]
+    inner, table = pl.pallas_call(
         functools.partial(inner_kernel, nblocks, slots),
-        out_shape=[blocks(INNER, jnp.float32), blocks(1), jax.ShapeDtypeStruct(table_shape, jnp.int32)],
+        out_shape=[blocks(INNER, jnp.float32), jax.ShapeDtypeStruct(table_shape, jnp.int32)],
         in_specs=[hbm] * 2 + [smem] + [vmem] * 2,
-        out_specs=[vmem] * 3,
+        out_specs=[vmem] * 2,
         scratch_shapes=[
             pltpu.VMEM((2, NCOL * BLK, 2 * BLK), values.dtype),
             pltpu.SMEM(table_shape, jnp.int32),
@@ -340,7 +381,7 @@
         cost_estimate=cost(3 * 2 * 17, 4 * values.size),
         name="inner",
     )(*places, counts, left, left_other)
-    got.append(towards("e", message))
+    *got, inner = lax.optimization_barrier((*got, inner))
     staged = swapped(
         pl.pallas_call(
             stage_kernel,

time: 28.2 us -> 30.1 us (1.067)
  waiting for transfers between devices: 11.5 us -> 13.4 us
    ppermute x5, waiting for transfers between devices: 10.7 us -> 12.7 us  [towards(): return lax.ppermute(message, ('row', 'col'), pairs)]
  transfers between devices with their start and end apart: 7 -> 7, of which waited for: 3 -> 5; matrix products, arithmetic and copies ran while one was open for 0% -> 0% of each run, Pallas kernels for 10% -> 10%
where the time goes in v4:
time: 30.1 us; the launch traced here: 29.9 us
  waiting for transfers between devices  13.4 us (45%)
  starting transfers between devices  8.83 us (29%)
  Pallas kernels  6.92 us (23%)
  between operations  0.71 us (2%)
    ppermute x5, waiting for transfers between devices, towards(): return lax.ppermute(message, ('row', 'col'), pairs)  12.7 us
    ppermute x5, starting transfers between devices, towards(): return lax.ppermute(message, ('row', 'col'), pairs)  8.25 us
    pallas_call x1, Pallas kernels, local(): pl.pallas_call(functools.partial(multiply_kernel, slots), out_shape=jax.S...  2.54 us
    pallas_call x1, Pallas kernels, local(): pl.pallas_call(functools.partial(inner_kernel, nblocks, slots), out_shape...  1.62 us
    pallas_call x1, Pallas kernels, local(): pl.pallas_call(functools.partial(pack_kernel, nblocks, slots), out_shape=...  1.36 us
    pallas_call x1, Pallas kernels, local(): pl.pallas_call(outer_kernel, out_shape=blocks(BR * NCOL, jnp.float32), in...  1.31 us
    ppermute x2, waiting for transfers between devices, swapped(): return lax.ppermute(block, 'col', [(0, 1), (1, 0)])  0.77 us
  transfers between devices with their start and end apart: 7, of which 5 were waited for; matrix products, arithmetic and copies ran while one was open for 0% of the time, Pallas kernels for 10%

profile of v4, /device:TPU:0, one launch (start us, length us, event | category | flops | bytes accessed | tf_op | source)
XLA Modules:
  0.0 29.9 jit_solution(2701226209948122843)
XLA Ops:
  0.0 1.4 %pack.1 = (bf16[11,128,128]{2,1,0:T(8,128)(2,1)S(1)}, bf16[7,128,128]{2,1,0:T(8,128)(2,1)S(1)}, bf16[7,128,128]{2,1,0:T(8,128)(2,1)S(1)}, bf16[7,128,128]{2,1,0:T(8,128)(2,1)S(1)}, bf16[384,1152]{1,0:T(8,128)(2,1)S(1)}) custom-call(s32[1,23]{1,0:T(1,128)} %rows_ref.3, s32[1,23]{1,0:T(1,128)} %cols_ref.3, bf16[1,23,128,128]{3,2,1,0:T(8,128)(2,1)} %values_ref.1), custom_call_target="tpu_custom_call" | custom-call | tf_op jit(solution)/shard_map/pack/pallas_call | solution.py:326
  1.4 0.5 %collective-permute-start = (bf16[384,1152]{1,0:T(8,128)(2,1)S(1)}, bf16[384,1152]{1,0:T(8,128)(2,1)S(1)}, u32[]{:S(2)}, u32[]{:S(2)}) collective-permute-start(bf16[384,1152]{1,0:T(8,128)(2,1)S(1)} %get-tuple-element.18.left_ref), channel_id=1, source_target_pairs={{0,1},{1,0},{2,3},{3,2},{4,5},{5,4},{6,7},{7,6},{8,9},{9,8},{10,11... | collective-permute-start | bytes 2654216 | tf_op jit(solution)/shard_map/ppermute | solution.py:357
  1.9 2.6 %collective-permute-start.1 = (bf16[11,128,128]{2,1,0:T(8,128)(2,1)S(1)}, bf16[11,128,128]{2,1,0:T(8,128)(2,1)S(1)}, u32[]{:S(2)}, u32[]{:S(2)}) collective-permute-start(bf16[11,128,128]{2,1,0:T(8,128)(2,1)S(1)} %get-tuple-element.19), channel_id=1, source_target_pairs={{2,0},{3,1},{0,2},{1,3},{6,4},{7,5},{4,6},{5,7},{10,8},{11,9},{8,1... | collective-permute-start | bytes 1081352 | tf_op jit(solution)/shard_map/ppermute | solution.py:354
  4.4 1.6 %collective-permute-start.2 = (bf16[7,128,128]{2,1,0:T(8,128)(2,1)S(1)}, bf16[7,128,128]{2,1,0:T(8,128)(2,1)S(1)}, u32[]{:S(2)}, u32[]{:S(2)}) collective-permute-start(bf16[7,128,128]{2,1,0:T(8,128)(2,1)S(1)} %get-tuple-element.20), channel_id=1, source_target_pairs={{4,0},{5,1},{6,2},{7,3},{0,4},{1,5},{2,6},{3,7},{12,8},{13,9},{14,... | collective-permute-start | bytes 688136 | tf_op jit(solution)/shard_map/ppermute | solution.py:354
  6.0 2.5 %collective-permute-start.3 = (bf16[7,128,128]{2,1,0:T(8,128)(2,1)S(1)}, bf16[7,128,128]{2,1,0:T(8,128)(2,1)S(1)}, u32[]{:S(2)}, u32[]{:S(2)}) collective-permute-start(bf16[7,128,128]{2,1,0:T(8,128)(2,1)S(1)} %get-tuple-element.21), channel_id=1, source_target_pairs={{12,0},{13,1},{14,2},{15,3},{8,4},{9,5},{10,6},{11,7},{4,8},{5,9},... | collective-permute-start | bytes 688136 | tf_op jit(solution)/shard_map/ppermute | solution.py:354
  8.5 1.3 %collective-permute-start.4 = (bf16[7,128,128]{2,1,0:T(8,128)(2,1)S(1)}, bf16[7,128,128]{2,1,0:T(8,128)(2,1)S(1)}, u32[]{:S(2)}, u32[]{:S(2)}) collective-permute-start(bf16[7,128,128]{2,1,0:T(8,128)(2,1)S(1)} %get-tuple-element.22), channel_id=1, source_target_pairs={{14,0},{15,1},{4,2},{5,3},{2,4},{3,5},{8,6},{9,7},{6,8},{7,9},{12,... | collective-permute-start | bytes 688136 | tf_op jit(solution)/shard_map/ppermute | solution.py:354
  10.5 0.0 collective-permute-done.left_other_ref
  10.5 0.3 %collective-permute-start.5 = (bf16[1,128,128]{2,1,0:T(8,128)(2,1)S(1)}, bf16[1,128,128]{2,1,0:T(8,128)(2,1)S(1)}, u32[]{:S(2)}, u32[]{:S(2)}) collective-permute-start(bf16[1,128,128]{2,1,0:T(8,128)(2,1)S(1)} %pack_e.1), channel_id=1, source_target_pairs={{10,0},{7,1},{12,2},{9,3},{14,4},{11,5},{0,6},{13,7},{2,8},{15,9},... | collective-permute-start | bytes 98312 | tf_op jit(solution)/shard_map/ppermute | solution.py:354
  10.8 1.6 %inner.1 = (f32[6,128,128]{2,1,0:T(8,128)S(1)}, s32[1,128]{1,0:T(1,128)S(1)}) custom-call(s32[1,23]{1,0:T(1,128)} %rows_ref.3, s32[1,23]{1,0:T(1,128)} %cols_ref.3, s32[1,1]{1,0:T(1,128)S(6)} %copy.5.counts_ref, bf16[384,1152]{1,0:T(8,128)(2,1)S(1)} %get-tuple-element.18.left_ref, bf16[384,1152]{1,0:T(8,128)(2,1)S(1)} %collective-permute-done.left_other_ref), custom_call_target="tpu_custom_call" | custom-call | flops 427819008 | bytes 1507328 | tf_op jit(solution)/shard_map/inner/pallas_call | solution.py:369
  12.5 0.4 %collective-permute-done.2.refs_1_.rest_1_ = bf16[7,128,128]{2,1,0:T(8,128)(2,1)S(1)} collective-permute-done((bf16[7,128,128]{2,1,0:T(8,128)(2,1)S(1)}, bf16[7,128,128]{2,1,0:T(8,128)(2,1)S(1)}, u32[]{:S(2)}, u32[]{:S(2)}) %collective-permute-start.2) | collective-permute-done | bytes 229408 | tf_op jit(solution)/shard_map/ppermute | solution.py:354
  12.9 7.0 %collective-permute-done.3.refs_2_.rest_2_ = bf16[7,128,128]{2,1,0:T(8,128)(2,1)S(1)} collective-permute-done((bf16[7,128,128]{2,1,0:T(8,128)(2,1)S(1)}, bf16[7,128,128]{2,1,0:T(8,128)(2,1)S(1)}, u32[]{:S(2)}, u32[]{:S(2)}) %collective-permute-start.3) | collective-permute-done | bytes 229408 | tf_op jit(solution)/shard_map/ppermute | solution.py:354
  19.9 4.5 %collective-permute-done.4.refs_3_.rest_3_ = bf16[7,128,128]{2,1,0:T(8,128)(2,1)S(1)} collective-permute-done((bf16[7,128,128]{2,1,0:T(8,128)(2,1)S(1)}, bf16[7,128,128]{2,1,0:T(8,128)(2,1)S(1)}, u32[]{:S(2)}, u32[]{:S(2)}) %collective-permute-start.4) | collective-permute-done | bytes 229408 | tf_op jit(solution)/shard_map/ppermute | solution.py:354
  24.4 0.0 collective-permute-done.1.refs_0_.rest_0_
  24.4 0.7 %collective-permute-done.5.refs_4_.rest_4_ = bf16[1,128,128]{2,1,0:T(8,128)(2,1)S(1)} collective-permute-done((bf16[1,128,128]{2,1,0:T(8,128)(2,1)S(1)}, bf16[1,128,128]{2,1,0:T(8,128)(2,1)S(1)}, u32[]{:S(2)}, u32[]{:S(2)}) %collective-permute-start.5) | collective-permute-done | bytes 32800 | tf_op jit(solution)/shard_map/ppermute | solution.py:354
  25.1 0.1 stage.1
  25.2 0.1 collective-permute-start.6
  25.3 1.3 %outer.1.outer_ref = f32[27,128,128]{2,1,0:T(8,128)S(1)} custom-call(bf16[384,1152]{1,0:T(8,128)(2,1)S(1)} %get-tuple-element.18.left_ref, bf16[384,1152]{1,0:T(8,128)(2,1)S(1)} %collective-permute-done.left_other_ref, bf16[11,128,128]{2,1,0:T(8,128)(2,1)S(1)} %collective-permute-done.1.refs_0_.rest_0_, ...), custom_call_target="tpu_custom_call" | custom-call | flops 1409286144 | bytes 3768320 | tf_op jit(solution)/shard_map/outer/pallas_call | solution.py:395
  26.6 0.8 %collective-permute-done.6.staged_ref = bf16[20,128,128]{2,1,0:T(8,128)(2,1)S(1)} collective-permute-done((bf16[20,128,128]{2,1,0:T(8,128)(2,1)S(1)}, bf16[20,128,128]{2,1,0:T(8,128)(2,1)S(1)}, u32[]{:S(2)}, u32[]{:S(2)}) %collective-permute-start.6) | collective-permute-done | bytes 655392 | tf_op jit(solution)/shard_map/ppermute | solution.py:357
  27.4 2.5 %multiply.1 = f32[1,23,128,128]{3,2,1,0:T(8,128)} custom-call(bf16[384,1152]{1,0:T(8,128)(2,1)S(1)} %get-tuple-element.18.left_ref, bf16[384,1152]{1,0:T(8,128)(2,1)S(1)} %collective-permute-done.left_other_ref, bf16[20,128,128]{2,1,0:T(8,128)(2,1)S(1)} %collective-permute-done.6.staged_ref, f32[27,128,128]{2,1,0:T(8,128)S(1)} %outer.1.outer_ref, ...), custom_call_target="tpu_custom_call" | custom-call | tf_op jit(solution)/shard_map/multiply/pallas_call | solution.py:405
  (1 shorter events, 0.0 us)
Async XLA Ops:
  1.4 9.1 %collective-permute-start = (bf16[384,1152]{1,0:T(8,128)(2,1)S(1)}, bf16[384,1152]{1,0:T(8,128)(2,1)S(1)}, u32[]{:S(2)}, u32[]{:S(2)}) collective-permute-start(bf16[384,1152]{1,0:T(8,128)(2,1)S(1)} %get-tuple-element.18.left_ref), channel_id=1, source_target_pairs={{0,1},{1,0},{2,3},{3,2},{4,5},{5,4},{6,7},{7,6},{8,9},{9,8},{10,11... | collective-permute-start | bytes 2654216 | tf_op jit(solution)/shard_map/ppermute | solution.py:357
  1.9 22.5 %collective-permute-start.1 = (bf16[11,128,128]{2,1,0:T(8,128)(2,1)S(1)}, bf16[11,128,128]{2,1,0:T(8,128)(2,1)S(1)}, u32[]{:S(2)}, u32[]{:S(2)}) collective-permute-start(bf16[11,128,128]{2,1,0:T(8,128)(2,1)S(1)} %get-tuple-element.19), channel_id=1, source_target_pairs={{2,0},{3,1},{0,2},{1,3},{6,4},{7,5},{4,6},{5,7},{10,8},{11,9},{8,1... | collective-permute-start | bytes 1081352 | tf_op jit(solution)/shard_map/ppermute | solution.py:354
  4.4 8.4 %collective-permute-start.2 = (bf16[7,128,128]{2,1,0:T(8,128)(2,1)S(1)}, bf16[7,128,128]{2,1,0:T(8,128)(2,1)S(1)}, u32[]{:S(2)}, u32[]{:S(2)}) collective-permute-start(bf16[7,128,128]{2,1,0:T(8,128)(2,1)S(1)} %get-tuple-element.20), channel_id=1, source_target_pairs={{4,0},{5,1},{6,2},{7,3},{0,4},{1,5},{2,6},{3,7},{12,8},{13,9},{14,... | collective-permute-start | bytes 688136 | tf_op jit(solution)/shard_map/ppermute | solution.py:354
  6.0 13.9 %collective-permute-start.3 = (bf16[7,128,128]{2,1,0:T(8,128)(2,1)S(1)}, bf16[7,128,128]{2,1,0:T(8,128)(2,1)S(1)}, u32[]{:S(2)}, u32[]{:S(2)}) collective-permute-start(bf16[7,128,128]{2,1,0:T(8,128)(2,1)S(1)} %get-tuple-element.21), channel_id=1, source_target_pairs={{12,0},{13,1},{14,2},{15,3},{8,4},{9,5},{10,6},{11,7},{4,8},{5,9},... | collective-permute-start | bytes 688136 | tf_op jit(solution)/shard_map/ppermute | solution.py:354
  8.5 15.9 %collective-permute-start.4 = (bf16[7,128,128]{2,1,0:T(8,128)(2,1)S(1)}, bf16[7,128,128]{2,1,0:T(8,128)(2,1)S(1)}, u32[]{:S(2)}, u32[]{:S(2)}) collective-permute-start(bf16[7,128,128]{2,1,0:T(8,128)(2,1)S(1)} %get-tuple-element.22), channel_id=1, source_target_pairs={{14,0},{15,1},{4,2},{5,3},{2,4},{3,5},{8,6},{9,7},{6,8},{7,9},{12,... | collective-permute-start | bytes 688136 | tf_op jit(solution)/shard_map/ppermute | solution.py:354
  10.5 14.6 %collective-permute-start.5 = (bf16[1,128,128]{2,1,0:T(8,128)(2,1)S(1)}, bf16[1,128,128]{2,1,0:T(8,128)(2,1)S(1)}, u32[]{:S(2)}, u32[]{:S(2)}) collective-permute-start(bf16[1,128,128]{2,1,0:T(8,128)(2,1)S(1)} %pack_e.1), channel_id=1, source_target_pairs={{10,0},{7,1},{12,2},{9,3},{14,4},{11,5},{0,6},{13,7},{2,8},{15,9},... | collective-permute-start | bytes 98312 | tf_op jit(solution)/shard_map/ppermute | solution.py:354
  25.2 2.2 %collective-permute-start.6 = (bf16[20,128,128]{2,1,0:T(8,128)(2,1)S(1)}, bf16[20,128,128]{2,1,0:T(8,128)(2,1)S(1)}, u32[]{:S(2)}, u32[]{:S(2)}) collective-permute-start(bf16[20,128,128]{2,1,0:T(8,128)(2,1)S(1)} %stage.1), channel_id=1, source_target_pairs={{0,1},{1,0},{2,3},{3,2},{4,5},{5,4},{6,7},{7,6},{8,9},{9,8},{10,11... | collective-permute-start | bytes 1966088 | tf_op jit(solution)/shard_map/ppermute | solution.py:357

commit v5 on v4

--- a/solution.py
+++ b/solution.py
@@ -17,31 +17,37 @@
 PLACES = 32
 VMEM_LIMIT = 12 * 2**20
 
-DISTANCES = {"a": 1, "b": -1, "c": -2, "d": 2, "e": None}
+DISTANCES = {"a": 1, "c": -2, "d": 2, "w": 1, "e": None}
 SENT = {
-    ("a", 1): [(3, 3), (5, 5), (3, 5), (3, 9), (4, 9), (5, 9), (3, -3), (3, -1), (4, -3), (4, -1), (5, -1)],
-    ("a", 0): [(4, 4), (3, 4), (5, 4), (3, 6), (4, 6), (5, 6), (3, 8), (5, 8), (3, -2), (5, -2), (3, -4)],
-    ("b", 1): [(-1, -1), (-3, -3), (-1, -3), (-1, -7), (-2, -7), (-3, -7), (-2, -5)],
-    ("b", 0): [(-2, -2), (-1, -2), (-3, -2), (-2, 4), (-1, -4), (-1, -6), (-3, -6)],
-    ("c", 1): [(-5, -5), (-4, -7), (-5, -7), (-6, -7), (-5, -1), (-5, -3), (-4, -3)],
-    ("c", 0): [(-4, -4), (-6, -6), (-4, -6), (-5, -4), (-5, -6), (-4, -2), (-6, -2)],
-    ("d", 1): [(7, 7), (6, 9), (7, 9), (8, 9), (6, -1), (7, 3), (7, 5)],
-    ("d", 0): [(6, 6), (8, 8), (6, 8), (7, 6), (7, 8), (7, 4), (8, 4)],
+    ("a", 1): [(3, 3), (5, 5), (3, 5), (3, 7), (4, 7), (5, 7), (3, 9), (4, 9), (5, 9), (3, -3), (3, -1), (4, -3), (5, -1)],
+    ("a", 0): [(4, 4), (3, 4), (5, 4), (3, 6), (4, 6), (5, 6), (3, 8), (4, 8), (5, 8), (3, -2), (4, -2), (5, -2), (3, -4)],
+    ("c", 1): [(-5, -5), (-4, -7), (-5, -7), (-6, -7), (-5, -1), (-5, -3), (-6, -1), (-6, -3)],
+    ("c", 0): [(-4, -4), (-6, -6), (-4, -6), (-5, -4), (-5, -6), (-5, -2), (-6, -2)],
+    ("d", 1): [(7, 7), (6, 7), (6, 9), (7, 9), (8, 9), (6, -1), (6, 1)],
+    ("d", 0): [(6, 6), (8, 8), (6, 8), (7, 8), (6, 12), (7, 12), (8, 12)],
     ("e", 1): [(9, 9)],
     ("e", 0): [(-7, -7)],
 }
-PERMUTES = ("a", "f", "g", "b", "e")
-SIZES = {name: len(SENT[name, 1]) for name in DISTANCES}
-SIZES["f"] = SIZES["g"] = SIZES["c"]
-STAGED = {
-    parity: [
+for parity in (0, 1):
+    SENT["w", parity] = [(5 - k, 5 - j) for k, j in SENT["d", 1 - parity]]
+SIZES = {name: max(len(SENT[name, parity]) for parity in (0, 1)) for name in DISTANCES}
+
+
+def outside(k, j):
+    return all(LOW <= w <= HIGH and not 0 <= w < BR for w in (k, j))
+
+
+def needed_by_other_core(parity):
+    there = [{k, j} for name in DISTANCES for k, j in SENT[name, 1 - parity]]
+    return [
         (name, n, (k, j))
         for name in DISTANCES
         for n, (k, j) in enumerate(SENT[name, parity])
-        if k % 2 != j % 2 or (k, j) == (-7, -7)
+        if outside(k, j) and (k % 2 != j % 2 and {k, j} not in there or (k, j) == (-7, -7))
     ]
-    for parity in (0, 1)
-}
+
+
+STAGED = {parity: needed_by_other_core(parity) for parity in (0, 1)}
 STAGED_SIZE = max(len(found) for found in STAGED.values())
 
 
@@ -57,11 +63,6 @@
     parity = own_parity()
     for mine in (0, 1):
         pl.when(parity == mine)(functools.partial(body, mine))
-
-
-def received_c_first():
-    place = lax.axis_index("row") % 4
-    return (place == 1) | (place == 2)
 
 
 def slot_position(rows_ref, cols_ref, slot, nblocks):
@@ -85,7 +86,7 @@
 
 
 def pack_kernel(nblocks, slots, rows_ref, cols_ref, values_ref, *rest):
-    a_ref, f_ref, g_ref, b_ref, left_ref, held, table, *index, sems, value_sem = rest
+    a_ref, c_ref, d_ref, left_ref, held, table, *index, sems, value_sem = rest
     load = pltpu.make_async_copy(values_ref.at[0], held.at[pl.ds(0, slots)], value_sem)
     load.start()
     copies = index_copies((rows_ref, cols_ref), index, sems)
@@ -100,7 +101,6 @@
         real_row, row, band = slot_position(*index, m, nblocks)
         table[jnp.where(real_row >= 0, row * WIDTH + band, BR * WIDTH)] = m
     load.wait()
-    sends_c_in_f = ~received_c_first()
 
     def table_place(name, k, j):
         row, col = position_at_sender(name, k, j)
@@ -108,13 +108,13 @@
 
     @for_own_parity
     def _(mine):
-        for name, ref in (("a", a_ref), ("b", b_ref)):
-            for n, (k, j) in enumerate(SENT[name, 1 - mine]):
-                ref[n] = held[table[table_place(name, k, j)]]
-        for n in range(SIZES["f"]):
-            c, d = (table_place(name, *SENT[name, mine][n]) for name in "cd")
-            f_ref[n] = held[table[jnp.where(sends_c_in_f, c, d)]]
-            g_ref[n] = held[table[jnp.where(sends_c_in_f, d, c)]]
+        for name, ref in (("a", a_ref), ("c", c_ref), ("d", d_ref)):
+            wanted = SENT[name, (mine + DISTANCES[name]) % 2]
+            for n in range(SIZES[name]):
+                if n < len(wanted):
+                    ref[n] = held[table[table_place(name, *wanted[n])]]
+                else:
+                    ref[n] = jnp.zeros((BLK, BLK), ref.dtype)
         columns = columns_of(mine)
         for i in range(BR):
             for n in range(NCOL):
@@ -153,9 +153,6 @@
 def read_block(refs, source, place):
     if isinstance(place, tuple):
         return refs[source][pl.ds(place[0] * BLK, BLK), pl.ds(place[1] * BLK, BLK)]
-    if source in ("c", "d"):
-        f, g = refs["f"][place], refs["g"][place]
-        return jnp.where(received_c_first(), *((f, g) if source == "c" else (g, f)))
     return refs[source][place]
 
 
@@ -233,7 +230,7 @@
 
 
 def stage_kernel(*refs):
-    got = dict(zip(PERMUTES, refs))
+    got = dict(zip(DISTANCES, refs))
     out_ref = refs[-1]
 
     @for_own_parity
@@ -245,8 +242,8 @@
 
 
 def outer_kernel(left_ref, left_other_ref, *rest):
-    refs = {("left", True): left_ref, ("left", False): left_other_ref, **dict(zip(PERMUTES, rest))}
-    out_ref, right = rest[len(PERMUTES) :]
+    refs = {("left", True): left_ref, ("left", False): left_other_ref, **dict(zip(DISTANCES, rest))}
+    out_ref, right = rest[len(DISTANCES) :]
 
     @for_own_parity
     def _(mine):
@@ -325,10 +322,10 @@
 
     *packed, left = pl.pallas_call(
         functools.partial(pack_kernel, nblocks, slots),
-        out_shape=[blocks(SIZES[name]) for name in "afgb"]
+        out_shape=[blocks(SIZES[name]) for name in "acd"]
         + [jax.ShapeDtypeStruct((BR * BLK, NCOL * BLK), values.dtype)],
         in_specs=[hbm] * 3,
-        out_specs=[vmem] * 5,
+        out_specs=[vmem] * 4,
         scratch_shapes=[
             pltpu.VMEM((slots + 1, BLK, BLK), values.dtype),
             pltpu.SMEM((BR * WIDTH + 1,), jnp.int32),
@@ -343,13 +340,8 @@
         pairs = []
         for r in range(row_count):
             for c in range(col_count):
-                if name == "f":
-                    distance = 2 if r % 4 < 2 else -2
-                elif name == "g":
-                    distance = -2 if r % 4 < 2 else 2
-                else:
-                    distance = DISTANCES[name] or (3 if (r + c) % 2 == 1 else -3)
-                    distance = -distance if r % 2 == 1 else distance
+                distance = DISTANCES[name] or (3 if (r + c) % 2 == 1 else -3)
+                distance = -distance if r % 2 == 1 else distance
                 pairs.append(((r + distance) % row_count * col_count + c, r * col_count + c))
         return lax.ppermute(message, ("row", "col"), pairs)
 
@@ -365,7 +357,8 @@
         compiler_params=params,
         name="pack_e",
     )(left, left_other)
-    got = [towards(name, message) for name, message in zip(PERMUTES, (*packed, message_e))]
+    a, c, d = (towards(name, message) for name, message in zip("acd", packed))
+    got = [a, c, d, towards("w", d), towards("e", message_e)]
     inner, table = pl.pallas_call(
         functools.partial(inner_kernel, nblocks, slots),
         out_shape=[blocks(INNER, jnp.float32), jax.ShapeDtypeStruct(table_shape, jnp.int32)],

time: 30.1 us -> 28.7 us (0.953)
  waiting for transfers between devices: 13.4 us -> 12.5 us
    ppermute x5, waiting for transfers between devices: 12.7 us -> 11.8 us  [towards(): return lax.ppermute(message, ('row', 'col'), pairs)]
  transfers between devices with their start and end apart: 7 -> 7, of which waited for: 5 -> 5; matrix products, arithmetic and copies ran while one was open for 0% -> 0% of each run, Pallas kernels for 10% -> 11%
where the time goes in v5:
time: 28.7 us; the launch traced here: 28.6 us
  waiting for transfers between devices  12.5 us (44%)
  starting transfers between devices  8.55 us (30%)
  Pallas kernels  6.81 us (24%)
  between operations  0.72 us (3%)
    ppermute x5, waiting for transfers between devices, towards(): return lax.ppermute(message, ('row', 'col'), pairs)  11.8 us
    ppermute x5, starting transfers between devices, towards(): return lax.ppermute(message, ('row', 'col'), pairs)  7.97 us
    pallas_call x1, Pallas kernels, local(): pl.pallas_call(functools.partial(multiply_kernel, slots), out_shape=jax.S...  2.4 us
    pallas_call x1, Pallas kernels, local(): pl.pallas_call(functools.partial(inner_kernel, nblocks, slots), out_shape...  1.64 us
    pallas_call x1, Pallas kernels, local(): pl.pallas_call(functools.partial(pack_kernel, nblocks, slots), out_shape=...  1.35 us
    pallas_call x1, Pallas kernels, local(): pl.pallas_call(outer_kernel, out_shape=blocks(BR * NCOL, jnp.float32), in...  1.35 us
    ppermute x2, waiting for transfers between devices, swapped(): return lax.ppermute(block, 'col', [(0, 1), (1, 0)])  0.64 us
    ppermute x2, starting transfers between devices, swapped(): return lax.ppermute(block, 'col', [(0, 1), (1, 0)])  0.59 us
  transfers between devices with their start and end apart: 7, of which 5 were waited for; matrix products, arithmetic and copies ran while one was open for 0% of the time, Pallas kernels for 11%

profile of v5, /device:TPU:0, one launch (start us, length us, event | category | flops | bytes accessed | tf_op | source)
XLA Modules:
  0.0 28.6 jit_solution(11229048715302992081)
XLA Ops:
  0.0 1.4 %pack.1 = (bf16[13,128,128]{2,1,0:T(8,128)(2,1)S(1)}, bf16[8,128,128]{2,1,0:T(8,128)(2,1)S(1)}, bf16[7,128,128]{2,1,0:T(8,128)(2,1)S(1)}, bf16[384,1152]{1,0:T(8,128)(2,1)S(1)}) custom-call(s32[1,23]{1,0:T(1,128)} %rows_ref.3, s32[1,23]{1,0:T(1,128)} %cols_ref.3, bf16[1,23,128,128]{3,2,1,0:T(8,128)(2,1)} %values_ref.1), custom_call_target="tpu_custom_call" | custom-call | tf_op jit(solution)/shard_map/pack/pallas_call | solution.py:323
  1.4 0.5 %collective-permute-start = (bf16[384,1152]{1,0:T(8,128)(2,1)S(1)}, bf16[384,1152]{1,0:T(8,128)(2,1)S(1)}, u32[]{:S(2)}, u32[]{:S(2)}) collective-permute-start(bf16[384,1152]{1,0:T(8,128)(2,1)S(1)} %get-tuple-element.17.left_ref), channel_id=1, source_target_pairs={{0,1},{1,0},{2,3},{3,2},{4,5},{5,4},{6,7},{7,6},{8,9},{9,8},{10,11... | collective-permute-start | bytes 2654216 | tf_op jit(solution)/shard_map/ppermute | solution.py:349
  1.9 4.7 %collective-permute-start.3 = (bf16[7,128,128]{2,1,0:T(8,128)(2,1)S(1)}, bf16[7,128,128]{2,1,0:T(8,128)(2,1)S(1)}, u32[]{:S(2)}, u32[]{:S(2)}) collective-permute-start(bf16[7,128,128]{2,1,0:T(8,128)(2,1)S(1)} %get-tuple-element.20), channel_id=1, source_target_pairs={{4,0},{5,1},{14,2},{15,3},{8,4},{9,5},{2,6},{3,7},{12,8},{13,9},{6... | collective-permute-start | bytes 688136 | tf_op jit(solution)/shard_map/ppermute | solution.py:346
  6.5 0.0 collective-permute-start.1
  6.5 1.0 %collective-permute-start.2 = (bf16[8,128,128]{2,1,0:T(8,128)(2,1)S(1)}, bf16[8,128,128]{2,1,0:T(8,128)(2,1)S(1)}, u32[]{:S(2)}, u32[]{:S(2)}) collective-permute-start(bf16[8,128,128]{2,1,0:T(8,128)(2,1)S(1)} %get-tuple-element.19), channel_id=1, source_target_pairs={{12,0},{13,1},{6,2},{7,3},{0,4},{1,5},{10,6},{11,7},{4,8},{5,9},{1... | collective-permute-start | bytes 786440 | tf_op jit(solution)/shard_map/ppermute | solution.py:346
  7.6 4.9 %collective-permute-done.3.refs_2_.rest_2_ = bf16[7,128,128]{2,1,0:T(8,128)(2,1)S(1)} collective-permute-done((bf16[7,128,128]{2,1,0:T(8,128)(2,1)S(1)}, bf16[7,128,128]{2,1,0:T(8,128)(2,1)S(1)}, u32[]{:S(2)}, u32[]{:S(2)}) %collective-permute-start.3) | collective-permute-done | bytes 229408 | tf_op jit(solution)/shard_map/ppermute | solution.py:346
  12.5 2.2 %collective-permute-start.4 = (bf16[7,128,128]{2,1,0:T(8,128)(2,1)S(1)}, bf16[7,128,128]{2,1,0:T(8,128)(2,1)S(1)}, u32[]{:S(2)}, u32[]{:S(2)}) collective-permute-start(bf16[7,128,128]{2,1,0:T(8,128)(2,1)S(1)} %collective-permute-done.3.refs_2_.rest_2_), channel_id=1, source_target_pairs={{2,0},{3,1},{0,2},{1,3},{6,4},{7,5},{4,6},{5,7},{10,8},{11,9},{8,1... | collective-permute-start | bytes 688136 | tf_op jit(solution)/shard_map/ppermute | solution.py:346
  15.4 0.0 collective-permute-done.left_other_ref
  15.4 0.1 collective-permute-start.5
  15.5 1.6 %inner.1 = (f32[6,128,128]{2,1,0:T(8,128)S(1)}, s32[1,128]{1,0:T(1,128)S(1)}) custom-call(s32[1,23]{1,0:T(1,128)} %rows_ref.3, s32[1,23]{1,0:T(1,128)} %cols_ref.3, s32[1,1]{1,0:T(1,128)S(6)} %copy.5.counts_ref, bf16[384,1152]{1,0:T(8,128)(2,1)S(1)} %get-tuple-element.17.left_ref, bf16[384,1152]{1,0:T(8,128)(2,1)S(1)} %collective-permute-done.left_other_ref), custom_call_target="tpu_custom_call" | custom-call | flops 427819008 | bytes 1507328 | tf_op jit(solution)/shard_map/inner/pallas_call | solution.py:362
  17.1 1.9 %collective-permute-done.2.refs_1_.rest_1_ = bf16[8,128,128]{2,1,0:T(8,128)(2,1)S(1)} collective-permute-done((bf16[8,128,128]{2,1,0:T(8,128)(2,1)S(1)}, bf16[8,128,128]{2,1,0:T(8,128)(2,1)S(1)}, u32[]{:S(2)}, u32[]{:S(2)}) %collective-permute-start.2) | collective-permute-done | bytes 262176 | tf_op jit(solution)/shard_map/ppermute | solution.py:346
  19.0 0.2 collective-permute-done.1.refs_0_.rest_0_
  19.2 4.8 %collective-permute-done.4.refs_3_.rest_3_ = bf16[7,128,128]{2,1,0:T(8,128)(2,1)S(1)} collective-permute-done((bf16[7,128,128]{2,1,0:T(8,128)(2,1)S(1)}, bf16[7,128,128]{2,1,0:T(8,128)(2,1)S(1)}, u32[]{:S(2)}, u32[]{:S(2)}) %collective-permute-start.4) | collective-permute-done | bytes 229408 | tf_op jit(solution)/shard_map/ppermute | solution.py:346
  24.0 0.0 collective-permute-done.5.refs_4_.rest_4_
  24.1 0.1 collective-permute-start.6
  24.2 1.3 %outer.1.outer_ref = f32[27,128,128]{2,1,0:T(8,128)S(1)} custom-call(bf16[384,1152]{1,0:T(8,128)(2,1)S(1)} %get-tuple-element.17.left_ref, bf16[384,1152]{1,0:T(8,128)(2,1)S(1)} %collective-permute-done.left_other_ref, bf16[13,128,128]{2,1,0:T(8,128)(2,1)S(1)} %collective-permute-done.1.refs_0_.rest_0_, ...), custom_call_target="tpu_custom_call" | custom-call | flops 1409286144 | bytes 3768320 | tf_op jit(solution)/shard_map/outer/pallas_call | solution.py:388
  25.5 0.6 %collective-permute-done.6.staged_ref = bf16[18,128,128]{2,1,0:T(8,128)(2,1)S(1)} collective-permute-done((bf16[18,128,128]{2,1,0:T(8,128)(2,1)S(1)}, bf16[18,128,128]{2,1,0:T(8,128)(2,1)S(1)}, u32[]{:S(2)}, u32[]{:S(2)}) %collective-permute-start.6) | collective-permute-done | bytes 589856 | tf_op jit(solution)/shard_map/ppermute | solution.py:349
  26.2 2.4 %multiply.1 = f32[1,23,128,128]{3,2,1,0:T(8,128)} custom-call(bf16[384,1152]{1,0:T(8,128)(2,1)S(1)} %get-tuple-element.17.left_ref, bf16[384,1152]{1,0:T(8,128)(2,1)S(1)} %collective-permute-done.left_other_ref, bf16[18,128,128]{2,1,0:T(8,128)(2,1)S(1)} %collective-permute-done.6.staged_ref, f32[27,128,128]{2,1,0:T(8,128)S(1)} %outer.1.outer_ref, ...), custom_call_target="tpu_custom_call" | custom-call | tf_op jit(solution)/shard_map/multiply/pallas_call | solution.py:398
  (2 shorter events, 0.1 us)
Async XLA Ops:
  1.4 14.0 %collective-permute-start = (bf16[384,1152]{1,0:T(8,128)(2,1)S(1)}, bf16[384,1152]{1,0:T(8,128)(2,1)S(1)}, u32[]{:S(2)}, u32[]{:S(2)}) collective-permute-start(bf16[384,1152]{1,0:T(8,128)(2,1)S(1)} %get-tuple-element.17.left_ref), channel_id=1, source_target_pairs={{0,1},{1,0},{2,3},{3,2},{4,5},{5,4},{6,7},{7,6},{8,9},{9,8},{10,11... | collective-permute-start | bytes 2654216 | tf_op jit(solution)/shard_map/ppermute | solution.py:349
  1.9 10.6 %collective-permute-start.3 = (bf16[7,128,128]{2,1,0:T(8,128)(2,1)S(1)}, bf16[7,128,128]{2,1,0:T(8,128)(2,1)S(1)}, u32[]{:S(2)}, u32[]{:S(2)}) collective-permute-start(bf16[7,128,128]{2,1,0:T(8,128)(2,1)S(1)} %get-tuple-element.20), channel_id=1, source_target_pairs={{4,0},{5,1},{14,2},{15,3},{8,4},{9,5},{2,6},{3,7},{12,8},{13,9},{6... | collective-permute-start | bytes 688136 | tf_op jit(solution)/shard_map/ppermute | solution.py:346
  6.5 12.7 %collective-permute-start.1 = (bf16[13,128,128]{2,1,0:T(8,128)(2,1)S(1)}, bf16[13,128,128]{2,1,0:T(8,128)(2,1)S(1)}, u32[]{:S(2)}, u32[]{:S(2)}) collective-permute-start(bf16[13,128,128]{2,1,0:T(8,128)(2,1)S(1)} %get-tuple-element.18), channel_id=1, source_target_pairs={{2,0},{3,1},{0,2},{1,3},{6,4},{7,5},{4,6},{5,7},{10,8},{11,9},{8,1... | collective-permute-start | bytes 1277960 | tf_op jit(solution)/shard_map/ppermute | solution.py:346
  6.5 12.4 %collective-permute-start.2 = (bf16[8,128,128]{2,1,0:T(8,128)(2,1)S(1)}, bf16[8,128,128]{2,1,0:T(8,128)(2,1)S(1)}, u32[]{:S(2)}, u32[]{:S(2)}) collective-permute-start(bf16[8,128,128]{2,1,0:T(8,128)(2,1)S(1)} %get-tuple-element.19), channel_id=1, source_target_pairs={{12,0},{13,1},{6,2},{7,3},{0,4},{1,5},{10,6},{11,7},{4,8},{5,9},{1... | collective-permute-start | bytes 786440 | tf_op jit(solution)/shard_map/ppermute | solution.py:346
  12.5 11.5 %collective-permute-start.4 = (bf16[7,128,128]{2,1,0:T(8,128)(2,1)S(1)}, bf16[7,128,128]{2,1,0:T(8,128)(2,1)S(1)}, u32[]{:S(2)}, u32[]{:S(2)}) collective-permute-start(bf16[7,128,128]{2,1,0:T(8,128)(2,1)S(1)} %collective-permute-done.3.refs_2_.rest_2_), channel_id=1, source_target_pairs={{2,0},{3,1},{0,2},{1,3},{6,4},{7,5},{4,6},{5,7},{10,8},{11,9},{8,1... | collective-permute-start | bytes 688136 | tf_op jit(solution)/shard_map/ppermute | solution.py:346
  15.4 8.6 %collective-permute-start.5 = (bf16[1,128,128]{2,1,0:T(8,128)(2,1)S(1)}, bf16[1,128,128]{2,1,0:T(8,128)(2,1)S(1)}, u32[]{:S(2)}, u32[]{:S(2)}) collective-permute-start(bf16[1,128,128]{2,1,0:T(8,128)(2,1)S(1)} %pack_e.1), channel_id=1, source_target_pairs={{10,0},{7,1},{12,2},{9,3},{14,4},{11,5},{0,6},{13,7},{2,8},{15,9},... | collective-permute-start | bytes 98312 | tf_op jit(solution)/shard_map/ppermute | solution.py:346
  24.1 2.1 %collective-permute-start.6 = (bf16[18,128,128]{2,1,0:T(8,128)(2,1)S(1)}, bf16[18,128,128]{2,1,0:T(8,128)(2,1)S(1)}, u32[]{:S(2)}, u32[]{:S(2)}) collective-permute-start(bf16[18,128,128]{2,1,0:T(8,128)(2,1)S(1)} %stage.1), channel_id=1, source_target_pairs={{0,1},{1,0},{2,3},{3,2},{4,5},{5,4},{6,7},{7,6},{8,9},{9,8},{10,11... | collective-permute-start | bytes 1769480 | tf_op jit(solution)/shard_map/ppermute | solution.py:349

commit v6 on v3

--- a/solution.py
+++ b/solution.py
@@ -172,7 +172,7 @@
 
 
 def inner_kernel(nblocks, slots, rows_ref, cols_ref, counts_ref, left_ref, left_other_ref, *rest):
-    made_ref, message_ref, table_ref, right, table, *index, sems, table_sem = rest
+    table_ref, out_ref, right, made, table, *index, sems, table_sem, out_sems = rest
     copies = index_copies((rows_ref, cols_ref), index, sems)
     for copy in copies:
         copy.start()
@@ -184,24 +184,42 @@
         total = columns_product(refs, right, mine, js, lambda source: True)
         for i in range(BR):
             for y in range(2):
-                made_ref[i * 2 + y] = block_of(total, i, y) if y < len(js) else jnp.zeros((BLK, BLK), made_ref.dtype)
-        i = 2 if mine == 0 else 0
-        n = columns_of(0).index(i)
-        message_ref[0] = refs["left", mine == 0][pl.ds(i * BLK, BLK), pl.ds(n * BLK, BLK)]
-
+                made[i * 2 + y] = block_of(total, i, y) if y < len(js) else jnp.zeros((BLK, BLK), made.dtype)
+
+    made[INNER] = jnp.zeros((BLK, BLK), made.dtype)
     for i in range(BR * NCOL + 1):
         table[0, i] = -1
     for copy in copies:
         copy.wait()
     count = counts_ref[0, 0]
+    parity = own_parity()
+    first, last = jnp.where(parity == 1, 4, 3), 4
+    stores = []
     for m in range(slots):
         _, row, band = slot_position(*index, m, nblocks)
-        place = jnp.where(m < count, row * NCOL + (row + band) // 2, BR * NCOL)
+        column = (row + band) // 2
+        used = m < count
+        place = jnp.where(used, row * NCOL + column, BR * NCOL)
         table[0, place] = m
-        table[0, PLACES + m] = place
+        here = ~used | ((column >= first) & (column <= last))
+        table[0, PLACES + m] = jnp.where(here, 0, 1)
+        source = jnp.where(used, row * 2 + column - first, INNER)
+        stores.append((here, pltpu.make_async_copy(made.at[jnp.where(here, source, 0)], out_ref.at[0, m], out_sems.at[m])))
     copy = pltpu.make_async_copy(table, table_ref, table_sem)
     copy.start()
+    for here, store in stores:
+        pl.when(here)(store.start)
     copy.wait()
+    for here, store in stores:
+        pl.when(here)(store.wait)
+
+
+def pack_e_kernel(left_ref, left_other_ref, e_ref):
+    @for_own_parity
+    def _(mine):
+        i = 2 if mine == 0 else 0
+        n = columns_of(0).index(i)
+        e_ref[0] = (left_ref if mine == 0 else left_other_ref)[pl.ds(i * BLK, BLK), pl.ds(n * BLK, BLK)]
 
 
 def stage_kernel(*refs):
@@ -230,44 +248,34 @@
                         out_ref[i * NCOL + columns_of(mine).index(j)] = block_of(total, i, y)
 
 
-def multiply_kernel(slots, left_ref, left_other_ref, staged_ref, outer_ref, inner_ref, table_ref, out_ref, *rest):
-    right, made, zero, table, table_sem, out_sems = rest
+def multiply_kernel(slots, left_ref, left_other_ref, staged_ref, outer_ref, table_ref, _, out_ref, *rest):
+    right, made, table, table_sem, out_sems = rest
     refs = {("left", True): left_ref, ("left", False): left_other_ref, "staged": staged_ref}
     load = pltpu.make_async_copy(table_ref, table, table_sem)
     load.start()
-    zero[...] = jnp.zeros((BLK, BLK), zero.dtype)
-    load.wait()
-
-    def store(block, place):
-        slot = table[0, place]
-
-        @pl.when(slot >= 0)
-        def _():
-            pltpu.make_async_copy(block, out_ref.at[0, slot], out_sems.at[slot]).start()
-
-    @for_own_parity
-    def _(mine):
-        columns = columns_of(mine)
+
+    @for_own_parity
+    def _(mine):
         for pair, js in enumerate(outer_pairs(mine)):
             total = columns_product(refs, right.at[pair], mine, js, lambda source: source == "staged")
+            if pair == 0:
+                load.wait()
             for i in range(BR):
                 for y, j in enumerate(js):
                     if abs(i - j) <= HB:
-                        place = i * NCOL + columns.index(j)
+                        place = i * NCOL + columns_of(mine).index(j)
                         made[place] = outer_ref[place] + block_of(total, i, y)
-                        store(made.at[place], place)
-        for i in range(BR):
-            for y, j in enumerate(j for j in columns if 0 <= j < BR):
-                store(inner_ref.at[i * 2 + y], i * NCOL + columns.index(j))
+                        slot = table[0, place]
+
+                        @pl.when(slot >= 0)
+                        def _(place=place, slot=slot):
+                            pltpu.make_async_copy(made.at[place], out_ref.at[0, slot], out_sems.at[slot]).start()
 
     for m in range(slots):
 
-        @pl.when(table[0, PLACES + m] == BR * NCOL)
+        @pl.when(table[0, PLACES + m] == 1)
         def _(m=m):
-            pltpu.make_async_copy(zero, out_ref.at[0, m], out_sems.at[m]).start()
-
-    for m in range(slots):
-        pltpu.make_async_copy(zero, out_ref.at[0, m], out_sems.at[m]).wait()
+            pltpu.make_async_copy(made.at[0], out_ref.at[0, m], out_sems.at[m]).wait()
 
 
 def local(values, block_rows, block_cols, counts):
@@ -325,22 +333,33 @@
 
     left_other = swapped(left)
     got = [towards(name, message) for name, message in zip("abcd", packed)]
-    inner, message, table = pl.pallas_call(
+    message = pl.pallas_call(
+        pack_e_kernel,
+        out_shape=blocks(SIZES["e"]),
+        in_specs=[vmem] * 2,
+        out_specs=vmem,
+        compiler_params=params,
+        name="pack_e",
+    )(left, left_other)
+    got.append(towards("e", message))
+    table, out = pl.pallas_call(
         functools.partial(inner_kernel, nblocks, slots),
-        out_shape=[blocks(INNER, jnp.float32), blocks(1), jax.ShapeDtypeStruct(table_shape, jnp.int32)],
+        out_shape=[jax.ShapeDtypeStruct(table_shape, jnp.int32), jax.ShapeDtypeStruct(values.shape, jnp.float32)],
         in_specs=[hbm] * 2 + [smem] + [vmem] * 2,
-        out_specs=[vmem] * 3,
+        out_specs=[vmem, hbm],
         scratch_shapes=[
             pltpu.VMEM((2, NCOL * BLK, 2 * BLK), values.dtype),
+            pltpu.VMEM((INNER + 1, BLK, BLK), jnp.float32),
             pltpu.SMEM(table_shape, jnp.int32),
             *index_scratch,
             pltpu.SemaphoreType.DMA,
+            pltpu.SemaphoreType.DMA((slots,)),
         ],
         compiler_params=params,
         cost_estimate=cost(3 * 2 * 17, 4 * values.size),
         name="inner",
     )(*places, counts, left, left_other)
-    got.append(towards("e", message))
+    *got, table = lax.optimization_barrier((*got, table))
     staged = swapped(
         pl.pallas_call(
             stage_kernel,
@@ -364,19 +383,19 @@
     return pl.pallas_call(
         functools.partial(multiply_kernel, slots),
         out_shape=jax.ShapeDtypeStruct(values.shape, jnp.float32),
-        in_specs=[vmem] * 6,
+        in_specs=[vmem] * 5 + [hbm],
         out_specs=hbm,
         scratch_shapes=[
             right_scratch(4),
             pltpu.VMEM((BR * NCOL, BLK, BLK), jnp.float32),
-            pltpu.VMEM((BLK, BLK), jnp.float32),
             pltpu.SMEM(table_shape, jnp.int32),
             pltpu.SemaphoreType.DMA,
             pltpu.SemaphoreType.DMA((slots,)),
         ],
+        input_output_aliases={5: 0},
         compiler_params=params,
         name="multiply",
-    )(left, left_other, staged, outer, inner, table)
+    )(left, left_other, staged, outer, table, out)
 
 
 def solution(mesh):

time: 28.2 us -> 27.2 us (0.965)
  waiting for transfers between devices: 11.5 us -> 10.3 us
    ppermute x5, waiting for transfers between devices: 10.7 us -> 9.46 us  [towards(): return lax.ppermute(message, ('row', 'col'), pairs)]
    pallas_call x1, Pallas kernels: 1.64 us -> 2.04 us  [local(): pl.pallas_call(functools.partial(inner_kernel, nblocks, slots), out_shape...]
  transfers between devices with their start and end apart: 7 -> 7, of which waited for: 3 -> 2; matrix products, arithmetic and copies ran while one was open for 0% -> 0% of each run, Pallas kernels for 10% -> 12%
where the time goes in v6:
time: 27.2 us; the launch traced here: 27.1 us
  waiting for transfers between devices  10.3 us (38%)
  starting transfers between devices  9.08 us (33%)
  Pallas kernels  7 us (26%)
  between operations  0.72 us (3%)
    ppermute x5, waiting for transfers between devices, towards(): return lax.ppermute(message, ('row', 'col'), pairs)  9.46 us
    ppermute x5, starting transfers between devices, towards(): return lax.ppermute(message, ('row', 'col'), pairs)  8.47 us
    pallas_call x1, Pallas kernels, local(): pl.pallas_call(functools.partial(multiply_kernel, slots), out_shape=jax.S...  2.27 us
    pallas_call x1, Pallas kernels, local(): pl.pallas_call(functools.partial(inner_kernel, nblocks, slots), out_shape...  2.04 us
    pallas_call x1, Pallas kernels, local(): pl.pallas_call(functools.partial(pack_kernel, nblocks, slots), out_shape=...  1.36 us
    pallas_call x1, Pallas kernels, local(): pl.pallas_call(outer_kernel, out_shape=blocks(BR * NCOL, jnp.float32), in...  1.24 us
    ppermute x2, waiting for transfers between devices, swapped(): return lax.ppermute(block, 'col', [(0, 1), (1, 0)])  0.82 us
    ppermute x2, starting transfers between devices, swapped(): return lax.ppermute(block, 'col', [(0, 1), (1, 0)])  0.62 us
  transfers between devices with their start and end apart: 7, of which 2 were waited for; matrix products, arithmetic and copies ran while one was open for 0% of the time, Pallas kernels for 12%

profile of v6, /device:TPU:0, one launch (start us, length us, event | category | flops | bytes accessed | tf_op | source)
XLA Modules:
  0.0 27.1 jit_solution(714780312109768441)
XLA Ops:
  0.0 1.4 %pack.1 = (bf16[13,128,128]{2,1,0:T(8,128)(2,1)S(1)}, bf16[6,128,128]{2,1,0:T(8,128)(2,1)S(1)}, bf16[8,128,128]{2,1,0:T(8,128)(2,1)S(1)}, bf16[5,128,128]{2,1,0:T(8,128)(2,1)S(1)}, bf16[384,1152]{1,0:T(8,128)(2,1)S(1)}) custom-call(s32[1,23]{1,0:T(1,128)} %rows_ref.3, s32[1,23]{1,0:T(1,128)} %cols_ref.3, bf16[1,23,128,128]{3,2,1,0:T(8,128)(2,1)} %values_ref.1), custom_call_target="tpu_custom_call" | custom-call | tf_op jit(solution)/shard_map/pack/pallas_call | solution.py:306
  1.4 0.5 %collective-permute-start = (bf16[384,1152]{1,0:T(8,128)(2,1)S(1)}, bf16[384,1152]{1,0:T(8,128)(2,1)S(1)}, u32[]{:S(2)}, u32[]{:S(2)}) collective-permute-start(bf16[384,1152]{1,0:T(8,128)(2,1)S(1)} %get-tuple-element.18.left_ref), channel_id=1, source_target_pairs={{0,1},{1,0},{2,3},{3,2},{4,5},{5,4},{6,7},{7,6},{8,9},{9,8},{10,11... | collective-permute-start | bytes 2654216 | tf_op jit(solution)/shard_map/ppermute | solution.py:332
  1.9 2.6 %collective-permute-start.1 = (bf16[13,128,128]{2,1,0:T(8,128)(2,1)S(1)}, bf16[13,128,128]{2,1,0:T(8,128)(2,1)S(1)}, u32[]{:S(2)}, u32[]{:S(2)}) collective-permute-start(bf16[13,128,128]{2,1,0:T(8,128)(2,1)S(1)} %get-tuple-element.19), channel_id=1, source_target_pairs={{2,0},{3,1},{0,2},{1,3},{6,4},{7,5},{4,6},{5,7},{10,8},{11,9},{8,1... | collective-permute-start | bytes 1277960 | tf_op jit(solution)/shard_map/ppermute | solution.py:329
  4.4 1.6 %collective-permute-start.3 = (bf16[8,128,128]{2,1,0:T(8,128)(2,1)S(1)}, bf16[8,128,128]{2,1,0:T(8,128)(2,1)S(1)}, u32[]{:S(2)}, u32[]{:S(2)}) collective-permute-start(bf16[8,128,128]{2,1,0:T(8,128)(2,1)S(1)} %get-tuple-element.21), channel_id=1, source_target_pairs={{12,0},{13,1},{6,2},{7,3},{0,4},{1,5},{10,6},{11,7},{4,8},{5,9},{1... | collective-permute-start | bytes 786440 | tf_op jit(solution)/shard_map/ppermute | solution.py:329
  6.0 2.4 %collective-permute-start.2 = (bf16[6,128,128]{2,1,0:T(8,128)(2,1)S(1)}, bf16[6,128,128]{2,1,0:T(8,128)(2,1)S(1)}, u32[]{:S(2)}, u32[]{:S(2)}) collective-permute-start(bf16[6,128,128]{2,1,0:T(8,128)(2,1)S(1)} %get-tuple-element.20), channel_id=1, source_target_pairs={{14,0},{15,1},{4,2},{5,3},{2,4},{3,5},{8,6},{9,7},{6,8},{7,9},{12,... | collective-permute-start | bytes 589832 | tf_op jit(solution)/shard_map/ppermute | solution.py:329
  8.5 0.4 %collective-permute-start.4 = (bf16[5,128,128]{2,1,0:T(8,128)(2,1)S(1)}, bf16[5,128,128]{2,1,0:T(8,128)(2,1)S(1)}, u32[]{:S(2)}, u32[]{:S(2)}) collective-permute-start(bf16[5,128,128]{2,1,0:T(8,128)(2,1)S(1)} %get-tuple-element.22), channel_id=1, source_target_pairs={{4,0},{5,1},{14,2},{15,3},{8,4},{9,5},{2,6},{3,7},{12,8},{13,9},{6... | collective-permute-start | bytes 491528 | tf_op jit(solution)/shard_map/ppermute | solution.py:329
  9.6 0.0 collective-permute-done.left_other_ref
  9.6 1.4 %collective-permute-start.5 = (bf16[1,128,128]{2,1,0:T(8,128)(2,1)S(1)}, bf16[1,128,128]{2,1,0:T(8,128)(2,1)S(1)}, u32[]{:S(2)}, u32[]{:S(2)}) collective-permute-start(bf16[1,128,128]{2,1,0:T(8,128)(2,1)S(1)} %pack_e.1), channel_id=1, source_target_pairs={{10,0},{7,1},{12,2},{9,3},{14,4},{11,5},{0,6},{13,7},{2,8},{15,9},... | collective-permute-start | bytes 98312 | tf_op jit(solution)/shard_map/ppermute | solution.py:329
  11.1 2.0 %inner.1 = (s32[1,128]{1,0:T(1,128)S(1)}, f32[1,23,128,128]{3,2,1,0:T(8,128)}) custom-call(s32[1,23]{1,0:T(1,128)} %rows_ref.3, s32[1,23]{1,0:T(1,128)} %cols_ref.3, s32[1,1]{1,0:T(1,128)S(6)} %copy.7.counts_ref, bf16[384,1152]{1,0:T(8,128)(2,1)S(1)} %get-tuple-element.18.left_ref, bf16[384,1152]{1,0:T(8,128)(2,1)S(1)} %collective-permute-done.left_other_ref), custom_call_target="tpu_custom_call" | custom-call | flops 427819008 | bytes 1507328 | tf_op jit(solution)/shard_map/inner/pallas_call | solution.py:345
  13.1 9.5 %collective-permute-done.4.refs_3_.rest_3_ = bf16[5,128,128]{2,1,0:T(8,128)(2,1)S(1)} collective-permute-done((bf16[5,128,128]{2,1,0:T(8,128)(2,1)S(1)}, bf16[5,128,128]{2,1,0:T(8,128)(2,1)S(1)}, u32[]{:S(2)}, u32[]{:S(2)}) %collective-permute-start.4) | collective-permute-done | bytes 163872 | tf_op jit(solution)/shard_map/ppermute | solution.py:329
  22.6 0.0 collective-permute-done.2.refs_1_.rest_1_
  22.6 0.0 collective-permute-done.3.refs_2_.rest_2_
  22.6 0.0 collective-permute-done.1.refs_0_.rest_0_
  22.6 0.0 collective-permute-done.5.refs_4_.rest_4_
  22.6 0.1 stage.1
  22.7 0.1 collective-permute-start.6
  22.8 1.2 %outer.1.outer_ref = f32[27,128,128]{2,1,0:T(8,128)S(1)} custom-call(bf16[384,1152]{1,0:T(8,128)(2,1)S(1)} %get-tuple-element.18.left_ref, bf16[384,1152]{1,0:T(8,128)(2,1)S(1)} %collective-permute-done.left_other_ref, bf16[13,128,128]{2,1,0:T(8,128)(2,1)S(1)} %collective-permute-done.1.refs_0_.rest_0_, ...), custom_call_target="tpu_custom_call" | custom-call | flops 1409286144 | bytes 3768320 | tf_op jit(solution)/shard_map/outer/pallas_call | solution.py:373
  24.0 0.8 %collective-permute-done.6.staged_ref = bf16[20,128,128]{2,1,0:T(8,128)(2,1)S(1)} collective-permute-done((bf16[20,128,128]{2,1,0:T(8,128)(2,1)S(1)}, bf16[20,128,128]{2,1,0:T(8,128)(2,1)S(1)}, u32[]{:S(2)}, u32[]{:S(2)}) %collective-permute-start.6) | collective-permute-done | bytes 655392 | tf_op jit(solution)/shard_map/ppermute | solution.py:332
  24.8 2.3 %multiply.1 = f32[1,23,128,128]{3,2,1,0:T(8,128)} custom-call(bf16[384,1152]{1,0:T(8,128)(2,1)S(1)} %get-tuple-element.18.left_ref, bf16[384,1152]{1,0:T(8,128)(2,1)S(1)} %collective-permute-done.left_other_ref, bf16[20,128,128]{2,1,0:T(8,128)(2,1)S(1)} %collective-permute-done.6.staged_ref, ...), custom_call_target="tpu_custom_call", output_to_operand_aliasing={{}: (5, {})} | custom-call | tf_op jit(solution)/shard_map/multiply/pallas_call | solution.py:383
  (1 shorter events, 0.0 us)
Async XLA Ops:
  1.4 8.2 %collective-permute-start = (bf16[384,1152]{1,0:T(8,128)(2,1)S(1)}, bf16[384,1152]{1,0:T(8,128)(2,1)S(1)}, u32[]{:S(2)}, u32[]{:S(2)}) collective-permute-start(bf16[384,1152]{1,0:T(8,128)(2,1)S(1)} %get-tuple-element.18.left_ref), channel_id=1, source_target_pairs={{0,1},{1,0},{2,3},{3,2},{4,5},{5,4},{6,7},{7,6},{8,9},{9,8},{10,11... | collective-permute-start | bytes 2654216 | tf_op jit(solution)/shard_map/ppermute | solution.py:332
  1.9 20.7 %collective-permute-start.1 = (bf16[13,128,128]{2,1,0:T(8,128)(2,1)S(1)}, bf16[13,128,128]{2,1,0:T(8,128)(2,1)S(1)}, u32[]{:S(2)}, u32[]{:S(2)}) collective-permute-start(bf16[13,128,128]{2,1,0:T(8,128)(2,1)S(1)} %get-tuple-element.19), channel_id=1, source_target_pairs={{2,0},{3,1},{0,2},{1,3},{6,4},{7,5},{4,6},{5,7},{10,8},{11,9},{8,1... | collective-permute-start | bytes 1277960 | tf_op jit(solution)/shard_map/ppermute | solution.py:329
  4.4 18.1 %collective-permute-start.3 = (bf16[8,128,128]{2,1,0:T(8,128)(2,1)S(1)}, bf16[8,128,128]{2,1,0:T(8,128)(2,1)S(1)}, u32[]{:S(2)}, u32[]{:S(2)}) collective-permute-start(bf16[8,128,128]{2,1,0:T(8,128)(2,1)S(1)} %get-tuple-element.21), channel_id=1, source_target_pairs={{12,0},{13,1},{6,2},{7,3},{0,4},{1,5},{10,6},{11,7},{4,8},{5,9},{1... | collective-permute-start | bytes 786440 | tf_op jit(solution)/shard_map/ppermute | solution.py:329
  6.0 16.5 %collective-permute-start.2 = (bf16[6,128,128]{2,1,0:T(8,128)(2,1)S(1)}, bf16[6,128,128]{2,1,0:T(8,128)(2,1)S(1)}, u32[]{:S(2)}, u32[]{:S(2)}) collective-permute-start(bf16[6,128,128]{2,1,0:T(8,128)(2,1)S(1)} %get-tuple-element.20), channel_id=1, source_target_pairs={{14,0},{15,1},{4,2},{5,3},{2,4},{3,5},{8,6},{9,7},{6,8},{7,9},{12,... | collective-permute-start | bytes 589832 | tf_op jit(solution)/shard_map/ppermute | solution.py:329
  8.5 14.1 %collective-permute-start.4 = (bf16[5,128,128]{2,1,0:T(8,128)(2,1)S(1)}, bf16[5,128,128]{2,1,0:T(8,128)(2,1)S(1)}, u32[]{:S(2)}, u32[]{:S(2)}) collective-permute-start(bf16[5,128,128]{2,1,0:T(8,128)(2,1)S(1)} %get-tuple-element.22), channel_id=1, source_target_pairs={{4,0},{5,1},{14,2},{15,3},{8,4},{9,5},{2,6},{3,7},{12,8},{13,9},{6... | collective-permute-start | bytes 491528 | tf_op jit(solution)/shard_map/ppermute | solution.py:329
  9.6 12.9 %collective-permute-start.5 = (bf16[1,128,128]{2,1,0:T(8,128)(2,1)S(1)}, bf16[1,128,128]{2,1,0:T(8,128)(2,1)S(1)}, u32[]{:S(2)}, u32[]{:S(2)}) collective-permute-start(bf16[1,128,128]{2,1,0:T(8,128)(2,1)S(1)} %pack_e.1), channel_id=1, source_target_pairs={{10,0},{7,1},{12,2},{9,3},{14,4},{11,5},{0,6},{13,7},{2,8},{15,9},... | collective-permute-start | bytes 98312 | tf_op jit(solution)/shard_map/ppermute | solution.py:329
  22.7 2.2 %collective-permute-start.6 = (bf16[20,128,128]{2,1,0:T(8,128)(2,1)S(1)}, bf16[20,128,128]{2,1,0:T(8,128)(2,1)S(1)}, u32[]{:S(2)}, u32[]{:S(2)}) collective-permute-start(bf16[20,128,128]{2,1,0:T(8,128)(2,1)S(1)} %stage.1), channel_id=1, source_target_pairs={{0,1},{1,0},{2,3},{3,2},{4,5},{5,4},{6,7},{7,6},{8,9},{9,8},{10,11... | collective-permute-start | bytes 1966088 | tf_op jit(solution)/shard_map/ppermute | solution.py:332

commit v7 on v3

--- a/solution.py
+++ b/solution.py
@@ -14,7 +14,7 @@
 LOW, HIGH = -HB, BR - 1 + HB
 NCOL = 9
 INNER = 6
-PLACES = 32
+CHUNK = 6
 VMEM_LIMIT = 12 * 2**20
 
 DISTANCES = {"a": 1, "b": -1, "c": -2, "d": 2, "e": None}
@@ -73,9 +73,12 @@
 
 def pack_kernel(nblocks, slots, rows_ref, cols_ref, values_ref, *rest):
     out_refs = dict(zip("abcd", rest[:4]))
-    left_ref, held, table, *index, sems, value_sem = rest[4:]
-    load = pltpu.make_async_copy(values_ref.at[0], held.at[pl.ds(0, slots)], value_sem)
-    load.start()
+    left_ref, held, table, *index, sems, value_sems = rest[4:]
+    loads = []
+    for n, first in enumerate(range(0, slots, CHUNK)):
+        part = pl.ds(first, min(CHUNK, slots - first))
+        loads.append(pltpu.make_async_copy(values_ref.at[0, part], held.at[part], value_sems.at[n]))
+        loads[-1].start()
     copies = index_copies((rows_ref, cols_ref), index, sems)
     for copy in copies:
         copy.start()
@@ -87,7 +90,8 @@
     for m in reversed(range(slots)):
         real_row, row, band = slot_position(*index, m, nblocks)
         table[jnp.where(real_row >= 0, row * WIDTH + band, BR * WIDTH)] = m
-    load.wait()
+    for load in loads:
+        load.wait()
 
     @for_own_parity
     def _(mine):
@@ -172,7 +176,7 @@
 
 
 def inner_kernel(nblocks, slots, rows_ref, cols_ref, counts_ref, left_ref, left_other_ref, *rest):
-    made_ref, message_ref, table_ref, right, table, *index, sems, table_sem = rest
+    made_ref, places_ref, right, places, *index, sems, places_sem = rest
     copies = index_copies((rows_ref, cols_ref), index, sems)
     for copy in copies:
         copy.start()
@@ -185,23 +189,24 @@
         for i in range(BR):
             for y in range(2):
                 made_ref[i * 2 + y] = block_of(total, i, y) if y < len(js) else jnp.zeros((BLK, BLK), made_ref.dtype)
-        i = 2 if mine == 0 else 0
-        n = columns_of(0).index(i)
-        message_ref[0] = refs["left", mine == 0][pl.ds(i * BLK, BLK), pl.ds(n * BLK, BLK)]
-
-    for i in range(BR * NCOL + 1):
-        table[0, i] = -1
+
     for copy in copies:
         copy.wait()
     count = counts_ref[0, 0]
     for m in range(slots):
         _, row, band = slot_position(*index, m, nblocks)
-        place = jnp.where(m < count, row * NCOL + (row + band) // 2, BR * NCOL)
-        table[0, place] = m
-        table[0, PLACES + m] = place
-    copy = pltpu.make_async_copy(table, table_ref, table_sem)
+        places[0, m] = jnp.where(m < count, row * NCOL + (row + band) // 2, BR * NCOL)
+    copy = pltpu.make_async_copy(places, places_ref, places_sem)
     copy.start()
     copy.wait()
+
+
+def pack_e_kernel(left_ref, left_other_ref, e_ref):
+    @for_own_parity
+    def _(mine):
+        i = 2 if mine == 0 else 0
+        n = columns_of(0).index(i)
+        e_ref[0] = (left_ref if mine == 0 else left_other_ref)[pl.ds(i * BLK, BLK), pl.ds(n * BLK, BLK)]
 
 
 def stage_kernel(*refs):
@@ -230,20 +235,11 @@
                         out_ref[i * NCOL + columns_of(mine).index(j)] = block_of(total, i, y)
 
 
-def multiply_kernel(slots, left_ref, left_other_ref, staged_ref, outer_ref, inner_ref, table_ref, out_ref, *rest):
-    right, made, zero, table, table_sem, out_sems = rest
+def multiply_kernel(slots, left_ref, left_other_ref, staged_ref, outer_ref, inner_ref, places_ref, out_ref, *rest):
+    right, made, places, places_sem, out_sem = rest
     refs = {("left", True): left_ref, ("left", False): left_other_ref, "staged": staged_ref}
-    load = pltpu.make_async_copy(table_ref, table, table_sem)
+    load = pltpu.make_async_copy(places_ref, places, places_sem)
     load.start()
-    zero[...] = jnp.zeros((BLK, BLK), zero.dtype)
-    load.wait()
-
-    def store(block, place):
-        slot = table[0, place]
-
-        @pl.when(slot >= 0)
-        def _():
-            pltpu.make_async_copy(block, out_ref.at[0, slot], out_sems.at[slot]).start()
 
     @for_own_parity
     def _(mine):
@@ -255,19 +251,15 @@
                     if abs(i - j) <= HB:
                         place = i * NCOL + columns.index(j)
                         made[place] = outer_ref[place] + block_of(total, i, y)
-                        store(made.at[place], place)
         for i in range(BR):
             for y, j in enumerate(j for j in columns if 0 <= j < BR):
-                store(inner_ref.at[i * 2 + y], i * NCOL + columns.index(j))
-
+                made[i * NCOL + columns.index(j)] = inner_ref[i * 2 + y]
+        made[BR * NCOL] = jnp.zeros((BLK, BLK), made.dtype)
+
+    load.wait()
     for m in range(slots):
-
-        @pl.when(table[0, PLACES + m] == BR * NCOL)
-        def _(m=m):
-            pltpu.make_async_copy(zero, out_ref.at[0, m], out_sems.at[m]).start()
-
-    for m in range(slots):
-        pltpu.make_async_copy(zero, out_ref.at[0, m], out_sems.at[m]).wait()
+        pltpu.make_async_copy(made.at[places[0, m]], out_ref.at[0, m], out_sem).start()
+    pltpu.make_async_copy(made.at[pl.ds(0, slots)], out_ref.at[0], out_sem).wait()
 
 
 def local(values, block_rows, block_cols, counts):
@@ -284,7 +276,7 @@
         pltpu.SMEM((1, slots), jnp.int32),
         pltpu.SemaphoreType.DMA((2,)),
     ]
-    table_shape = (1, BLK)
+    places_shape = (1, BLK)
 
     def blocks(count, dtype=values.dtype):
         return jax.ShapeDtypeStruct((count, BLK, BLK), dtype)
@@ -305,7 +297,7 @@
             pltpu.VMEM((slots + 1, BLK, BLK), values.dtype),
             pltpu.SMEM((BR * WIDTH + 1,), jnp.int32),
             *index_scratch,
-            pltpu.SemaphoreType.DMA,
+            pltpu.SemaphoreType.DMA((-(-slots // CHUNK),)),
         ],
         compiler_params=params,
         name="pack",
@@ -325,14 +317,23 @@
 
     left_other = swapped(left)
     got = [towards(name, message) for name, message in zip("abcd", packed)]
-    inner, message, table = pl.pallas_call(
+    message = pl.pallas_call(
+        pack_e_kernel,
+        out_shape=blocks(SIZES["e"]),
+        in_specs=[vmem] * 2,
+        out_specs=vmem,
+        compiler_params=params,
+        name="pack_e",
+    )(left, left_other)
+    got.append(towards("e", message))
+    inner, slot_places = pl.pallas_call(
         functools.partial(inner_kernel, nblocks, slots),
-        out_shape=[blocks(INNER, jnp.float32), blocks(1), jax.ShapeDtypeStruct(table_shape, jnp.int32)],
+        out_shape=[blocks(INNER, jnp.float32), jax.ShapeDtypeStruct(places_shape, jnp.int32)],
         in_specs=[hbm] * 2 + [smem] + [vmem] * 2,
-        out_specs=[vmem] * 3,
+        out_specs=[vmem] * 2,
         scratch_shapes=[
             pltpu.VMEM((2, NCOL * BLK, 2 * BLK), values.dtype),
-            pltpu.SMEM(table_shape, jnp.int32),
+            pltpu.SMEM(places_shape, jnp.int32),
             *index_scratch,
             pltpu.SemaphoreType.DMA,
         ],
@@ -340,7 +341,7 @@
         cost_estimate=cost(3 * 2 * 17, 4 * values.size),
         name="inner",
     )(*places, counts, left, left_other)
-    got.append(towards("e", message))
+    *got, inner = lax.optimization_barrier((*got, inner))
     staged = swapped(
         pl.pallas_call(
             stage_kernel,
@@ -368,15 +369,14 @@
         out_specs=hbm,
         scratch_shapes=[
             right_scratch(4),
-            pltpu.VMEM((BR * NCOL, BLK, BLK), jnp.float32),
-            pltpu.VMEM((BLK, BLK), jnp.float32),
-            pltpu.SMEM(table_shape, jnp.int32),
+            pltpu.VMEM((BR * NCOL + 1, BLK, BLK), jnp.float32),
+            pltpu.SMEM(places_shape, jnp.int32),
             pltpu.SemaphoreType.DMA,
-            pltpu.SemaphoreType.DMA((slots,)),
+            pltpu.SemaphoreType.DMA,
         ],
         compiler_params=params,
         name="multiply",
-    )(left, left_other, staged, outer, inner, table)
+    )(left, left_other, staged, outer, inner, slot_places)
 
 
 def solution(mesh):

time: 28.2 us -> 27 us (0.957)
  waiting for transfers between devices: 11.5 us -> 10.7 us
  Pallas kernels: 6.86 us -> 6.34 us
    ppermute x5, waiting for transfers between devices: 10.7 us -> 9.92 us  [towards(): return lax.ppermute(message, ('row', 'col'), pairs)]
    pallas_call x1, Pallas kernels: 2.55 us -> 1.95 us  [local(): pl.pallas_call(functools.partial(multiply_kernel, slots), out_shape=jax.S...]
  transfers between devices with their start and end apart: 7 -> 7, of which waited for: 3 -> 2; matrix products, arithmetic and copies ran while one was open for 0% -> 0% of each run, Pallas kernels for 10% -> 11%
where the time goes in v7:
time: 27 us; the launch traced here: 26.9 us
  waiting for transfers between devices  10.7 us (40%)
  starting transfers between devices  9.08 us (34%)
  Pallas kernels  6.34 us (23%)
  between operations  0.72 us (3%)
    ppermute x5, waiting for transfers between devices, towards(): return lax.ppermute(message, ('row', 'col'), pairs)  9.92 us
    ppermute x5, starting transfers between devices, towards(): return lax.ppermute(message, ('row', 'col'), pairs)  8.47 us
    pallas_call x1, Pallas kernels, local(): pl.pallas_call(functools.partial(multiply_kernel, slots), out_shape=jax.S...  1.95 us
    pallas_call x1, Pallas kernels, local(): pl.pallas_call(functools.partial(inner_kernel, nblocks, slots), out_shape...  1.59 us
    pallas_call x1, Pallas kernels, local(): pl.pallas_call(functools.partial(pack_kernel, nblocks, slots), out_shape=...  1.47 us
    pallas_call x1, Pallas kernels, local(): pl.pallas_call(outer_kernel, out_shape=blocks(BR * NCOL, jnp.float32), in...  1.24 us
    ppermute x2, waiting for transfers between devices, swapped(): return lax.ppermute(block, 'col', [(0, 1), (1, 0)])  0.81 us
    ppermute x2, starting transfers between devices, swapped(): return lax.ppermute(block, 'col', [(0, 1), (1, 0)])  0.62 us
  transfers between devices with their start and end apart: 7, of which 2 were waited for; matrix products, arithmetic and copies ran while one was open for 0% of the time, Pallas kernels for 11%

profile of v7, /device:TPU:0, one launch (start us, length us, event | category | flops | bytes accessed | tf_op | source)
XLA Modules:
  0.0 26.9 jit_solution(18240068970652975919)
XLA Ops:
  0.0 1.5 %pack.1 = (bf16[13,128,128]{2,1,0:T(8,128)(2,1)S(1)}, bf16[6,128,128]{2,1,0:T(8,128)(2,1)S(1)}, bf16[8,128,128]{2,1,0:T(8,128)(2,1)S(1)}, bf16[5,128,128]{2,1,0:T(8,128)(2,1)S(1)}, bf16[384,1152]{1,0:T(8,128)(2,1)S(1)}) custom-call(s32[1,23]{1,0:T(1,128)} %rows_ref.3, s32[1,23]{1,0:T(1,128)} %cols_ref.3, bf16[1,23,128,128]{3,2,1,0:T(8,128)(2,1)} %values_ref.1), custom_call_target="tpu_custom_call" | custom-call | tf_op jit(solution)/shard_map/pack/pallas_call | solution.py:290
  1.5 0.5 %collective-permute-start = (bf16[384,1152]{1,0:T(8,128)(2,1)S(1)}, bf16[384,1152]{1,0:T(8,128)(2,1)S(1)}, u32[]{:S(2)}, u32[]{:S(2)}) collective-permute-start(bf16[384,1152]{1,0:T(8,128)(2,1)S(1)} %get-tuple-element.18.left_ref), channel_id=1, source_target_pairs={{0,1},{1,0},{2,3},{3,2},{4,5},{5,4},{6,7},{7,6},{8,9},{9,8},{10,11... | collective-permute-start | bytes 2654216 | tf_op jit(solution)/shard_map/ppermute | solution.py:316
  2.0 2.6 %collective-permute-start.1 = (bf16[13,128,128]{2,1,0:T(8,128)(2,1)S(1)}, bf16[13,128,128]{2,1,0:T(8,128)(2,1)S(1)}, u32[]{:S(2)}, u32[]{:S(2)}) collective-permute-start(bf16[13,128,128]{2,1,0:T(8,128)(2,1)S(1)} %get-tuple-element.19), channel_id=1, source_target_pairs={{2,0},{3,1},{0,2},{1,3},{6,4},{7,5},{4,6},{5,7},{10,8},{11,9},{8,1... | collective-permute-start | bytes 1277960 | tf_op jit(solution)/shard_map/ppermute | solution.py:313
  4.6 1.6 %collective-permute-start.3 = (bf16[8,128,128]{2,1,0:T(8,128)(2,1)S(1)}, bf16[8,128,128]{2,1,0:T(8,128)(2,1)S(1)}, u32[]{:S(2)}, u32[]{:S(2)}) collective-permute-start(bf16[8,128,128]{2,1,0:T(8,128)(2,1)S(1)} %get-tuple-element.21), channel_id=1, source_target_pairs={{12,0},{13,1},{6,2},{7,3},{0,4},{1,5},{10,6},{11,7},{4,8},{5,9},{1... | collective-permute-start | bytes 786440 | tf_op jit(solution)/shard_map/ppermute | solution.py:313
  6.1 2.4 %collective-permute-start.2 = (bf16[6,128,128]{2,1,0:T(8,128)(2,1)S(1)}, bf16[6,128,128]{2,1,0:T(8,128)(2,1)S(1)}, u32[]{:S(2)}, u32[]{:S(2)}) collective-permute-start(bf16[6,128,128]{2,1,0:T(8,128)(2,1)S(1)} %get-tuple-element.20), channel_id=1, source_target_pairs={{14,0},{15,1},{4,2},{5,3},{2,4},{3,5},{8,6},{9,7},{6,8},{7,9},{12,... | collective-permute-start | bytes 589832 | tf_op jit(solution)/shard_map/ppermute | solution.py:313
  8.6 0.4 %collective-permute-start.4 = (bf16[5,128,128]{2,1,0:T(8,128)(2,1)S(1)}, bf16[5,128,128]{2,1,0:T(8,128)(2,1)S(1)}, u32[]{:S(2)}, u32[]{:S(2)}) collective-permute-start(bf16[5,128,128]{2,1,0:T(8,128)(2,1)S(1)} %get-tuple-element.22), channel_id=1, source_target_pairs={{4,0},{5,1},{14,2},{15,3},{8,4},{9,5},{2,6},{3,7},{12,8},{13,9},{6... | collective-permute-start | bytes 491528 | tf_op jit(solution)/shard_map/ppermute | solution.py:313
  9.7 0.0 collective-permute-done.left_other_ref
  9.7 1.4 %collective-permute-start.5 = (bf16[1,128,128]{2,1,0:T(8,128)(2,1)S(1)}, bf16[1,128,128]{2,1,0:T(8,128)(2,1)S(1)}, u32[]{:S(2)}, u32[]{:S(2)}) collective-permute-start(bf16[1,128,128]{2,1,0:T(8,128)(2,1)S(1)} %pack_e.1), channel_id=1, source_target_pairs={{10,0},{7,1},{12,2},{9,3},{14,4},{11,5},{0,6},{13,7},{2,8},{15,9},... | collective-permute-start | bytes 98312 | tf_op jit(solution)/shard_map/ppermute | solution.py:313
  11.2 1.6 %inner.1 = (f32[6,128,128]{2,1,0:T(8,128)S(1)}, s32[1,128]{1,0:T(1,128)S(1)}) custom-call(s32[1,23]{1,0:T(1,128)} %rows_ref.3, s32[1,23]{1,0:T(1,128)} %cols_ref.3, s32[1,1]{1,0:T(1,128)S(6)} %copy.5.counts_ref, bf16[384,1152]{1,0:T(8,128)(2,1)S(1)} %get-tuple-element.18.left_ref, bf16[384,1152]{1,0:T(8,128)(2,1)S(1)} %collective-permute-done.left_other_ref), custom_call_target="tpu_custom_call" | custom-call | flops 427819008 | bytes 1507328 | tf_op jit(solution)/shard_map/inner/pallas_call | solution.py:329
  12.8 9.9 %collective-permute-done.4.refs_3_.rest_3_ = bf16[5,128,128]{2,1,0:T(8,128)(2,1)S(1)} collective-permute-done((bf16[5,128,128]{2,1,0:T(8,128)(2,1)S(1)}, bf16[5,128,128]{2,1,0:T(8,128)(2,1)S(1)}, u32[]{:S(2)}, u32[]{:S(2)}) %collective-permute-start.4) | collective-permute-done | bytes 163872 | tf_op jit(solution)/shard_map/ppermute | solution.py:313
  22.7 0.0 collective-permute-done.2.refs_1_.rest_1_
  22.7 0.0 collective-permute-done.3.refs_2_.rest_2_
  22.7 0.0 collective-permute-done.1.refs_0_.rest_0_
  22.7 0.0 collective-permute-done.5.refs_4_.rest_4_
  22.7 0.1 stage.1
  22.8 0.1 collective-permute-start.6
  22.9 1.2 %outer.1.outer_ref = f32[27,128,128]{2,1,0:T(8,128)S(1)} custom-call(bf16[384,1152]{1,0:T(8,128)(2,1)S(1)} %get-tuple-element.18.left_ref, bf16[384,1152]{1,0:T(8,128)(2,1)S(1)} %collective-permute-done.left_other_ref, bf16[13,128,128]{2,1,0:T(8,128)(2,1)S(1)} %collective-permute-done.1.refs_0_.rest_0_, ...), custom_call_target="tpu_custom_call" | custom-call | flops 1409286144 | bytes 3768320 | tf_op jit(solution)/shard_map/outer/pallas_call | solution.py:355
  24.1 0.8 %collective-permute-done.6.staged_ref = bf16[20,128,128]{2,1,0:T(8,128)(2,1)S(1)} collective-permute-done((bf16[20,128,128]{2,1,0:T(8,128)(2,1)S(1)}, bf16[20,128,128]{2,1,0:T(8,128)(2,1)S(1)}, u32[]{:S(2)}, u32[]{:S(2)}) %collective-permute-start.6) | collective-permute-done | bytes 655392 | tf_op jit(solution)/shard_map/ppermute | solution.py:316
  24.9 1.9 %multiply.1 = f32[1,23,128,128]{3,2,1,0:T(8,128)} custom-call(bf16[384,1152]{1,0:T(8,128)(2,1)S(1)} %get-tuple-element.18.left_ref, bf16[384,1152]{1,0:T(8,128)(2,1)S(1)} %collective-permute-done.left_other_ref, bf16[20,128,128]{2,1,0:T(8,128)(2,1)S(1)} %collective-permute-done.6.staged_ref, f32[27,128,128]{2,1,0:T(8,128)S(1)} %outer.1.outer_ref, ...), custom_call_target="tpu_custom_call" | custom-call | tf_op jit(solution)/shard_map/multiply/pallas_call | solution.py:365
  (1 shorter events, 0.0 us)
Async XLA Ops:
  1.5 8.2 %collective-permute-start = (bf16[384,1152]{1,0:T(8,128)(2,1)S(1)}, bf16[384,1152]{1,0:T(8,128)(2,1)S(1)}, u32[]{:S(2)}, u32[]{:S(2)}) collective-permute-start(bf16[384,1152]{1,0:T(8,128)(2,1)S(1)} %get-tuple-element.18.left_ref), channel_id=1, source_target_pairs={{0,1},{1,0},{2,3},{3,2},{4,5},{5,4},{6,7},{7,6},{8,9},{9,8},{10,11... | collective-permute-start | bytes 2654216 | tf_op jit(solution)/shard_map/ppermute | solution.py:316
  2.0 20.7 %collective-permute-start.1 = (bf16[13,128,128]{2,1,0:T(8,128)(2,1)S(1)}, bf16[13,128,128]{2,1,0:T(8,128)(2,1)S(1)}, u32[]{:S(2)}, u32[]{:S(2)}) collective-permute-start(bf16[13,128,128]{2,1,0:T(8,128)(2,1)S(1)} %get-tuple-element.19), channel_id=1, source_target_pairs={{2,0},{3,1},{0,2},{1,3},{6,4},{7,5},{4,6},{5,7},{10,8},{11,9},{8,1... | collective-permute-start | bytes 1277960 | tf_op jit(solution)/shard_map/ppermute | solution.py:313
  4.6 18.1 %collective-permute-start.3 = (bf16[8,128,128]{2,1,0:T(8,128)(2,1)S(1)}, bf16[8,128,128]{2,1,0:T(8,128)(2,1)S(1)}, u32[]{:S(2)}, u32[]{:S(2)}) collective-permute-start(bf16[8,128,128]{2,1,0:T(8,128)(2,1)S(1)} %get-tuple-element.21), channel_id=1, source_target_pairs={{12,0},{13,1},{6,2},{7,3},{0,4},{1,5},{10,6},{11,7},{4,8},{5,9},{1... | collective-permute-start | bytes 786440 | tf_op jit(solution)/shard_map/ppermute | solution.py:313
  6.1 16.5 %collective-permute-start.2 = (bf16[6,128,128]{2,1,0:T(8,128)(2,1)S(1)}, bf16[6,128,128]{2,1,0:T(8,128)(2,1)S(1)}, u32[]{:S(2)}, u32[]{:S(2)}) collective-permute-start(bf16[6,128,128]{2,1,0:T(8,128)(2,1)S(1)} %get-tuple-element.20), channel_id=1, source_target_pairs={{14,0},{15,1},{4,2},{5,3},{2,4},{3,5},{8,6},{9,7},{6,8},{7,9},{12,... | collective-permute-start | bytes 589832 | tf_op jit(solution)/shard_map/ppermute | solution.py:313
  8.6 14.1 %collective-permute-start.4 = (bf16[5,128,128]{2,1,0:T(8,128)(2,1)S(1)}, bf16[5,128,128]{2,1,0:T(8,128)(2,1)S(1)}, u32[]{:S(2)}, u32[]{:S(2)}) collective-permute-start(bf16[5,128,128]{2,1,0:T(8,128)(2,1)S(1)} %get-tuple-element.22), channel_id=1, source_target_pairs={{4,0},{5,1},{14,2},{15,3},{8,4},{9,5},{2,6},{3,7},{12,8},{13,9},{6... | collective-permute-start | bytes 491528 | tf_op jit(solution)/shard_map/ppermute | solution.py:313
  9.7 12.9 %collective-permute-start.5 = (bf16[1,128,128]{2,1,0:T(8,128)(2,1)S(1)}, bf16[1,128,128]{2,1,0:T(8,128)(2,1)S(1)}, u32[]{:S(2)}, u32[]{:S(2)}) collective-permute-start(bf16[1,128,128]{2,1,0:T(8,128)(2,1)S(1)} %pack_e.1), channel_id=1, source_target_pairs={{10,0},{7,1},{12,2},{9,3},{14,4},{11,5},{0,6},{13,7},{2,8},{15,9},... | collective-permute-start | bytes 98312 | tf_op jit(solution)/shard_map/ppermute | solution.py:313
  22.8 2.2 %collective-permute-start.6 = (bf16[20,128,128]{2,1,0:T(8,128)(2,1)S(1)}, bf16[20,128,128]{2,1,0:T(8,128)(2,1)S(1)}, u32[]{:S(2)}, u32[]{:S(2)}) collective-permute-start(bf16[20,128,128]{2,1,0:T(8,128)(2,1)S(1)} %stage.1), channel_id=1, source_target_pairs={{0,1},{1,0},{2,3},{3,2},{4,5},{5,4},{6,7},{7,6},{8,9},{9,8},{10,11... | collective-permute-start | bytes 1966088 | tf_op jit(solution)/shard_map/ppermute | solution.py:316

commit v8 on v7

--- a/solution.py
+++ b/solution.py
@@ -14,7 +14,6 @@
 LOW, HIGH = -HB, BR - 1 + HB
 NCOL = 9
 INNER = 6
-CHUNK = 6
 VMEM_LIMIT = 12 * 2**20
 
 DISTANCES = {"a": 1, "b": -1, "c": -2, "d": 2, "e": None}
@@ -73,14 +72,10 @@
 
 def pack_kernel(nblocks, slots, rows_ref, cols_ref, values_ref, *rest):
     out_refs = dict(zip("abcd", rest[:4]))
-    left_ref, held, table, *index, sems, value_sems = rest[4:]
-    loads = []
-    for n, first in enumerate(range(0, slots, CHUNK)):
-        part = pl.ds(first, min(CHUNK, slots - first))
-        loads.append(pltpu.make_async_copy(values_ref.at[0, part], held.at[part], value_sems.at[n]))
-        loads[-1].start()
+    left_ref, held, table, *index, sems, value_sem = rest[4:]
     copies = index_copies((rows_ref, cols_ref), index, sems)
-    for copy in copies:
+    load = pltpu.make_async_copy(values_ref.at[0], held.at[pl.ds(0, slots)], value_sem)
+    for copy in (*copies, load):
         copy.start()
     held[slots] = jnp.zeros((BLK, BLK), held.dtype)
     for i in range(BR * WIDTH + 1):
@@ -90,8 +85,7 @@
     for m in reversed(range(slots)):
         real_row, row, band = slot_position(*index, m, nblocks)
         table[jnp.where(real_row >= 0, row * WIDTH + band, BR * WIDTH)] = m
-    for load in loads:
-        load.wait()
+    load.wait()
 
     @for_own_parity
     def _(mine):
@@ -209,6 +203,10 @@
         e_ref[0] = (left_ref if mine == 0 else left_other_ref)[pl.ds(i * BLK, BLK), pl.ds(n * BLK, BLK)]
 
 
+def keep_kernel(*refs):
+    pass
+
+
 def stage_kernel(*refs):
     got = dict(zip(DISTANCES, refs))
     out_ref = refs[-1]
@@ -297,7 +295,7 @@
             pltpu.VMEM((slots + 1, BLK, BLK), values.dtype),
             pltpu.SMEM((BR * WIDTH + 1,), jnp.int32),
             *index_scratch,
-            pltpu.SemaphoreType.DMA((-(-slots // CHUNK),)),
+            pltpu.SemaphoreType.DMA,
         ],
         compiler_params=params,
         name="pack",
@@ -311,6 +309,18 @@
                 source = (r - distance if r % 2 == 1 else r + distance) % row_count
                 pairs.append((source * col_count + c, r * col_count + c))
         return lax.ppermute(message, ("row", "col"), pairs)
+
+    def keep(arrays, flops):
+        return pl.pallas_call(
+            keep_kernel,
+            out_shape=[jax.ShapeDtypeStruct(x.shape, x.dtype) for x in arrays],
+            in_specs=[vmem] * len(arrays),
+            out_specs=[vmem] * len(arrays),
+            input_output_aliases={n: n for n in range(len(arrays))},
+            compiler_params=params,
+            cost_estimate=pl.CostEstimate(flops=flops, bytes_accessed=0, transcendentals=0),
+            name="keep",
+        )(*arrays)
 
     def swapped(block):
         return lax.ppermute(block, "col", [(0, 1), (1, 0)])
@@ -341,6 +351,7 @@
         cost_estimate=cost(3 * 2 * 17, 4 * values.size),
         name="inner",
     )(*places, counts, left, left_other)
+    got[2], inner, = keep((got[2], inner,), 4000000000)
     *got, inner = lax.optimization_barrier((*got, inner))
     staged = swapped(
         pl.pallas_call(

time: 27 us -> 27.4 us (1.015)
  starting transfers between devices: 9.08 us -> 10.1 us
  waiting for transfers between devices: 10.7 us -> 10.2 us
    ppermute x5, starting transfers between devices: 8.47 us -> 9.47 us  [towards(): return lax.ppermute(message, ('row', 'col'), pairs)]
    ppermute x5, waiting for transfers between devices: 9.92 us -> 9.41 us  [towards(): return lax.ppermute(message, ('row', 'col'), pairs)]
  transfers between devices with their start and end apart: 7 -> 7, of which waited for: 2 -> 5; matrix products, arithmetic and copies ran while one was open for 0% -> 0% of each run, Pallas kernels for 11% -> 11%
where the time goes in v8:
time: 27.4 us; the launch traced here: 27.3 us
  waiting for transfers between devices  10.2 us (37%)
  starting transfers between devices  10.1 us (37%)
  Pallas kernels  6.25 us (23%)
  between operations  0.72 us (3%)
    ppermute x5, starting transfers between devices, towards(): return lax.ppermute(message, ('row', 'col'), pairs)  9.47 us
    ppermute x5, waiting for transfers between devices, towards(): return lax.ppermute(message, ('row', 'col'), pairs)  9.41 us
    pallas_call x1, Pallas kernels, local(): pl.pallas_call(functools.partial(multiply_kernel, slots), out_shape=jax.S...  1.95 us
    pallas_call x1, Pallas kernels, local(): pl.pallas_call(functools.partial(inner_kernel, nblocks, slots), out_shape...  1.61 us
    pallas_call x1, Pallas kernels, local(): pl.pallas_call(functools.partial(pack_kernel, nblocks, slots), out_shape=...  1.36 us
    pallas_call x1, Pallas kernels, local(): pl.pallas_call(outer_kernel, out_shape=blocks(BR * NCOL, jnp.float32), in...  1.26 us
    ppermute x2, waiting for transfers between devices, swapped(): return lax.ppermute(block, 'col', [(0, 1), (1, 0)])  0.82 us
    ppermute x2, starting transfers between devices, swapped(): return lax.ppermute(block, 'col', [(0, 1), (1, 0)])  0.59 us
  transfers between devices with their start and end apart: 7, of which 5 were waited for; matrix products, arithmetic and copies ran while one was open for 0% of the time, Pallas kernels for 11%

profile of v8, /device:TPU:0, one launch (start us, length us, event | category | flops | bytes accessed | tf_op | source)
XLA Modules:
  0.0 27.3 jit_solution(10498646114919268416)
XLA Ops:
  0.0 1.4 %pack.1 = (bf16[13,128,128]{2,1,0:T(8,128)(2,1)S(1)}, bf16[6,128,128]{2,1,0:T(8,128)(2,1)S(1)}, bf16[8,128,128]{2,1,0:T(8,128)(2,1)S(1)}, bf16[5,128,128]{2,1,0:T(8,128)(2,1)S(1)}, bf16[384,1152]{1,0:T(8,128)(2,1)S(1)}) custom-call(s32[1,23]{1,0:T(1,128)} %rows_ref.3, s32[1,23]{1,0:T(1,128)} %cols_ref.3, bf16[1,23,128,128]{3,2,1,0:T(8,128)(2,1)} %values_ref.1), custom_call_target="tpu_custom_call" | custom-call | tf_op jit(solution)/shard_map/pack/pallas_call | solution.py:288
  1.4 0.5 %collective-permute-start = (bf16[384,1152]{1,0:T(8,128)(2,1)S(1)}, bf16[384,1152]{1,0:T(8,128)(2,1)S(1)}, u32[]{:S(2)}, u32[]{:S(2)}) collective-permute-start(bf16[384,1152]{1,0:T(8,128)(2,1)S(1)} %get-tuple-element.20.left_ref), channel_id=1, source_target_pairs={{0,1},{1,0},{2,3},{3,2},{4,5},{5,4},{6,7},{7,6},{8,9},{9,8},{10,11... | collective-permute-start | bytes 2654216 | tf_op jit(solution)/shard_map/ppermute | solution.py:326
  1.9 2.6 %collective-permute-start.3 = (bf16[8,128,128]{2,1,0:T(8,128)(2,1)S(1)}, bf16[8,128,128]{2,1,0:T(8,128)(2,1)S(1)}, u32[]{:S(2)}, u32[]{:S(2)}) collective-permute-start(bf16[8,128,128]{2,1,0:T(8,128)(2,1)S(1)} %get-tuple-element.23), channel_id=1, source_target_pairs={{12,0},{13,1},{6,2},{7,3},{0,4},{1,5},{10,6},{11,7},{4,8},{5,9},{1... | collective-permute-start | bytes 786440 | tf_op jit(solution)/shard_map/ppermute | solution.py:311
  4.5 3.5 %collective-permute-start.1 = (bf16[13,128,128]{2,1,0:T(8,128)(2,1)S(1)}, bf16[13,128,128]{2,1,0:T(8,128)(2,1)S(1)}, u32[]{:S(2)}, u32[]{:S(2)}) collective-permute-start(bf16[13,128,128]{2,1,0:T(8,128)(2,1)S(1)} %get-tuple-element.21), channel_id=1, source_target_pairs={{2,0},{3,1},{0,2},{1,3},{6,4},{7,5},{4,6},{5,7},{10,8},{11,9},{8,1... | collective-permute-start | bytes 1277960 | tf_op jit(solution)/shard_map/ppermute | solution.py:311
  8.0 0.4 %collective-permute-start.4 = (bf16[5,128,128]{2,1,0:T(8,128)(2,1)S(1)}, bf16[5,128,128]{2,1,0:T(8,128)(2,1)S(1)}, u32[]{:S(2)}, u32[]{:S(2)}) collective-permute-start(bf16[5,128,128]{2,1,0:T(8,128)(2,1)S(1)} %get-tuple-element.26), channel_id=1, source_target_pairs={{4,0},{5,1},{14,2},{15,3},{8,4},{9,5},{2,6},{3,7},{12,8},{13,9},{6... | collective-permute-start | bytes 491528 | tf_op jit(solution)/shard_map/ppermute | solution.py:311
  8.5 2.8 %collective-permute-start.2 = (bf16[6,128,128]{2,1,0:T(8,128)(2,1)S(1)}, bf16[6,128,128]{2,1,0:T(8,128)(2,1)S(1)}, u32[]{:S(2)}, u32[]{:S(2)}) collective-permute-start(bf16[6,128,128]{2,1,0:T(8,128)(2,1)S(1)} %get-tuple-element.22), channel_id=1, source_target_pairs={{14,0},{15,1},{4,2},{5,3},{2,4},{3,5},{8,6},{9,7},{6,8},{7,9},{12,... | collective-permute-start | bytes 589832 | tf_op jit(solution)/shard_map/ppermute | solution.py:311
  12.0 0.0 collective-permute-done.left_other_ref
  12.0 0.1 collective-permute-start.5
  12.1 1.6 %inner.1 = (f32[6,128,128]{2,1,0:T(8,128)S(1)}, s32[1,128]{1,0:T(1,128)S(1)}) custom-call(s32[1,23]{1,0:T(1,128)} %rows_ref.3, s32[1,23]{1,0:T(1,128)} %cols_ref.3, s32[1,1]{1,0:T(1,128)S(6)} %copy.9.counts_ref, bf16[384,1152]{1,0:T(8,128)(2,1)S(1)} %get-tuple-element.20.left_ref, bf16[384,1152]{1,0:T(8,128)(2,1)S(1)} %collective-permute-done.left_other_ref), custom_call_target="tpu_custom_call" | custom-call | flops 427819008 | bytes 1507328 | tf_op jit(solution)/shard_map/inner/pallas_call | solution.py:339
  13.7 0.1 collective-permute-done.3.refs_0_
  13.8 3.4 %collective-permute-done.4.refs_3_.rest_3_ = bf16[5,128,128]{2,1,0:T(8,128)(2,1)S(1)} collective-permute-done((bf16[5,128,128]{2,1,0:T(8,128)(2,1)S(1)}, bf16[5,128,128]{2,1,0:T(8,128)(2,1)S(1)}, u32[]{:S(2)}, u32[]{:S(2)}) %collective-permute-start.4) | collective-permute-done | bytes 163872 | tf_op jit(solution)/shard_map/ppermute | solution.py:311
  17.2 5.6 %collective-permute-done.2.refs_1_.rest_1_ = bf16[6,128,128]{2,1,0:T(8,128)(2,1)S(1)} collective-permute-done((bf16[6,128,128]{2,1,0:T(8,128)(2,1)S(1)}, bf16[6,128,128]{2,1,0:T(8,128)(2,1)S(1)}, u32[]{:S(2)}, u32[]{:S(2)}) %collective-permute-start.2) | collective-permute-done | bytes 196640 | tf_op jit(solution)/shard_map/ppermute | solution.py:311
  22.8 0.3 %collective-permute-done.1.refs_0_.rest_0_ = bf16[13,128,128]{2,1,0:T(8,128)(2,1)S(1)} collective-permute-done((bf16[13,128,128]{2,1,0:T(8,128)(2,1)S(1)}, bf16[13,128,128]{2,1,0:T(8,128)(2,1)S(1)}, u32[]{:S(2)}, u32[]{:S(2)}) %collective-permute-start.1) | collective-permute-done | bytes 426016 | tf_op jit(solution)/shard_map/ppermute | solution.py:311
  23.1 0.0 collective-permute-done.5.refs_4_.rest_4_
  23.2 0.1 collective-permute-start.6
  23.2 1.3 %outer.1.outer_ref = f32[27,128,128]{2,1,0:T(8,128)S(1)} custom-call(bf16[384,1152]{1,0:T(8,128)(2,1)S(1)} %get-tuple-element.20.left_ref, bf16[384,1152]{1,0:T(8,128)(2,1)S(1)} %collective-permute-done.left_other_ref, bf16[13,128,128]{2,1,0:T(8,128)(2,1)S(1)} %collective-permute-done.1.refs_0_.rest_0_, ...), custom_call_target="tpu_custom_call" | custom-call | flops 1409286144 | bytes 3768320 | tf_op jit(solution)/shard_map/outer/pallas_call | solution.py:366
  24.5 0.8 %collective-permute-done.6.staged_ref = bf16[20,128,128]{2,1,0:T(8,128)(2,1)S(1)} collective-permute-done((bf16[20,128,128]{2,1,0:T(8,128)(2,1)S(1)}, bf16[20,128,128]{2,1,0:T(8,128)(2,1)S(1)}, u32[]{:S(2)}, u32[]{:S(2)}) %collective-permute-start.6) | collective-permute-done | bytes 655392 | tf_op jit(solution)/shard_map/ppermute | solution.py:326
  25.3 1.9 %multiply.1 = f32[1,23,128,128]{3,2,1,0:T(8,128)} custom-call(bf16[384,1152]{1,0:T(8,128)(2,1)S(1)} %get-tuple-element.20.left_ref, bf16[384,1152]{1,0:T(8,128)(2,1)S(1)} %collective-permute-done.left_other_ref, bf16[20,128,128]{2,1,0:T(8,128)(2,1)S(1)} %collective-permute-done.6.staged_ref, f32[27,128,128]{2,1,0:T(8,128)S(1)} %outer.1.outer_ref, ...), custom_call_target="tpu_custom_call" | custom-call | tf_op jit(solution)/shard_map/multiply/pallas_call | solution.py:376
  (3 shorter events, 0.1 us)
Async XLA Ops:
  1.4 10.6 %collective-permute-start = (bf16[384,1152]{1,0:T(8,128)(2,1)S(1)}, bf16[384,1152]{1,0:T(8,128)(2,1)S(1)}, u32[]{:S(2)}, u32[]{:S(2)}) collective-permute-start(bf16[384,1152]{1,0:T(8,128)(2,1)S(1)} %get-tuple-element.20.left_ref), channel_id=1, source_target_pairs={{0,1},{1,0},{2,3},{3,2},{4,5},{5,4},{6,7},{7,6},{8,9},{9,8},{10,11... | collective-permute-start | bytes 2654216 | tf_op jit(solution)/shard_map/ppermute | solution.py:326
  1.9 11.9 %collective-permute-start.3 = (bf16[8,128,128]{2,1,0:T(8,128)(2,1)S(1)}, bf16[8,128,128]{2,1,0:T(8,128)(2,1)S(1)}, u32[]{:S(2)}, u32[]{:S(2)}) collective-permute-start(bf16[8,128,128]{2,1,0:T(8,128)(2,1)S(1)} %get-tuple-element.23), channel_id=1, source_target_pairs={{12,0},{13,1},{6,2},{7,3},{0,4},{1,5},{10,6},{11,7},{4,8},{5,9},{1... | collective-permute-start | bytes 786440 | tf_op jit(solution)/shard_map/ppermute | solution.py:311
  4.5 18.6 %collective-permute-start.1 = (bf16[13,128,128]{2,1,0:T(8,128)(2,1)S(1)}, bf16[13,128,128]{2,1,0:T(8,128)(2,1)S(1)}, u32[]{:S(2)}, u32[]{:S(2)}) collective-permute-start(bf16[13,128,128]{2,1,0:T(8,128)(2,1)S(1)} %get-tuple-element.21), channel_id=1, source_target_pairs={{2,0},{3,1},{0,2},{1,3},{6,4},{7,5},{4,6},{5,7},{10,8},{11,9},{8,1... | collective-permute-start | bytes 1277960 | tf_op jit(solution)/shard_map/ppermute | solution.py:311
  8.0 9.1 %collective-permute-start.4 = (bf16[5,128,128]{2,1,0:T(8,128)(2,1)S(1)}, bf16[5,128,128]{2,1,0:T(8,128)(2,1)S(1)}, u32[]{:S(2)}, u32[]{:S(2)}) collective-permute-start(bf16[5,128,128]{2,1,0:T(8,128)(2,1)S(1)} %get-tuple-element.26), channel_id=1, source_target_pairs={{4,0},{5,1},{14,2},{15,3},{8,4},{9,5},{2,6},{3,7},{12,8},{13,9},{6... | collective-permute-start | bytes 491528 | tf_op jit(solution)/shard_map/ppermute | solution.py:311
  8.5 14.3 %collective-permute-start.2 = (bf16[6,128,128]{2,1,0:T(8,128)(2,1)S(1)}, bf16[6,128,128]{2,1,0:T(8,128)(2,1)S(1)}, u32[]{:S(2)}, u32[]{:S(2)}) collective-permute-start(bf16[6,128,128]{2,1,0:T(8,128)(2,1)S(1)} %get-tuple-element.22), channel_id=1, source_target_pairs={{14,0},{15,1},{4,2},{5,3},{2,4},{3,5},{8,6},{9,7},{6,8},{7,9},{12,... | collective-permute-start | bytes 589832 | tf_op jit(solution)/shard_map/ppermute | solution.py:311
  12.0 11.1 %collective-permute-start.5 = (bf16[1,128,128]{2,1,0:T(8,128)(2,1)S(1)}, bf16[1,128,128]{2,1,0:T(8,128)(2,1)S(1)}, u32[]{:S(2)}, u32[]{:S(2)}) collective-permute-start(bf16[1,128,128]{2,1,0:T(8,128)(2,1)S(1)} %pack_e.1), channel_id=1, source_target_pairs={{10,0},{7,1},{12,2},{9,3},{14,4},{11,5},{0,6},{13,7},{2,8},{15,9},... | collective-permute-start | bytes 98312 | tf_op jit(solution)/shard_map/ppermute | solution.py:311
  23.2 2.2 %collective-permute-start.6 = (bf16[20,128,128]{2,1,0:T(8,128)(2,1)S(1)}, bf16[20,128,128]{2,1,0:T(8,128)(2,1)S(1)}, u32[]{:S(2)}, u32[]{:S(2)}) collective-permute-start(bf16[20,128,128]{2,1,0:T(8,128)(2,1)S(1)} %stage.1), channel_id=1, source_target_pairs={{0,1},{1,0},{2,3},{3,2},{4,5},{5,4},{6,7},{7,6},{8,9},{9,8},{10,11... | collective-permute-start | bytes 1966088 | tf_op jit(solution)/shard_map/ppermute | solution.py:326

commit v9 on v8

--- a/solution.py
+++ b/solution.py
@@ -14,6 +14,8 @@
 LOW, HIGH = -HB, BR - 1 + HB
 NCOL = 9
 INNER = 6
+EARLY_COST = 1000
+LATE_COST = 50
 VMEM_LIMIT = 12 * 2**20
 
 DISTANCES = {"a": 1, "b": -1, "c": -2, "d": 2, "e": None}
@@ -30,16 +32,18 @@
     ("e", 0): [(-7, -7)],
 }
 SIZES = {name: len(SENT[name, 1]) for name in DISTANCES}
+PARTS = {"early": "ac", "late": "bde"}
 STAGED = {
-    parity: [
+    (part, parity): [
         (name, n, (k, j))
-        for name in DISTANCES
+        for name in names
         for n, (k, j) in enumerate(SENT[name, parity])
         if k % 2 != j % 2 or (k, j) == (-7, -7)
     ]
+    for part, names in PARTS.items()
     for parity in (0, 1)
 }
-STAGED_SIZE = max(len(found) for found in STAGED.values())
+STAGED_SIZE = {part: max(len(STAGED[part, parity]) for parity in (0, 1)) for part in PARTS}
 
 
 def columns_of(parity):
@@ -117,9 +121,10 @@
         for name in DISTANCES:
             if (a, b) in SENT[name, parity]:
                 return name, SENT[name, parity].index((a, b)), flip
-        staged = [position for _, _, position in STAGED[1 - parity]]
-        if (a, b) in staged:
-            return "staged", staged.index((a, b)), flip
+        for part in PARTS:
+            staged = [position for _, _, position in STAGED[part, 1 - parity]]
+            if (a, b) in staged:
+                return part, staged.index((a, b)), flip
     raise AssertionError((k, j))
 
 
@@ -131,7 +136,7 @@
         for k in columns_of(kind):
             for j in js:
                 place = find_block(parity, k, j)
-                if place is not None and wanted(place[0]):
+                if place is not None and place[0] in wanted:
                     found[k, j] = place
         if not found:
             continue
@@ -160,6 +165,9 @@
     return total
 
 
+LEFT = (("left", True), ("left", False))
+
+
 def block_of(total, i, y):
     return total[i * BLK : (i + 1) * BLK, y * BLK : (y + 1) * BLK]
 
@@ -179,7 +187,7 @@
     @for_own_parity
     def _(mine):
         js = [j for j in columns_of(mine) if 0 <= j < BR]
-        total = columns_product(refs, right, mine, js, lambda source: True)
+        total = columns_product(refs, right, mine, js, LEFT)
         for i in range(BR):
             for y in range(2):
                 made_ref[i * 2 + y] = block_of(total, i, y) if y < len(js) else jnp.zeros((BLK, BLK), made_ref.dtype)
@@ -203,52 +211,57 @@
         e_ref[0] = (left_ref if mine == 0 else left_other_ref)[pl.ds(i * BLK, BLK), pl.ds(n * BLK, BLK)]
 
 
-def keep_kernel(*refs):
-    pass
-
-
-def stage_kernel(*refs):
-    got = dict(zip(DISTANCES, refs))
+def stage_kernel(part, *refs):
+    got = dict(zip(PARTS[part], refs))
     out_ref = refs[-1]
 
     @for_own_parity
     def _(mine):
-        for n, (name, place, _) in enumerate(STAGED[mine]):
+        staged = STAGED[part, mine]
+        for n, (name, place, _) in enumerate(staged):
             out_ref[n] = got[name][place]
-        for n in range(len(STAGED[mine]), STAGED_SIZE):
+        for n in range(len(staged), STAGED_SIZE[part]):
             out_ref[n] = jnp.zeros((BLK, BLK), out_ref.dtype)
 
 
-def outer_kernel(left_ref, left_other_ref, *rest):
-    refs = {("left", True): left_ref, ("left", False): left_other_ref, **dict(zip(DISTANCES, rest))}
-    out_ref, right = rest[len(DISTANCES) :]
+def add_columns(refs, wanted, old_ref, new_ref, right, mine):
+    for pair, js in enumerate(outer_pairs(mine)):
+        total = columns_product(refs, right.at[pair], mine, js, wanted)
+        for i in range(BR):
+            for y, j in enumerate(js):
+                if abs(i - j) <= HB:
+                    place = i * NCOL + columns_of(mine).index(j)
+                    if old_ref is None:
+                        new_ref[place] = block_of(total, i, y)
+                    else:
+                        new_ref[place] = old_ref[place] if total is None else old_ref[place] + block_of(total, i, y)
+
+
+def early_kernel(left_ref, left_other_ref, a_ref, c_ref, out_ref, right):
+    refs = {("left", True): left_ref, ("left", False): left_other_ref, "a": a_ref, "c": c_ref}
+    for_own_parity(functools.partial(add_columns, refs, (*LEFT, "a", "c"), None, out_ref, right))
+
+
+def staged_early_kernel(left_ref, left_other_ref, staged_ref, old_ref, out_ref, right):
+    refs = {("left", True): left_ref, ("left", False): left_other_ref, "early": staged_ref}
+    for_own_parity(functools.partial(add_columns, refs, ("early",), old_ref, out_ref, right))
+
+
+def late_kernel(left_ref, left_other_ref, b_ref, d_ref, e_ref, old_ref, out_ref, right):
+    refs = {("left", True): left_ref, ("left", False): left_other_ref, "b": b_ref, "d": d_ref, "e": e_ref}
+    for_own_parity(functools.partial(add_columns, refs, ("b", "d", "e"), old_ref, out_ref, right))
+
+
+def multiply_kernel(slots, left_ref, left_other_ref, staged_ref, old_ref, inner_ref, places_ref, out_ref, *rest):
+    right, made, places, places_sem, out_sem = rest
+    refs = {("left", True): left_ref, ("left", False): left_other_ref, "late": staged_ref}
+    load = pltpu.make_async_copy(places_ref, places, places_sem)
+    load.start()
 
     @for_own_parity
     def _(mine):
-        for pair, js in enumerate(outer_pairs(mine)):
-            total = columns_product(refs, right.at[pair], mine, js, lambda source: source != "staged")
-            for i in range(BR):
-                for y, j in enumerate(js):
-                    if abs(i - j) <= HB:
-                        out_ref[i * NCOL + columns_of(mine).index(j)] = block_of(total, i, y)
-
-
-def multiply_kernel(slots, left_ref, left_other_ref, staged_ref, outer_ref, inner_ref, places_ref, out_ref, *rest):
-    right, made, places, places_sem, out_sem = rest
-    refs = {("left", True): left_ref, ("left", False): left_other_ref, "staged": staged_ref}
-    load = pltpu.make_async_copy(places_ref, places, places_sem)
-    load.start()
-
-    @for_own_parity
-    def _(mine):
+        add_columns(refs, ("late",), old_ref, made, right, mine)
         columns = columns_of(mine)
-        for pair, js in enumerate(outer_pairs(mine)):
-            total = columns_product(refs, right.at[pair], mine, js, lambda source: source == "staged")
-            for i in range(BR):
-                for y, j in enumerate(js):
-                    if abs(i - j) <= HB:
-                        place = i * NCOL + columns.index(j)
-                        made[place] = outer_ref[place] + block_of(total, i, y)
         for i in range(BR):
             for y, j in enumerate(j for j in columns if 0 <= j < BR):
                 made[i * NCOL + columns.index(j)] = inner_ref[i * 2 + y]
@@ -309,18 +322,6 @@
                 source = (r - distance if r % 2 == 1 else r + distance) % row_count
                 pairs.append((source * col_count + c, r * col_count + c))
         return lax.ppermute(message, ("row", "col"), pairs)
-
-    def keep(arrays, flops):
-        return pl.pallas_call(
-            keep_kernel,
-            out_shape=[jax.ShapeDtypeStruct(x.shape, x.dtype) for x in arrays],
-            in_specs=[vmem] * len(arrays),
-            out_specs=[vmem] * len(arrays),
-            input_output_aliases={n: n for n in range(len(arrays))},
-            compiler_params=params,
-            cost_estimate=pl.CostEstimate(flops=flops, bytes_accessed=0, transcendentals=0),
-            name="keep",
-        )(*arrays)
 
     def swapped(block):
         return lax.ppermute(block, "col", [(0, 1), (1, 0)])
@@ -351,28 +352,39 @@
         cost_estimate=cost(3 * 2 * 17, 4 * values.size),
         name="inner",
     )(*places, counts, left, left_other)
-    got[2], inner, = keep((got[2], inner,), 4000000000)
-    *got, inner = lax.optimization_barrier((*got, inner))
-    staged = swapped(
-        pl.pallas_call(
-            stage_kernel,
-            out_shape=blocks(STAGED_SIZE),
-            in_specs=[vmem] * 5,
+    a, b, c, d, e = got
+
+    def staged(part, arrays):
+        return swapped(
+            pl.pallas_call(
+                functools.partial(stage_kernel, part),
+                out_shape=blocks(STAGED_SIZE[part]),
+                in_specs=[vmem] * len(arrays),
+                out_specs=vmem,
+                compiler_params=params,
+                name="stage_" + part,
+            )(*arrays)
+        )
+
+    def added(kernel, name, products, arrays):
+        return pl.pallas_call(
+            kernel,
+            out_shape=blocks(BR * NCOL, jnp.float32),
+            in_specs=[vmem] * len(arrays),
             out_specs=vmem,
+            scratch_shapes=[right_scratch(4)],
             compiler_params=params,
-            name="stage",
-        )(*got)
-    )
-    outer = pl.pallas_call(
-        outer_kernel,
-        out_shape=blocks(BR * NCOL, jnp.float32),
-        in_specs=[vmem] * 7,
-        out_specs=vmem,
-        scratch_shapes=[right_scratch(4)],
-        compiler_params=params,
-        cost_estimate=cost(3 * 2 * 56, 10 * values.size),
-        name="outer",
-    )(left, left_other, *got)
+            cost_estimate=cost(products, 0),
+            name=name,
+        )(*arrays)
+
+    a, c, inner = lax.optimization_barrier((a, c, inner))
+    staged_early = staged("early", (a, c))
+    early = added(early_kernel, "early", EARLY_COST, (left, left_other, a, c))
+    early = added(staged_early_kernel, "staged_early", 1, (left, left_other, staged_early, early))
+    b, d, e, early = lax.optimization_barrier((b, d, e, early))
+    staged_late = staged("late", (b, d, e))
+    late = added(late_kernel, "late", LATE_COST, (left, left_other, b, d, e, early))
     return pl.pallas_call(
         functools.partial(multiply_kernel, slots),
         out_shape=jax.ShapeDtypeStruct(values.shape, jnp.float32),
@@ -387,7 +399,7 @@
         ],
         compiler_params=params,
         name="multiply",
-    )(left, left_other, staged, outer, inner, slot_places)
+    )(left, left_other, staged_late, late, inner, slot_places)
 
 
 def solution(mesh):

time: 27.4 us -> 29.4 us (1.073)
  the two profiles are of different devices: /device:TPU:0 before, /device:TPU:25 now
where the time goes in v9:
time: 29.4 us; the launch traced here: 29.2 us
  waiting for transfers between devices  14.7 us (50%)
  Pallas kernels  7.15 us (24%)
  starting transfers between devices  6.62 us (23%)
  between operations  0.74 us (3%)
    ppermute x5, waiting for transfers between devices, towards(): return lax.ppermute(message, ('row', 'col'), pairs)  14.1 us
    ppermute x3, starting transfers between devices, swapped(): return lax.ppermute(block, 'col', [(0, 1), (1, 0)])  3.93 us
    ppermute x5, starting transfers between devices, towards(): return lax.ppermute(message, ('row', 'col'), pairs)  2.69 us
    pallas_call x3, Pallas kernels, added(): pl.pallas_call(kernel, out_shape=blocks(BR * NCOL, jnp.float32), in_specs...  2.54 us
    pallas_call x1, Pallas kernels, local(): pl.pallas_call(functools.partial(multiply_kernel, slots), out_shape=jax.S...  1.65 us
    pallas_call x1, Pallas kernels, local(): pl.pallas_call(functools.partial(inner_kernel, nblocks, slots), out_shape...  1.53 us
    pallas_call x1, Pallas kernels, local(): pl.pallas_call(functools.partial(pack_kernel, nblocks, slots), out_shape=...  1.36 us
    ppermute x3, waiting for transfers between devices, swapped(): return lax.ppermute(block, 'col', [(0, 1), (1, 0)])  0.59 us
  transfers between devices with their start and end apart: 8, of which 4 were waited for; matrix products, arithmetic and copies ran while one was open for 0% of the time, Pallas kernels for 14%

profile of v9, /device:TPU:25, one launch (start us, length us, event | category | flops | bytes accessed | tf_op | source)
XLA Modules:
  0.0 29.2 jit_solution(17460087996522549271)
XLA Ops:
  0.0 1.4 %pack.1 = (bf16[13,128,128]{2,1,0:T(8,128)(2,1)S(1)}, bf16[6,128,128]{2,1,0:T(8,128)(2,1)S(1)}, bf16[8,128,128]{2,1,0:T(8,128)(2,1)S(1)}, bf16[5,128,128]{2,1,0:T(8,128)(2,1)S(1)}, bf16[384,1152]{1,0:T(8,128)(2,1)S(1)}) custom-call(s32[1,23]{1,0:T(1,128)} %rows_ref.3, s32[1,23]{1,0:T(1,128)} %cols_ref.3, bf16[1,23,128,128]{3,2,1,0:T(8,128)(2,1)} %values_ref.1), custom_call_target="tpu_custom_call" | custom-call | tf_op jit(solution)/shard_map/pack/pallas_call | solution.py:301
  1.4 0.7 %collective-permute-start = (bf16[384,1152]{1,0:T(8,128)(2,1)S(1)}, bf16[384,1152]{1,0:T(8,128)(2,1)S(1)}, u32[]{:S(2)}, u32[]{:S(2)}) collective-permute-start(bf16[384,1152]{1,0:T(8,128)(2,1)S(1)} %get-tuple-element.19.left_ref), channel_id=1, source_target_pairs={{0,1},{1,0},{2,3},{3,2},{4,5},{5,4},{6,7},{7,6},{8,9},{9,8},{10,11... | collective-permute-start | bytes 2654216 | tf_op jit(solution)/shard_map/ppermute | solution.py:327
  2.1 1.2 %collective-permute-start.4 = (bf16[13,128,128]{2,1,0:T(8,128)(2,1)S(1)}, bf16[13,128,128]{2,1,0:T(8,128)(2,1)S(1)}, u32[]{:S(2)}, u32[]{:S(2)}) collective-permute-start(bf16[13,128,128]{2,1,0:T(8,128)(2,1)S(1)} %get-tuple-element.22), channel_id=1, source_target_pairs={{2,0},{3,1},{0,2},{1,3},{6,4},{7,5},{4,6},{5,7},{10,8},{11,9},{8,1... | collective-permute-start | bytes 1277960 | tf_op jit(solution)/shard_map/ppermute | solution.py:324
  3.3 0.0 collective-permute-start.5
  3.3 0.3 %collective-permute-start.1 = (bf16[6,128,128]{2,1,0:T(8,128)(2,1)S(1)}, bf16[6,128,128]{2,1,0:T(8,128)(2,1)S(1)}, u32[]{:S(2)}, u32[]{:S(2)}) collective-permute-start(bf16[6,128,128]{2,1,0:T(8,128)(2,1)S(1)} %get-tuple-element.20), channel_id=1, source_target_pairs={{14,0},{15,1},{4,2},{5,3},{2,4},{3,5},{8,6},{9,7},{6,8},{7,9},{12,... | collective-permute-start | bytes 589832 | tf_op jit(solution)/shard_map/ppermute | solution.py:324
  3.6 1.2 %collective-permute-start.2 = (bf16[5,128,128]{2,1,0:T(8,128)(2,1)S(1)}, bf16[5,128,128]{2,1,0:T(8,128)(2,1)S(1)}, u32[]{:S(2)}, u32[]{:S(2)}) collective-permute-start(bf16[5,128,128]{2,1,0:T(8,128)(2,1)S(1)} %get-tuple-element.21), channel_id=1, source_target_pairs={{4,0},{5,1},{14,2},{15,3},{8,4},{9,5},{2,6},{3,7},{12,8},{13,9},{6... | collective-permute-start | bytes 491528 | tf_op jit(solution)/shard_map/ppermute | solution.py:324
  5.5 0.0 collective-permute-done.left_other_ref
  5.5 1.5 %inner.1 = (f32[6,128,128]{2,1,0:T(8,128)S(1)}, s32[1,128]{1,0:T(1,128)S(1)}) custom-call(s32[1,23]{1,0:T(1,128)} %rows_ref.3, s32[1,23]{1,0:T(1,128)} %cols_ref.3, s32[1,1]{1,0:T(1,128)S(6)} %copy.5.counts_ref, bf16[384,1152]{1,0:T(8,128)(2,1)S(1)} %get-tuple-element.19.left_ref, bf16[384,1152]{1,0:T(8,128)(2,1)S(1)} %collective-permute-done.left_other_ref), custom_call_target="tpu_custom_call" | custom-call | flops 427819008 | bytes 1507328 | tf_op jit(solution)/shard_map/inner/pallas_call | solution.py:340
  7.0 4.1 %collective-permute-done.5.refs_1_.c_ref = bf16[8,128,128]{2,1,0:T(8,128)(2,1)S(1)} collective-permute-done((bf16[8,128,128]{2,1,0:T(8,128)(2,1)S(1)}, bf16[8,128,128]{2,1,0:T(8,128)(2,1)S(1)}, u32[]{:S(2)}, u32[]{:S(2)}) %collective-permute-start.5) | collective-permute-done | bytes 262176 | tf_op jit(solution)/shard_map/ppermute | solution.py:324
  11.1 6.6 %collective-permute-done.4.refs_0_.a_ref = bf16[13,128,128]{2,1,0:T(8,128)(2,1)S(1)} collective-permute-done((bf16[13,128,128]{2,1,0:T(8,128)(2,1)S(1)}, bf16[13,128,128]{2,1,0:T(8,128)(2,1)S(1)}, u32[]{:S(2)}, u32[]{:S(2)}) %collective-permute-start.4) | collective-permute-done | bytes 426016 | tf_op jit(solution)/shard_map/ppermute | solution.py:324
  17.7 2.2 %collective-permute-start.6 = (bf16[12,128,128]{2,1,0:T(8,128)(2,1)S(1)}, bf16[12,128,128]{2,1,0:T(8,128)(2,1)S(1)}, u32[]{:S(2)}, u32[]{:S(2)}) collective-permute-start(bf16[12,128,128]{2,1,0:T(8,128)(2,1)S(1)} %stage_early.1), channel_id=1, source_target_pairs={{0,1},{1,0},{2,3},{3,2},{4,5},{5,4},{6,7},{7,6},{8,9},{9,8},{10,11... | collective-permute-start | bytes 1179656 | tf_op jit(solution)/shard_map/ppermute | solution.py:327
  19.9 0.0 collective-permute-start.3
  19.9 1.4 %early.1.old_ref = f32[27,128,128]{2,1,0:T(8,128)S(1)} custom-call(bf16[384,1152]{1,0:T(8,128)(2,1)S(1)} %get-tuple-element.19.left_ref, bf16[384,1152]{1,0:T(8,128)(2,1)S(1)} %collective-permute-done.left_other_ref, bf16[13,128,128]{2,1,0:T(8,128)(2,1)S(1)} %collective-permute-done.4.refs_0_.a_ref, bf16[8,128,128]{2,1,0:T(8,128)(2,1)S(1)} %collective-permute-done.5.refs_1_.c_ref), custom_call_target="tpu_custom_call" | custom-call | flops 4194304000 | tf_op jit(solution)/shard_map/early/pallas_call | solution.py:370
  21.3 0.0 collective-permute-done.6.staged_ref
  21.3 0.6 %staged_early.1.old_ref = f32[27,128,128]{2,1,0:T(8,128)S(1)} custom-call(bf16[384,1152]{1,0:T(8,128)(2,1)S(1)} %get-tuple-element.19.left_ref, bf16[384,1152]{1,0:T(8,128)(2,1)S(1)} %collective-permute-done.left_other_ref, bf16[12,128,128]{2,1,0:T(8,128)(2,1)S(1)} %collective-permute-done.6.staged_ref, f32[27,128,128]{2,1,0:T(8,128)S(1)} %early.1.old_ref), custom_call_target="tpu_custom_call" | custom-call | flops 4194304 | tf_op jit(solution)/shard_map/staged_early/pallas_call | solution.py:370
  21.9 0.0 collective-permute-done.2.refs_1_.d_ref
  21.9 0.0 collective-permute-done.1.refs_0_.b_ref
  21.9 3.4 %collective-permute-done.3.refs_2_.e_ref = bf16[1,128,128]{2,1,0:T(8,128)(2,1)S(1)} collective-permute-done((bf16[1,128,128]{2,1,0:T(8,128)(2,1)S(1)}, bf16[1,128,128]{2,1,0:T(8,128)(2,1)S(1)}, u32[]{:S(2)}, u32[]{:S(2)}) %collective-permute-start.3) | collective-permute-done | bytes 32800 | tf_op jit(solution)/shard_map/ppermute | solution.py:324
  25.4 1.0 %collective-permute-start.7 = (bf16[8,128,128]{2,1,0:T(8,128)(2,1)S(1)}, bf16[8,128,128]{2,1,0:T(8,128)(2,1)S(1)}, u32[]{:S(2)}, u32[]{:S(2)}) collective-permute-start(bf16[8,128,128]{2,1,0:T(8,128)(2,1)S(1)} %stage_late.1), channel_id=1, source_target_pairs={{0,1},{1,0},{2,3},{3,2},{4,5},{5,4},{6,7},{7,6},{8,9},{9,8},{10,11... | collective-permute-start | bytes 786440 | tf_op jit(solution)/shard_map/ppermute | solution.py:327
  26.4 0.6 %late.1.old_ref = f32[27,128,128]{2,1,0:T(8,128)S(1)} custom-call(bf16[384,1152]{1,0:T(8,128)(2,1)S(1)} %get-tuple-element.19.left_ref, bf16[384,1152]{1,0:T(8,128)(2,1)S(1)} %collective-permute-done.left_other_ref, bf16[6,128,128]{2,1,0:T(8,128)(2,1)S(1)} %collective-permute-done.1.refs_0_.b_ref, ...), custom_call_target="tpu_custom_call" | custom-call | flops 209715200 | tf_op jit(solution)/shard_map/late/pallas_call | solution.py:370
  27.0 0.6 %collective-permute-done.7.staged_ref = bf16[8,128,128]{2,1,0:T(8,128)(2,1)S(1)} collective-permute-done((bf16[8,128,128]{2,1,0:T(8,128)(2,1)S(1)}, bf16[8,128,128]{2,1,0:T(8,128)(2,1)S(1)}, u32[]{:S(2)}, u32[]{:S(2)}) %collective-permute-start.7) | collective-permute-done | bytes 262176 | tf_op jit(solution)/shard_map/ppermute | solution.py:327
  27.5 1.7 %multiply.1 = f32[1,23,128,128]{3,2,1,0:T(8,128)} custom-call(bf16[384,1152]{1,0:T(8,128)(2,1)S(1)} %get-tuple-element.19.left_ref, bf16[384,1152]{1,0:T(8,128)(2,1)S(1)} %collective-permute-done.left_other_ref, bf16[8,128,128]{2,1,0:T(8,128)(2,1)S(1)} %collective-permute-done.7.staged_ref, f32[27,128,128]{2,1,0:T(8,128)S(1)} %late.1.old_ref, ...), custom_call_target="tpu_custom_call" | custom-call | tf_op jit(solution)/shard_map/multiply/pallas_call | solution.py:388
  (3 shorter events, 0.1 us)
Async XLA Ops:
  1.4 4.1 %collective-permute-start = (bf16[384,1152]{1,0:T(8,128)(2,1)S(1)}, bf16[384,1152]{1,0:T(8,128)(2,1)S(1)}, u32[]{:S(2)}, u32[]{:S(2)}) collective-permute-start(bf16[384,1152]{1,0:T(8,128)(2,1)S(1)} %get-tuple-element.19.left_ref), channel_id=1, source_target_pairs={{0,1},{1,0},{2,3},{3,2},{4,5},{5,4},{6,7},{7,6},{8,9},{9,8},{10,11... | collective-permute-start | bytes 2654216 | tf_op jit(solution)/shard_map/ppermute | solution.py:327
  2.1 15.5 %collective-permute-start.4 = (bf16[13,128,128]{2,1,0:T(8,128)(2,1)S(1)}, bf16[13,128,128]{2,1,0:T(8,128)(2,1)S(1)}, u32[]{:S(2)}, u32[]{:S(2)}) collective-permute-start(bf16[13,128,128]{2,1,0:T(8,128)(2,1)S(1)} %get-tuple-element.22), channel_id=1, source_target_pairs={{2,0},{3,1},{0,2},{1,3},{6,4},{7,5},{4,6},{5,7},{10,8},{11,9},{8,1... | collective-permute-start | bytes 1277960 | tf_op jit(solution)/shard_map/ppermute | solution.py:324
  3.3 7.8 %collective-permute-start.5 = (bf16[8,128,128]{2,1,0:T(8,128)(2,1)S(1)}, bf16[8,128,128]{2,1,0:T(8,128)(2,1)S(1)}, u32[]{:S(2)}, u32[]{:S(2)}) collective-permute-start(bf16[8,128,128]{2,1,0:T(8,128)(2,1)S(1)} %get-tuple-element.23), channel_id=1, source_target_pairs={{12,0},{13,1},{6,2},{7,3},{0,4},{1,5},{10,6},{11,7},{4,8},{5,9},{1... | collective-permute-start | bytes 786440 | tf_op jit(solution)/shard_map/ppermute | solution.py:324
  3.3 18.6 %collective-permute-start.1 = (bf16[6,128,128]{2,1,0:T(8,128)(2,1)S(1)}, bf16[6,128,128]{2,1,0:T(8,128)(2,1)S(1)}, u32[]{:S(2)}, u32[]{:S(2)}) collective-permute-start(bf16[6,128,128]{2,1,0:T(8,128)(2,1)S(1)} %get-tuple-element.20), channel_id=1, source_target_pairs={{14,0},{15,1},{4,2},{5,3},{2,4},{3,5},{8,6},{9,7},{6,8},{7,9},{12,... | collective-permute-start | bytes 589832 | tf_op jit(solution)/shard_map/ppermute | solution.py:324
  3.6 18.3 %collective-permute-start.2 = (bf16[5,128,128]{2,1,0:T(8,128)(2,1)S(1)}, bf16[5,128,128]{2,1,0:T(8,128)(2,1)S(1)}, u32[]{:S(2)}, u32[]{:S(2)}) collective-permute-start(bf16[5,128,128]{2,1,0:T(8,128)(2,1)S(1)} %get-tuple-element.21), channel_id=1, source_target_pairs={{4,0},{5,1},{14,2},{15,3},{8,4},{9,5},{2,6},{3,7},{12,8},{13,9},{6... | collective-permute-start | bytes 491528 | tf_op jit(solution)/shard_map/ppermute | solution.py:324
  17.7 3.6 %collective-permute-start.6 = (bf16[12,128,128]{2,1,0:T(8,128)(2,1)S(1)}, bf16[12,128,128]{2,1,0:T(8,128)(2,1)S(1)}, u32[]{:S(2)}, u32[]{:S(2)}) collective-permute-start(bf16[12,128,128]{2,1,0:T(8,128)(2,1)S(1)} %stage_early.1), channel_id=1, source_target_pairs={{0,1},{1,0},{2,3},{3,2},{4,5},{5,4},{6,7},{7,6},{8,9},{9,8},{10,11... | collective-permute-start | bytes 1179656 | tf_op jit(solution)/shard_map/ppermute | solution.py:327
  19.9 5.5 %collective-permute-start.3 = (bf16[1,128,128]{2,1,0:T(8,128)(2,1)S(1)}, bf16[1,128,128]{2,1,0:T(8,128)(2,1)S(1)}, u32[]{:S(2)}, u32[]{:S(2)}) collective-permute-start(bf16[1,128,128]{2,1,0:T(8,128)(2,1)S(1)} %pack_e.1), channel_id=1, source_target_pairs={{10,0},{7,1},{12,2},{9,3},{14,4},{11,5},{0,6},{13,7},{2,8},{15,9},... | collective-permute-start | bytes 98312 | tf_op jit(solution)/shard_map/ppermute | solution.py:324
  25.4 2.2 %collective-permute-start.7 = (bf16[8,128,128]{2,1,0:T(8,128)(2,1)S(1)}, bf16[8,128,128]{2,1,0:T(8,128)(2,1)S(1)}, u32[]{:S(2)}, u32[]{:S(2)}) collective-permute-start(bf16[8,128,128]{2,1,0:T(8,128)(2,1)S(1)} %stage_late.1), channel_id=1, source_target_pairs={{0,1},{1,0},{2,3},{3,2},{4,5},{5,4},{6,7},{7,6},{8,9},{9,8},{10,11... | collective-permute-start | bytes 786440 | tf_op jit(solution)/shard_map/ppermute | solution.py:327

commit v10 on v8

--- a/solution.py
+++ b/solution.py
@@ -13,7 +13,7 @@
 WIDTH = 2 * HB + 1
 LOW, HIGH = -HB, BR - 1 + HB
 NCOL = 9
-INNER = 6
+SOURCES = 32
 VMEM_LIMIT = 12 * 2**20
 
 DISTANCES = {"a": 1, "b": -1, "c": -2, "d": 2, "e": None}
@@ -164,13 +164,18 @@
     return total[i * BLK : (i + 1) * BLK, y * BLK : (y + 1) * BLK]
 
 
+def stored_places(parity):
+    columns = columns_of(parity)
+    return [i * NCOL + n for i in range(BR) for n, j in enumerate(columns) if abs(i - j) <= HB]
+
+
 def outer_pairs(parity):
     outer = [j for j in columns_of(parity) if not 0 <= j < BR]
     return [outer[n : n + 2] for n in range(0, len(outer), 2)]
 
 
 def inner_kernel(nblocks, slots, rows_ref, cols_ref, counts_ref, left_ref, left_other_ref, *rest):
-    made_ref, places_ref, right, places, *index, sems, places_sem = rest
+    made_ref, table_ref, right, table, *index, sems, table_sem = rest
     copies = index_copies((rows_ref, cols_ref), index, sems)
     for copy in copies:
         copy.start()
@@ -182,15 +187,31 @@
         total = columns_product(refs, right, mine, js, lambda source: True)
         for i in range(BR):
             for y in range(2):
-                made_ref[i * 2 + y] = block_of(total, i, y) if y < len(js) else jnp.zeros((BLK, BLK), made_ref.dtype)
+                if y < len(js):
+                    made_ref[i * NCOL + columns_of(mine).index(js[y])] = block_of(total, i, y)
+        made_ref[BR * NCOL] = jnp.zeros((BLK, BLK), made_ref.dtype)
 
     for copy in copies:
         copy.wait()
+    for place in range(BR * NCOL + 1):
+        table[0, place] = -1
     count = counts_ref[0, 0]
     for m in range(slots):
         _, row, band = slot_position(*index, m, nblocks)
-        places[0, m] = jnp.where(m < count, row * NCOL + (row + band) // 2, BR * NCOL)
-    copy = pltpu.make_async_copy(places, places_ref, places_sem)
+        table[0, jnp.where(m < count, row * NCOL + (row + band) // 2, BR * NCOL)] = m
+
+    @for_own_parity
+    def _(mine):
+        unused = count
+        for place in stored_places(mine):
+            slot = table[0, place]
+            absent = slot < 0
+            table[0, place] = jnp.where(absent, unused, slot)
+            table[0, SOURCES + place] = jnp.where(absent, BR * NCOL, place)
+            unused = jnp.where(absent, unused + 1, unused)
+        table[0, BR * NCOL] = unused
+
+    copy = pltpu.make_async_copy(table, table_ref, table_sem)
     copy.start()
     copy.wait()
 
@@ -201,10 +222,6 @@
         i = 2 if mine == 0 else 0
         n = columns_of(0).index(i)
         e_ref[0] = (left_ref if mine == 0 else left_other_ref)[pl.ds(i * BLK, BLK), pl.ds(n * BLK, BLK)]
-
-
-def keep_kernel(*refs):
-    pass
 
 
 def stage_kernel(*refs):
@@ -233,30 +250,36 @@
                         out_ref[i * NCOL + columns_of(mine).index(j)] = block_of(total, i, y)
 
 
-def multiply_kernel(slots, left_ref, left_other_ref, staged_ref, outer_ref, inner_ref, places_ref, out_ref, *rest):
-    right, made, places, places_sem, out_sem = rest
+def multiply_kernel(slots, left_ref, left_other_ref, staged_ref, outer_ref, inner_ref, table_ref, out_ref, *rest):
+    right, made, table, table_sem, out_sem = rest
     refs = {("left", True): left_ref, ("left", False): left_other_ref, "staged": staged_ref}
-    load = pltpu.make_async_copy(places_ref, places, places_sem)
+    load = pltpu.make_async_copy(table_ref, table, table_sem)
     load.start()
+    made[BR * NCOL] = jnp.zeros((BLK, BLK), made.dtype)
+
+    def store(source_ref, place):
+        source = source_ref.at[table[0, SOURCES + place]]
+        pltpu.make_async_copy(source, out_ref.at[0, table[0, place]], out_sem).start()
 
     @for_own_parity
     def _(mine):
         columns = columns_of(mine)
-        for pair, js in enumerate(outer_pairs(mine)):
+        pairs = outer_pairs(mine)
+        inner = [n for n, j in enumerate(columns) if 0 <= j < BR]
+        load.wait()
+        for i in range(BR):
+            for n in inner:
+                store(inner_ref, i * NCOL + n)
+        for pair, js in enumerate(pairs):
             total = columns_product(refs, right.at[pair], mine, js, lambda source: source == "staged")
-            for i in range(BR):
-                for y, j in enumerate(js):
-                    if abs(i - j) <= HB:
-                        place = i * NCOL + columns.index(j)
-                        made[place] = outer_ref[place] + block_of(total, i, y)
-        for i in range(BR):
-            for y, j in enumerate(j for j in columns if 0 <= j < BR):
-                made[i * NCOL + columns.index(j)] = inner_ref[i * 2 + y]
-        made[BR * NCOL] = jnp.zeros((BLK, BLK), made.dtype)
-
-    load.wait()
-    for m in range(slots):
-        pltpu.make_async_copy(made.at[places[0, m]], out_ref.at[0, m], out_sem).start()
+            places = [(i, y, i * NCOL + columns.index(j)) for i in range(BR) for y, j in enumerate(js) if abs(i - j) <= HB]
+            for i, y, place in places:
+                made[place] = outer_ref[place] + block_of(total, i, y)
+            for _, _, place in places:
+                store(made, place)
+        if len(stored_places(mine)) < slots:
+            pltpu.make_async_copy(made.at[BR * NCOL], out_ref.at[0, table[0, BR * NCOL]], out_sem).start()
+
     pltpu.make_async_copy(made.at[pl.ds(0, slots)], out_ref.at[0], out_sem).wait()
 
 
@@ -274,7 +297,7 @@
         pltpu.SMEM((1, slots), jnp.int32),
         pltpu.SemaphoreType.DMA((2,)),
     ]
-    places_shape = (1, BLK)
+    table_shape = (1, BLK)
 
     def blocks(count, dtype=values.dtype):
         return jax.ShapeDtypeStruct((count, BLK, BLK), dtype)
@@ -310,18 +333,6 @@
                 pairs.append((source * col_count + c, r * col_count + c))
         return lax.ppermute(message, ("row", "col"), pairs)
 
-    def keep(arrays, flops):
-        return pl.pallas_call(
-            keep_kernel,
-            out_shape=[jax.ShapeDtypeStruct(x.shape, x.dtype) for x in arrays],
-            in_specs=[vmem] * len(arrays),
-            out_specs=[vmem] * len(arrays),
-            input_output_aliases={n: n for n in range(len(arrays))},
-            compiler_params=params,
-            cost_estimate=pl.CostEstimate(flops=flops, bytes_accessed=0, transcendentals=0),
-            name="keep",
-        )(*arrays)
-
     def swapped(block):
         return lax.ppermute(block, "col", [(0, 1), (1, 0)])
 
@@ -336,14 +347,14 @@
         name="pack_e",
     )(left, left_other)
     got.append(towards("e", message))
-    inner, slot_places = pl.pallas_call(
+    inner, table = pl.pallas_call(
         functools.partial(inner_kernel, nblocks, slots),
-        out_shape=[blocks(INNER, jnp.float32), jax.ShapeDtypeStruct(places_shape, jnp.int32)],
+        out_shape=[blocks(BR * NCOL + 1, jnp.float32), jax.ShapeDtypeStruct(table_shape, jnp.int32)],
         in_specs=[hbm] * 2 + [smem] + [vmem] * 2,
         out_specs=[vmem] * 2,
         scratch_shapes=[
             pltpu.VMEM((2, NCOL * BLK, 2 * BLK), values.dtype),
-            pltpu.SMEM(places_shape, jnp.int32),
+            pltpu.SMEM(table_shape, jnp.int32),
             *index_scratch,
             pltpu.SemaphoreType.DMA,
         ],
@@ -351,7 +362,6 @@
         cost_estimate=cost(3 * 2 * 17, 4 * values.size),
         name="inner",
     )(*places, counts, left, left_other)
-    got[2], inner, = keep((got[2], inner,), 4000000000)
     *got, inner = lax.optimization_barrier((*got, inner))
     staged = swapped(
         pl.pallas_call(
@@ -381,13 +391,13 @@
         scratch_shapes=[
             right_scratch(4),
             pltpu.VMEM((BR * NCOL + 1, BLK, BLK), jnp.float32),
-            pltpu.SMEM(places_shape, jnp.int32),
+            pltpu.SMEM(table_shape, jnp.int32),
             pltpu.SemaphoreType.DMA,
             pltpu.SemaphoreType.DMA,
         ],
         compiler_params=params,
         name="multiply",
-    )(left, left_other, staged, outer, inner, slot_places)
+    )(left, left_other, staged, outer, inner, table)
 
 
 def solution(mesh):

time: 27.4 us -> 27.2 us (level)
  starting transfers between devices: 10.1 us -> 9.08 us
  Pallas kernels: 6.25 us -> 6.67 us
  waiting for transfers between devices: 10.2 us -> 10.6 us
    ppermute x5, starting transfers between devices: 9.47 us -> 8.47 us  [towards(): return lax.ppermute(message, ('row', 'col'), pairs)]
    ppermute x5, waiting for transfers between devices: 9.41 us -> 9.81 us  [towards(): return lax.ppermute(message, ('row', 'col'), pairs)]
    pallas_call x1, Pallas kernels: 1.95 us -> 2.24 us  [local(): pl.pallas_call(functools.partial(multiply_kernel, slots), out_shape=jax.S...]
  transfers between devices with their start and end apart: 7 -> 7, of which waited for: 5 -> 2; matrix products, arithmetic and copies ran while one was open for 0% -> 0% of each run, Pallas kernels for 11% -> 11%
where the time goes in v10:
time: 27.2 us; the launch traced here: 27.1 us
  waiting for transfers between devices  10.6 us (39%)
  starting transfers between devices  9.08 us (33%)
  Pallas kernels  6.67 us (25%)
  between operations  0.72 us (3%)
    ppermute x5, waiting for transfers between devices, towards(): return lax.ppermute(message, ('row', 'col'), pairs)  9.81 us
    ppermute x5, starting transfers between devices, towards(): return lax.ppermute(message, ('row', 'col'), pairs)  8.47 us
    pallas_call x1, Pallas kernels, local(): pl.pallas_call(functools.partial(multiply_kernel, slots), out_shape=jax.S...  2.24 us
    pallas_call x1, Pallas kernels, local(): pl.pallas_call(functools.partial(inner_kernel, nblocks, slots), out_shape...  1.69 us
    pallas_call x1, Pallas kernels, local(): pl.pallas_call(functools.partial(pack_kernel, nblocks, slots), out_shape=...  1.36 us
    pallas_call x1, Pallas kernels, local(): pl.pallas_call(outer_kernel, out_shape=blocks(BR * NCOL, jnp.float32), in...  1.28 us
    ppermute x2, waiting for transfers between devices, swapped(): return lax.ppermute(block, 'col', [(0, 1), (1, 0)])  0.78 us
    ppermute x2, starting transfers between devices, swapped(): return lax.ppermute(block, 'col', [(0, 1), (1, 0)])  0.62 us
  transfers between devices with their start and end apart: 7, of which 2 were waited for; matrix products, arithmetic and copies ran while one was open for 0% of the time, Pallas kernels for 11%

profile of v10, /device:TPU:0, one launch (start us, length us, event | category | flops | bytes accessed | tf_op | source)
XLA Modules:
  0.0 27.1 jit_solution(2101861535999563161)
XLA Ops:
  0.0 1.4 %pack.1 = (bf16[13,128,128]{2,1,0:T(8,128)(2,1)S(1)}, bf16[6,128,128]{2,1,0:T(8,128)(2,1)S(1)}, bf16[8,128,128]{2,1,0:T(8,128)(2,1)S(1)}, bf16[5,128,128]{2,1,0:T(8,128)(2,1)S(1)}, bf16[384,1152]{1,0:T(8,128)(2,1)S(1)}) custom-call(s32[1,23]{1,0:T(1,128)} %rows_ref.3, s32[1,23]{1,0:T(1,128)} %cols_ref.3, bf16[1,23,128,128]{3,2,1,0:T(8,128)(2,1)} %values_ref.1), custom_call_target="tpu_custom_call" | custom-call | tf_op jit(solution)/shard_map/pack/pallas_call | solution.py:311
  1.4 0.5 %collective-permute-start = (bf16[384,1152]{1,0:T(8,128)(2,1)S(1)}, bf16[384,1152]{1,0:T(8,128)(2,1)S(1)}, u32[]{:S(2)}, u32[]{:S(2)}) collective-permute-start(bf16[384,1152]{1,0:T(8,128)(2,1)S(1)} %get-tuple-element.18.left_ref), channel_id=1, source_target_pairs={{0,1},{1,0},{2,3},{3,2},{4,5},{5,4},{6,7},{7,6},{8,9},{9,8},{10,11... | collective-permute-start | bytes 2654216 | tf_op jit(solution)/shard_map/ppermute | solution.py:337
  1.9 2.6 %collective-permute-start.1 = (bf16[13,128,128]{2,1,0:T(8,128)(2,1)S(1)}, bf16[13,128,128]{2,1,0:T(8,128)(2,1)S(1)}, u32[]{:S(2)}, u32[]{:S(2)}) collective-permute-start(bf16[13,128,128]{2,1,0:T(8,128)(2,1)S(1)} %get-tuple-element.19), channel_id=1, source_target_pairs={{2,0},{3,1},{0,2},{1,3},{6,4},{7,5},{4,6},{5,7},{10,8},{11,9},{8,1... | collective-permute-start | bytes 1277960 | tf_op jit(solution)/shard_map/ppermute | solution.py:334
  4.4 1.6 %collective-permute-start.3 = (bf16[8,128,128]{2,1,0:T(8,128)(2,1)S(1)}, bf16[8,128,128]{2,1,0:T(8,128)(2,1)S(1)}, u32[]{:S(2)}, u32[]{:S(2)}) collective-permute-start(bf16[8,128,128]{2,1,0:T(8,128)(2,1)S(1)} %get-tuple-element.21), channel_id=1, source_target_pairs={{12,0},{13,1},{6,2},{7,3},{0,4},{1,5},{10,6},{11,7},{4,8},{5,9},{1... | collective-permute-start | bytes 786440 | tf_op jit(solution)/shard_map/ppermute | solution.py:334
  6.0 2.4 %collective-permute-start.2 = (bf16[6,128,128]{2,1,0:T(8,128)(2,1)S(1)}, bf16[6,128,128]{2,1,0:T(8,128)(2,1)S(1)}, u32[]{:S(2)}, u32[]{:S(2)}) collective-permute-start(bf16[6,128,128]{2,1,0:T(8,128)(2,1)S(1)} %get-tuple-element.20), channel_id=1, source_target_pairs={{14,0},{15,1},{4,2},{5,3},{2,4},{3,5},{8,6},{9,7},{6,8},{7,9},{12,... | collective-permute-start | bytes 589832 | tf_op jit(solution)/shard_map/ppermute | solution.py:334
  8.5 0.4 %collective-permute-start.4 = (bf16[5,128,128]{2,1,0:T(8,128)(2,1)S(1)}, bf16[5,128,128]{2,1,0:T(8,128)(2,1)S(1)}, u32[]{:S(2)}, u32[]{:S(2)}) collective-permute-start(bf16[5,128,128]{2,1,0:T(8,128)(2,1)S(1)} %get-tuple-element.22), channel_id=1, source_target_pairs={{4,0},{5,1},{14,2},{15,3},{8,4},{9,5},{2,6},{3,7},{12,8},{13,9},{6... | collective-permute-start | bytes 491528 | tf_op jit(solution)/shard_map/ppermute | solution.py:334
  9.6 0.0 collective-permute-done.left_other_ref
  9.6 1.4 %collective-permute-start.5 = (bf16[1,128,128]{2,1,0:T(8,128)(2,1)S(1)}, bf16[1,128,128]{2,1,0:T(8,128)(2,1)S(1)}, u32[]{:S(2)}, u32[]{:S(2)}) collective-permute-start(bf16[1,128,128]{2,1,0:T(8,128)(2,1)S(1)} %pack_e.1), channel_id=1, source_target_pairs={{10,0},{7,1},{12,2},{9,3},{14,4},{11,5},{0,6},{13,7},{2,8},{15,9},... | collective-permute-start | bytes 98312 | tf_op jit(solution)/shard_map/ppermute | solution.py:334
  11.1 1.7 %inner.1 = (f32[28,128,128]{2,1,0:T(8,128)S(1)}, s32[1,128]{1,0:T(1,128)S(1)}) custom-call(s32[1,23]{1,0:T(1,128)} %rows_ref.3, s32[1,23]{1,0:T(1,128)} %cols_ref.3, s32[1,1]{1,0:T(1,128)S(6)} %copy.5.counts_ref, bf16[384,1152]{1,0:T(8,128)(2,1)S(1)} %get-tuple-element.18.left_ref, bf16[384,1152]{1,0:T(8,128)(2,1)S(1)} %collective-permute-done.left_other_ref), custom_call_target="tpu_custom_call" | custom-call | flops 427819008 | bytes 1507328 | tf_op jit(solution)/shard_map/inner/pallas_call | solution.py:350
  12.8 9.8 %collective-permute-done.4.refs_3_.rest_3_ = bf16[5,128,128]{2,1,0:T(8,128)(2,1)S(1)} collective-permute-done((bf16[5,128,128]{2,1,0:T(8,128)(2,1)S(1)}, bf16[5,128,128]{2,1,0:T(8,128)(2,1)S(1)}, u32[]{:S(2)}, u32[]{:S(2)}) %collective-permute-start.4) | collective-permute-done | bytes 163872 | tf_op jit(solution)/shard_map/ppermute | solution.py:334
  22.6 0.0 collective-permute-done.2.refs_1_.rest_1_
  22.6 0.0 collective-permute-done.3.refs_2_.rest_2_
  22.6 0.0 collective-permute-done.1.refs_0_.rest_0_
  22.6 0.0 collective-permute-done.5.refs_4_.rest_4_
  22.6 0.1 stage.1
  22.7 0.1 collective-permute-start.6
  22.8 1.3 %outer.1.outer_ref = f32[27,128,128]{2,1,0:T(8,128)S(1)} custom-call(bf16[384,1152]{1,0:T(8,128)(2,1)S(1)} %get-tuple-element.18.left_ref, bf16[384,1152]{1,0:T(8,128)(2,1)S(1)} %collective-permute-done.left_other_ref, bf16[13,128,128]{2,1,0:T(8,128)(2,1)S(1)} %collective-permute-done.1.refs_0_.rest_0_, ...), custom_call_target="tpu_custom_call" | custom-call | flops 1409286144 | bytes 3768320 | tf_op jit(solution)/shard_map/outer/pallas_call | solution.py:376
  24.0 0.8 %collective-permute-done.6.staged_ref = bf16[20,128,128]{2,1,0:T(8,128)(2,1)S(1)} collective-permute-done((bf16[20,128,128]{2,1,0:T(8,128)(2,1)S(1)}, bf16[20,128,128]{2,1,0:T(8,128)(2,1)S(1)}, u32[]{:S(2)}, u32[]{:S(2)}) %collective-permute-start.6) | collective-permute-done | bytes 655392 | tf_op jit(solution)/shard_map/ppermute | solution.py:337
  24.8 2.2 %multiply.1 = f32[1,23,128,128]{3,2,1,0:T(8,128)} custom-call(bf16[384,1152]{1,0:T(8,128)(2,1)S(1)} %get-tuple-element.18.left_ref, bf16[384,1152]{1,0:T(8,128)(2,1)S(1)} %collective-permute-done.left_other_ref, bf16[20,128,128]{2,1,0:T(8,128)(2,1)S(1)} %collective-permute-done.6.staged_ref, f32[27,128,128]{2,1,0:T(8,128)S(1)} %outer.1.outer_ref, ...), custom_call_target="tpu_custom_call" | custom-call | tf_op jit(solution)/shard_map/multiply/pallas_call | solution.py:386
  (1 shorter events, 0.0 us)
Async XLA Ops:
  1.4 8.2 %collective-permute-start = (bf16[384,1152]{1,0:T(8,128)(2,1)S(1)}, bf16[384,1152]{1,0:T(8,128)(2,1)S(1)}, u32[]{:S(2)}, u32[]{:S(2)}) collective-permute-start(bf16[384,1152]{1,0:T(8,128)(2,1)S(1)} %get-tuple-element.18.left_ref), channel_id=1, source_target_pairs={{0,1},{1,0},{2,3},{3,2},{4,5},{5,4},{6,7},{7,6},{8,9},{9,8},{10,11... | collective-permute-start | bytes 2654216 | tf_op jit(solution)/shard_map/ppermute | solution.py:337
  1.9 20.7 %collective-permute-start.1 = (bf16[13,128,128]{2,1,0:T(8,128)(2,1)S(1)}, bf16[13,128,128]{2,1,0:T(8,128)(2,1)S(1)}, u32[]{:S(2)}, u32[]{:S(2)}) collective-permute-start(bf16[13,128,128]{2,1,0:T(8,128)(2,1)S(1)} %get-tuple-element.19), channel_id=1, source_target_pairs={{2,0},{3,1},{0,2},{1,3},{6,4},{7,5},{4,6},{5,7},{10,8},{11,9},{8,1... | collective-permute-start | bytes 1277960 | tf_op jit(solution)/shard_map/ppermute | solution.py:334
  4.4 18.1 %collective-permute-start.3 = (bf16[8,128,128]{2,1,0:T(8,128)(2,1)S(1)}, bf16[8,128,128]{2,1,0:T(8,128)(2,1)S(1)}, u32[]{:S(2)}, u32[]{:S(2)}) collective-permute-start(bf16[8,128,128]{2,1,0:T(8,128)(2,1)S(1)} %get-tuple-element.21), channel_id=1, source_target_pairs={{12,0},{13,1},{6,2},{7,3},{0,4},{1,5},{10,6},{11,7},{4,8},{5,9},{1... | collective-permute-start | bytes 786440 | tf_op jit(solution)/shard_map/ppermute | solution.py:334
  6.0 16.5 %collective-permute-start.2 = (bf16[6,128,128]{2,1,0:T(8,128)(2,1)S(1)}, bf16[6,128,128]{2,1,0:T(8,128)(2,1)S(1)}, u32[]{:S(2)}, u32[]{:S(2)}) collective-permute-start(bf16[6,128,128]{2,1,0:T(8,128)(2,1)S(1)} %get-tuple-element.20), channel_id=1, source_target_pairs={{14,0},{15,1},{4,2},{5,3},{2,4},{3,5},{8,6},{9,7},{6,8},{7,9},{12,... | collective-permute-start | bytes 589832 | tf_op jit(solution)/shard_map/ppermute | solution.py:334
  8.5 14.1 %collective-permute-start.4 = (bf16[5,128,128]{2,1,0:T(8,128)(2,1)S(1)}, bf16[5,128,128]{2,1,0:T(8,128)(2,1)S(1)}, u32[]{:S(2)}, u32[]{:S(2)}) collective-permute-start(bf16[5,128,128]{2,1,0:T(8,128)(2,1)S(1)} %get-tuple-element.22), channel_id=1, source_target_pairs={{4,0},{5,1},{14,2},{15,3},{8,4},{9,5},{2,6},{3,7},{12,8},{13,9},{6... | collective-permute-start | bytes 491528 | tf_op jit(solution)/shard_map/ppermute | solution.py:334
  9.6 12.9 %collective-permute-start.5 = (bf16[1,128,128]{2,1,0:T(8,128)(2,1)S(1)}, bf16[1,128,128]{2,1,0:T(8,128)(2,1)S(1)}, u32[]{:S(2)}, u32[]{:S(2)}) collective-permute-start(bf16[1,128,128]{2,1,0:T(8,128)(2,1)S(1)} %pack_e.1), channel_id=1, source_target_pairs={{10,0},{7,1},{12,2},{9,3},{14,4},{11,5},{0,6},{13,7},{2,8},{15,9},... | collective-permute-start | bytes 98312 | tf_op jit(solution)/shard_map/ppermute | solution.py:334
  22.7 2.2 %collective-permute-start.6 = (bf16[20,128,128]{2,1,0:T(8,128)(2,1)S(1)}, bf16[20,128,128]{2,1,0:T(8,128)(2,1)S(1)}, u32[]{:S(2)}, u32[]{:S(2)}) collective-permute-start(bf16[20,128,128]{2,1,0:T(8,128)(2,1)S(1)} %stage.1), channel_id=1, source_target_pairs={{0,1},{1,0},{2,3},{3,2},{4,5},{5,4},{6,7},{7,6},{8,9},{9,8},{10,11... | collective-permute-start | bytes 1966088 | tf_op jit(solution)/shard_map/ppermute | solution.py:337

commit v11 on v10

--- a/solution.py
+++ b/solution.py
@@ -33,12 +33,14 @@
 STAGED = {
     parity: [
         (name, n, (k, j))
-        for name in DISTANCES
+        for name in "acbde"
         for n, (k, j) in enumerate(SENT[name, parity])
         if k % 2 != j % 2 or (k, j) == (-7, -7)
     ]
     for parity in (0, 1)
 }
+EARLY = {parity: [found for found in STAGED[parity] if found[0] in "ac"] for parity in (0, 1)}
+EARLY_SIZE = max(len(found) for found in EARLY.values())
 STAGED_SIZE = max(len(found) for found in STAGED.values())
 
 
@@ -119,7 +121,7 @@
                 return name, SENT[name, parity].index((a, b)), flip
         staged = [position for _, _, position in STAGED[1 - parity]]
         if (a, b) in staged:
-            return "staged", staged.index((a, b)), flip
+            return "staged", staged.index((a, b)), not flip
     raise AssertionError((k, j))
 
 
@@ -169,13 +171,26 @@
     return [i * NCOL + n for i in range(BR) for n, j in enumerate(columns) if abs(i - j) <= HB]
 
 
+def inner_places(parity):
+    return [i * NCOL + n for i in range(BR) for n, j in enumerate(columns_of(parity)) if 0 <= j < BR]
+
+
+def store(made, table, out_ref, place, sem):
+    source = made.at[table[0, SOURCES + place]]
+    pltpu.make_async_copy(source, out_ref.at[0, table[0, place]], sem).start()
+
+
+def wait_for(count, made, out_ref, sem):
+    pltpu.make_async_copy(made.at[pl.ds(0, count)], out_ref.at[0, pl.ds(0, count)], sem).wait()
+
+
 def outer_pairs(parity):
     outer = [j for j in columns_of(parity) if not 0 <= j < BR]
     return [outer[n : n + 2] for n in range(0, len(outer), 2)]
 
 
 def inner_kernel(nblocks, slots, rows_ref, cols_ref, counts_ref, left_ref, left_other_ref, *rest):
-    made_ref, table_ref, right, table, *index, sems, table_sem = rest
+    table_ref, out_ref, right, made, table, *index, sems, table_sem, out_sem = rest
     copies = index_copies((rows_ref, cols_ref), index, sems)
     for copy in copies:
         copy.start()
@@ -188,8 +203,8 @@
         for i in range(BR):
             for y in range(2):
                 if y < len(js):
-                    made_ref[i * NCOL + columns_of(mine).index(js[y])] = block_of(total, i, y)
-        made_ref[BR * NCOL] = jnp.zeros((BLK, BLK), made_ref.dtype)
+                    made[i * NCOL + columns_of(mine).index(js[y])] = block_of(total, i, y)
+        made[BR * NCOL] = jnp.zeros((BLK, BLK), made.dtype)
 
     for copy in copies:
         copy.wait()
@@ -210,6 +225,14 @@
             table[0, SOURCES + place] = jnp.where(absent, BR * NCOL, place)
             unused = jnp.where(absent, unused + 1, unused)
         table[0, BR * NCOL] = unused
+        here = [place for place in stored_places(mine) if place in inner_places(mine)]
+        for place in here:
+            store(made, table, out_ref, place, out_sem)
+        stored = len(here)
+        if len(stored_places(mine)) < slots:
+            pltpu.make_async_copy(made.at[BR * NCOL], out_ref.at[0, unused], out_sem).start()
+            stored += 1
+        wait_for(stored, made, out_ref, out_sem)
 
     copy = pltpu.make_async_copy(table, table_ref, table_sem)
     copy.start()
@@ -224,16 +247,32 @@
         e_ref[0] = (left_ref if mine == 0 else left_other_ref)[pl.ds(i * BLK, BLK), pl.ds(n * BLK, BLK)]
 
 
-def stage_kernel(*refs):
-    got = dict(zip(DISTANCES, refs))
-    out_ref = refs[-1]
-
-    @for_own_parity
-    def _(mine):
-        for n, (name, place, _) in enumerate(STAGED[mine]):
-            out_ref[n] = got[name][place]
-        for n in range(len(STAGED[mine]), STAGED_SIZE):
-            out_ref[n] = jnp.zeros((BLK, BLK), out_ref.dtype)
+def stage_early_kernel(a_ref, c_ref, out_ref):
+    got = {"a": a_ref, "c": c_ref}
+
+    @for_own_parity
+    def _(mine):
+        for n in range(EARLY_SIZE):
+            if n < len(EARLY[mine]):
+                name, place, _ = EARLY[mine][n]
+                out_ref[n] = got[name][place].T
+            else:
+                out_ref[n] = jnp.zeros((BLK, BLK), out_ref.dtype)
+
+
+def stage_kernel(early_ref, b_ref, d_ref, e_ref, out_ref):
+    got = {"b": b_ref, "d": d_ref, "e": e_ref}
+
+    @for_own_parity
+    def _(mine):
+        for n in range(STAGED_SIZE):
+            if n < len(EARLY[mine]):
+                out_ref[n] = early_ref[n]
+            elif n < len(STAGED[mine]):
+                name, place, _ = STAGED[mine][n]
+                out_ref[n] = got[name][place].T
+            else:
+                out_ref[n] = jnp.zeros((BLK, BLK), out_ref.dtype)
 
 
 def outer_kernel(left_ref, left_other_ref, *rest):
@@ -250,37 +289,27 @@
                         out_ref[i * NCOL + columns_of(mine).index(j)] = block_of(total, i, y)
 
 
-def multiply_kernel(slots, left_ref, left_other_ref, staged_ref, outer_ref, inner_ref, table_ref, out_ref, *rest):
+def multiply_kernel(left_ref, left_other_ref, staged_ref, outer_ref, table_ref, _, out_ref, *rest):
     right, made, table, table_sem, out_sem = rest
     refs = {("left", True): left_ref, ("left", False): left_other_ref, "staged": staged_ref}
     load = pltpu.make_async_copy(table_ref, table, table_sem)
     load.start()
     made[BR * NCOL] = jnp.zeros((BLK, BLK), made.dtype)
 
-    def store(source_ref, place):
-        source = source_ref.at[table[0, SOURCES + place]]
-        pltpu.make_async_copy(source, out_ref.at[0, table[0, place]], out_sem).start()
-
-    @for_own_parity
-    def _(mine):
-        columns = columns_of(mine)
-        pairs = outer_pairs(mine)
-        inner = [n for n, j in enumerate(columns) if 0 <= j < BR]
+    @for_own_parity
+    def _(mine):
+        for pair, js in enumerate(outer_pairs(mine)):
+            total = columns_product(refs, right.at[pair], mine, js, lambda source: source == "staged")
+            for i in range(BR):
+                for y, j in enumerate(js):
+                    if abs(i - j) <= HB:
+                        place = i * NCOL + columns_of(mine).index(j)
+                        made[place] = outer_ref[place] + block_of(total, i, y)
         load.wait()
-        for i in range(BR):
-            for n in inner:
-                store(inner_ref, i * NCOL + n)
-        for pair, js in enumerate(pairs):
-            total = columns_product(refs, right.at[pair], mine, js, lambda source: source == "staged")
-            places = [(i, y, i * NCOL + columns.index(j)) for i in range(BR) for y, j in enumerate(js) if abs(i - j) <= HB]
-            for i, y, place in places:
-                made[place] = outer_ref[place] + block_of(total, i, y)
-            for _, _, place in places:
-                store(made, place)
-        if len(stored_places(mine)) < slots:
-            pltpu.make_async_copy(made.at[BR * NCOL], out_ref.at[0, table[0, BR * NCOL]], out_sem).start()
-
-    pltpu.make_async_copy(made.at[pl.ds(0, slots)], out_ref.at[0], out_sem).wait()
+        here = [place for place in stored_places(mine) if place not in inner_places(mine)]
+        for place in here:
+            store(made, table, out_ref, place, out_sem)
+        wait_for(len(here), made, out_ref, out_sem)
 
 
 def local(values, block_rows, block_cols, counts):
@@ -347,31 +376,44 @@
         name="pack_e",
     )(left, left_other)
     got.append(towards("e", message))
-    inner, table = pl.pallas_call(
+    table, out = pl.pallas_call(
         functools.partial(inner_kernel, nblocks, slots),
-        out_shape=[blocks(BR * NCOL + 1, jnp.float32), jax.ShapeDtypeStruct(table_shape, jnp.int32)],
+        out_shape=[jax.ShapeDtypeStruct(table_shape, jnp.int32), jax.ShapeDtypeStruct(values.shape, jnp.float32)],
         in_specs=[hbm] * 2 + [smem] + [vmem] * 2,
-        out_specs=[vmem] * 2,
+        out_specs=[vmem, hbm],
         scratch_shapes=[
             pltpu.VMEM((2, NCOL * BLK, 2 * BLK), values.dtype),
+            pltpu.VMEM((BR * NCOL + 1, BLK, BLK), jnp.float32),
             pltpu.SMEM(table_shape, jnp.int32),
             *index_scratch,
             pltpu.SemaphoreType.DMA,
+            pltpu.SemaphoreType.DMA,
         ],
         compiler_params=params,
         cost_estimate=cost(3 * 2 * 17, 4 * values.size),
         name="inner",
     )(*places, counts, left, left_other)
-    *got, inner = lax.optimization_barrier((*got, inner))
+    a, b, c, d, e = got
+    a, c, table = lax.optimization_barrier((a, c, table))
+    early = pl.pallas_call(
+        stage_early_kernel,
+        out_shape=blocks(EARLY_SIZE),
+        in_specs=[vmem] * 2,
+        out_specs=vmem,
+        compiler_params=params,
+        name="stage_early",
+    )(a, c)
+    b, d, e, early = lax.optimization_barrier((b, d, e, early))
+    got = [a, b, c, d, e]
     staged = swapped(
         pl.pallas_call(
             stage_kernel,
             out_shape=blocks(STAGED_SIZE),
-            in_specs=[vmem] * 5,
+            in_specs=[vmem] * 4,
             out_specs=vmem,
             compiler_params=params,
             name="stage",
-        )(*got)
+        )(early, b, d, e)
     )
     outer = pl.pallas_call(
         outer_kernel,
@@ -384,9 +426,9 @@
         name="outer",
     )(left, left_other, *got)
     return pl.pallas_call(
-        functools.partial(multiply_kernel, slots),
+        multiply_kernel,
         out_shape=jax.ShapeDtypeStruct(values.shape, jnp.float32),
-        in_specs=[vmem] * 6,
+        in_specs=[vmem] * 5 + [hbm],
         out_specs=hbm,
         scratch_shapes=[
             right_scratch(4),
@@ -395,9 +437,10 @@
             pltpu.SemaphoreType.DMA,
             pltpu.SemaphoreType.DMA,
         ],
+        input_output_aliases={5: 0},
         compiler_params=params,
         name="multiply",
-    )(left, left_other, staged, outer, inner, table)
+    )(left, left_other, staged, outer, table, out)
 
 
 def solution(mesh):

time: 27.2 us -> 26.8 us (0.985)
  waiting for transfers between devices: 10.6 us -> 9.77 us
  Pallas kernels: 6.67 us -> 7.11 us
    ppermute x5, waiting for transfers between devices: 9.81 us -> 8.95 us  [towards(): return lax.ppermute(message, ('row', 'col'), pairs)]
    pallas_call x1, Pallas kernels: 1.69 us -> 2.39 us  [local(): pl.pallas_call(functools.partial(inner_kernel, nblocks, slots), out_shape...]
    pallas_call x1 -> x2, Pallas kernels: 2.24 us -> 1.95 us  [the longest x1 1.79 us: local(): pl.pallas_call(multiply_kernel, out_shape=jax.ShapeDtypeStruct(values.sha...]
  transfers between devices with their start and end apart: 7 -> 7, of which waited for: 2 -> 4; matrix products, arithmetic and copies ran while one was open for 0% -> 0% of each run, Pallas kernels for 11% -> 14%
where the time goes in v11:
time: 26.8 us; the launch traced here: 26.7 us
  waiting for transfers between devices  9.77 us (36%)
  starting transfers between devices  9.05 us (34%)
  Pallas kernels  7.11 us (27%)
  between operations  0.72 us (3%)
    ppermute x5, waiting for transfers between devices, towards(): return lax.ppermute(message, ('row', 'col'), pairs)  8.95 us
    ppermute x5, starting transfers between devices, towards(): return lax.ppermute(message, ('row', 'col'), pairs)  8.47 us
    pallas_call x1, Pallas kernels, local(): pl.pallas_call(functools.partial(inner_kernel, nblocks, slots), out_shape...  2.39 us
    pallas_call x1, Pallas kernels, local(): pl.pallas_call(multiply_kernel, out_shape=jax.ShapeDtypeStruct(values.sha...  1.79 us
    pallas_call x1, Pallas kernels, local(): pl.pallas_call(functools.partial(pack_kernel, nblocks, slots), out_shape=...  1.36 us
    pallas_call x1, Pallas kernels, local(): pl.pallas_call(outer_kernel, out_shape=blocks(BR * NCOL, jnp.float32), in...  1.26 us
    ppermute x2, waiting for transfers between devices, swapped(): return lax.ppermute(block, 'col', [(0, 1), (1, 0)])  0.82 us
    ppermute x2, starting transfers between devices, swapped(): return lax.ppermute(block, 'col', [(0, 1), (1, 0)])  0.59 us
  transfers between devices with their start and end apart: 7, of which 4 were waited for; matrix products, arithmetic and copies ran while one was open for 0% of the time, Pallas kernels for 14%

profile of v11, /device:TPU:0, one launch (start us, length us, event | category | flops | bytes accessed | tf_op | source)
XLA Modules:
  0.0 26.7 jit_solution(3636286768929520258)
XLA Ops:
  0.0 1.4 %pack.1 = (bf16[13,128,128]{2,1,0:T(8,128)(2,1)S(1)}, bf16[6,128,128]{2,1,0:T(8,128)(2,1)S(1)}, bf16[8,128,128]{2,1,0:T(8,128)(2,1)S(1)}, bf16[5,128,128]{2,1,0:T(8,128)(2,1)S(1)}, bf16[384,1152]{1,0:T(8,128)(2,1)S(1)}) custom-call(s32[1,23]{1,0:T(1,128)} %rows_ref.3, s32[1,23]{1,0:T(1,128)} %cols_ref.3, bf16[1,23,128,128]{3,2,1,0:T(8,128)(2,1)} %values_ref.1), custom_call_target="tpu_custom_call" | custom-call | tf_op jit(solution)/shard_map/pack/pallas_call | solution.py:340
  1.4 0.5 %collective-permute-start = (bf16[384,1152]{1,0:T(8,128)(2,1)S(1)}, bf16[384,1152]{1,0:T(8,128)(2,1)S(1)}, u32[]{:S(2)}, u32[]{:S(2)}) collective-permute-start(bf16[384,1152]{1,0:T(8,128)(2,1)S(1)} %get-tuple-element.19.left_ref), channel_id=1, source_target_pairs={{0,1},{1,0},{2,3},{3,2},{4,5},{5,4},{6,7},{7,6},{8,9},{9,8},{10,11... | collective-permute-start | bytes 2654216 | tf_op jit(solution)/shard_map/ppermute | solution.py:366
  1.9 2.6 %collective-permute-start.4 = (bf16[13,128,128]{2,1,0:T(8,128)(2,1)S(1)}, bf16[13,128,128]{2,1,0:T(8,128)(2,1)S(1)}, u32[]{:S(2)}, u32[]{:S(2)}) collective-permute-start(bf16[13,128,128]{2,1,0:T(8,128)(2,1)S(1)} %get-tuple-element.22), channel_id=1, source_target_pairs={{2,0},{3,1},{0,2},{1,3},{6,4},{7,5},{4,6},{5,7},{10,8},{11,9},{8,1... | collective-permute-start | bytes 1277960 | tf_op jit(solution)/shard_map/ppermute | solution.py:363
  4.4 1.6 %collective-permute-start.5 = (bf16[8,128,128]{2,1,0:T(8,128)(2,1)S(1)}, bf16[8,128,128]{2,1,0:T(8,128)(2,1)S(1)}, u32[]{:S(2)}, u32[]{:S(2)}) collective-permute-start(bf16[8,128,128]{2,1,0:T(8,128)(2,1)S(1)} %get-tuple-element.23), channel_id=1, source_target_pairs={{12,0},{13,1},{6,2},{7,3},{0,4},{1,5},{10,6},{11,7},{4,8},{5,9},{1... | collective-permute-start | bytes 786440 | tf_op jit(solution)/shard_map/ppermute | solution.py:363
  6.0 2.4 %collective-permute-start.1 = (bf16[6,128,128]{2,1,0:T(8,128)(2,1)S(1)}, bf16[6,128,128]{2,1,0:T(8,128)(2,1)S(1)}, u32[]{:S(2)}, u32[]{:S(2)}) collective-permute-start(bf16[6,128,128]{2,1,0:T(8,128)(2,1)S(1)} %get-tuple-element.20), channel_id=1, source_target_pairs={{14,0},{15,1},{4,2},{5,3},{2,4},{3,5},{8,6},{9,7},{6,8},{7,9},{12,... | collective-permute-start | bytes 589832 | tf_op jit(solution)/shard_map/ppermute | solution.py:363
  8.5 0.4 %collective-permute-start.2 = (bf16[5,128,128]{2,1,0:T(8,128)(2,1)S(1)}, bf16[5,128,128]{2,1,0:T(8,128)(2,1)S(1)}, u32[]{:S(2)}, u32[]{:S(2)}) collective-permute-start(bf16[5,128,128]{2,1,0:T(8,128)(2,1)S(1)} %get-tuple-element.21), channel_id=1, source_target_pairs={{4,0},{5,1},{14,2},{15,3},{8,4},{9,5},{2,6},{3,7},{12,8},{13,9},{6... | collective-permute-start | bytes 491528 | tf_op jit(solution)/shard_map/ppermute | solution.py:363
  9.6 0.0 collective-permute-done.left_other_ref
  9.6 1.4 %collective-permute-start.3 = (bf16[1,128,128]{2,1,0:T(8,128)(2,1)S(1)}, bf16[1,128,128]{2,1,0:T(8,128)(2,1)S(1)}, u32[]{:S(2)}, u32[]{:S(2)}) collective-permute-start(bf16[1,128,128]{2,1,0:T(8,128)(2,1)S(1)} %pack_e.1), channel_id=1, source_target_pairs={{10,0},{7,1},{12,2},{9,3},{14,4},{11,5},{0,6},{13,7},{2,8},{15,9},... | collective-permute-start | bytes 98312 | tf_op jit(solution)/shard_map/ppermute | solution.py:363
  11.1 2.4 %inner.1 = (s32[1,128]{1,0:T(1,128)S(1)}, f32[1,23,128,128]{3,2,1,0:T(8,128)}) custom-call(s32[1,23]{1,0:T(1,128)} %rows_ref.3, s32[1,23]{1,0:T(1,128)} %cols_ref.3, s32[1,1]{1,0:T(1,128)S(6)} %copy.7.counts_ref, bf16[384,1152]{1,0:T(8,128)(2,1)S(1)} %get-tuple-element.19.left_ref, bf16[384,1152]{1,0:T(8,128)(2,1)S(1)} %collective-permute-done.left_other_ref), custom_call_target="tpu_custom_call" | custom-call | flops 427819008 | bytes 1507328 | tf_op jit(solution)/shard_map/inner/pallas_call | solution.py:379
  13.4 2.0 %collective-permute-done.5.c_ref.rest_2_ = bf16[8,128,128]{2,1,0:T(8,128)(2,1)S(1)} collective-permute-done((bf16[8,128,128]{2,1,0:T(8,128)(2,1)S(1)}, bf16[8,128,128]{2,1,0:T(8,128)(2,1)S(1)}, u32[]{:S(2)}, u32[]{:S(2)}) %collective-permute-start.5) | collective-permute-done | bytes 262176 | tf_op jit(solution)/shard_map/ppermute | solution.py:363
  15.5 4.2 %collective-permute-done.4.a_ref.rest_0_ = bf16[13,128,128]{2,1,0:T(8,128)(2,1)S(1)} collective-permute-done((bf16[13,128,128]{2,1,0:T(8,128)(2,1)S(1)}, bf16[13,128,128]{2,1,0:T(8,128)(2,1)S(1)}, u32[]{:S(2)}, u32[]{:S(2)}) %collective-permute-start.4) | collective-permute-done | bytes 426016 | tf_op jit(solution)/shard_map/ppermute | solution.py:363
  19.7 0.2 stage_early.1.early_ref
  19.8 2.7 %collective-permute-done.2.d_ref.rest_3_ = bf16[5,128,128]{2,1,0:T(8,128)(2,1)S(1)} collective-permute-done((bf16[5,128,128]{2,1,0:T(8,128)(2,1)S(1)}, bf16[5,128,128]{2,1,0:T(8,128)(2,1)S(1)}, u32[]{:S(2)}, u32[]{:S(2)}) %collective-permute-start.2) | collective-permute-done | bytes 163872 | tf_op jit(solution)/shard_map/ppermute | solution.py:363
  22.6 0.0 collective-permute-done.1.b_ref.rest_1_
  22.6 0.0 collective-permute-done.3.e_ref.rest_4_
  22.6 0.1 stage.1
  22.7 0.1 collective-permute-start.6
  22.8 1.3 %outer.1.outer_ref = f32[27,128,128]{2,1,0:T(8,128)S(1)} custom-call(bf16[384,1152]{1,0:T(8,128)(2,1)S(1)} %get-tuple-element.19.left_ref, bf16[384,1152]{1,0:T(8,128)(2,1)S(1)} %collective-permute-done.left_other_ref, bf16[13,128,128]{2,1,0:T(8,128)(2,1)S(1)} %collective-permute-done.4.a_ref.rest_0_, ...), custom_call_target="tpu_custom_call" | custom-call | flops 1409286144 | bytes 3768320 | tf_op jit(solution)/shard_map/outer/pallas_call | solution.py:418
  24.0 0.8 %collective-permute-done.6.staged_ref = bf16[20,128,128]{2,1,0:T(8,128)(2,1)S(1)} collective-permute-done((bf16[20,128,128]{2,1,0:T(8,128)(2,1)S(1)}, bf16[20,128,128]{2,1,0:T(8,128)(2,1)S(1)}, u32[]{:S(2)}, u32[]{:S(2)}) %collective-permute-start.6) | collective-permute-done | bytes 655392 | tf_op jit(solution)/shard_map/ppermute | solution.py:366
  24.9 1.8 %multiply.1 = f32[1,23,128,128]{3,2,1,0:T(8,128)} custom-call(bf16[384,1152]{1,0:T(8,128)(2,1)S(1)} %get-tuple-element.19.left_ref, bf16[384,1152]{1,0:T(8,128)(2,1)S(1)} %collective-permute-done.left_other_ref, bf16[20,128,128]{2,1,0:T(8,128)(2,1)S(1)} %collective-permute-done.6.staged_ref, ...), custom_call_target="tpu_custom_call", output_to_operand_aliasing={{}: (5, {})} | custom-call | tf_op jit(solution)/shard_map/multiply/pallas_call | solution.py:428
  (1 shorter events, 0.0 us)
Async XLA Ops:
  1.4 8.2 %collective-permute-start = (bf16[384,1152]{1,0:T(8,128)(2,1)S(1)}, bf16[384,1152]{1,0:T(8,128)(2,1)S(1)}, u32[]{:S(2)}, u32[]{:S(2)}) collective-permute-start(bf16[384,1152]{1,0:T(8,128)(2,1)S(1)} %get-tuple-element.19.left_ref), channel_id=1, source_target_pairs={{0,1},{1,0},{2,3},{3,2},{4,5},{5,4},{6,7},{7,6},{8,9},{9,8},{10,11... | collective-permute-start | bytes 2654216 | tf_op jit(solution)/shard_map/ppermute | solution.py:366
  1.9 17.8 %collective-permute-start.4 = (bf16[13,128,128]{2,1,0:T(8,128)(2,1)S(1)}, bf16[13,128,128]{2,1,0:T(8,128)(2,1)S(1)}, u32[]{:S(2)}, u32[]{:S(2)}) collective-permute-start(bf16[13,128,128]{2,1,0:T(8,128)(2,1)S(1)} %get-tuple-element.22), channel_id=1, source_target_pairs={{2,0},{3,1},{0,2},{1,3},{6,4},{7,5},{4,6},{5,7},{10,8},{11,9},{8,1... | collective-permute-start | bytes 1277960 | tf_op jit(solution)/shard_map/ppermute | solution.py:363
  4.4 11.0 %collective-permute-start.5 = (bf16[8,128,128]{2,1,0:T(8,128)(2,1)S(1)}, bf16[8,128,128]{2,1,0:T(8,128)(2,1)S(1)}, u32[]{:S(2)}, u32[]{:S(2)}) collective-permute-start(bf16[8,128,128]{2,1,0:T(8,128)(2,1)S(1)} %get-tuple-element.23), channel_id=1, source_target_pairs={{12,0},{13,1},{6,2},{7,3},{0,4},{1,5},{10,6},{11,7},{4,8},{5,9},{1... | collective-permute-start | bytes 786440 | tf_op jit(solution)/shard_map/ppermute | solution.py:363
  6.0 16.5 %collective-permute-start.1 = (bf16[6,128,128]{2,1,0:T(8,128)(2,1)S(1)}, bf16[6,128,128]{2,1,0:T(8,128)(2,1)S(1)}, u32[]{:S(2)}, u32[]{:S(2)}) collective-permute-start(bf16[6,128,128]{2,1,0:T(8,128)(2,1)S(1)} %get-tuple-element.20), channel_id=1, source_target_pairs={{14,0},{15,1},{4,2},{5,3},{2,4},{3,5},{8,6},{9,7},{6,8},{7,9},{12,... | collective-permute-start | bytes 589832 | tf_op jit(solution)/shard_map/ppermute | solution.py:363
  8.5 14.1 %collective-permute-start.2 = (bf16[5,128,128]{2,1,0:T(8,128)(2,1)S(1)}, bf16[5,128,128]{2,1,0:T(8,128)(2,1)S(1)}, u32[]{:S(2)}, u32[]{:S(2)}) collective-permute-start(bf16[5,128,128]{2,1,0:T(8,128)(2,1)S(1)} %get-tuple-element.21), channel_id=1, source_target_pairs={{4,0},{5,1},{14,2},{15,3},{8,4},{9,5},{2,6},{3,7},{12,8},{13,9},{6... | collective-permute-start | bytes 491528 | tf_op jit(solution)/shard_map/ppermute | solution.py:363
  9.6 12.9 %collective-permute-start.3 = (bf16[1,128,128]{2,1,0:T(8,128)(2,1)S(1)}, bf16[1,128,128]{2,1,0:T(8,128)(2,1)S(1)}, u32[]{:S(2)}, u32[]{:S(2)}) collective-permute-start(bf16[1,128,128]{2,1,0:T(8,128)(2,1)S(1)} %pack_e.1), channel_id=1, source_target_pairs={{10,0},{7,1},{12,2},{9,3},{14,4},{11,5},{0,6},{13,7},{2,8},{15,9},... | collective-permute-start | bytes 98312 | tf_op jit(solution)/shard_map/ppermute | solution.py:363
  22.7 2.2 %collective-permute-start.6 = (bf16[20,128,128]{2,1,0:T(8,128)(2,1)S(1)}, bf16[20,128,128]{2,1,0:T(8,128)(2,1)S(1)}, u32[]{:S(2)}, u32[]{:S(2)}) collective-permute-start(bf16[20,128,128]{2,1,0:T(8,128)(2,1)S(1)} %stage.1), channel_id=1, source_target_pairs={{0,1},{1,0},{2,3},{3,2},{4,5},{5,4},{6,7},{7,6},{8,9},{9,8},{10,11... | collective-permute-start | bytes 1966088 | tf_op jit(solution)/shard_map/ppermute | solution.py:366

commit v12 on v11

--- a/solution.py
+++ b/solution.py
@@ -14,22 +14,25 @@
 LOW, HIGH = -HB, BR - 1 + HB
 NCOL = 9
 SOURCES = 32
+EARLY_COST = 500
 VMEM_LIMIT = 12 * 2**20
 
 DISTANCES = {"a": 1, "b": -1, "c": -2, "d": 2, "e": None}
 SENT = {
-    ("a", 1): [(3, 3), (5, 5), (3, 5), (3, 7), (4, 7), (5, 7), (3, 9), (4, 9), (5, 9), (3, -3), (3, -1), (4, -3), (5, -1)],
-    ("a", 0): [(4, 4), (3, 4), (5, 4), (3, 6), (4, 6), (5, 6), (3, 8), (4, 8), (5, 8), (3, -2), (4, -2), (5, -2), (3, -4)],
-    ("b", 1): [(-1, -1), (-3, -3), (-1, -3), (-1, -7), (-2, -7), (-3, -7)],
-    ("b", 0): [(-2, -2), (-1, -2), (-3, -2), (-1, 4), (-1, -4), (-1, -6)],
-    ("c", 1): [(-5, -5), (-4, -7), (-5, -7), (-6, -7), (-4, -3), (-5, -1), (-5, -3), (-6, -3)],
-    ("c", 0): [(-4, -4), (-6, -6), (-4, -6), (-4, -2), (-5, -2), (-6, -2), (-5, -4), (-5, -6)],
-    ("d", 1): [(6, 9), (7, 7), (7, 9), (8, 9), (6, -1)],
-    ("d", 0): [(6, 6), (6, 8), (8, 8), (7, 6), (7, 8)],
+    ("a", 1): [(3, 3), (5, 5), (3, 5), (3, 7), (3, 9), (4, 9), (5, 9), (3, -3), (3, -1), (4, -3), (4, -1), (5, -1)],
+    ("a", 0): [(4, 4), (3, 4), (5, 4), (3, 6), (4, 6), (5, 6), (3, 8), (4, 8), (5, 8), (3, -2), (5, -2), (3, -4)],
+    ("b", 1): [(-1, -1), (-3, -3), (-1, -3), (-1, -7), (-2, -7), (-3, -7), (-1, -5), (-2, -5)],
+    ("b", 0): [(-2, -2), (-1, -2), (-3, -2), (-2, 4), (-1, -4), (-3, -4), (-1, -6), (-3, -6)],
+    ("c", 1): [(-5, -5), (-4, -7), (-5, -7), (-6, -7), (-5, -3), (-4, -5)],
+    ("c", 0): [(-4, -4), (-6, -6), (-4, -6), (-4, -2), (-6, -2), (-5, -6)],
+    ("d", 1): [(7, 7), (6, 9), (7, 9), (8, 9), (6, -1), (7, 5)],
+    ("d", 0): [(6, 6), (8, 8), (6, 8), (7, 6), (7, 8), (7, 4)],
     ("e", 1): [(9, 9)],
     ("e", 0): [(-7, -7)],
 }
+PERMUTES = ("a", "f", "g", "b", "e")
 SIZES = {name: len(SENT[name, 1]) for name in DISTANCES}
+SIZES["f"] = SIZES["g"] = SIZES["c"]
 STAGED = {
     parity: [
         (name, n, (k, j))
@@ -39,7 +42,7 @@
     ]
     for parity in (0, 1)
 }
-EARLY = {parity: [found for found in STAGED[parity] if found[0] in "ac"] for parity in (0, 1)}
+EARLY = {parity: [found for found in STAGED[parity] if found[0] == "a"] for parity in (0, 1)}
 EARLY_SIZE = max(len(found) for found in EARLY.values())
 STAGED_SIZE = max(len(found) for found in STAGED.values())
 
@@ -50,6 +53,10 @@
 
 def own_parity():
     return (lax.axis_index("row") + lax.axis_index("col")) % 2
+
+
+def c_is_in_f():
+    return lax.axis_index("col") == 0
 
 
 def for_own_parity(body):
@@ -72,8 +79,14 @@
     return [pltpu.make_async_copy(a, b, sems.at[i]) for i, (a, b) in enumerate(zip(hbm_refs, smem_refs))]
 
 
+def place_at_sender(name, k, j):
+    distance = DISTANCES[name]
+    place = (k - BR * distance) * WIDTH + j - k + HB
+    return BR * WIDTH - 1 - place if distance % 2 == 1 else place
+
+
 def pack_kernel(nblocks, slots, rows_ref, cols_ref, values_ref, *rest):
-    out_refs = dict(zip("abcd", rest[:4]))
+    out_refs = dict(zip(PERMUTES, rest[:4]))
     left_ref, held, table, *index, sems, value_sem = rest[4:]
     copies = index_copies((rows_ref, cols_ref), index, sems)
     load = pltpu.make_async_copy(values_ref.at[0], held.at[pl.ds(0, slots)], value_sem)
@@ -91,13 +104,13 @@
 
     @for_own_parity
     def _(mine):
-        for name, ref in out_refs.items():
-            distance = DISTANCES[name]
-            for n, (k, j) in enumerate(SENT[name, (mine + distance) % 2]):
-                at = (k - BR * distance) * WIDTH + j - k + HB
-                if distance % 2 == 1:
-                    at = BR * WIDTH - 1 - at
-                ref[n] = held[table[at]]
+        for name in "ab":
+            for n, (k, j) in enumerate(SENT[name, 1 - mine]):
+                out_refs[name][n] = held[table[place_at_sender(name, k, j)]]
+        for n in range(SIZES["f"]):
+            c, d = (place_at_sender(name, *SENT[name, mine][n]) for name in "cd")
+            out_refs["f"][n] = held[table[jnp.where(c_is_in_f(), c, d)]]
+            out_refs["g"][n] = held[table[jnp.where(c_is_in_f(), d, c)]]
         columns = columns_of(mine)
         for i in range(BR):
             for n in range(NCOL):
@@ -123,6 +136,15 @@
         if (a, b) in staged:
             return "staged", staged.index((a, b)), not flip
     raise AssertionError((k, j))
+
+
+def read_block(refs, source, place):
+    if isinstance(place, tuple):
+        return refs[source][pl.ds(place[0] * BLK, BLK), pl.ds(place[1] * BLK, BLK)]
+    if source in ("c", "d"):
+        f, g = refs["f"][place], refs["g"][place]
+        return jnp.where(c_is_in_f(), *((f, g) if source == "c" else (g, f)))
+    return refs[source][place]
 
 
 def columns_product(refs, right, parity, js, wanted):
@@ -144,10 +166,7 @@
             for y, j in enumerate(js):
                 if (k, j) in found:
                     source, place, flip = found[k, j]
-                    if isinstance(place, tuple):
-                        block = refs[source][pl.ds(place[0] * BLK, BLK), pl.ds(place[1] * BLK, BLK)]
-                    else:
-                        block = refs[source][place]
+                    block = read_block(refs, source, place)
                     block = block.T if flip else block
                 else:
                     block = jnp.zeros((BLK, BLK), right.dtype)
@@ -247,21 +266,19 @@
         e_ref[0] = (left_ref if mine == 0 else left_other_ref)[pl.ds(i * BLK, BLK), pl.ds(n * BLK, BLK)]
 
 
-def stage_early_kernel(a_ref, c_ref, out_ref):
-    got = {"a": a_ref, "c": c_ref}
-
+def stage_early_kernel(a_ref, out_ref):
     @for_own_parity
     def _(mine):
         for n in range(EARLY_SIZE):
             if n < len(EARLY[mine]):
-                name, place, _ = EARLY[mine][n]
-                out_ref[n] = got[name][place].T
+                out_ref[n] = a_ref[EARLY[mine][n][1]].T
             else:
                 out_ref[n] = jnp.zeros((BLK, BLK), out_ref.dtype)
 
 
-def stage_kernel(early_ref, b_ref, d_ref, e_ref, out_ref):
-    got = {"b": b_ref, "d": d_ref, "e": e_ref}
+def stage_kernel(early_ref, *refs):
+    got = dict(zip(PERMUTES[1:], refs))
+    out_ref = refs[-1]
 
     @for_own_parity
     def _(mine):
@@ -270,14 +287,14 @@
                 out_ref[n] = early_ref[n]
             elif n < len(STAGED[mine]):
                 name, place, _ = STAGED[mine][n]
-                out_ref[n] = got[name][place].T
+                out_ref[n] = read_block(got, name, place).T
             else:
                 out_ref[n] = jnp.zeros((BLK, BLK), out_ref.dtype)
 
 
 def outer_kernel(left_ref, left_other_ref, *rest):
-    refs = {("left", True): left_ref, ("left", False): left_other_ref, **dict(zip(DISTANCES, rest))}
-    out_ref, right = rest[len(DISTANCES) :]
+    refs = {("left", True): left_ref, ("left", False): left_other_ref, **dict(zip(PERMUTES, rest))}
+    out_ref, right = rest[len(PERMUTES) :]
 
     @for_own_parity
     def _(mine):
@@ -339,7 +356,7 @@
 
     *packed, left = pl.pallas_call(
         functools.partial(pack_kernel, nblocks, slots),
-        out_shape=[blocks(SIZES[name]) for name in "abcd"]
+        out_shape=[blocks(SIZES[name]) for name in PERMUTES[:4]]
         + [jax.ShapeDtypeStruct((BR * BLK, NCOL * BLK), values.dtype)],
         in_specs=[hbm] * 3,
         out_specs=[vmem] * 5,
@@ -357,7 +374,10 @@
         pairs = []
         for r in range(row_count):
             for c in range(col_count):
-                distance = DISTANCES[name] or (3 if (r + c) % 2 == 1 else -3)
+                if name in ("f", "g"):
+                    distance = DISTANCES["c" if (name == "f") == (c == 0) else "d"]
+                else:
+                    distance = DISTANCES[name] or (3 if (r + c) % 2 == 1 else -3)
                 source = (r - distance if r % 2 == 1 else r + distance) % row_count
                 pairs.append((source * col_count + c, r * col_count + c))
         return lax.ppermute(message, ("row", "col"), pairs)
@@ -366,7 +386,7 @@
         return lax.ppermute(block, "col", [(0, 1), (1, 0)])
 
     left_other = swapped(left)
-    got = [towards(name, message) for name, message in zip("abcd", packed)]
+    got = [towards(name, message) for name, message in zip(PERMUTES, packed)]
     message = pl.pallas_call(
         pack_e_kernel,
         out_shape=blocks(SIZES["e"]),
@@ -393,27 +413,28 @@
         cost_estimate=cost(3 * 2 * 17, 4 * values.size),
         name="inner",
     )(*places, counts, left, left_other)
-    a, b, c, d, e = got
-    a, c, table = lax.optimization_barrier((a, c, table))
+    a, f, g, b, e = got
+    a, f, table = lax.optimization_barrier((a, f, table))
     early = pl.pallas_call(
         stage_early_kernel,
         out_shape=blocks(EARLY_SIZE),
-        in_specs=[vmem] * 2,
+        in_specs=[vmem],
         out_specs=vmem,
         compiler_params=params,
+        cost_estimate=cost(EARLY_COST, 0),
         name="stage_early",
-    )(a, c)
-    b, d, e, early = lax.optimization_barrier((b, d, e, early))
-    got = [a, b, c, d, e]
+    )(a)
+    f, g, b, e, early = lax.optimization_barrier((f, g, b, e, early))
+    got = [a, f, g, b, e]
     staged = swapped(
         pl.pallas_call(
             stage_kernel,
             out_shape=blocks(STAGED_SIZE),
-            in_specs=[vmem] * 4,
+            in_specs=[vmem] * 5,
             out_specs=vmem,
             compiler_params=params,
             name="stage",
-        )(early, b, d, e)
+        )(early, f, g, b, e)
     )
     outer = pl.pallas_call(
         outer_kernel,

time: 26.8 us -> 27.7 us (1.034)
  waiting for transfers between devices: 9.77 us -> 10.7 us
    ppermute x5, waiting for transfers between devices: 8.95 us -> 9.89 us  [towards(): return lax.ppermute(message, ('row', 'col'), pairs)]
  transfers between devices with their start and end apart: 7 -> 7, of which waited for: 4 -> 5; matrix products, arithmetic and copies ran while one was open for 0% -> 0% of each run, Pallas kernels for 14% -> 14%
where the time goes in v12:
time: 27.7 us; the launch traced here: 27.6 us
  waiting for transfers between devices  10.7 us (39%)
  starting transfers between devices  9.06 us (33%)
  Pallas kernels  7.08 us (26%)
  between operations  0.72 us (3%)
    ppermute x5, waiting for transfers between devices, towards(): return lax.ppermute(message, ('row', 'col'), pairs)  9.89 us
    ppermute x5, starting transfers between devices, towards(): return lax.ppermute(message, ('row', 'col'), pairs)  8.47 us
    pallas_call x1, Pallas kernels, local(): pl.pallas_call(functools.partial(inner_kernel, nblocks, slots), out_shape...  2.39 us
    pallas_call x1, Pallas kernels, local(): pl.pallas_call(multiply_kernel, out_shape=jax.ShapeDtypeStruct(values.sha...  1.73 us
    pallas_call x1, Pallas kernels, local(): pl.pallas_call(functools.partial(pack_kernel, nblocks, slots), out_shape=...  1.36 us
    pallas_call x1, Pallas kernels, local(): pl.pallas_call(outer_kernel, out_shape=blocks(BR * NCOL, jnp.float32), in...  1.28 us
    ppermute x2, waiting for transfers between devices, swapped(): return lax.ppermute(block, 'col', [(0, 1), (1, 0)])  0.8 us
    ppermute x2, starting transfers between devices, swapped(): return lax.ppermute(block, 'col', [(0, 1), (1, 0)])  0.59 us
  transfers between devices with their start and end apart: 7, of which 5 were waited for; matrix products, arithmetic and copies ran while one was open for 0% of the time, Pallas kernels for 14%

profile of v12, /device:TPU:0, one launch (start us, length us, event | category | flops | bytes accessed | tf_op | source)
XLA Modules:
  0.0 27.6 jit_solution(14792097217378503959)
XLA Ops:
  0.0 1.4 %pack.1 = (bf16[12,128,128]{2,1,0:T(8,128)(2,1)S(1)}, bf16[6,128,128]{2,1,0:T(8,128)(2,1)S(1)}, bf16[6,128,128]{2,1,0:T(8,128)(2,1)S(1)}, bf16[8,128,128]{2,1,0:T(8,128)(2,1)S(1)}, bf16[384,1152]{1,0:T(8,128)(2,1)S(1)}) custom-call(s32[1,23]{1,0:T(1,128)} %rows_ref.3, s32[1,23]{1,0:T(1,128)} %cols_ref.3, bf16[1,23,128,128]{3,2,1,0:T(8,128)(2,1)} %values_ref.1), custom_call_target="tpu_custom_call" | custom-call | tf_op jit(solution)/shard_map/pack/pallas_call | solution.py:357
  1.4 0.5 %collective-permute-start = (bf16[384,1152]{1,0:T(8,128)(2,1)S(1)}, bf16[384,1152]{1,0:T(8,128)(2,1)S(1)}, u32[]{:S(2)}, u32[]{:S(2)}) collective-permute-start(bf16[384,1152]{1,0:T(8,128)(2,1)S(1)} %get-tuple-element.20.left_ref), channel_id=1, source_target_pairs={{0,1},{1,0},{2,3},{3,2},{4,5},{5,4},{6,7},{7,6},{8,9},{9,8},{10,11... | collective-permute-start | bytes 2654216 | tf_op jit(solution)/shard_map/ppermute | solution.py:386
  1.9 2.6 %collective-permute-start.1 = (bf16[12,128,128]{2,1,0:T(8,128)(2,1)S(1)}, bf16[12,128,128]{2,1,0:T(8,128)(2,1)S(1)}, u32[]{:S(2)}, u32[]{:S(2)}) collective-permute-start(bf16[12,128,128]{2,1,0:T(8,128)(2,1)S(1)} %get-tuple-element.21), channel_id=1, source_target_pairs={{2,0},{3,1},{0,2},{1,3},{6,4},{7,5},{4,6},{5,7},{10,8},{11,9},{8,1... | collective-permute-start | bytes 1179656 | tf_op jit(solution)/shard_map/ppermute | solution.py:383
  4.5 1.6 %collective-permute-start.2 = (bf16[6,128,128]{2,1,0:T(8,128)(2,1)S(1)}, bf16[6,128,128]{2,1,0:T(8,128)(2,1)S(1)}, u32[]{:S(2)}, u32[]{:S(2)}) collective-permute-start(bf16[6,128,128]{2,1,0:T(8,128)(2,1)S(1)} %get-tuple-element.22), channel_id=1, source_target_pairs={{12,0},{5,1},{6,2},{15,3},{0,4},{9,5},{10,6},{3,7},{4,8},{13,9},{1... | collective-permute-start | bytes 589832 | tf_op jit(solution)/shard_map/ppermute | solution.py:383
  6.0 2.4 %collective-permute-start.4 = (bf16[8,128,128]{2,1,0:T(8,128)(2,1)S(1)}, bf16[8,128,128]{2,1,0:T(8,128)(2,1)S(1)}, u32[]{:S(2)}, u32[]{:S(2)}) collective-permute-start(bf16[8,128,128]{2,1,0:T(8,128)(2,1)S(1)} %get-tuple-element.26), channel_id=1, source_target_pairs={{14,0},{15,1},{4,2},{5,3},{2,4},{3,5},{8,6},{9,7},{6,8},{7,9},{12,... | collective-permute-start | bytes 786440 | tf_op jit(solution)/shard_map/ppermute | solution.py:383
  8.5 0.4 %collective-permute-start.3 = (bf16[6,128,128]{2,1,0:T(8,128)(2,1)S(1)}, bf16[6,128,128]{2,1,0:T(8,128)(2,1)S(1)}, u32[]{:S(2)}, u32[]{:S(2)}) collective-permute-start(bf16[6,128,128]{2,1,0:T(8,128)(2,1)S(1)} %get-tuple-element.25), channel_id=1, source_target_pairs={{4,0},{13,1},{14,2},{7,3},{8,4},{1,5},{2,6},{11,7},{12,8},{5,9},{6... | collective-permute-start | bytes 589832 | tf_op jit(solution)/shard_map/ppermute | solution.py:383
  9.6 0.0 collective-permute-done.left_other_ref
  9.6 1.4 %collective-permute-start.5 = (bf16[1,128,128]{2,1,0:T(8,128)(2,1)S(1)}, bf16[1,128,128]{2,1,0:T(8,128)(2,1)S(1)}, u32[]{:S(2)}, u32[]{:S(2)}) collective-permute-start(bf16[1,128,128]{2,1,0:T(8,128)(2,1)S(1)} %pack_e.1), channel_id=1, source_target_pairs={{10,0},{7,1},{12,2},{9,3},{14,4},{11,5},{0,6},{13,7},{2,8},{15,9},... | collective-permute-start | bytes 98312 | tf_op jit(solution)/shard_map/ppermute | solution.py:383
  11.1 2.4 %inner.1 = (s32[1,128]{1,0:T(1,128)S(1)}, f32[1,23,128,128]{3,2,1,0:T(8,128)}) custom-call(s32[1,23]{1,0:T(1,128)} %rows_ref.3, s32[1,23]{1,0:T(1,128)} %cols_ref.3, s32[1,1]{1,0:T(1,128)S(6)} %copy.7.counts_ref, bf16[384,1152]{1,0:T(8,128)(2,1)S(1)} %get-tuple-element.20.left_ref, bf16[384,1152]{1,0:T(8,128)(2,1)S(1)} %collective-permute-done.left_other_ref), custom_call_target="tpu_custom_call" | custom-call | flops 427819008 | bytes 1507328 | tf_op jit(solution)/shard_map/inner/pallas_call | solution.py:399
  13.4 0.5 %collective-permute-done.2.refs_0_.rest_1_ = bf16[6,128,128]{2,1,0:T(8,128)(2,1)S(1)} collective-permute-done((bf16[6,128,128]{2,1,0:T(8,128)(2,1)S(1)}, bf16[6,128,128]{2,1,0:T(8,128)(2,1)S(1)}, u32[]{:S(2)}, u32[]{:S(2)}) %collective-permute-start.2) | collective-permute-done | bytes 196640 | tf_op jit(solution)/shard_map/ppermute | solution.py:383
  14.0 5.8 %collective-permute-done.1.a_ref.rest_0_ = bf16[12,128,128]{2,1,0:T(8,128)(2,1)S(1)} collective-permute-done((bf16[12,128,128]{2,1,0:T(8,128)(2,1)S(1)}, bf16[12,128,128]{2,1,0:T(8,128)(2,1)S(1)}, u32[]{:S(2)}, u32[]{:S(2)}) %collective-permute-start.1) | collective-permute-done | bytes 393248 | tf_op jit(solution)/shard_map/ppermute | solution.py:383
  19.8 0.1 stage_early.1.early_ref
  19.9 0.5 %collective-permute-done.3.refs_1_.rest_2_ = bf16[6,128,128]{2,1,0:T(8,128)(2,1)S(1)} collective-permute-done((bf16[6,128,128]{2,1,0:T(8,128)(2,1)S(1)}, bf16[6,128,128]{2,1,0:T(8,128)(2,1)S(1)}, u32[]{:S(2)}, u32[]{:S(2)}) %collective-permute-start.3) | collective-permute-done | bytes 196640 | tf_op jit(solution)/shard_map/ppermute | solution.py:383
  20.4 0.0 collective-permute-done.4.refs_2_.rest_3_
  20.4 3.1 %collective-permute-done.5.refs_3_.rest_4_ = bf16[1,128,128]{2,1,0:T(8,128)(2,1)S(1)} collective-permute-done((bf16[1,128,128]{2,1,0:T(8,128)(2,1)S(1)}, bf16[1,128,128]{2,1,0:T(8,128)(2,1)S(1)}, u32[]{:S(2)}, u32[]{:S(2)}) %collective-permute-start.5) | collective-permute-done | bytes 32800 | tf_op jit(solution)/shard_map/ppermute | solution.py:383
  23.5 0.2 stage.1
  23.7 0.1 collective-permute-start.6
  23.7 1.3 %outer.1.outer_ref = f32[27,128,128]{2,1,0:T(8,128)S(1)} custom-call(bf16[384,1152]{1,0:T(8,128)(2,1)S(1)} %get-tuple-element.20.left_ref, bf16[384,1152]{1,0:T(8,128)(2,1)S(1)} %collective-permute-done.left_other_ref, bf16[12,128,128]{2,1,0:T(8,128)(2,1)S(1)} %collective-permute-done.1.a_ref.rest_0_, ...), custom_call_target="tpu_custom_call" | custom-call | flops 1409286144 | bytes 3768320 | tf_op jit(solution)/shard_map/outer/pallas_call | solution.py:439
  25.0 0.8 %collective-permute-done.6.staged_ref = bf16[20,128,128]{2,1,0:T(8,128)(2,1)S(1)} collective-permute-done((bf16[20,128,128]{2,1,0:T(8,128)(2,1)S(1)}, bf16[20,128,128]{2,1,0:T(8,128)(2,1)S(1)}, u32[]{:S(2)}, u32[]{:S(2)}) %collective-permute-start.6) | collective-permute-done | bytes 655392 | tf_op jit(solution)/shard_map/ppermute | solution.py:386
  25.8 1.7 %multiply.1 = f32[1,23,128,128]{3,2,1,0:T(8,128)} custom-call(bf16[384,1152]{1,0:T(8,128)(2,1)S(1)} %get-tuple-element.20.left_ref, bf16[384,1152]{1,0:T(8,128)(2,1)S(1)} %collective-permute-done.left_other_ref, bf16[20,128,128]{2,1,0:T(8,128)(2,1)S(1)} %collective-permute-done.6.staged_ref, ...), custom_call_target="tpu_custom_call", output_to_operand_aliasing={{}: (5, {})} | custom-call | tf_op jit(solution)/shard_map/multiply/pallas_call | solution.py:449
  (1 shorter events, 0.0 us)
Async XLA Ops:
  1.4 8.2 %collective-permute-start = (bf16[384,1152]{1,0:T(8,128)(2,1)S(1)}, bf16[384,1152]{1,0:T(8,128)(2,1)S(1)}, u32[]{:S(2)}, u32[]{:S(2)}) collective-permute-start(bf16[384,1152]{1,0:T(8,128)(2,1)S(1)} %get-tuple-element.20.left_ref), channel_id=1, source_target_pairs={{0,1},{1,0},{2,3},{3,2},{4,5},{5,4},{6,7},{7,6},{8,9},{9,8},{10,11... | collective-permute-start | bytes 2654216 | tf_op jit(solution)/shard_map/ppermute | solution.py:386
  1.9 17.9 %collective-permute-start.1 = (bf16[12,128,128]{2,1,0:T(8,128)(2,1)S(1)}, bf16[12,128,128]{2,1,0:T(8,128)(2,1)S(1)}, u32[]{:S(2)}, u32[]{:S(2)}) collective-permute-start(bf16[12,128,128]{2,1,0:T(8,128)(2,1)S(1)} %get-tuple-element.21), channel_id=1, source_target_pairs={{2,0},{3,1},{0,2},{1,3},{6,4},{7,5},{4,6},{5,7},{10,8},{11,9},{8,1... | collective-permute-start | bytes 1179656 | tf_op jit(solution)/shard_map/ppermute | solution.py:383
  4.5 9.5 %collective-permute-start.2 = (bf16[6,128,128]{2,1,0:T(8,128)(2,1)S(1)}, bf16[6,128,128]{2,1,0:T(8,128)(2,1)S(1)}, u32[]{:S(2)}, u32[]{:S(2)}) collective-permute-start(bf16[6,128,128]{2,1,0:T(8,128)(2,1)S(1)} %get-tuple-element.22), channel_id=1, source_target_pairs={{12,0},{5,1},{6,2},{15,3},{0,4},{9,5},{10,6},{3,7},{4,8},{13,9},{1... | collective-permute-start | bytes 589832 | tf_op jit(solution)/shard_map/ppermute | solution.py:383
  6.0 14.4 %collective-permute-start.4 = (bf16[8,128,128]{2,1,0:T(8,128)(2,1)S(1)}, bf16[8,128,128]{2,1,0:T(8,128)(2,1)S(1)}, u32[]{:S(2)}, u32[]{:S(2)}) collective-permute-start(bf16[8,128,128]{2,1,0:T(8,128)(2,1)S(1)} %get-tuple-element.26), channel_id=1, source_target_pairs={{14,0},{15,1},{4,2},{5,3},{2,4},{3,5},{8,6},{9,7},{6,8},{7,9},{12,... | collective-permute-start | bytes 786440 | tf_op jit(solution)/shard_map/ppermute | solution.py:383
  8.5 11.9 %collective-permute-start.3 = (bf16[6,128,128]{2,1,0:T(8,128)(2,1)S(1)}, bf16[6,128,128]{2,1,0:T(8,128)(2,1)S(1)}, u32[]{:S(2)}, u32[]{:S(2)}) collective-permute-start(bf16[6,128,128]{2,1,0:T(8,128)(2,1)S(1)} %get-tuple-element.25), channel_id=1, source_target_pairs={{4,0},{13,1},{14,2},{7,3},{8,4},{1,5},{2,6},{11,7},{12,8},{5,9},{6... | collective-permute-start | bytes 589832 | tf_op jit(solution)/shard_map/ppermute | solution.py:383
  9.6 13.9 %collective-permute-start.5 = (bf16[1,128,128]{2,1,0:T(8,128)(2,1)S(1)}, bf16[1,128,128]{2,1,0:T(8,128)(2,1)S(1)}, u32[]{:S(2)}, u32[]{:S(2)}) collective-permute-start(bf16[1,128,128]{2,1,0:T(8,128)(2,1)S(1)} %pack_e.1), channel_id=1, source_target_pairs={{10,0},{7,1},{12,2},{9,3},{14,4},{11,5},{0,6},{13,7},{2,8},{15,9},... | collective-permute-start | bytes 98312 | tf_op jit(solution)/shard_map/ppermute | solution.py:383
  23.7 2.2 %collective-permute-start.6 = (bf16[20,128,128]{2,1,0:T(8,128)(2,1)S(1)}, bf16[20,128,128]{2,1,0:T(8,128)(2,1)S(1)}, u32[]{:S(2)}, u32[]{:S(2)}) collective-permute-start(bf16[20,128,128]{2,1,0:T(8,128)(2,1)S(1)} %stage.1), channel_id=1, source_target_pairs={{0,1},{1,0},{2,3},{3,2},{4,5},{5,4},{6,7},{7,6},{8,9},{9,8},{10,11... | collective-permute-start | bytes 1966088 | tf_op jit(solution)/shard_map/ppermute | solution.py:386

commit v13 on v9

--- a/solution.py
+++ b/solution.py
@@ -13,9 +13,9 @@
 WIDTH = 2 * HB + 1
 LOW, HIGH = -HB, BR - 1 + HB
 NCOL = 9
-INNER = 6
-EARLY_COST = 1000
-LATE_COST = 50
+SOURCES = 32
+EARLY_COST = 1
+LATE_COST = 4000
 VMEM_LIMIT = 12 * 2**20
 
 DISTANCES = {"a": 1, "b": -1, "c": -2, "d": 2, "e": None}
@@ -124,7 +124,7 @@
         for part in PARTS:
             staged = [position for _, _, position in STAGED[part, 1 - parity]]
             if (a, b) in staged:
-                return part, staged.index((a, b)), flip
+                return part, staged.index((a, b)), not flip
     raise AssertionError((k, j))
 
 
@@ -172,13 +172,31 @@
     return total[i * BLK : (i + 1) * BLK, y * BLK : (y + 1) * BLK]
 
 
+def stored_places(parity):
+    columns = columns_of(parity)
+    return [i * NCOL + n for i in range(BR) for n, j in enumerate(columns) if abs(i - j) <= HB]
+
+
+def inner_places(parity):
+    return [i * NCOL + n for i in range(BR) for n, j in enumerate(columns_of(parity)) if 0 <= j < BR]
+
+
+def store(made, table, out_ref, place, sem):
+    source = made.at[table[0, SOURCES + place]]
+    pltpu.make_async_copy(source, out_ref.at[0, table[0, place]], sem).start()
+
+
+def wait_for(count, made, out_ref, sem):
+    pltpu.make_async_copy(made.at[pl.ds(0, count)], out_ref.at[0, pl.ds(0, count)], sem).wait()
+
+
 def outer_pairs(parity):
     outer = [j for j in columns_of(parity) if not 0 <= j < BR]
     return [outer[n : n + 2] for n in range(0, len(outer), 2)]
 
 
 def inner_kernel(nblocks, slots, rows_ref, cols_ref, counts_ref, left_ref, left_other_ref, *rest):
-    made_ref, places_ref, right, places, *index, sems, places_sem = rest
+    table_ref, out_ref, right, made, table, *index, sems, table_sem, out_sem = rest
     copies = index_copies((rows_ref, cols_ref), index, sems)
     for copy in copies:
         copy.start()
@@ -190,15 +208,39 @@
         total = columns_product(refs, right, mine, js, LEFT)
         for i in range(BR):
             for y in range(2):
-                made_ref[i * 2 + y] = block_of(total, i, y) if y < len(js) else jnp.zeros((BLK, BLK), made_ref.dtype)
+                if y < len(js):
+                    made[i * NCOL + columns_of(mine).index(js[y])] = block_of(total, i, y)
+        made[BR * NCOL] = jnp.zeros((BLK, BLK), made.dtype)
 
     for copy in copies:
         copy.wait()
+    for place in range(BR * NCOL + 1):
+        table[0, place] = -1
     count = counts_ref[0, 0]
     for m in range(slots):
         _, row, band = slot_position(*index, m, nblocks)
-        places[0, m] = jnp.where(m < count, row * NCOL + (row + band) // 2, BR * NCOL)
-    copy = pltpu.make_async_copy(places, places_ref, places_sem)
+        table[0, jnp.where(m < count, row * NCOL + (row + band) // 2, BR * NCOL)] = m
+
+    @for_own_parity
+    def _(mine):
+        unused = count
+        for place in stored_places(mine):
+            slot = table[0, place]
+            absent = slot < 0
+            table[0, place] = jnp.where(absent, unused, slot)
+            table[0, SOURCES + place] = jnp.where(absent, BR * NCOL, place)
+            unused = jnp.where(absent, unused + 1, unused)
+        table[0, BR * NCOL] = unused
+        here = [place for place in stored_places(mine) if place in inner_places(mine)]
+        for place in here:
+            store(made, table, out_ref, place, out_sem)
+        stored = len(here)
+        if len(stored_places(mine)) < slots:
+            pltpu.make_async_copy(made.at[BR * NCOL], out_ref.at[0, unused], out_sem).start()
+            stored += 1
+        wait_for(stored, made, out_ref, out_sem)
+
+    copy = pltpu.make_async_copy(table, table_ref, table_sem)
     copy.start()
     copy.wait()
 
@@ -219,7 +261,7 @@
     def _(mine):
         staged = STAGED[part, mine]
         for n, (name, place, _) in enumerate(staged):
-            out_ref[n] = got[name][place]
+            out_ref[n] = got[name][place].T
         for n in range(len(staged), STAGED_SIZE[part]):
             out_ref[n] = jnp.zeros((BLK, BLK), out_ref.dtype)
 
@@ -231,10 +273,9 @@
             for y, j in enumerate(js):
                 if abs(i - j) <= HB:
                     place = i * NCOL + columns_of(mine).index(j)
-                    if old_ref is None:
-                        new_ref[place] = block_of(total, i, y)
-                    else:
-                        new_ref[place] = old_ref[place] if total is None else old_ref[place] + block_of(total, i, y)
+                    terms = [] if old_ref is None else [old_ref[place]]
+                    terms += [] if total is None else [block_of(total, i, y)]
+                    new_ref[place] = functools.reduce(jnp.add, terms)
 
 
 def early_kernel(left_ref, left_other_ref, a_ref, c_ref, out_ref, right):
@@ -242,35 +283,26 @@
     for_own_parity(functools.partial(add_columns, refs, (*LEFT, "a", "c"), None, out_ref, right))
 
 
-def staged_early_kernel(left_ref, left_other_ref, staged_ref, old_ref, out_ref, right):
-    refs = {("left", True): left_ref, ("left", False): left_other_ref, "early": staged_ref}
-    for_own_parity(functools.partial(add_columns, refs, ("early",), old_ref, out_ref, right))
-
-
 def late_kernel(left_ref, left_other_ref, b_ref, d_ref, e_ref, old_ref, out_ref, right):
     refs = {("left", True): left_ref, ("left", False): left_other_ref, "b": b_ref, "d": d_ref, "e": e_ref}
     for_own_parity(functools.partial(add_columns, refs, ("b", "d", "e"), old_ref, out_ref, right))
 
 
-def multiply_kernel(slots, left_ref, left_other_ref, staged_ref, old_ref, inner_ref, places_ref, out_ref, *rest):
-    right, made, places, places_sem, out_sem = rest
-    refs = {("left", True): left_ref, ("left", False): left_other_ref, "late": staged_ref}
-    load = pltpu.make_async_copy(places_ref, places, places_sem)
+def multiply_kernel(left_ref, left_other_ref, early_ref, late_ref, old_ref, table_ref, _, out_ref, *rest):
+    right, made, table, table_sem, out_sem = rest
+    refs = {("left", True): left_ref, ("left", False): left_other_ref, "early": early_ref, "late": late_ref}
+    load = pltpu.make_async_copy(table_ref, table, table_sem)
     load.start()
-
-    @for_own_parity
-    def _(mine):
-        add_columns(refs, ("late",), old_ref, made, right, mine)
-        columns = columns_of(mine)
-        for i in range(BR):
-            for y, j in enumerate(j for j in columns if 0 <= j < BR):
-                made[i * NCOL + columns.index(j)] = inner_ref[i * 2 + y]
-        made[BR * NCOL] = jnp.zeros((BLK, BLK), made.dtype)
-
-    load.wait()
-    for m in range(slots):
-        pltpu.make_async_copy(made.at[places[0, m]], out_ref.at[0, m], out_sem).start()
-    pltpu.make_async_copy(made.at[pl.ds(0, slots)], out_ref.at[0], out_sem).wait()
+    made[BR * NCOL] = jnp.zeros((BLK, BLK), made.dtype)
+
+    @for_own_parity
+    def _(mine):
+        add_columns(refs, tuple(PARTS), old_ref, made, right, mine)
+        load.wait()
+        here = [place for place in stored_places(mine) if place not in inner_places(mine)]
+        for place in here:
+            store(made, table, out_ref, place, out_sem)
+        wait_for(len(here), made, out_ref, out_sem)
 
 
 def local(values, block_rows, block_cols, counts):
@@ -287,7 +319,7 @@
         pltpu.SMEM((1, slots), jnp.int32),
         pltpu.SemaphoreType.DMA((2,)),
     ]
-    places_shape = (1, BLK)
+    table_shape = (1, BLK)
 
     def blocks(count, dtype=values.dtype):
         return jax.ShapeDtypeStruct((count, BLK, BLK), dtype)
@@ -337,15 +369,17 @@
         name="pack_e",
     )(left, left_other)
     got.append(towards("e", message))
-    inner, slot_places = pl.pallas_call(
+    table, out = pl.pallas_call(
         functools.partial(inner_kernel, nblocks, slots),
-        out_shape=[blocks(INNER, jnp.float32), jax.ShapeDtypeStruct(places_shape, jnp.int32)],
+        out_shape=[jax.ShapeDtypeStruct(table_shape, jnp.int32), jax.ShapeDtypeStruct(values.shape, jnp.float32)],
         in_specs=[hbm] * 2 + [smem] + [vmem] * 2,
-        out_specs=[vmem] * 2,
+        out_specs=[vmem, hbm],
         scratch_shapes=[
             pltpu.VMEM((2, NCOL * BLK, 2 * BLK), values.dtype),
-            pltpu.SMEM(places_shape, jnp.int32),
+            pltpu.VMEM((BR * NCOL + 1, BLK, BLK), jnp.float32),
+            pltpu.SMEM(table_shape, jnp.int32),
             *index_scratch,
+            pltpu.SemaphoreType.DMA,
             pltpu.SemaphoreType.DMA,
         ],
         compiler_params=params,
@@ -378,28 +412,28 @@
             name=name,
         )(*arrays)
 
-    a, c, inner = lax.optimization_barrier((a, c, inner))
+    a, c, table = lax.optimization_barrier((a, c, table))
     staged_early = staged("early", (a, c))
-    early = added(early_kernel, "early", EARLY_COST, (left, left_other, a, c))
-    early = added(staged_early_kernel, "staged_early", 1, (left, left_other, staged_early, early))
-    b, d, e, early = lax.optimization_barrier((b, d, e, early))
+    total = added(early_kernel, "early", EARLY_COST, (left, left_other, a, c))
+    b, d, e, total = lax.optimization_barrier((b, d, e, total))
     staged_late = staged("late", (b, d, e))
-    late = added(late_kernel, "late", LATE_COST, (left, left_other, b, d, e, early))
+    total = added(late_kernel, "late", LATE_COST, (left, left_other, b, d, e, total))
     return pl.pallas_call(
-        functools.partial(multiply_kernel, slots),
+        multiply_kernel,
         out_shape=jax.ShapeDtypeStruct(values.shape, jnp.float32),
-        in_specs=[vmem] * 6,
+        in_specs=[vmem] * 6 + [hbm],
         out_specs=hbm,
         scratch_shapes=[
             right_scratch(4),
             pltpu.VMEM((BR * NCOL + 1, BLK, BLK), jnp.float32),
-            pltpu.SMEM(places_shape, jnp.int32),
+            pltpu.SMEM(table_shape, jnp.int32),
             pltpu.SemaphoreType.DMA,
             pltpu.SemaphoreType.DMA,
         ],
+        input_output_aliases={6: 0},
         compiler_params=params,
         name="multiply",
-    )(left, left_other, staged_late, late, inner, slot_places)
+    )(left, left_other, staged_early, staged_late, total, table, out)
 
 
 def solution(mesh):

time: 29.4 us -> 26.3 us (0.89)
  the two profiles are of different devices: /device:TPU:25 before, /device:TPU:0 now
where the time goes in v13:
time: 26.3 us; the launch traced here: 26.1 us
  starting transfers between devices  9.12 us (35%)
  waiting for transfers between devices  8.75 us (33%)
  Pallas kernels  7.49 us (28%)
  between operations  0.74 us (3%)
    ppermute x5, starting transfers between devices, towards(): return lax.ppermute(message, ('row', 'col'), pairs)  8.47 us
    ppermute x5, waiting for transfers between devices, towards(): return lax.ppermute(message, ('row', 'col'), pairs)  7.69 us
    pallas_call x1, Pallas kernels, local(): pl.pallas_call(functools.partial(inner_kernel, nblocks, slots), out_shape...  2.39 us
    pallas_call x1, Pallas kernels, local(): pl.pallas_call(multiply_kernel, out_shape=jax.ShapeDtypeStruct(values.sha...  1.8 us
    pallas_call x2, Pallas kernels, added(): pl.pallas_call(kernel, out_shape=blocks(BR * NCOL, jnp.float32), in_specs...  1.63 us
    pallas_call x1, Pallas kernels, local(): pl.pallas_call(functools.partial(pack_kernel, nblocks, slots), out_shape=...  1.36 us
    ppermute x3, waiting for transfers between devices, swapped(): return lax.ppermute(block, 'col', [(0, 1), (1, 0)])  1.06 us
    ppermute x3, starting transfers between devices, swapped(): return lax.ppermute(block, 'col', [(0, 1), (1, 0)])  0.66 us
  transfers between devices with their start and end apart: 8, of which 4 were waited for; matrix products, arithmetic and copies ran while one was open for 0% of the time, Pallas kernels for 17%

profile of v13, /device:TPU:0, one launch (start us, length us, event | category | flops | bytes accessed | tf_op | source)
XLA Modules:
  0.0 26.1 jit_solution(16202683941598981782)
XLA Ops:
  0.0 1.4 %pack.1 = (bf16[13,128,128]{2,1,0:T(8,128)(2,1)S(1)}, bf16[6,128,128]{2,1,0:T(8,128)(2,1)S(1)}, bf16[8,128,128]{2,1,0:T(8,128)(2,1)S(1)}, bf16[5,128,128]{2,1,0:T(8,128)(2,1)S(1)}, bf16[384,1152]{1,0:T(8,128)(2,1)S(1)}) custom-call(s32[1,23]{1,0:T(1,128)} %rows_ref.3, s32[1,23]{1,0:T(1,128)} %cols_ref.3, bf16[1,23,128,128]{3,2,1,0:T(8,128)(2,1)} %values_ref.1), custom_call_target="tpu_custom_call" | custom-call | tf_op jit(solution)/shard_map/pack/pallas_call | solution.py:333
  1.4 0.5 %collective-permute-start = (bf16[384,1152]{1,0:T(8,128)(2,1)S(1)}, bf16[384,1152]{1,0:T(8,128)(2,1)S(1)}, u32[]{:S(2)}, u32[]{:S(2)}) collective-permute-start(bf16[384,1152]{1,0:T(8,128)(2,1)S(1)} %get-tuple-element.19.left_ref), channel_id=1, source_target_pairs={{0,1},{1,0},{2,3},{3,2},{4,5},{5,4},{6,7},{7,6},{8,9},{9,8},{10,11... | collective-permute-start | bytes 2654216 | tf_op jit(solution)/shard_map/ppermute | solution.py:359
  1.9 2.6 %collective-permute-start.1 = (bf16[13,128,128]{2,1,0:T(8,128)(2,1)S(1)}, bf16[13,128,128]{2,1,0:T(8,128)(2,1)S(1)}, u32[]{:S(2)}, u32[]{:S(2)}) collective-permute-start(bf16[13,128,128]{2,1,0:T(8,128)(2,1)S(1)} %get-tuple-element.20), channel_id=1, source_target_pairs={{2,0},{3,1},{0,2},{1,3},{6,4},{7,5},{4,6},{5,7},{10,8},{11,9},{8,1... | collective-permute-start | bytes 1277960 | tf_op jit(solution)/shard_map/ppermute | solution.py:356
  4.4 1.6 %collective-permute-start.2 = (bf16[8,128,128]{2,1,0:T(8,128)(2,1)S(1)}, bf16[8,128,128]{2,1,0:T(8,128)(2,1)S(1)}, u32[]{:S(2)}, u32[]{:S(2)}) collective-permute-start(bf16[8,128,128]{2,1,0:T(8,128)(2,1)S(1)} %get-tuple-element.21), channel_id=1, source_target_pairs={{12,0},{13,1},{6,2},{7,3},{0,4},{1,5},{10,6},{11,7},{4,8},{5,9},{1... | collective-permute-start | bytes 786440 | tf_op jit(solution)/shard_map/ppermute | solution.py:356
  6.0 2.4 %collective-permute-start.4 = (bf16[6,128,128]{2,1,0:T(8,128)(2,1)S(1)}, bf16[6,128,128]{2,1,0:T(8,128)(2,1)S(1)}, u32[]{:S(2)}, u32[]{:S(2)}) collective-permute-start(bf16[6,128,128]{2,1,0:T(8,128)(2,1)S(1)} %get-tuple-element.25), channel_id=1, source_target_pairs={{14,0},{15,1},{4,2},{5,3},{2,4},{3,5},{8,6},{9,7},{6,8},{7,9},{12,... | collective-permute-start | bytes 589832 | tf_op jit(solution)/shard_map/ppermute | solution.py:356
  8.5 0.4 %collective-permute-start.5 = (bf16[5,128,128]{2,1,0:T(8,128)(2,1)S(1)}, bf16[5,128,128]{2,1,0:T(8,128)(2,1)S(1)}, u32[]{:S(2)}, u32[]{:S(2)}) collective-permute-start(bf16[5,128,128]{2,1,0:T(8,128)(2,1)S(1)} %get-tuple-element.26), channel_id=1, source_target_pairs={{4,0},{5,1},{14,2},{15,3},{8,4},{9,5},{2,6},{3,7},{12,8},{13,9},{6... | collective-permute-start | bytes 491528 | tf_op jit(solution)/shard_map/ppermute | solution.py:356
  9.6 0.0 collective-permute-done.left_other_ref
  9.6 1.4 %collective-permute-start.6 = (bf16[1,128,128]{2,1,0:T(8,128)(2,1)S(1)}, bf16[1,128,128]{2,1,0:T(8,128)(2,1)S(1)}, u32[]{:S(2)}, u32[]{:S(2)}) collective-permute-start(bf16[1,128,128]{2,1,0:T(8,128)(2,1)S(1)} %pack_e.1), channel_id=1, source_target_pairs={{10,0},{7,1},{12,2},{9,3},{14,4},{11,5},{0,6},{13,7},{2,8},{15,9},... | collective-permute-start | bytes 98312 | tf_op jit(solution)/shard_map/ppermute | solution.py:356
  11.1 2.4 %inner.1 = (s32[1,128]{1,0:T(1,128)S(1)}, f32[1,23,128,128]{3,2,1,0:T(8,128)}) custom-call(s32[1,23]{1,0:T(1,128)} %rows_ref.3, s32[1,23]{1,0:T(1,128)} %cols_ref.3, s32[1,1]{1,0:T(1,128)S(6)} %copy.7.counts_ref, bf16[384,1152]{1,0:T(8,128)(2,1)S(1)} %get-tuple-element.19.left_ref, bf16[384,1152]{1,0:T(8,128)(2,1)S(1)} %collective-permute-done.left_other_ref), custom_call_target="tpu_custom_call" | custom-call | flops 427819008 | bytes 1507328 | tf_op jit(solution)/shard_map/inner/pallas_call | solution.py:372
  13.4 2.0 %collective-permute-done.2.refs_1_.c_ref = bf16[8,128,128]{2,1,0:T(8,128)(2,1)S(1)} collective-permute-done((bf16[8,128,128]{2,1,0:T(8,128)(2,1)S(1)}, bf16[8,128,128]{2,1,0:T(8,128)(2,1)S(1)}, u32[]{:S(2)}, u32[]{:S(2)}) %collective-permute-start.2) | collective-permute-done | bytes 262176 | tf_op jit(solution)/shard_map/ppermute | solution.py:356
  15.5 4.2 %collective-permute-done.1.refs_0_.a_ref = bf16[13,128,128]{2,1,0:T(8,128)(2,1)S(1)} collective-permute-done((bf16[13,128,128]{2,1,0:T(8,128)(2,1)S(1)}, bf16[13,128,128]{2,1,0:T(8,128)(2,1)S(1)}, u32[]{:S(2)}, u32[]{:S(2)}) %collective-permute-start.1) | collective-permute-done | bytes 426016 | tf_op jit(solution)/shard_map/ppermute | solution.py:356
  19.7 0.2 stage_early.1
  19.8 0.1 collective-permute-start.3
  19.9 1.2 %early.1.old_ref = f32[27,128,128]{2,1,0:T(8,128)S(1)} custom-call(bf16[384,1152]{1,0:T(8,128)(2,1)S(1)} %get-tuple-element.19.left_ref, bf16[384,1152]{1,0:T(8,128)(2,1)S(1)} %collective-permute-done.left_other_ref, bf16[13,128,128]{2,1,0:T(8,128)(2,1)S(1)} %collective-permute-done.1.refs_0_.a_ref, bf16[8,128,128]{2,1,0:T(8,128)(2,1)S(1)} %collective-permute-done.2.refs_1_.c_ref), custom_call_target="tpu_custom_call" | custom-call | flops 4194304 | tf_op jit(solution)/shard_map/early/pallas_call | solution.py:404
  21.1 1.5 %collective-permute-done.5.refs_1_.d_ref = bf16[5,128,128]{2,1,0:T(8,128)(2,1)S(1)} collective-permute-done((bf16[5,128,128]{2,1,0:T(8,128)(2,1)S(1)}, bf16[5,128,128]{2,1,0:T(8,128)(2,1)S(1)}, u32[]{:S(2)}, u32[]{:S(2)}) %collective-permute-start.5) | collective-permute-done | bytes 163872 | tf_op jit(solution)/shard_map/ppermute | solution.py:356
  22.6 0.0 collective-permute-done.4.refs_0_.b_ref
  22.6 0.0 collective-permute-done.6.refs_2_.e_ref
  22.6 0.1 stage_late.1
  22.7 0.1 collective-permute-start.7
  22.8 0.5 %late.1.old_ref = f32[27,128,128]{2,1,0:T(8,128)S(1)} custom-call(bf16[384,1152]{1,0:T(8,128)(2,1)S(1)} %get-tuple-element.19.left_ref, bf16[384,1152]{1,0:T(8,128)(2,1)S(1)} %collective-permute-done.left_other_ref, bf16[6,128,128]{2,1,0:T(8,128)(2,1)S(1)} %collective-permute-done.4.refs_0_.b_ref, ...), custom_call_target="tpu_custom_call" | custom-call | flops 16777216000 | tf_op jit(solution)/shard_map/late/pallas_call | solution.py:404
  23.2 1.1 %collective-permute-done.7.late_ref = bf16[8,128,128]{2,1,0:T(8,128)(2,1)S(1)} collective-permute-done((bf16[8,128,128]{2,1,0:T(8,128)(2,1)S(1)}, bf16[8,128,128]{2,1,0:T(8,128)(2,1)S(1)}, u32[]{:S(2)}, u32[]{:S(2)}) %collective-permute-start.7) | collective-permute-done | bytes 262176 | tf_op jit(solution)/shard_map/ppermute | solution.py:359
  24.3 0.0 collective-permute-done.3.early_ref
  24.3 1.8 %multiply.1 = f32[1,23,128,128]{3,2,1,0:T(8,128)} custom-call(bf16[384,1152]{1,0:T(8,128)(2,1)S(1)} %get-tuple-element.19.left_ref, bf16[384,1152]{1,0:T(8,128)(2,1)S(1)} %collective-permute-done.left_other_ref, bf16[12,128,128]{2,1,0:T(8,128)(2,1)S(1)} %collective-permute-done.3.early_ref, ...), custom_call_target="tpu_custom_call", output_to_operand_aliasing={{}: (6, {})} | custom-call | tf_op jit(solution)/shard_map/multiply/pallas_call | solution.py:421
  (1 shorter events, 0.0 us)
Async XLA Ops:
  1.4 8.2 %collective-permute-start = (bf16[384,1152]{1,0:T(8,128)(2,1)S(1)}, bf16[384,1152]{1,0:T(8,128)(2,1)S(1)}, u32[]{:S(2)}, u32[]{:S(2)}) collective-permute-start(bf16[384,1152]{1,0:T(8,128)(2,1)S(1)} %get-tuple-element.19.left_ref), channel_id=1, source_target_pairs={{0,1},{1,0},{2,3},{3,2},{4,5},{5,4},{6,7},{7,6},{8,9},{9,8},{10,11... | collective-permute-start | bytes 2654216 | tf_op jit(solution)/shard_map/ppermute | solution.py:359
  1.9 17.8 %collective-permute-start.1 = (bf16[13,128,128]{2,1,0:T(8,128)(2,1)S(1)}, bf16[13,128,128]{2,1,0:T(8,128)(2,1)S(1)}, u32[]{:S(2)}, u32[]{:S(2)}) collective-permute-start(bf16[13,128,128]{2,1,0:T(8,128)(2,1)S(1)} %get-tuple-element.20), channel_id=1, source_target_pairs={{2,0},{3,1},{0,2},{1,3},{6,4},{7,5},{4,6},{5,7},{10,8},{11,9},{8,1... | collective-permute-start | bytes 1277960 | tf_op jit(solution)/shard_map/ppermute | solution.py:356
  4.4 11.0 %collective-permute-start.2 = (bf16[8,128,128]{2,1,0:T(8,128)(2,1)S(1)}, bf16[8,128,128]{2,1,0:T(8,128)(2,1)S(1)}, u32[]{:S(2)}, u32[]{:S(2)}) collective-permute-start(bf16[8,128,128]{2,1,0:T(8,128)(2,1)S(1)} %get-tuple-element.21), channel_id=1, source_target_pairs={{12,0},{13,1},{6,2},{7,3},{0,4},{1,5},{10,6},{11,7},{4,8},{5,9},{1... | collective-permute-start | bytes 786440 | tf_op jit(solution)/shard_map/ppermute | solution.py:356
  6.0 16.5 %collective-permute-start.4 = (bf16[6,128,128]{2,1,0:T(8,128)(2,1)S(1)}, bf16[6,128,128]{2,1,0:T(8,128)(2,1)S(1)}, u32[]{:S(2)}, u32[]{:S(2)}) collective-permute-start(bf16[6,128,128]{2,1,0:T(8,128)(2,1)S(1)} %get-tuple-element.25), channel_id=1, source_target_pairs={{14,0},{15,1},{4,2},{5,3},{2,4},{3,5},{8,6},{9,7},{6,8},{7,9},{12,... | collective-permute-start | bytes 589832 | tf_op jit(solution)/shard_map/ppermute | solution.py:356
  8.5 14.1 %collective-permute-start.5 = (bf16[5,128,128]{2,1,0:T(8,128)(2,1)S(1)}, bf16[5,128,128]{2,1,0:T(8,128)(2,1)S(1)}, u32[]{:S(2)}, u32[]{:S(2)}) collective-permute-start(bf16[5,128,128]{2,1,0:T(8,128)(2,1)S(1)} %get-tuple-element.26), channel_id=1, source_target_pairs={{4,0},{5,1},{14,2},{15,3},{8,4},{9,5},{2,6},{3,7},{12,8},{13,9},{6... | collective-permute-start | bytes 491528 | tf_op jit(solution)/shard_map/ppermute | solution.py:356
  9.6 12.9 %collective-permute-start.6 = (bf16[1,128,128]{2,1,0:T(8,128)(2,1)S(1)}, bf16[1,128,128]{2,1,0:T(8,128)(2,1)S(1)}, u32[]{:S(2)}, u32[]{:S(2)}) collective-permute-start(bf16[1,128,128]{2,1,0:T(8,128)(2,1)S(1)} %pack_e.1), channel_id=1, source_target_pairs={{10,0},{7,1},{12,2},{9,3},{14,4},{11,5},{0,6},{13,7},{2,8},{15,9},... | collective-permute-start | bytes 98312 | tf_op jit(solution)/shard_map/ppermute | solution.py:356
  19.8 4.5 %collective-permute-start.3 = (bf16[12,128,128]{2,1,0:T(8,128)(2,1)S(1)}, bf16[12,128,128]{2,1,0:T(8,128)(2,1)S(1)}, u32[]{:S(2)}, u32[]{:S(2)}) collective-permute-start(bf16[12,128,128]{2,1,0:T(8,128)(2,1)S(1)} %stage_early.1), channel_id=1, source_target_pairs={{0,1},{1,0},{2,3},{3,2},{4,5},{5,4},{6,7},{7,6},{8,9},{9,8},{10,11... | collective-permute-start | bytes 1179656 | tf_op jit(solution)/shard_map/ppermute | solution.py:359
  22.7 1.6 %collective-permute-start.7 = (bf16[8,128,128]{2,1,0:T(8,128)(2,1)S(1)}, bf16[8,128,128]{2,1,0:T(8,128)(2,1)S(1)}, u32[]{:S(2)}, u32[]{:S(2)}) collective-permute-start(bf16[8,128,128]{2,1,0:T(8,128)(2,1)S(1)} %stage_late.1), channel_id=1, source_target_pairs={{0,1},{1,0},{2,3},{3,2},{4,5},{5,4},{6,7},{7,6},{8,9},{9,8},{10,11... | collective-permute-start | bytes 786440 | tf_op jit(solution)/shard_map/ppermute | solution.py:359

commit v14 on v13

--- a/solution.py
+++ b/solution.py
@@ -288,16 +288,21 @@
     for_own_parity(functools.partial(add_columns, refs, ("b", "d", "e"), old_ref, out_ref, right))
 
 
-def multiply_kernel(left_ref, left_other_ref, early_ref, late_ref, old_ref, table_ref, _, out_ref, *rest):
+def staged_early_kernel(left_ref, left_other_ref, staged_ref, old_ref, out_ref, right):
+    refs = {("left", True): left_ref, ("left", False): left_other_ref, "early": staged_ref}
+    for_own_parity(functools.partial(add_columns, refs, ("early",), old_ref, out_ref, right))
+
+
+def multiply_kernel(left_ref, left_other_ref, staged_ref, old_ref, table_ref, _, out_ref, *rest):
     right, made, table, table_sem, out_sem = rest
-    refs = {("left", True): left_ref, ("left", False): left_other_ref, "early": early_ref, "late": late_ref}
+    refs = {("left", True): left_ref, ("left", False): left_other_ref, "late": staged_ref}
     load = pltpu.make_async_copy(table_ref, table, table_sem)
     load.start()
     made[BR * NCOL] = jnp.zeros((BLK, BLK), made.dtype)
 
     @for_own_parity
     def _(mine):
-        add_columns(refs, tuple(PARTS), old_ref, made, right, mine)
+        add_columns(refs, ("late",), old_ref, made, right, mine)
         load.wait()
         here = [place for place in stored_places(mine) if place not in inner_places(mine)]
         for place in here:
@@ -418,10 +423,11 @@
     b, d, e, total = lax.optimization_barrier((b, d, e, total))
     staged_late = staged("late", (b, d, e))
     total = added(late_kernel, "late", LATE_COST, (left, left_other, b, d, e, total))
+    total = added(staged_early_kernel, "staged_early", EARLY_COST, (left, left_other, staged_early, total))
     return pl.pallas_call(
         multiply_kernel,
         out_shape=jax.ShapeDtypeStruct(values.shape, jnp.float32),
-        in_specs=[vmem] * 6 + [hbm],
+        in_specs=[vmem] * 5 + [hbm],
         out_specs=hbm,
         scratch_shapes=[
             right_scratch(4),
@@ -430,10 +436,10 @@
             pltpu.SemaphoreType.DMA,
             pltpu.SemaphoreType.DMA,
         ],
-        input_output_aliases={6: 0},
+        input_output_aliases={5: 0},
         compiler_params=params,
         name="multiply",
-    )(left, left_other, staged_early, staged_late, total, table, out)
+    )(left, left_other, staged_late, total, table, out)
 
 
 def solution(mesh):

time: 26.3 us -> 26 us (0.989)
  waiting for transfers between devices: 8.75 us -> 8.17 us
    ppermute x3, waiting for transfers between devices: 1.06 us -> 0.48 us  [swapped(): return lax.ppermute(block, 'col', [(0, 1), (1, 0)])]
    pallas_call x2 -> x3, Pallas kernels: 1.63 us -> 2.19 us  [added(): pl.pallas_call(kernel, out_shape=blocks(BR * NCOL, jnp.float32), in_specs...]
    pallas_call x1, Pallas kernels: 1.8 us -> 1.51 us  [local(): pl.pallas_call(multiply_kernel, out_shape=jax.ShapeDtypeStruct(values.sha...]
  transfers between devices with their start and end apart: 8 -> 8, of which waited for: 4 -> 4; matrix products, arithmetic and copies ran while one was open for 0% -> 0% of each run, Pallas kernels for 17% -> 19%
where the time goes in v14:
time: 26 us; the launch traced here: 25.8 us
  starting transfers between devices  9.12 us (35%)
  waiting for transfers between devices  8.17 us (31%)
  Pallas kernels  7.75 us (30%)
  between operations  0.75 us (3%)
    ppermute x5, starting transfers between devices, towards(): return lax.ppermute(message, ('row', 'col'), pairs)  8.47 us
    ppermute x5, waiting for transfers between devices, towards(): return lax.ppermute(message, ('row', 'col'), pairs)  7.69 us
    pallas_call x1, Pallas kernels, local(): pl.pallas_call(functools.partial(inner_kernel, nblocks, slots), out_shape...  2.39 us
    pallas_call x3, Pallas kernels, added(): pl.pallas_call(kernel, out_shape=blocks(BR * NCOL, jnp.float32), in_specs...  2.19 us
    pallas_call x1, Pallas kernels, local(): pl.pallas_call(multiply_kernel, out_shape=jax.ShapeDtypeStruct(values.sha...  1.51 us
    pallas_call x1, Pallas kernels, local(): pl.pallas_call(functools.partial(pack_kernel, nblocks, slots), out_shape=...  1.36 us
    ppermute x3, starting transfers between devices, swapped(): return lax.ppermute(block, 'col', [(0, 1), (1, 0)])  0.66 us
  transfers between devices with their start and end apart: 8, of which 4 were waited for; matrix products, arithmetic and copies ran while one was open for 0% of the time, Pallas kernels for 19%

profile of v14, /device:TPU:0, one launch (start us, length us, event | category | flops | bytes accessed | tf_op | source)
XLA Modules:
  0.0 25.8 jit_solution(5855684372755759552)
XLA Ops:
  0.0 1.4 %pack.1 = (bf16[13,128,128]{2,1,0:T(8,128)(2,1)S(1)}, bf16[6,128,128]{2,1,0:T(8,128)(2,1)S(1)}, bf16[8,128,128]{2,1,0:T(8,128)(2,1)S(1)}, bf16[5,128,128]{2,1,0:T(8,128)(2,1)S(1)}, bf16[384,1152]{1,0:T(8,128)(2,1)S(1)}) custom-call(s32[1,23]{1,0:T(1,128)} %rows_ref.3, s32[1,23]{1,0:T(1,128)} %cols_ref.3, bf16[1,23,128,128]{3,2,1,0:T(8,128)(2,1)} %values_ref.1), custom_call_target="tpu_custom_call" | custom-call | tf_op jit(solution)/shard_map/pack/pallas_call | solution.py:338
  1.4 0.5 %collective-permute-start = (bf16[384,1152]{1,0:T(8,128)(2,1)S(1)}, bf16[384,1152]{1,0:T(8,128)(2,1)S(1)}, u32[]{:S(2)}, u32[]{:S(2)}) collective-permute-start(bf16[384,1152]{1,0:T(8,128)(2,1)S(1)} %get-tuple-element.19.left_ref), channel_id=1, source_target_pairs={{0,1},{1,0},{2,3},{3,2},{4,5},{5,4},{6,7},{7,6},{8,9},{9,8},{10,11... | collective-permute-start | bytes 2654216 | tf_op jit(solution)/shard_map/ppermute | solution.py:364
  1.9 2.6 %collective-permute-start.4 = (bf16[13,128,128]{2,1,0:T(8,128)(2,1)S(1)}, bf16[13,128,128]{2,1,0:T(8,128)(2,1)S(1)}, u32[]{:S(2)}, u32[]{:S(2)}) collective-permute-start(bf16[13,128,128]{2,1,0:T(8,128)(2,1)S(1)} %get-tuple-element.22), channel_id=1, source_target_pairs={{2,0},{3,1},{0,2},{1,3},{6,4},{7,5},{4,6},{5,7},{10,8},{11,9},{8,1... | collective-permute-start | bytes 1277960 | tf_op jit(solution)/shard_map/ppermute | solution.py:361
  4.4 1.6 %collective-permute-start.5 = (bf16[8,128,128]{2,1,0:T(8,128)(2,1)S(1)}, bf16[8,128,128]{2,1,0:T(8,128)(2,1)S(1)}, u32[]{:S(2)}, u32[]{:S(2)}) collective-permute-start(bf16[8,128,128]{2,1,0:T(8,128)(2,1)S(1)} %get-tuple-element.23), channel_id=1, source_target_pairs={{12,0},{13,1},{6,2},{7,3},{0,4},{1,5},{10,6},{11,7},{4,8},{5,9},{1... | collective-permute-start | bytes 786440 | tf_op jit(solution)/shard_map/ppermute | solution.py:361
  6.0 2.4 %collective-permute-start.1 = (bf16[6,128,128]{2,1,0:T(8,128)(2,1)S(1)}, bf16[6,128,128]{2,1,0:T(8,128)(2,1)S(1)}, u32[]{:S(2)}, u32[]{:S(2)}) collective-permute-start(bf16[6,128,128]{2,1,0:T(8,128)(2,1)S(1)} %get-tuple-element.20), channel_id=1, source_target_pairs={{14,0},{15,1},{4,2},{5,3},{2,4},{3,5},{8,6},{9,7},{6,8},{7,9},{12,... | collective-permute-start | bytes 589832 | tf_op jit(solution)/shard_map/ppermute | solution.py:361
  8.5 0.4 %collective-permute-start.2 = (bf16[5,128,128]{2,1,0:T(8,128)(2,1)S(1)}, bf16[5,128,128]{2,1,0:T(8,128)(2,1)S(1)}, u32[]{:S(2)}, u32[]{:S(2)}) collective-permute-start(bf16[5,128,128]{2,1,0:T(8,128)(2,1)S(1)} %get-tuple-element.21), channel_id=1, source_target_pairs={{4,0},{5,1},{14,2},{15,3},{8,4},{9,5},{2,6},{3,7},{12,8},{13,9},{6... | collective-permute-start | bytes 491528 | tf_op jit(solution)/shard_map/ppermute | solution.py:361
  9.6 0.0 collective-permute-done.left_other_ref
  9.6 1.4 %collective-permute-start.3 = (bf16[1,128,128]{2,1,0:T(8,128)(2,1)S(1)}, bf16[1,128,128]{2,1,0:T(8,128)(2,1)S(1)}, u32[]{:S(2)}, u32[]{:S(2)}) collective-permute-start(bf16[1,128,128]{2,1,0:T(8,128)(2,1)S(1)} %pack_e.1), channel_id=1, source_target_pairs={{10,0},{7,1},{12,2},{9,3},{14,4},{11,5},{0,6},{13,7},{2,8},{15,9},... | collective-permute-start | bytes 98312 | tf_op jit(solution)/shard_map/ppermute | solution.py:361
  11.1 2.4 %inner.1 = (s32[1,128]{1,0:T(1,128)S(1)}, f32[1,23,128,128]{3,2,1,0:T(8,128)}) custom-call(s32[1,23]{1,0:T(1,128)} %rows_ref.3, s32[1,23]{1,0:T(1,128)} %cols_ref.3, s32[1,1]{1,0:T(1,128)S(6)} %copy.7.counts_ref, bf16[384,1152]{1,0:T(8,128)(2,1)S(1)} %get-tuple-element.19.left_ref, bf16[384,1152]{1,0:T(8,128)(2,1)S(1)} %collective-permute-done.left_other_ref), custom_call_target="tpu_custom_call" | custom-call | flops 427819008 | bytes 1507328 | tf_op jit(solution)/shard_map/inner/pallas_call | solution.py:377
  13.4 2.0 %collective-permute-done.5.c_ref.refs_1_ = bf16[8,128,128]{2,1,0:T(8,128)(2,1)S(1)} collective-permute-done((bf16[8,128,128]{2,1,0:T(8,128)(2,1)S(1)}, bf16[8,128,128]{2,1,0:T(8,128)(2,1)S(1)}, u32[]{:S(2)}, u32[]{:S(2)}) %collective-permute-start.5) | collective-permute-done | bytes 262176 | tf_op jit(solution)/shard_map/ppermute | solution.py:361
  15.5 4.2 %collective-permute-done.4.a_ref.refs_0_ = bf16[13,128,128]{2,1,0:T(8,128)(2,1)S(1)} collective-permute-done((bf16[13,128,128]{2,1,0:T(8,128)(2,1)S(1)}, bf16[13,128,128]{2,1,0:T(8,128)(2,1)S(1)}, u32[]{:S(2)}, u32[]{:S(2)}) %collective-permute-start.4) | collective-permute-done | bytes 426016 | tf_op jit(solution)/shard_map/ppermute | solution.py:361
  19.7 0.2 stage_early.1
  19.8 0.1 collective-permute-start.7
  19.9 1.2 %early.1.old_ref = f32[27,128,128]{2,1,0:T(8,128)S(1)} custom-call(bf16[384,1152]{1,0:T(8,128)(2,1)S(1)} %get-tuple-element.19.left_ref, bf16[384,1152]{1,0:T(8,128)(2,1)S(1)} %collective-permute-done.left_other_ref, bf16[13,128,128]{2,1,0:T(8,128)(2,1)S(1)} %collective-permute-done.4.a_ref.refs_0_, bf16[8,128,128]{2,1,0:T(8,128)(2,1)S(1)} %collective-permute-done.5.c_ref.refs_1_), custom_call_target="tpu_custom_call" | custom-call | flops 4194304 | tf_op jit(solution)/shard_map/early/pallas_call | solution.py:409
  21.1 1.5 %collective-permute-done.2.refs_1_.d_ref = bf16[5,128,128]{2,1,0:T(8,128)(2,1)S(1)} collective-permute-done((bf16[5,128,128]{2,1,0:T(8,128)(2,1)S(1)}, bf16[5,128,128]{2,1,0:T(8,128)(2,1)S(1)}, u32[]{:S(2)}, u32[]{:S(2)}) %collective-permute-start.2) | collective-permute-done | bytes 163872 | tf_op jit(solution)/shard_map/ppermute | solution.py:361
  22.6 0.0 collective-permute-done.1.refs_0_.b_ref
  22.6 0.0 collective-permute-done.3.refs_2_.e_ref
  22.6 0.1 stage_late.1
  22.7 0.1 collective-permute-start.6
  22.8 0.5 %late.1.old_ref = f32[27,128,128]{2,1,0:T(8,128)S(1)} custom-call(bf16[384,1152]{1,0:T(8,128)(2,1)S(1)} %get-tuple-element.19.left_ref, bf16[384,1152]{1,0:T(8,128)(2,1)S(1)} %collective-permute-done.left_other_ref, bf16[6,128,128]{2,1,0:T(8,128)(2,1)S(1)} %collective-permute-done.1.refs_0_.b_ref, ...), custom_call_target="tpu_custom_call" | custom-call | flops 16777216000 | tf_op jit(solution)/shard_map/late/pallas_call | solution.py:409
  23.2 0.0 collective-permute-done.7.staged_ref
  23.3 0.6 %staged_early.1.old_ref = f32[27,128,128]{2,1,0:T(8,128)S(1)} custom-call(bf16[384,1152]{1,0:T(8,128)(2,1)S(1)} %get-tuple-element.19.left_ref, bf16[384,1152]{1,0:T(8,128)(2,1)S(1)} %collective-permute-done.left_other_ref, bf16[12,128,128]{2,1,0:T(8,128)(2,1)S(1)} %collective-permute-done.7.staged_ref, f32[27,128,128]{2,1,0:T(8,128)S(1)} %late.1.old_ref), custom_call_target="tpu_custom_call" | custom-call | flops 4194304 | tf_op jit(solution)/shard_map/staged_early/pallas_call | solution.py:409
  23.8 0.5 %collective-permute-done.6.staged_ref = bf16[8,128,128]{2,1,0:T(8,128)(2,1)S(1)} collective-permute-done((bf16[8,128,128]{2,1,0:T(8,128)(2,1)S(1)}, bf16[8,128,128]{2,1,0:T(8,128)(2,1)S(1)}, u32[]{:S(2)}, u32[]{:S(2)}) %collective-permute-start.6) | collective-permute-done | bytes 262176 | tf_op jit(solution)/shard_map/ppermute | solution.py:364
  24.3 1.5 %multiply.1 = f32[1,23,128,128]{3,2,1,0:T(8,128)} custom-call(bf16[384,1152]{1,0:T(8,128)(2,1)S(1)} %get-tuple-element.19.left_ref, bf16[384,1152]{1,0:T(8,128)(2,1)S(1)} %collective-permute-done.left_other_ref, bf16[8,128,128]{2,1,0:T(8,128)(2,1)S(1)} %collective-permute-done.6.staged_ref, ...), custom_call_target="tpu_custom_call", output_to_operand_aliasing={{}: (5, {})} | custom-call | tf_op jit(solution)/shard_map/multiply/pallas_call | solution.py:427
  (1 shorter events, 0.0 us)
Async XLA Ops:
  1.4 8.2 %collective-permute-start = (bf16[384,1152]{1,0:T(8,128)(2,1)S(1)}, bf16[384,1152]{1,0:T(8,128)(2,1)S(1)}, u32[]{:S(2)}, u32[]{:S(2)}) collective-permute-start(bf16[384,1152]{1,0:T(8,128)(2,1)S(1)} %get-tuple-element.19.left_ref), channel_id=1, source_target_pairs={{0,1},{1,0},{2,3},{3,2},{4,5},{5,4},{6,7},{7,6},{8,9},{9,8},{10,11... | collective-permute-start | bytes 2654216 | tf_op jit(solution)/shard_map/ppermute | solution.py:364
  1.9 17.8 %collective-permute-start.4 = (bf16[13,128,128]{2,1,0:T(8,128)(2,1)S(1)}, bf16[13,128,128]{2,1,0:T(8,128)(2,1)S(1)}, u32[]{:S(2)}, u32[]{:S(2)}) collective-permute-start(bf16[13,128,128]{2,1,0:T(8,128)(2,1)S(1)} %get-tuple-element.22), channel_id=1, source_target_pairs={{2,0},{3,1},{0,2},{1,3},{6,4},{7,5},{4,6},{5,7},{10,8},{11,9},{8,1... | collective-permute-start | bytes 1277960 | tf_op jit(solution)/shard_map/ppermute | solution.py:361
  4.4 11.0 %collective-permute-start.5 = (bf16[8,128,128]{2,1,0:T(8,128)(2,1)S(1)}, bf16[8,128,128]{2,1,0:T(8,128)(2,1)S(1)}, u32[]{:S(2)}, u32[]{:S(2)}) collective-permute-start(bf16[8,128,128]{2,1,0:T(8,128)(2,1)S(1)} %get-tuple-element.23), channel_id=1, source_target_pairs={{12,0},{13,1},{6,2},{7,3},{0,4},{1,5},{10,6},{11,7},{4,8},{5,9},{1... | collective-permute-start | bytes 786440 | tf_op jit(solution)/shard_map/ppermute | solution.py:361
  6.0 16.5 %collective-permute-start.1 = (bf16[6,128,128]{2,1,0:T(8,128)(2,1)S(1)}, bf16[6,128,128]{2,1,0:T(8,128)(2,1)S(1)}, u32[]{:S(2)}, u32[]{:S(2)}) collective-permute-start(bf16[6,128,128]{2,1,0:T(8,128)(2,1)S(1)} %get-tuple-element.20), channel_id=1, source_target_pairs={{14,0},{15,1},{4,2},{5,3},{2,4},{3,5},{8,6},{9,7},{6,8},{7,9},{12,... | collective-permute-start | bytes 589832 | tf_op jit(solution)/shard_map/ppermute | solution.py:361
  8.5 14.1 %collective-permute-start.2 = (bf16[5,128,128]{2,1,0:T(8,128)(2,1)S(1)}, bf16[5,128,128]{2,1,0:T(8,128)(2,1)S(1)}, u32[]{:S(2)}, u32[]{:S(2)}) collective-permute-start(bf16[5,128,128]{2,1,0:T(8,128)(2,1)S(1)} %get-tuple-element.21), channel_id=1, source_target_pairs={{4,0},{5,1},{14,2},{15,3},{8,4},{9,5},{2,6},{3,7},{12,8},{13,9},{6... | collective-permute-start | bytes 491528 | tf_op jit(solution)/shard_map/ppermute | solution.py:361
  9.6 12.9 %collective-permute-start.3 = (bf16[1,128,128]{2,1,0:T(8,128)(2,1)S(1)}, bf16[1,128,128]{2,1,0:T(8,128)(2,1)S(1)}, u32[]{:S(2)}, u32[]{:S(2)}) collective-permute-start(bf16[1,128,128]{2,1,0:T(8,128)(2,1)S(1)} %pack_e.1), channel_id=1, source_target_pairs={{10,0},{7,1},{12,2},{9,3},{14,4},{11,5},{0,6},{13,7},{2,8},{15,9},... | collective-permute-start | bytes 98312 | tf_op jit(solution)/shard_map/ppermute | solution.py:361
  19.8 3.4 %collective-permute-start.7 = (bf16[12,128,128]{2,1,0:T(8,128)(2,1)S(1)}, bf16[12,128,128]{2,1,0:T(8,128)(2,1)S(1)}, u32[]{:S(2)}, u32[]{:S(2)}) collective-permute-start(bf16[12,128,128]{2,1,0:T(8,128)(2,1)S(1)} %stage_early.1), channel_id=1, source_target_pairs={{0,1},{1,0},{2,3},{3,2},{4,5},{5,4},{6,7},{7,6},{8,9},{9,8},{10,11... | collective-permute-start | bytes 1179656 | tf_op jit(solution)/shard_map/ppermute | solution.py:364
  22.7 1.6 %collective-permute-start.6 = (bf16[8,128,128]{2,1,0:T(8,128)(2,1)S(1)}, bf16[8,128,128]{2,1,0:T(8,128)(2,1)S(1)}, u32[]{:S(2)}, u32[]{:S(2)}) collective-permute-start(bf16[8,128,128]{2,1,0:T(8,128)(2,1)S(1)} %stage_late.1), channel_id=1, source_target_pairs={{0,1},{1,0},{2,3},{3,2},{4,5},{5,4},{6,7},{7,6},{8,9},{9,8},{10,11... | collective-permute-start | bytes 786440 | tf_op jit(solution)/shard_map/ppermute | solution.py:364

commit v15 on v14

--- a/solution.py
+++ b/solution.py
@@ -266,8 +266,19 @@
             out_ref[n] = jnp.zeros((BLK, BLK), out_ref.dtype)
 
 
-def add_columns(refs, wanted, old_ref, new_ref, right, mine):
-    for pair, js in enumerate(outer_pairs(mine)):
+def late_columns(parity):
+    found = [[find_block(parity, k, j) for k in range(LOW, HIGH + 1)] for j in columns_of(parity)]
+    return [j for j, blocks in zip(columns_of(parity), found) if any(b is not None and b[0] == "late" for b in blocks)]
+
+
+def late_pairs(parity):
+    near = [j for j in late_columns(parity) if -BR <= j < 0]
+    rest = [j for j in late_columns(parity) if j not in near]
+    return [js[n : n + 2] for js in (near, rest) for n in range(0, len(js), 2)]
+
+
+def add_columns(refs, wanted, old_ref, new_ref, right, mine, pairs=outer_pairs):
+    for pair, js in enumerate(pairs(mine)):
         total = columns_product(refs, right.at[pair], mine, js, wanted)
         for i in range(BR):
             for y, j in enumerate(js):
@@ -291,6 +302,7 @@
 def staged_early_kernel(left_ref, left_other_ref, staged_ref, old_ref, out_ref, right):
     refs = {("left", True): left_ref, ("left", False): left_other_ref, "early": staged_ref}
     for_own_parity(functools.partial(add_columns, refs, ("early",), old_ref, out_ref, right))
+    out_ref[BR * NCOL] = jnp.zeros((BLK, BLK), out_ref.dtype)
 
 
 def multiply_kernel(left_ref, left_other_ref, staged_ref, old_ref, table_ref, _, out_ref, *rest):
@@ -302,11 +314,12 @@
 
     @for_own_parity
     def _(mine):
-        add_columns(refs, ("late",), old_ref, made, right, mine)
+        add_columns(refs, ("late",), old_ref, made, right, mine, late_pairs)
         load.wait()
         here = [place for place in stored_places(mine) if place not in inner_places(mine)]
+        late = [columns_of(mine).index(j) for j in late_columns(mine)]
         for place in here:
-            store(made, table, out_ref, place, out_sem)
+            store(made if place % NCOL in late else old_ref, table, out_ref, place, out_sem)
         wait_for(len(here), made, out_ref, out_sem)
 
 
@@ -408,7 +421,7 @@
     def added(kernel, name, products, arrays):
         return pl.pallas_call(
             kernel,
-            out_shape=blocks(BR * NCOL, jnp.float32),
+            out_shape=blocks(BR * NCOL + 1, jnp.float32),
             in_specs=[vmem] * len(arrays),
             out_specs=vmem,
             scratch_shapes=[right_scratch(4)],

time: 26 us -> 26 us (level)
  no operation moved by 1% of the time
where the time goes in v15:
time: 26 us; the launch traced here: 25.8 us
  starting transfers between devices  9.12 us (35%)
  waiting for transfers between devices  8.17 us (31%)
  Pallas kernels  7.76 us (30%)
  between operations  0.75 us (3%)
    ppermute x5, starting transfers between devices, towards(): return lax.ppermute(message, ('row', 'col'), pairs)  8.47 us
    ppermute x5, waiting for transfers between devices, towards(): return lax.ppermute(message, ('row', 'col'), pairs)  7.69 us
    pallas_call x1, Pallas kernels, local(): pl.pallas_call(functools.partial(inner_kernel, nblocks, slots), out_shape...  2.39 us
    pallas_call x3, Pallas kernels, added(): pl.pallas_call(kernel, out_shape=blocks(BR * NCOL + 1, jnp.float32), in_s...  2.19 us
    pallas_call x1, Pallas kernels, local(): pl.pallas_call(multiply_kernel, out_shape=jax.ShapeDtypeStruct(values.sha...  1.51 us
    pallas_call x1, Pallas kernels, local(): pl.pallas_call(functools.partial(pack_kernel, nblocks, slots), out_shape=...  1.36 us
    ppermute x3, starting transfers between devices, swapped(): return lax.ppermute(block, 'col', [(0, 1), (1, 0)])  0.66 us
  transfers between devices with their start and end apart: 8, of which 4 were waited for; matrix products, arithmetic and copies ran while one was open for 0% of the time, Pallas kernels for 19%

profile of v15, /device:TPU:0, one launch (start us, length us, event | category | flops | bytes accessed | tf_op | source)
XLA Modules:
  0.0 25.8 jit_solution(16993980286474777448)
XLA Ops:
  0.0 1.4 %pack.1 = (bf16[13,128,128]{2,1,0:T(8,128)(2,1)S(1)}, bf16[6,128,128]{2,1,0:T(8,128)(2,1)S(1)}, bf16[8,128,128]{2,1,0:T(8,128)(2,1)S(1)}, bf16[5,128,128]{2,1,0:T(8,128)(2,1)S(1)}, bf16[384,1152]{1,0:T(8,128)(2,1)S(1)}) custom-call(s32[1,23]{1,0:T(1,128)} %rows_ref.3, s32[1,23]{1,0:T(1,128)} %cols_ref.3, bf16[1,23,128,128]{3,2,1,0:T(8,128)(2,1)} %values_ref.1), custom_call_target="tpu_custom_call" | custom-call | tf_op jit(solution)/shard_map/pack/pallas_call | solution.py:351
  1.4 0.5 %collective-permute-start = (bf16[384,1152]{1,0:T(8,128)(2,1)S(1)}, bf16[384,1152]{1,0:T(8,128)(2,1)S(1)}, u32[]{:S(2)}, u32[]{:S(2)}) collective-permute-start(bf16[384,1152]{1,0:T(8,128)(2,1)S(1)} %get-tuple-element.19.left_ref), channel_id=1, source_target_pairs={{0,1},{1,0},{2,3},{3,2},{4,5},{5,4},{6,7},{7,6},{8,9},{9,8},{10,11... | collective-permute-start | bytes 2654216 | tf_op jit(solution)/shard_map/ppermute | solution.py:377
  1.9 2.6 %collective-permute-start.4 = (bf16[13,128,128]{2,1,0:T(8,128)(2,1)S(1)}, bf16[13,128,128]{2,1,0:T(8,128)(2,1)S(1)}, u32[]{:S(2)}, u32[]{:S(2)}) collective-permute-start(bf16[13,128,128]{2,1,0:T(8,128)(2,1)S(1)} %get-tuple-element.22), channel_id=1, source_target_pairs={{2,0},{3,1},{0,2},{1,3},{6,4},{7,5},{4,6},{5,7},{10,8},{11,9},{8,1... | collective-permute-start | bytes 1277960 | tf_op jit(solution)/shard_map/ppermute | solution.py:374
  4.4 1.6 %collective-permute-start.5 = (bf16[8,128,128]{2,1,0:T(8,128)(2,1)S(1)}, bf16[8,128,128]{2,1,0:T(8,128)(2,1)S(1)}, u32[]{:S(2)}, u32[]{:S(2)}) collective-permute-start(bf16[8,128,128]{2,1,0:T(8,128)(2,1)S(1)} %get-tuple-element.23), channel_id=1, source_target_pairs={{12,0},{13,1},{6,2},{7,3},{0,4},{1,5},{10,6},{11,7},{4,8},{5,9},{1... | collective-permute-start | bytes 786440 | tf_op jit(solution)/shard_map/ppermute | solution.py:374
  6.0 2.4 %collective-permute-start.1 = (bf16[6,128,128]{2,1,0:T(8,128)(2,1)S(1)}, bf16[6,128,128]{2,1,0:T(8,128)(2,1)S(1)}, u32[]{:S(2)}, u32[]{:S(2)}) collective-permute-start(bf16[6,128,128]{2,1,0:T(8,128)(2,1)S(1)} %get-tuple-element.20), channel_id=1, source_target_pairs={{14,0},{15,1},{4,2},{5,3},{2,4},{3,5},{8,6},{9,7},{6,8},{7,9},{12,... | collective-permute-start | bytes 589832 | tf_op jit(solution)/shard_map/ppermute | solution.py:374
  8.5 0.4 %collective-permute-start.2 = (bf16[5,128,128]{2,1,0:T(8,128)(2,1)S(1)}, bf16[5,128,128]{2,1,0:T(8,128)(2,1)S(1)}, u32[]{:S(2)}, u32[]{:S(2)}) collective-permute-start(bf16[5,128,128]{2,1,0:T(8,128)(2,1)S(1)} %get-tuple-element.21), channel_id=1, source_target_pairs={{4,0},{5,1},{14,2},{15,3},{8,4},{9,5},{2,6},{3,7},{12,8},{13,9},{6... | collective-permute-start | bytes 491528 | tf_op jit(solution)/shard_map/ppermute | solution.py:374
  9.6 0.0 collective-permute-done.left_other_ref
  9.6 1.4 %collective-permute-start.3 = (bf16[1,128,128]{2,1,0:T(8,128)(2,1)S(1)}, bf16[1,128,128]{2,1,0:T(8,128)(2,1)S(1)}, u32[]{:S(2)}, u32[]{:S(2)}) collective-permute-start(bf16[1,128,128]{2,1,0:T(8,128)(2,1)S(1)} %pack_e.1), channel_id=1, source_target_pairs={{10,0},{7,1},{12,2},{9,3},{14,4},{11,5},{0,6},{13,7},{2,8},{15,9},... | collective-permute-start | bytes 98312 | tf_op jit(solution)/shard_map/ppermute | solution.py:374
  11.1 2.4 %inner.1 = (s32[1,128]{1,0:T(1,128)S(1)}, f32[1,23,128,128]{3,2,1,0:T(8,128)}) custom-call(s32[1,23]{1,0:T(1,128)} %rows_ref.3, s32[1,23]{1,0:T(1,128)} %cols_ref.3, s32[1,1]{1,0:T(1,128)S(6)} %copy.7.counts_ref, bf16[384,1152]{1,0:T(8,128)(2,1)S(1)} %get-tuple-element.19.left_ref, bf16[384,1152]{1,0:T(8,128)(2,1)S(1)} %collective-permute-done.left_other_ref), custom_call_target="tpu_custom_call" | custom-call | flops 427819008 | bytes 1507328 | tf_op jit(solution)/shard_map/inner/pallas_call | solution.py:390
  13.4 2.0 %collective-permute-done.5.c_ref.refs_1_ = bf16[8,128,128]{2,1,0:T(8,128)(2,1)S(1)} collective-permute-done((bf16[8,128,128]{2,1,0:T(8,128)(2,1)S(1)}, bf16[8,128,128]{2,1,0:T(8,128)(2,1)S(1)}, u32[]{:S(2)}, u32[]{:S(2)}) %collective-permute-start.5) | collective-permute-done | bytes 262176 | tf_op jit(solution)/shard_map/ppermute | solution.py:374
  15.5 4.2 %collective-permute-done.4.a_ref.refs_0_ = bf16[13,128,128]{2,1,0:T(8,128)(2,1)S(1)} collective-permute-done((bf16[13,128,128]{2,1,0:T(8,128)(2,1)S(1)}, bf16[13,128,128]{2,1,0:T(8,128)(2,1)S(1)}, u32[]{:S(2)}, u32[]{:S(2)}) %collective-permute-start.4) | collective-permute-done | bytes 426016 | tf_op jit(solution)/shard_map/ppermute | solution.py:374
  19.7 0.2 stage_early.1
  19.8 0.1 collective-permute-start.7
  19.9 1.2 %early.1.old_ref = f32[28,128,128]{2,1,0:T(8,128)S(1)} custom-call(bf16[384,1152]{1,0:T(8,128)(2,1)S(1)} %get-tuple-element.19.left_ref, bf16[384,1152]{1,0:T(8,128)(2,1)S(1)} %collective-permute-done.left_other_ref, bf16[13,128,128]{2,1,0:T(8,128)(2,1)S(1)} %collective-permute-done.4.a_ref.refs_0_, bf16[8,128,128]{2,1,0:T(8,128)(2,1)S(1)} %collective-permute-done.5.c_ref.refs_1_), custom_call_target="tpu_custom_call" | custom-call | flops 4194304 | tf_op jit(solution)/shard_map/early/pallas_call | solution.py:422
  21.1 1.5 %collective-permute-done.2.refs_1_.d_ref = bf16[5,128,128]{2,1,0:T(8,128)(2,1)S(1)} collective-permute-done((bf16[5,128,128]{2,1,0:T(8,128)(2,1)S(1)}, bf16[5,128,128]{2,1,0:T(8,128)(2,1)S(1)}, u32[]{:S(2)}, u32[]{:S(2)}) %collective-permute-start.2) | collective-permute-done | bytes 163872 | tf_op jit(solution)/shard_map/ppermute | solution.py:374
  22.6 0.0 collective-permute-done.1.refs_0_.b_ref
  22.6 0.0 collective-permute-done.3.refs_2_.e_ref
  22.6 0.1 stage_late.1
  22.7 0.1 collective-permute-start.6
  22.8 0.5 %late.1.old_ref = f32[28,128,128]{2,1,0:T(8,128)S(1)} custom-call(bf16[384,1152]{1,0:T(8,128)(2,1)S(1)} %get-tuple-element.19.left_ref, bf16[384,1152]{1,0:T(8,128)(2,1)S(1)} %collective-permute-done.left_other_ref, bf16[6,128,128]{2,1,0:T(8,128)(2,1)S(1)} %collective-permute-done.1.refs_0_.b_ref, ...), custom_call_target="tpu_custom_call" | custom-call | flops 16777216000 | tf_op jit(solution)/shard_map/late/pallas_call | solution.py:422
  23.2 0.0 collective-permute-done.7.staged_ref
  23.3 0.6 %staged_early.1.old_ref = f32[28,128,128]{2,1,0:T(8,128)S(1)} custom-call(bf16[384,1152]{1,0:T(8,128)(2,1)S(1)} %get-tuple-element.19.left_ref, bf16[384,1152]{1,0:T(8,128)(2,1)S(1)} %collective-permute-done.left_other_ref, bf16[12,128,128]{2,1,0:T(8,128)(2,1)S(1)} %collective-permute-done.7.staged_ref, f32[28,128,128]{2,1,0:T(8,128)S(1)} %late.1.old_ref), custom_call_target="tpu_custom_call" | custom-call | flops 4194304 | tf_op jit(solution)/shard_map/staged_early/pallas_call | solution.py:422
  23.8 0.5 %collective-permute-done.6.staged_ref = bf16[8,128,128]{2,1,0:T(8,128)(2,1)S(1)} collective-permute-done((bf16[8,128,128]{2,1,0:T(8,128)(2,1)S(1)}, bf16[8,128,128]{2,1,0:T(8,128)(2,1)S(1)}, u32[]{:S(2)}, u32[]{:S(2)}) %collective-permute-start.6) | collective-permute-done | bytes 262176 | tf_op jit(solution)/shard_map/ppermute | solution.py:377
  24.3 1.5 %multiply.1 = f32[1,23,128,128]{3,2,1,0:T(8,128)} custom-call(bf16[384,1152]{1,0:T(8,128)(2,1)S(1)} %get-tuple-element.19.left_ref, bf16[384,1152]{1,0:T(8,128)(2,1)S(1)} %collective-permute-done.left_other_ref, bf16[8,128,128]{2,1,0:T(8,128)(2,1)S(1)} %collective-permute-done.6.staged_ref, ...), custom_call_target="tpu_custom_call", output_to_operand_aliasing={{}: (5, {})} | custom-call | tf_op jit(solution)/shard_map/multiply/pallas_call | solution.py:440
  (1 shorter events, 0.0 us)
Async XLA Ops:
  1.4 8.2 %collective-permute-start = (bf16[384,1152]{1,0:T(8,128)(2,1)S(1)}, bf16[384,1152]{1,0:T(8,128)(2,1)S(1)}, u32[]{:S(2)}, u32[]{:S(2)}) collective-permute-start(bf16[384,1152]{1,0:T(8,128)(2,1)S(1)} %get-tuple-element.19.left_ref), channel_id=1, source_target_pairs={{0,1},{1,0},{2,3},{3,2},{4,5},{5,4},{6,7},{7,6},{8,9},{9,8},{10,11... | collective-permute-start | bytes 2654216 | tf_op jit(solution)/shard_map/ppermute | solution.py:377
  1.9 17.8 %collective-permute-start.4 = (bf16[13,128,128]{2,1,0:T(8,128)(2,1)S(1)}, bf16[13,128,128]{2,1,0:T(8,128)(2,1)S(1)}, u32[]{:S(2)}, u32[]{:S(2)}) collective-permute-start(bf16[13,128,128]{2,1,0:T(8,128)(2,1)S(1)} %get-tuple-element.22), channel_id=1, source_target_pairs={{2,0},{3,1},{0,2},{1,3},{6,4},{7,5},{4,6},{5,7},{10,8},{11,9},{8,1... | collective-permute-start | bytes 1277960 | tf_op jit(solution)/shard_map/ppermute | solution.py:374
  4.4 11.0 %collective-permute-start.5 = (bf16[8,128,128]{2,1,0:T(8,128)(2,1)S(1)}, bf16[8,128,128]{2,1,0:T(8,128)(2,1)S(1)}, u32[]{:S(2)}, u32[]{:S(2)}) collective-permute-start(bf16[8,128,128]{2,1,0:T(8,128)(2,1)S(1)} %get-tuple-element.23), channel_id=1, source_target_pairs={{12,0},{13,1},{6,2},{7,3},{0,4},{1,5},{10,6},{11,7},{4,8},{5,9},{1... | collective-permute-start | bytes 786440 | tf_op jit(solution)/shard_map/ppermute | solution.py:374
  6.0 16.5 %collective-permute-start.1 = (bf16[6,128,128]{2,1,0:T(8,128)(2,1)S(1)}, bf16[6,128,128]{2,1,0:T(8,128)(2,1)S(1)}, u32[]{:S(2)}, u32[]{:S(2)}) collective-permute-start(bf16[6,128,128]{2,1,0:T(8,128)(2,1)S(1)} %get-tuple-element.20), channel_id=1, source_target_pairs={{14,0},{15,1},{4,2},{5,3},{2,4},{3,5},{8,6},{9,7},{6,8},{7,9},{12,... | collective-permute-start | bytes 589832 | tf_op jit(solution)/shard_map/ppermute | solution.py:374
  8.5 14.1 %collective-permute-start.2 = (bf16[5,128,128]{2,1,0:T(8,128)(2,1)S(1)}, bf16[5,128,128]{2,1,0:T(8,128)(2,1)S(1)}, u32[]{:S(2)}, u32[]{:S(2)}) collective-permute-start(bf16[5,128,128]{2,1,0:T(8,128)(2,1)S(1)} %get-tuple-element.21), channel_id=1, source_target_pairs={{4,0},{5,1},{14,2},{15,3},{8,4},{9,5},{2,6},{3,7},{12,8},{13,9},{6... | collective-permute-start | bytes 491528 | tf_op jit(solution)/shard_map/ppermute | solution.py:374
  9.6 12.9 %collective-permute-start.3 = (bf16[1,128,128]{2,1,0:T(8,128)(2,1)S(1)}, bf16[1,128,128]{2,1,0:T(8,128)(2,1)S(1)}, u32[]{:S(2)}, u32[]{:S(2)}) collective-permute-start(bf16[1,128,128]{2,1,0:T(8,128)(2,1)S(1)} %pack_e.1), channel_id=1, source_target_pairs={{10,0},{7,1},{12,2},{9,3},{14,4},{11,5},{0,6},{13,7},{2,8},{15,9},... | collective-permute-start | bytes 98312 | tf_op jit(solution)/shard_map/ppermute | solution.py:374
  19.8 3.4 %collective-permute-start.7 = (bf16[12,128,128]{2,1,0:T(8,128)(2,1)S(1)}, bf16[12,128,128]{2,1,0:T(8,128)(2,1)S(1)}, u32[]{:S(2)}, u32[]{:S(2)}) collective-permute-start(bf16[12,128,128]{2,1,0:T(8,128)(2,1)S(1)} %stage_early.1), channel_id=1, source_target_pairs={{0,1},{1,0},{2,3},{3,2},{4,5},{5,4},{6,7},{7,6},{8,9},{9,8},{10,11... | collective-permute-start | bytes 1179656 | tf_op jit(solution)/shard_map/ppermute | solution.py:377
  22.7 1.6 %collective-permute-start.6 = (bf16[8,128,128]{2,1,0:T(8,128)(2,1)S(1)}, bf16[8,128,128]{2,1,0:T(8,128)(2,1)S(1)}, u32[]{:S(2)}, u32[]{:S(2)}) collective-permute-start(bf16[8,128,128]{2,1,0:T(8,128)(2,1)S(1)} %stage_late.1), channel_id=1, source_target_pairs={{0,1},{1,0},{2,3},{3,2},{4,5},{5,4},{6,7},{7,6},{8,9},{9,8},{10,11... | collective-permute-start | bytes 786440 | tf_op jit(solution)/shard_map/ppermute | solution.py:377

commit v16 on v15

--- a/solution.py
+++ b/solution.py
@@ -196,7 +196,7 @@
 
 
 def inner_kernel(nblocks, slots, rows_ref, cols_ref, counts_ref, left_ref, left_other_ref, *rest):
-    table_ref, out_ref, right, made, table, *index, sems, table_sem, out_sem = rest
+    table, out_ref, right, made, *index, sems, out_sem = rest
     copies = index_copies((rows_ref, cols_ref), index, sems)
     for copy in copies:
         copy.start()
@@ -240,10 +240,6 @@
             stored += 1
         wait_for(stored, made, out_ref, out_sem)
 
-    copy = pltpu.make_async_copy(table, table_ref, table_sem)
-    copy.start()
-    copy.wait()
-
 
 def pack_e_kernel(left_ref, left_other_ref, e_ref):
     @for_own_parity
@@ -305,21 +301,22 @@
     out_ref[BR * NCOL] = jnp.zeros((BLK, BLK), out_ref.dtype)
 
 
-def multiply_kernel(left_ref, left_other_ref, staged_ref, old_ref, table_ref, _, out_ref, *rest):
-    right, made, table, table_sem, out_sem = rest
+def multiply_kernel(left_ref, left_other_ref, staged_ref, old_ref, table, _, out_ref, *rest):
+    right, made, out_sem = rest
     refs = {("left", True): left_ref, ("left", False): left_other_ref, "late": staged_ref}
-    load = pltpu.make_async_copy(table_ref, table, table_sem)
-    load.start()
     made[BR * NCOL] = jnp.zeros((BLK, BLK), made.dtype)
 
     @for_own_parity
     def _(mine):
-        add_columns(refs, ("late",), old_ref, made, right, mine, late_pairs)
-        load.wait()
         here = [place for place in stored_places(mine) if place not in inner_places(mine)]
         late = [columns_of(mine).index(j) for j in late_columns(mine)]
         for place in here:
-            store(made if place % NCOL in late else old_ref, table, out_ref, place, out_sem)
+            if place % NCOL not in late:
+                store(old_ref, table, out_ref, place, out_sem)
+        add_columns(refs, ("late",), old_ref, made, right, mine, late_pairs)
+        for place in here:
+            if place % NCOL in late:
+                store(made, table, out_ref, place, out_sem)
         wait_for(len(here), made, out_ref, out_sem)
 
 
@@ -389,15 +386,13 @@
     got.append(towards("e", message))
     table, out = pl.pallas_call(
         functools.partial(inner_kernel, nblocks, slots),
-        out_shape=[jax.ShapeDtypeStruct(table_shape, jnp.int32), jax.ShapeDtypeStruct(values.shape, jnp.float32)],
+        out_shape=[pltpu.SMEM(table_shape, jnp.int32), jax.ShapeDtypeStruct(values.shape, jnp.float32)],
         in_specs=[hbm] * 2 + [smem] + [vmem] * 2,
-        out_specs=[vmem, hbm],
+        out_specs=[smem, hbm],
         scratch_shapes=[
             pltpu.VMEM((2, NCOL * BLK, 2 * BLK), values.dtype),
             pltpu.VMEM((BR * NCOL + 1, BLK, BLK), jnp.float32),
-            pltpu.SMEM(table_shape, jnp.int32),
             *index_scratch,
-            pltpu.SemaphoreType.DMA,
             pltpu.SemaphoreType.DMA,
         ],
         compiler_params=params,
@@ -440,19 +435,17 @@
     return pl.pallas_call(
         multiply_kernel,
         out_shape=jax.ShapeDtypeStruct(values.shape, jnp.float32),
-        in_specs=[vmem] * 5 + [hbm],
+        in_specs=[vmem] * 4 + [smem, hbm],
         out_specs=hbm,
         scratch_shapes=[
             right_scratch(4),
             pltpu.VMEM((BR * NCOL + 1, BLK, BLK), jnp.float32),
-            pltpu.SMEM(table_shape, jnp.int32),
-            pltpu.SemaphoreType.DMA,
             pltpu.SemaphoreType.DMA,
         ],
         input_output_aliases={5: 0},
         compiler_params=params,
         name="multiply",
-    )(left, left_other, staged_late, total, table, out)
+    )(left, left_other, staged_late, total, pltpu.with_memory_space_constraint(table, pltpu.SMEM), out)
 
 
 def solution(mesh):

time: 26 us -> 25.7 us (0.988)
  Pallas kernels: 7.76 us -> 6.98 us
  waiting for transfers between devices: 8.17 us -> 8.62 us
    ppermute x5, waiting for transfers between devices: 7.69 us -> 8.14 us  [towards(): return lax.ppermute(message, ('row', 'col'), pairs)]
    pallas_call x1, Pallas kernels: 2.39 us -> 1.93 us  [local(): pl.pallas_call(functools.partial(inner_kernel, nblocks, slots), out_shape...]
    pallas_call x1, Pallas kernels: 1.51 us -> 1.18 us  [local(): pl.pallas_call(multiply_kernel, out_shape=jax.ShapeDtypeStruct(values.sha...]
  transfers between devices with their start and end apart: 8 -> 8, of which waited for: 4 -> 4; matrix products, arithmetic and copies ran while one was open for 0% -> 0% of each run, Pallas kernels for 19% -> 17%
where the time goes in v16:
time: 25.7 us; the launch traced here: 25.5 us
  starting transfers between devices  9.12 us (35%)
  waiting for transfers between devices  8.62 us (34%)
  Pallas kernels  6.98 us (27%)
  between operations  0.75 us (3%)
    ppermute x5, starting transfers between devices, towards(): return lax.ppermute(message, ('row', 'col'), pairs)  8.47 us
    ppermute x5, waiting for transfers between devices, towards(): return lax.ppermute(message, ('row', 'col'), pairs)  8.14 us
    pallas_call x3, Pallas kernels, added(): pl.pallas_call(kernel, out_shape=blocks(BR * NCOL + 1, jnp.float32), in_s...  2.19 us
    pallas_call x1, Pallas kernels, local(): pl.pallas_call(functools.partial(inner_kernel, nblocks, slots), out_shape...  1.93 us
    pallas_call x1, Pallas kernels, local(): pl.pallas_call(functools.partial(pack_kernel, nblocks, slots), out_shape=...  1.36 us
    pallas_call x1, Pallas kernels, local(): pl.pallas_call(multiply_kernel, out_shape=jax.ShapeDtypeStruct(values.sha...  1.18 us
    ppermute x3, starting transfers between devices, swapped(): return lax.ppermute(block, 'col', [(0, 1), (1, 0)])  0.66 us
  transfers between devices with their start and end apart: 8, of which 4 were waited for; matrix products, arithmetic and copies ran while one was open for 0% of the time, Pallas kernels for 17%

profile of v16, /device:TPU:0, one launch (start us, length us, event | category | flops | bytes accessed | tf_op | source)
XLA Modules:
  0.0 25.5 jit_solution(17667907264857466147)
XLA Ops:
  0.0 1.4 %pack.1 = (bf16[13,128,128]{2,1,0:T(8,128)(2,1)S(1)}, bf16[6,128,128]{2,1,0:T(8,128)(2,1)S(1)}, bf16[8,128,128]{2,1,0:T(8,128)(2,1)S(1)}, bf16[5,128,128]{2,1,0:T(8,128)(2,1)S(1)}, bf16[384,1152]{1,0:T(8,128)(2,1)S(1)}) custom-call(s32[1,23]{1,0:T(1,128)} %rows_ref.3, s32[1,23]{1,0:T(1,128)} %cols_ref.3, bf16[1,23,128,128]{3,2,1,0:T(8,128)(2,1)} %values_ref.1), custom_call_target="tpu_custom_call" | custom-call | tf_op jit(solution)/shard_map/pack/pallas_call | solution.py:348
  1.4 0.5 %collective-permute-start = (bf16[384,1152]{1,0:T(8,128)(2,1)S(1)}, bf16[384,1152]{1,0:T(8,128)(2,1)S(1)}, u32[]{:S(2)}, u32[]{:S(2)}) collective-permute-start(bf16[384,1152]{1,0:T(8,128)(2,1)S(1)} %get-tuple-element.19.left_ref), channel_id=1, source_target_pairs={{0,1},{1,0},{2,3},{3,2},{4,5},{5,4},{6,7},{7,6},{8,9},{9,8},{10,11... | collective-permute-start | bytes 2654216 | tf_op jit(solution)/shard_map/ppermute | solution.py:374
  1.9 2.6 %collective-permute-start.4 = (bf16[13,128,128]{2,1,0:T(8,128)(2,1)S(1)}, bf16[13,128,128]{2,1,0:T(8,128)(2,1)S(1)}, u32[]{:S(2)}, u32[]{:S(2)}) collective-permute-start(bf16[13,128,128]{2,1,0:T(8,128)(2,1)S(1)} %get-tuple-element.22), channel_id=1, source_target_pairs={{2,0},{3,1},{0,2},{1,3},{6,4},{7,5},{4,6},{5,7},{10,8},{11,9},{8,1... | collective-permute-start | bytes 1277960 | tf_op jit(solution)/shard_map/ppermute | solution.py:371
  4.4 1.6 %collective-permute-start.5 = (bf16[8,128,128]{2,1,0:T(8,128)(2,1)S(1)}, bf16[8,128,128]{2,1,0:T(8,128)(2,1)S(1)}, u32[]{:S(2)}, u32[]{:S(2)}) collective-permute-start(bf16[8,128,128]{2,1,0:T(8,128)(2,1)S(1)} %get-tuple-element.23), channel_id=1, source_target_pairs={{12,0},{13,1},{6,2},{7,3},{0,4},{1,5},{10,6},{11,7},{4,8},{5,9},{1... | collective-permute-start | bytes 786440 | tf_op jit(solution)/shard_map/ppermute | solution.py:371
  6.0 2.4 %collective-permute-start.1 = (bf16[6,128,128]{2,1,0:T(8,128)(2,1)S(1)}, bf16[6,128,128]{2,1,0:T(8,128)(2,1)S(1)}, u32[]{:S(2)}, u32[]{:S(2)}) collective-permute-start(bf16[6,128,128]{2,1,0:T(8,128)(2,1)S(1)} %get-tuple-element.20), channel_id=1, source_target_pairs={{14,0},{15,1},{4,2},{5,3},{2,4},{3,5},{8,6},{9,7},{6,8},{7,9},{12,... | collective-permute-start | bytes 589832 | tf_op jit(solution)/shard_map/ppermute | solution.py:371
  8.5 0.4 %collective-permute-start.2 = (bf16[5,128,128]{2,1,0:T(8,128)(2,1)S(1)}, bf16[5,128,128]{2,1,0:T(8,128)(2,1)S(1)}, u32[]{:S(2)}, u32[]{:S(2)}) collective-permute-start(bf16[5,128,128]{2,1,0:T(8,128)(2,1)S(1)} %get-tuple-element.21), channel_id=1, source_target_pairs={{4,0},{5,1},{14,2},{15,3},{8,4},{9,5},{2,6},{3,7},{12,8},{13,9},{6... | collective-permute-start | bytes 491528 | tf_op jit(solution)/shard_map/ppermute | solution.py:371
  9.6 0.0 collective-permute-done.left_other_ref
  9.6 1.4 %collective-permute-start.3 = (bf16[1,128,128]{2,1,0:T(8,128)(2,1)S(1)}, bf16[1,128,128]{2,1,0:T(8,128)(2,1)S(1)}, u32[]{:S(2)}, u32[]{:S(2)}) collective-permute-start(bf16[1,128,128]{2,1,0:T(8,128)(2,1)S(1)} %pack_e.1), channel_id=1, source_target_pairs={{10,0},{7,1},{12,2},{9,3},{14,4},{11,5},{0,6},{13,7},{2,8},{15,9},... | collective-permute-start | bytes 98312 | tf_op jit(solution)/shard_map/ppermute | solution.py:371
  11.1 1.9 %inner.1 = (s32[1,128]{1,0:T(1,128)S(4)}, f32[1,23,128,128]{3,2,1,0:T(8,128)}) custom-call(s32[1,23]{1,0:T(1,128)} %rows_ref.3, s32[1,23]{1,0:T(1,128)} %cols_ref.3, s32[1,1]{1,0:T(1,128)S(6)} %copy.7.counts_ref, bf16[384,1152]{1,0:T(8,128)(2,1)S(1)} %get-tuple-element.19.left_ref, bf16[384,1152]{1,0:T(8,128)(2,1)S(1)} %collective-permute-done.left_other_ref), custom_call_target="tpu_custom_call" | custom-call | flops 427819008 | bytes 1507328 | tf_op jit(solution)/shard_map/inner/pallas_call | solution.py:387
  13.0 2.5 %collective-permute-done.5.c_ref.refs_1_ = bf16[8,128,128]{2,1,0:T(8,128)(2,1)S(1)} collective-permute-done((bf16[8,128,128]{2,1,0:T(8,128)(2,1)S(1)}, bf16[8,128,128]{2,1,0:T(8,128)(2,1)S(1)}, u32[]{:S(2)}, u32[]{:S(2)}) %collective-permute-start.5) | collective-permute-done | bytes 262176 | tf_op jit(solution)/shard_map/ppermute | solution.py:371
  15.5 4.2 %collective-permute-done.4.a_ref.refs_0_ = bf16[13,128,128]{2,1,0:T(8,128)(2,1)S(1)} collective-permute-done((bf16[13,128,128]{2,1,0:T(8,128)(2,1)S(1)}, bf16[13,128,128]{2,1,0:T(8,128)(2,1)S(1)}, u32[]{:S(2)}, u32[]{:S(2)}) %collective-permute-start.4) | collective-permute-done | bytes 426016 | tf_op jit(solution)/shard_map/ppermute | solution.py:371
  19.7 0.2 stage_early.1
  19.8 0.1 collective-permute-start.7
  19.9 1.2 %early.1.old_ref = f32[28,128,128]{2,1,0:T(8,128)S(1)} custom-call(bf16[384,1152]{1,0:T(8,128)(2,1)S(1)} %get-tuple-element.19.left_ref, bf16[384,1152]{1,0:T(8,128)(2,1)S(1)} %collective-permute-done.left_other_ref, bf16[13,128,128]{2,1,0:T(8,128)(2,1)S(1)} %collective-permute-done.4.a_ref.refs_0_, bf16[8,128,128]{2,1,0:T(8,128)(2,1)S(1)} %collective-permute-done.5.c_ref.refs_1_), custom_call_target="tpu_custom_call" | custom-call | flops 4194304 | tf_op jit(solution)/shard_map/early/pallas_call | solution.py:417
  21.1 1.5 %collective-permute-done.2.refs_1_.d_ref = bf16[5,128,128]{2,1,0:T(8,128)(2,1)S(1)} collective-permute-done((bf16[5,128,128]{2,1,0:T(8,128)(2,1)S(1)}, bf16[5,128,128]{2,1,0:T(8,128)(2,1)S(1)}, u32[]{:S(2)}, u32[]{:S(2)}) %collective-permute-start.2) | collective-permute-done | bytes 163872 | tf_op jit(solution)/shard_map/ppermute | solution.py:371
  22.6 0.0 collective-permute-done.1.refs_0_.b_ref
  22.6 0.0 collective-permute-done.3.refs_2_.e_ref
  22.6 0.1 stage_late.1
  22.7 0.1 collective-permute-start.6
  22.8 0.5 %late.1.old_ref = f32[28,128,128]{2,1,0:T(8,128)S(1)} custom-call(bf16[384,1152]{1,0:T(8,128)(2,1)S(1)} %get-tuple-element.19.left_ref, bf16[384,1152]{1,0:T(8,128)(2,1)S(1)} %collective-permute-done.left_other_ref, bf16[6,128,128]{2,1,0:T(8,128)(2,1)S(1)} %collective-permute-done.1.refs_0_.b_ref, ...), custom_call_target="tpu_custom_call" | custom-call | flops 16777216000 | tf_op jit(solution)/shard_map/late/pallas_call | solution.py:417
  23.2 0.0 collective-permute-done.7.staged_ref
  23.3 0.6 %staged_early.1.old_ref = f32[28,128,128]{2,1,0:T(8,128)S(1)} custom-call(bf16[384,1152]{1,0:T(8,128)(2,1)S(1)} %get-tuple-element.19.left_ref, bf16[384,1152]{1,0:T(8,128)(2,1)S(1)} %collective-permute-done.left_other_ref, bf16[12,128,128]{2,1,0:T(8,128)(2,1)S(1)} %collective-permute-done.7.staged_ref, f32[28,128,128]{2,1,0:T(8,128)S(1)} %late.1.old_ref), custom_call_target="tpu_custom_call" | custom-call | flops 4194304 | tf_op jit(solution)/shard_map/staged_early/pallas_call | solution.py:417
  23.8 0.5 %collective-permute-done.6.staged_ref = bf16[8,128,128]{2,1,0:T(8,128)(2,1)S(1)} collective-permute-done((bf16[8,128,128]{2,1,0:T(8,128)(2,1)S(1)}, bf16[8,128,128]{2,1,0:T(8,128)(2,1)S(1)}, u32[]{:S(2)}, u32[]{:S(2)}) %collective-permute-start.6) | collective-permute-done | bytes 262176 | tf_op jit(solution)/shard_map/ppermute | solution.py:374
  24.3 1.2 %multiply.1 = f32[1,23,128,128]{3,2,1,0:T(8,128)} custom-call(bf16[384,1152]{1,0:T(8,128)(2,1)S(1)} %get-tuple-element.19.left_ref, bf16[384,1152]{1,0:T(8,128)(2,1)S(1)} %collective-permute-done.left_other_ref, bf16[8,128,128]{2,1,0:T(8,128)(2,1)S(1)} %collective-permute-done.6.staged_ref, ...), custom_call_target="tpu_custom_call", output_to_operand_aliasing={{}: (5, {})} | custom-call | tf_op jit(solution)/shard_map/multiply/pallas_call | solution.py:435
  (1 shorter events, 0.0 us)
Async XLA Ops:
  1.4 8.2 %collective-permute-start = (bf16[384,1152]{1,0:T(8,128)(2,1)S(1)}, bf16[384,1152]{1,0:T(8,128)(2,1)S(1)}, u32[]{:S(2)}, u32[]{:S(2)}) collective-permute-start(bf16[384,1152]{1,0:T(8,128)(2,1)S(1)} %get-tuple-element.19.left_ref), channel_id=1, source_target_pairs={{0,1},{1,0},{2,3},{3,2},{4,5},{5,4},{6,7},{7,6},{8,9},{9,8},{10,11... | collective-permute-start | bytes 2654216 | tf_op jit(solution)/shard_map/ppermute | solution.py:374
  1.9 17.8 %collective-permute-start.4 = (bf16[13,128,128]{2,1,0:T(8,128)(2,1)S(1)}, bf16[13,128,128]{2,1,0:T(8,128)(2,1)S(1)}, u32[]{:S(2)}, u32[]{:S(2)}) collective-permute-start(bf16[13,128,128]{2,1,0:T(8,128)(2,1)S(1)} %get-tuple-element.22), channel_id=1, source_target_pairs={{2,0},{3,1},{0,2},{1,3},{6,4},{7,5},{4,6},{5,7},{10,8},{11,9},{8,1... | collective-permute-start | bytes 1277960 | tf_op jit(solution)/shard_map/ppermute | solution.py:371
  4.4 11.0 %collective-permute-start.5 = (bf16[8,128,128]{2,1,0:T(8,128)(2,1)S(1)}, bf16[8,128,128]{2,1,0:T(8,128)(2,1)S(1)}, u32[]{:S(2)}, u32[]{:S(2)}) collective-permute-start(bf16[8,128,128]{2,1,0:T(8,128)(2,1)S(1)} %get-tuple-element.23), channel_id=1, source_target_pairs={{12,0},{13,1},{6,2},{7,3},{0,4},{1,5},{10,6},{11,7},{4,8},{5,9},{1... | collective-permute-start | bytes 786440 | tf_op jit(solution)/shard_map/ppermute | solution.py:371
  6.0 16.5 %collective-permute-start.1 = (bf16[6,128,128]{2,1,0:T(8,128)(2,1)S(1)}, bf16[6,128,128]{2,1,0:T(8,128)(2,1)S(1)}, u32[]{:S(2)}, u32[]{:S(2)}) collective-permute-start(bf16[6,128,128]{2,1,0:T(8,128)(2,1)S(1)} %get-tuple-element.20), channel_id=1, source_target_pairs={{14,0},{15,1},{4,2},{5,3},{2,4},{3,5},{8,6},{9,7},{6,8},{7,9},{12,... | collective-permute-start | bytes 589832 | tf_op jit(solution)/shard_map/ppermute | solution.py:371
  8.5 14.1 %collective-permute-start.2 = (bf16[5,128,128]{2,1,0:T(8,128)(2,1)S(1)}, bf16[5,128,128]{2,1,0:T(8,128)(2,1)S(1)}, u32[]{:S(2)}, u32[]{:S(2)}) collective-permute-start(bf16[5,128,128]{2,1,0:T(8,128)(2,1)S(1)} %get-tuple-element.21), channel_id=1, source_target_pairs={{4,0},{5,1},{14,2},{15,3},{8,4},{9,5},{2,6},{3,7},{12,8},{13,9},{6... | collective-permute-start | bytes 491528 | tf_op jit(solution)/shard_map/ppermute | solution.py:371
  9.6 12.9 %collective-permute-start.3 = (bf16[1,128,128]{2,1,0:T(8,128)(2,1)S(1)}, bf16[1,128,128]{2,1,0:T(8,128)(2,1)S(1)}, u32[]{:S(2)}, u32[]{:S(2)}) collective-permute-start(bf16[1,128,128]{2,1,0:T(8,128)(2,1)S(1)} %pack_e.1), channel_id=1, source_target_pairs={{10,0},{7,1},{12,2},{9,3},{14,4},{11,5},{0,6},{13,7},{2,8},{15,9},... | collective-permute-start | bytes 98312 | tf_op jit(solution)/shard_map/ppermute | solution.py:371
  19.8 3.4 %collective-permute-start.7 = (bf16[12,128,128]{2,1,0:T(8,128)(2,1)S(1)}, bf16[12,128,128]{2,1,0:T(8,128)(2,1)S(1)}, u32[]{:S(2)}, u32[]{:S(2)}) collective-permute-start(bf16[12,128,128]{2,1,0:T(8,128)(2,1)S(1)} %stage_early.1), channel_id=1, source_target_pairs={{0,1},{1,0},{2,3},{3,2},{4,5},{5,4},{6,7},{7,6},{8,9},{9,8},{10,11... | collective-permute-start | bytes 1179656 | tf_op jit(solution)/shard_map/ppermute | solution.py:374
  22.7 1.6 %collective-permute-start.6 = (bf16[8,128,128]{2,1,0:T(8,128)(2,1)S(1)}, bf16[8,128,128]{2,1,0:T(8,128)(2,1)S(1)}, u32[]{:S(2)}, u32[]{:S(2)}) collective-permute-start(bf16[8,128,128]{2,1,0:T(8,128)(2,1)S(1)} %stage_late.1), channel_id=1, source_target_pairs={{0,1},{1,0},{2,3},{3,2},{4,5},{5,4},{6,7},{7,6},{8,9},{9,8},{10,11... | collective-permute-start | bytes 786440 | tf_op jit(solution)/shard_map/ppermute | solution.py:374

commit v17 on v16

--- a/solution.py
+++ b/solution.py
@@ -124,7 +124,7 @@
         for part in PARTS:
             staged = [position for _, _, position in STAGED[part, 1 - parity]]
             if (a, b) in staged:
-                return part, staged.index((a, b)), not flip
+                return part, staged.index((a, b)), flip if part == "late" else not flip
     raise AssertionError((k, j))
 
 
@@ -257,7 +257,7 @@
     def _(mine):
         staged = STAGED[part, mine]
         for n, (name, place, _) in enumerate(staged):
-            out_ref[n] = got[name][place].T
+            out_ref[n] = got[name][place] if part == "late" else got[name][place].T
         for n in range(len(staged), STAGED_SIZE[part]):
             out_ref[n] = jnp.zeros((BLK, BLK), out_ref.dtype)
 

time: 25.7 us -> 25.6 us (level)
  no operation moved by 1% of the time
where the time goes in v17:
time: 25.6 us; the launch traced here: 25.4 us
  starting transfers between devices  9.14 us (36%)
  waiting for transfers between devices  8.63 us (34%)
  Pallas kernels  6.88 us (27%)
  between operations  0.75 us (3%)
    ppermute x5, starting transfers between devices, towards(): return lax.ppermute(message, ('row', 'col'), pairs)  8.47 us
    ppermute x5, waiting for transfers between devices, towards(): return lax.ppermute(message, ('row', 'col'), pairs)  8.14 us
    pallas_call x3, Pallas kernels, added(): pl.pallas_call(kernel, out_shape=blocks(BR * NCOL + 1, jnp.float32), in_s...  2.18 us
    pallas_call x1, Pallas kernels, local(): pl.pallas_call(functools.partial(inner_kernel, nblocks, slots), out_shape...  1.93 us
    pallas_call x1, Pallas kernels, local(): pl.pallas_call(functools.partial(pack_kernel, nblocks, slots), out_shape=...  1.36 us
    pallas_call x1, Pallas kernels, local(): pl.pallas_call(multiply_kernel, out_shape=jax.ShapeDtypeStruct(values.sha...  1.2 us
    ppermute x3, starting transfers between devices, swapped(): return lax.ppermute(block, 'col', [(0, 1), (1, 0)])  0.67 us
  transfers between devices with their start and end apart: 8, of which 4 were waited for; matrix products, arithmetic and copies ran while one was open for 0% of the time, Pallas kernels for 17%

profile of v17, /device:TPU:0, one launch (start us, length us, event | category | flops | bytes accessed | tf_op | source)
XLA Modules:
  0.0 25.4 jit_solution(4861710876503266392)
XLA Ops:
  0.0 1.4 %pack.1 = (bf16[13,128,128]{2,1,0:T(8,128)(2,1)S(1)}, bf16[6,128,128]{2,1,0:T(8,128)(2,1)S(1)}, bf16[8,128,128]{2,1,0:T(8,128)(2,1)S(1)}, bf16[5,128,128]{2,1,0:T(8,128)(2,1)S(1)}, bf16[384,1152]{1,0:T(8,128)(2,1)S(1)}) custom-call(s32[1,23]{1,0:T(1,128)} %rows_ref.3, s32[1,23]{1,0:T(1,128)} %cols_ref.3, bf16[1,23,128,128]{3,2,1,0:T(8,128)(2,1)} %values_ref.1), custom_call_target="tpu_custom_call" | custom-call | tf_op jit(solution)/shard_map/pack/pallas_call | solution.py:348
  1.4 0.5 %collective-permute-start = (bf16[384,1152]{1,0:T(8,128)(2,1)S(1)}, bf16[384,1152]{1,0:T(8,128)(2,1)S(1)}, u32[]{:S(2)}, u32[]{:S(2)}) collective-permute-start(bf16[384,1152]{1,0:T(8,128)(2,1)S(1)} %get-tuple-element.19.left_ref), channel_id=1, source_target_pairs={{0,1},{1,0},{2,3},{3,2},{4,5},{5,4},{6,7},{7,6},{8,9},{9,8},{10,11... | collective-permute-start | bytes 2654216 | tf_op jit(solution)/shard_map/ppermute | solution.py:374
  1.9 2.6 %collective-permute-start.4 = (bf16[13,128,128]{2,1,0:T(8,128)(2,1)S(1)}, bf16[13,128,128]{2,1,0:T(8,128)(2,1)S(1)}, u32[]{:S(2)}, u32[]{:S(2)}) collective-permute-start(bf16[13,128,128]{2,1,0:T(8,128)(2,1)S(1)} %get-tuple-element.22), channel_id=1, source_target_pairs={{2,0},{3,1},{0,2},{1,3},{6,4},{7,5},{4,6},{5,7},{10,8},{11,9},{8,1... | collective-permute-start | bytes 1277960 | tf_op jit(solution)/shard_map/ppermute | solution.py:371
  4.4 1.6 %collective-permute-start.5 = (bf16[8,128,128]{2,1,0:T(8,128)(2,1)S(1)}, bf16[8,128,128]{2,1,0:T(8,128)(2,1)S(1)}, u32[]{:S(2)}, u32[]{:S(2)}) collective-permute-start(bf16[8,128,128]{2,1,0:T(8,128)(2,1)S(1)} %get-tuple-element.23), channel_id=1, source_target_pairs={{12,0},{13,1},{6,2},{7,3},{0,4},{1,5},{10,6},{11,7},{4,8},{5,9},{1... | collective-permute-start | bytes 786440 | tf_op jit(solution)/shard_map/ppermute | solution.py:371
  6.0 2.4 %collective-permute-start.1 = (bf16[6,128,128]{2,1,0:T(8,128)(2,1)S(1)}, bf16[6,128,128]{2,1,0:T(8,128)(2,1)S(1)}, u32[]{:S(2)}, u32[]{:S(2)}) collective-permute-start(bf16[6,128,128]{2,1,0:T(8,128)(2,1)S(1)} %get-tuple-element.20), channel_id=1, source_target_pairs={{14,0},{15,1},{4,2},{5,3},{2,4},{3,5},{8,6},{9,7},{6,8},{7,9},{12,... | collective-permute-start | bytes 589832 | tf_op jit(solution)/shard_map/ppermute | solution.py:371
  8.5 0.4 %collective-permute-start.2 = (bf16[5,128,128]{2,1,0:T(8,128)(2,1)S(1)}, bf16[5,128,128]{2,1,0:T(8,128)(2,1)S(1)}, u32[]{:S(2)}, u32[]{:S(2)}) collective-permute-start(bf16[5,128,128]{2,1,0:T(8,128)(2,1)S(1)} %get-tuple-element.21), channel_id=1, source_target_pairs={{4,0},{5,1},{14,2},{15,3},{8,4},{9,5},{2,6},{3,7},{12,8},{13,9},{6... | collective-permute-start | bytes 491528 | tf_op jit(solution)/shard_map/ppermute | solution.py:371
  9.6 0.0 collective-permute-done.left_other_ref
  9.6 1.4 %collective-permute-start.3 = (bf16[1,128,128]{2,1,0:T(8,128)(2,1)S(1)}, bf16[1,128,128]{2,1,0:T(8,128)(2,1)S(1)}, u32[]{:S(2)}, u32[]{:S(2)}) collective-permute-start(bf16[1,128,128]{2,1,0:T(8,128)(2,1)S(1)} %pack_e.1), channel_id=1, source_target_pairs={{10,0},{7,1},{12,2},{9,3},{14,4},{11,5},{0,6},{13,7},{2,8},{15,9},... | collective-permute-start | bytes 98312 | tf_op jit(solution)/shard_map/ppermute | solution.py:371
  11.1 1.9 %inner.1 = (s32[1,128]{1,0:T(1,128)S(4)}, f32[1,23,128,128]{3,2,1,0:T(8,128)}) custom-call(s32[1,23]{1,0:T(1,128)} %rows_ref.3, s32[1,23]{1,0:T(1,128)} %cols_ref.3, s32[1,1]{1,0:T(1,128)S(6)} %copy.7.counts_ref, bf16[384,1152]{1,0:T(8,128)(2,1)S(1)} %get-tuple-element.19.left_ref, bf16[384,1152]{1,0:T(8,128)(2,1)S(1)} %collective-permute-done.left_other_ref), custom_call_target="tpu_custom_call" | custom-call | flops 427819008 | bytes 1507328 | tf_op jit(solution)/shard_map/inner/pallas_call | solution.py:387
  13.0 2.5 %collective-permute-done.5.c_ref.refs_1_ = bf16[8,128,128]{2,1,0:T(8,128)(2,1)S(1)} collective-permute-done((bf16[8,128,128]{2,1,0:T(8,128)(2,1)S(1)}, bf16[8,128,128]{2,1,0:T(8,128)(2,1)S(1)}, u32[]{:S(2)}, u32[]{:S(2)}) %collective-permute-start.5) | collective-permute-done | bytes 262176 | tf_op jit(solution)/shard_map/ppermute | solution.py:371
  15.5 4.2 %collective-permute-done.4.a_ref.refs_0_ = bf16[13,128,128]{2,1,0:T(8,128)(2,1)S(1)} collective-permute-done((bf16[13,128,128]{2,1,0:T(8,128)(2,1)S(1)}, bf16[13,128,128]{2,1,0:T(8,128)(2,1)S(1)}, u32[]{:S(2)}, u32[]{:S(2)}) %collective-permute-start.4) | collective-permute-done | bytes 426016 | tf_op jit(solution)/shard_map/ppermute | solution.py:371
  19.7 0.2 stage_early.1
  19.8 0.1 collective-permute-start.7
  19.9 1.2 %early.1.old_ref = f32[28,128,128]{2,1,0:T(8,128)S(1)} custom-call(bf16[384,1152]{1,0:T(8,128)(2,1)S(1)} %get-tuple-element.19.left_ref, bf16[384,1152]{1,0:T(8,128)(2,1)S(1)} %collective-permute-done.left_other_ref, bf16[13,128,128]{2,1,0:T(8,128)(2,1)S(1)} %collective-permute-done.4.a_ref.refs_0_, bf16[8,128,128]{2,1,0:T(8,128)(2,1)S(1)} %collective-permute-done.5.c_ref.refs_1_), custom_call_target="tpu_custom_call" | custom-call | flops 4194304 | tf_op jit(solution)/shard_map/early/pallas_call | solution.py:417
  21.1 1.5 %collective-permute-done.2.refs_1_.d_ref = bf16[5,128,128]{2,1,0:T(8,128)(2,1)S(1)} collective-permute-done((bf16[5,128,128]{2,1,0:T(8,128)(2,1)S(1)}, bf16[5,128,128]{2,1,0:T(8,128)(2,1)S(1)}, u32[]{:S(2)}, u32[]{:S(2)}) %collective-permute-start.2) | collective-permute-done | bytes 163872 | tf_op jit(solution)/shard_map/ppermute | solution.py:371
  22.6 0.0 collective-permute-done.1.refs_0_.b_ref
  22.6 0.0 collective-permute-done.3.refs_2_.e_ref
  22.6 0.1 collective-permute-start.6
  22.7 0.5 %late.1.old_ref = f32[28,128,128]{2,1,0:T(8,128)S(1)} custom-call(bf16[384,1152]{1,0:T(8,128)(2,1)S(1)} %get-tuple-element.19.left_ref, bf16[384,1152]{1,0:T(8,128)(2,1)S(1)} %collective-permute-done.left_other_ref, bf16[6,128,128]{2,1,0:T(8,128)(2,1)S(1)} %collective-permute-done.1.refs_0_.b_ref, ...), custom_call_target="tpu_custom_call" | custom-call | flops 16777216000 | tf_op jit(solution)/shard_map/late/pallas_call | solution.py:417
  23.1 0.0 collective-permute-done.7.staged_ref
  23.1 0.6 %staged_early.1.old_ref = f32[28,128,128]{2,1,0:T(8,128)S(1)} custom-call(bf16[384,1152]{1,0:T(8,128)(2,1)S(1)} %get-tuple-element.19.left_ref, bf16[384,1152]{1,0:T(8,128)(2,1)S(1)} %collective-permute-done.left_other_ref, bf16[12,128,128]{2,1,0:T(8,128)(2,1)S(1)} %collective-permute-done.7.staged_ref, f32[28,128,128]{2,1,0:T(8,128)S(1)} %late.1.old_ref), custom_call_target="tpu_custom_call" | custom-call | flops 4194304 | tf_op jit(solution)/shard_map/staged_early/pallas_call | solution.py:417
  23.7 0.5 %collective-permute-done.6.staged_ref = bf16[8,128,128]{2,1,0:T(8,128)(2,1)S(1)} collective-permute-done((bf16[8,128,128]{2,1,0:T(8,128)(2,1)S(1)}, bf16[8,128,128]{2,1,0:T(8,128)(2,1)S(1)}, u32[]{:S(2)}, u32[]{:S(2)}) %collective-permute-start.6) | collective-permute-done | bytes 262176 | tf_op jit(solution)/shard_map/ppermute | solution.py:374
  24.2 1.2 %multiply.1 = f32[1,23,128,128]{3,2,1,0:T(8,128)} custom-call(bf16[384,1152]{1,0:T(8,128)(2,1)S(1)} %get-tuple-element.19.left_ref, bf16[384,1152]{1,0:T(8,128)(2,1)S(1)} %collective-permute-done.left_other_ref, bf16[8,128,128]{2,1,0:T(8,128)(2,1)S(1)} %collective-permute-done.6.staged_ref, ...), custom_call_target="tpu_custom_call", output_to_operand_aliasing={{}: (5, {})} | custom-call | tf_op jit(solution)/shard_map/multiply/pallas_call | solution.py:435
  (2 shorter events, 0.0 us)
Async XLA Ops:
  1.4 8.2 %collective-permute-start = (bf16[384,1152]{1,0:T(8,128)(2,1)S(1)}, bf16[384,1152]{1,0:T(8,128)(2,1)S(1)}, u32[]{:S(2)}, u32[]{:S(2)}) collective-permute-start(bf16[384,1152]{1,0:T(8,128)(2,1)S(1)} %get-tuple-element.19.left_ref), channel_id=1, source_target_pairs={{0,1},{1,0},{2,3},{3,2},{4,5},{5,4},{6,7},{7,6},{8,9},{9,8},{10,11... | collective-permute-start | bytes 2654216 | tf_op jit(solution)/shard_map/ppermute | solution.py:374
  1.9 17.8 %collective-permute-start.4 = (bf16[13,128,128]{2,1,0:T(8,128)(2,1)S(1)}, bf16[13,128,128]{2,1,0:T(8,128)(2,1)S(1)}, u32[]{:S(2)}, u32[]{:S(2)}) collective-permute-start(bf16[13,128,128]{2,1,0:T(8,128)(2,1)S(1)} %get-tuple-element.22), channel_id=1, source_target_pairs={{2,0},{3,1},{0,2},{1,3},{6,4},{7,5},{4,6},{5,7},{10,8},{11,9},{8,1... | collective-permute-start | bytes 1277960 | tf_op jit(solution)/shard_map/ppermute | solution.py:371
  4.4 11.0 %collective-permute-start.5 = (bf16[8,128,128]{2,1,0:T(8,128)(2,1)S(1)}, bf16[8,128,128]{2,1,0:T(8,128)(2,1)S(1)}, u32[]{:S(2)}, u32[]{:S(2)}) collective-permute-start(bf16[8,128,128]{2,1,0:T(8,128)(2,1)S(1)} %get-tuple-element.23), channel_id=1, source_target_pairs={{12,0},{13,1},{6,2},{7,3},{0,4},{1,5},{10,6},{11,7},{4,8},{5,9},{1... | collective-permute-start | bytes 786440 | tf_op jit(solution)/shard_map/ppermute | solution.py:371
  6.0 16.5 %collective-permute-start.1 = (bf16[6,128,128]{2,1,0:T(8,128)(2,1)S(1)}, bf16[6,128,128]{2,1,0:T(8,128)(2,1)S(1)}, u32[]{:S(2)}, u32[]{:S(2)}) collective-permute-start(bf16[6,128,128]{2,1,0:T(8,128)(2,1)S(1)} %get-tuple-element.20), channel_id=1, source_target_pairs={{14,0},{15,1},{4,2},{5,3},{2,4},{3,5},{8,6},{9,7},{6,8},{7,9},{12,... | collective-permute-start | bytes 589832 | tf_op jit(solution)/shard_map/ppermute | solution.py:371
  8.5 14.1 %collective-permute-start.2 = (bf16[5,128,128]{2,1,0:T(8,128)(2,1)S(1)}, bf16[5,128,128]{2,1,0:T(8,128)(2,1)S(1)}, u32[]{:S(2)}, u32[]{:S(2)}) collective-permute-start(bf16[5,128,128]{2,1,0:T(8,128)(2,1)S(1)} %get-tuple-element.21), channel_id=1, source_target_pairs={{4,0},{5,1},{14,2},{15,3},{8,4},{9,5},{2,6},{3,7},{12,8},{13,9},{6... | collective-permute-start | bytes 491528 | tf_op jit(solution)/shard_map/ppermute | solution.py:371
  9.6 12.9 %collective-permute-start.3 = (bf16[1,128,128]{2,1,0:T(8,128)(2,1)S(1)}, bf16[1,128,128]{2,1,0:T(8,128)(2,1)S(1)}, u32[]{:S(2)}, u32[]{:S(2)}) collective-permute-start(bf16[1,128,128]{2,1,0:T(8,128)(2,1)S(1)} %pack_e.1), channel_id=1, source_target_pairs={{10,0},{7,1},{12,2},{9,3},{14,4},{11,5},{0,6},{13,7},{2,8},{15,9},... | collective-permute-start | bytes 98312 | tf_op jit(solution)/shard_map/ppermute | solution.py:371
  19.8 3.3 %collective-permute-start.7 = (bf16[12,128,128]{2,1,0:T(8,128)(2,1)S(1)}, bf16[12,128,128]{2,1,0:T(8,128)(2,1)S(1)}, u32[]{:S(2)}, u32[]{:S(2)}) collective-permute-start(bf16[12,128,128]{2,1,0:T(8,128)(2,1)S(1)} %stage_early.1), channel_id=1, source_target_pairs={{0,1},{1,0},{2,3},{3,2},{4,5},{5,4},{6,7},{7,6},{8,9},{9,8},{10,11... | collective-permute-start | bytes 1179656 | tf_op jit(solution)/shard_map/ppermute | solution.py:374
  22.6 1.6 %collective-permute-start.6 = (bf16[8,128,128]{2,1,0:T(8,128)(2,1)S(1)}, bf16[8,128,128]{2,1,0:T(8,128)(2,1)S(1)}, u32[]{:S(2)}, u32[]{:S(2)}) collective-permute-start(bf16[8,128,128]{2,1,0:T(8,128)(2,1)S(1)} %stage_late.1), channel_id=1, source_target_pairs={{0,1},{1,0},{2,3},{3,2},{4,5},{5,4},{6,7},{7,6},{8,9},{9,8},{10,11... | collective-permute-start | bytes 786440 | tf_op jit(solution)/shard_map/ppermute | solution.py:374

commit v18 on v17

--- a/solution.py
+++ b/solution.py
@@ -46,6 +46,9 @@
 STAGED_SIZE = {part: max(len(STAGED[part, parity]) for parity in (0, 1)) for part in PARTS}
 
 
+BOTH_WAYS = min(len(STAGED["late", parity]) for parity in (0, 1))
+
+
 def columns_of(parity):
     return [j for j in range(LOW, HIGH + 1) if j % 2 == parity]
 
@@ -124,7 +127,10 @@
         for part in PARTS:
             staged = [position for _, _, position in STAGED[part, 1 - parity]]
             if (a, b) in staged:
-                return part, staged.index((a, b)), flip if part == "late" else not flip
+                n = staged.index((a, b))
+                if part == "early":
+                    return part, n, not flip
+                return ("late", n, flip) if n < BOTH_WAYS else ("last", n - BOTH_WAYS, flip)
     raise AssertionError((k, j))
 
 
@@ -264,13 +270,24 @@
 
 def late_columns(parity):
     found = [[find_block(parity, k, j) for k in range(LOW, HIGH + 1)] for j in columns_of(parity)]
-    return [j for j, blocks in zip(columns_of(parity), found) if any(b is not None and b[0] == "late" for b in blocks)]
+    return [j for j, blocks in zip(columns_of(parity), found) if any(b is not None and b[0] in ("late", "last") for b in blocks)]
 
 
 def late_pairs(parity):
     near = [j for j in late_columns(parity) if -BR <= j < 0]
     rest = [j for j in late_columns(parity) if j not in near]
     return [js[n : n + 2] for js in (near, rest) for n in range(0, len(js), 2)]
+
+
+def stage_late_kernel(b_ref, d_ref, e_ref, out_ref, last_ref):
+    got = {"b": b_ref, "d": d_ref, "e": e_ref}
+
+    @for_own_parity
+    def _(mine):
+        staged = STAGED["late", mine]
+        for n in range(STAGED_SIZE["late"]):
+            ref, at = (out_ref, n) if n < BOTH_WAYS else (last_ref, n - BOTH_WAYS)
+            ref[at] = got[staged[n][0]][staged[n][1]] if n < len(staged) else jnp.zeros((BLK, BLK), ref.dtype)
 
 
 def add_columns(refs, wanted, old_ref, new_ref, right, mine, pairs=outer_pairs):
@@ -301,9 +318,9 @@
     out_ref[BR * NCOL] = jnp.zeros((BLK, BLK), out_ref.dtype)
 
 
-def multiply_kernel(left_ref, left_other_ref, staged_ref, old_ref, table, _, out_ref, *rest):
+def multiply_kernel(left_ref, left_other_ref, late_ref, last_ref, old_ref, table, _, out_ref, *rest):
     right, made, out_sem = rest
-    refs = {("left", True): left_ref, ("left", False): left_other_ref, "late": staged_ref}
+    refs = {("left", True): left_ref, ("left", False): left_other_ref, "late": late_ref, "last": last_ref}
     made[BR * NCOL] = jnp.zeros((BLK, BLK), made.dtype)
 
     @for_own_parity
@@ -313,7 +330,7 @@
         for place in here:
             if place % NCOL not in late:
                 store(old_ref, table, out_ref, place, out_sem)
-        add_columns(refs, ("late",), old_ref, made, right, mine, late_pairs)
+        add_columns(refs, ("late", "last"), old_ref, made, right, mine, late_pairs)
         for place in here:
             if place % NCOL in late:
                 store(made, table, out_ref, place, out_sem)
@@ -429,23 +446,33 @@
     staged_early = staged("early", (a, c))
     total = added(early_kernel, "early", EARLY_COST, (left, left_other, a, c))
     b, d, e, total = lax.optimization_barrier((b, d, e, total))
-    staged_late = staged("late", (b, d, e))
+    staged_late, staged_last = pl.pallas_call(
+        stage_late_kernel,
+        out_shape=[blocks(BOTH_WAYS), blocks(STAGED_SIZE["late"] - BOTH_WAYS)],
+        in_specs=[vmem] * 3,
+        out_specs=[vmem] * 2,
+        compiler_params=params,
+        name="stage_late",
+    )(b, d, e)
+    one_way = [(r * col_count + r % 2, r * col_count + 1 - r % 2) for r in range(row_count)]
+    staged_late = swapped(staged_late)
+    staged_last = lax.ppermute(staged_last, ("row", "col"), one_way)
     total = added(late_kernel, "late", LATE_COST, (left, left_other, b, d, e, total))
     total = added(staged_early_kernel, "staged_early", EARLY_COST, (left, left_other, staged_early, total))
     return pl.pallas_call(
         multiply_kernel,
         out_shape=jax.ShapeDtypeStruct(values.shape, jnp.float32),
-        in_specs=[vmem] * 4 + [smem, hbm],
+        in_specs=[vmem] * 5 + [smem, hbm],
         out_specs=hbm,
         scratch_shapes=[
             right_scratch(4),
             pltpu.VMEM((BR * NCOL + 1, BLK, BLK), jnp.float32),
             pltpu.SemaphoreType.DMA,
         ],
-        input_output_aliases={5: 0},
+        input_output_aliases={6: 0},
         compiler_params=params,
         name="multiply",
-    )(left, left_other, staged_late, total, pltpu.with_memory_space_constraint(table, pltpu.SMEM), out)
+    )(left, left_other, staged_late, staged_last, total, pltpu.with_memory_space_constraint(table, pltpu.SMEM), out)
 
 
 def solution(mesh):

time: 25.6 us -> 27.6 us (1.078)
  starting transfers between devices: 9.14 us -> 11.5 us
  waiting for transfers between devices: 8.63 us -> 8.15 us
    ppermute x0 -> x1, starting transfers between devices: none -> 2.39 us  [local(): staged_last = lax.ppermute(staged_last, ('row', 'col'), one_way)]
    ppermute x3, waiting for transfers between devices: 0.48 us -> 0.01 us  [swapped(): return lax.ppermute(block, 'col', [(0, 1), (1, 0)])]
  transfers between devices with their start and end apart: 8 -> 9, of which waited for: 4 -> 3; matrix products, arithmetic and copies ran while one was open for 0% -> 0% of each run, Pallas kernels for 17% -> 16%
where the time goes in v18:
time: 27.6 us; the launch traced here: 27.4 us
  starting transfers between devices  11.5 us (42%)
  waiting for transfers between devices  8.15 us (30%)
  Pallas kernels  6.9 us (25%)
  between operations  0.77 us (3%)
    ppermute x5, starting transfers between devices, towards(): return lax.ppermute(message, ('row', 'col'), pairs)  8.47 us
    ppermute x5, waiting for transfers between devices, towards(): return lax.ppermute(message, ('row', 'col'), pairs)  8.14 us
    ppermute x1, starting transfers between devices, local(): staged_last = lax.ppermute(staged_last, ('row', 'col'), one_way)  2.39 us
    pallas_call x3, Pallas kernels, added(): pl.pallas_call(kernel, out_shape=blocks(BR * NCOL + 1, jnp.float32), in_s...  2.19 us
    pallas_call x1, Pallas kernels, local(): pl.pallas_call(functools.partial(inner_kernel, nblocks, slots), out_shape...  1.93 us
    pallas_call x1, Pallas kernels, local(): pl.pallas_call(functools.partial(pack_kernel, nblocks, slots), out_shape=...  1.36 us
    pallas_call x1, Pallas kernels, local(): pl.pallas_call(multiply_kernel, out_shape=jax.ShapeDtypeStruct(values.sha...  1.21 us
    ppermute x3, starting transfers between devices, swapped(): return lax.ppermute(block, 'col', [(0, 1), (1, 0)])  0.67 us
  transfers between devices with their start and end apart: 9, of which 3 were waited for; matrix products, arithmetic and copies ran while one was open for 0% of the time, Pallas kernels for 16%

profile of v18, /device:TPU:0, one launch (start us, length us, event | category | flops | bytes accessed | tf_op | source)
XLA Modules:
  0.0 27.4 jit_solution(11189004483557154212)
XLA Ops:
  0.0 1.4 %pack.1 = (bf16[13,128,128]{2,1,0:T(8,128)(2,1)S(1)}, bf16[6,128,128]{2,1,0:T(8,128)(2,1)S(1)}, bf16[8,128,128]{2,1,0:T(8,128)(2,1)S(1)}, bf16[5,128,128]{2,1,0:T(8,128)(2,1)S(1)}, bf16[384,1152]{1,0:T(8,128)(2,1)S(1)}) custom-call(s32[1,23]{1,0:T(1,128)} %rows_ref.3, s32[1,23]{1,0:T(1,128)} %cols_ref.3, bf16[1,23,128,128]{3,2,1,0:T(8,128)(2,1)} %values_ref.1), custom_call_target="tpu_custom_call" | custom-call | tf_op jit(solution)/shard_map/pack/pallas_call | solution.py:365
  1.4 0.5 %collective-permute-start = (bf16[384,1152]{1,0:T(8,128)(2,1)S(1)}, bf16[384,1152]{1,0:T(8,128)(2,1)S(1)}, u32[]{:S(2)}, u32[]{:S(2)}) collective-permute-start(bf16[384,1152]{1,0:T(8,128)(2,1)S(1)} %get-tuple-element.21.left_ref), channel_id=1, source_target_pairs={{0,1},{1,0},{2,3},{3,2},{4,5},{5,4},{6,7},{7,6},{8,9},{9,8},{10,11... | collective-permute-start | bytes 2654216 | tf_op jit(solution)/shard_map/ppermute | solution.py:391
  1.9 2.6 %collective-permute-start.4 = (bf16[13,128,128]{2,1,0:T(8,128)(2,1)S(1)}, bf16[13,128,128]{2,1,0:T(8,128)(2,1)S(1)}, u32[]{:S(2)}, u32[]{:S(2)}) collective-permute-start(bf16[13,128,128]{2,1,0:T(8,128)(2,1)S(1)} %get-tuple-element.24), channel_id=1, source_target_pairs={{2,0},{3,1},{0,2},{1,3},{6,4},{7,5},{4,6},{5,7},{10,8},{11,9},{8,1... | collective-permute-start | bytes 1277960 | tf_op jit(solution)/shard_map/ppermute | solution.py:388
  4.4 1.6 %collective-permute-start.5 = (bf16[8,128,128]{2,1,0:T(8,128)(2,1)S(1)}, bf16[8,128,128]{2,1,0:T(8,128)(2,1)S(1)}, u32[]{:S(2)}, u32[]{:S(2)}) collective-permute-start(bf16[8,128,128]{2,1,0:T(8,128)(2,1)S(1)} %get-tuple-element.25), channel_id=1, source_target_pairs={{12,0},{13,1},{6,2},{7,3},{0,4},{1,5},{10,6},{11,7},{4,8},{5,9},{1... | collective-permute-start | bytes 786440 | tf_op jit(solution)/shard_map/ppermute | solution.py:388
  6.0 2.4 %collective-permute-start.1 = (bf16[6,128,128]{2,1,0:T(8,128)(2,1)S(1)}, bf16[6,128,128]{2,1,0:T(8,128)(2,1)S(1)}, u32[]{:S(2)}, u32[]{:S(2)}) collective-permute-start(bf16[6,128,128]{2,1,0:T(8,128)(2,1)S(1)} %get-tuple-element.22), channel_id=1, source_target_pairs={{14,0},{15,1},{4,2},{5,3},{2,4},{3,5},{8,6},{9,7},{6,8},{7,9},{12,... | collective-permute-start | bytes 589832 | tf_op jit(solution)/shard_map/ppermute | solution.py:388
  8.5 0.4 %collective-permute-start.2 = (bf16[5,128,128]{2,1,0:T(8,128)(2,1)S(1)}, bf16[5,128,128]{2,1,0:T(8,128)(2,1)S(1)}, u32[]{:S(2)}, u32[]{:S(2)}) collective-permute-start(bf16[5,128,128]{2,1,0:T(8,128)(2,1)S(1)} %get-tuple-element.23), channel_id=1, source_target_pairs={{4,0},{5,1},{14,2},{15,3},{8,4},{9,5},{2,6},{3,7},{12,8},{13,9},{6... | collective-permute-start | bytes 491528 | tf_op jit(solution)/shard_map/ppermute | solution.py:388
  9.6 0.0 collective-permute-done.left_other_ref
  9.6 1.4 %collective-permute-start.3 = (bf16[1,128,128]{2,1,0:T(8,128)(2,1)S(1)}, bf16[1,128,128]{2,1,0:T(8,128)(2,1)S(1)}, u32[]{:S(2)}, u32[]{:S(2)}) collective-permute-start(bf16[1,128,128]{2,1,0:T(8,128)(2,1)S(1)} %pack_e.1), channel_id=1, source_target_pairs={{10,0},{7,1},{12,2},{9,3},{14,4},{11,5},{0,6},{13,7},{2,8},{15,9},... | collective-permute-start | bytes 98312 | tf_op jit(solution)/shard_map/ppermute | solution.py:388
  11.1 1.9 %inner.1 = (s32[1,128]{1,0:T(1,128)S(4)}, f32[1,23,128,128]{3,2,1,0:T(8,128)}) custom-call(s32[1,23]{1,0:T(1,128)} %rows_ref.3, s32[1,23]{1,0:T(1,128)} %cols_ref.3, s32[1,1]{1,0:T(1,128)S(6)} %copy.7.counts_ref, bf16[384,1152]{1,0:T(8,128)(2,1)S(1)} %get-tuple-element.21.left_ref, bf16[384,1152]{1,0:T(8,128)(2,1)S(1)} %collective-permute-done.left_other_ref), custom_call_target="tpu_custom_call" | custom-call | flops 427819008 | bytes 1507328 | tf_op jit(solution)/shard_map/inner/pallas_call | solution.py:404
  13.0 2.5 %collective-permute-done.5.c_ref.refs_1_ = bf16[8,128,128]{2,1,0:T(8,128)(2,1)S(1)} collective-permute-done((bf16[8,128,128]{2,1,0:T(8,128)(2,1)S(1)}, bf16[8,128,128]{2,1,0:T(8,128)(2,1)S(1)}, u32[]{:S(2)}, u32[]{:S(2)}) %collective-permute-start.5) | collective-permute-done | bytes 262176 | tf_op jit(solution)/shard_map/ppermute | solution.py:388
  15.5 4.2 %collective-permute-done.4.a_ref.refs_0_ = bf16[13,128,128]{2,1,0:T(8,128)(2,1)S(1)} collective-permute-done((bf16[13,128,128]{2,1,0:T(8,128)(2,1)S(1)}, bf16[13,128,128]{2,1,0:T(8,128)(2,1)S(1)}, u32[]{:S(2)}, u32[]{:S(2)}) %collective-permute-start.4) | collective-permute-done | bytes 426016 | tf_op jit(solution)/shard_map/ppermute | solution.py:388
  19.7 0.2 stage_early.1
  19.8 0.1 collective-permute-start.8
  19.9 1.2 %early.1.old_ref = f32[28,128,128]{2,1,0:T(8,128)S(1)} custom-call(bf16[384,1152]{1,0:T(8,128)(2,1)S(1)} %get-tuple-element.21.left_ref, bf16[384,1152]{1,0:T(8,128)(2,1)S(1)} %collective-permute-done.left_other_ref, bf16[13,128,128]{2,1,0:T(8,128)(2,1)S(1)} %collective-permute-done.4.a_ref.refs_0_, bf16[8,128,128]{2,1,0:T(8,128)(2,1)S(1)} %collective-permute-done.5.c_ref.refs_1_), custom_call_target="tpu_custom_call" | custom-call | flops 4194304 | tf_op jit(solution)/shard_map/early/pallas_call | solution.py:434
  21.1 1.5 %collective-permute-done.2.d_ref = bf16[5,128,128]{2,1,0:T(8,128)(2,1)S(1)} collective-permute-done((bf16[5,128,128]{2,1,0:T(8,128)(2,1)S(1)}, bf16[5,128,128]{2,1,0:T(8,128)(2,1)S(1)}, u32[]{:S(2)}, u32[]{:S(2)}) %collective-permute-start.2) | collective-permute-done | bytes 163872 | tf_op jit(solution)/shard_map/ppermute | solution.py:388
  22.6 0.0 collective-permute-done.1.b_ref
  22.6 0.0 collective-permute-done.3.e_ref
  22.6 0.1 collective-permute-start.6
  22.7 2.4 %collective-permute-start.7 = (bf16[4,128,128]{2,1,0:T(8,128)(2,1)S(1)}, bf16[4,128,128]{2,1,0:T(8,128)(2,1)S(1)}, u32[]{:S(2)}, u32[]{:S(2)}) collective-permute-start(bf16[4,128,128]{2,1,0:T(8,128)(2,1)S(1)} %get-tuple-element.33), channel_id=1, source_target_pairs={{0,1},{3,2},{4,5},{7,6},{8,9},{11,10},{12,13},{15,14},{16,17},{19,... | collective-permute-start | bytes 393224 | tf_op jit(solution)/shard_map/ppermute | solution.py:459
  25.1 0.5 %late.1.old_ref = f32[28,128,128]{2,1,0:T(8,128)S(1)} custom-call(bf16[384,1152]{1,0:T(8,128)(2,1)S(1)} %get-tuple-element.21.left_ref, bf16[384,1152]{1,0:T(8,128)(2,1)S(1)} %collective-permute-done.left_other_ref, bf16[6,128,128]{2,1,0:T(8,128)(2,1)S(1)} %collective-permute-done.1.b_ref, bf16[5,128,128]{2,1,0:T(8,128)(2,1)S(1)} %collective-permute-done.2.d_ref, ...), custom_call_target="tpu_custom_call" | custom-call | flops 16777216000 | tf_op jit(solution)/shard_map/late/pallas_call | solution.py:434
  25.5 0.0 collective-permute-done.8.staged_ref
  25.6 0.6 %staged_early.1.old_ref = f32[28,128,128]{2,1,0:T(8,128)S(1)} custom-call(bf16[384,1152]{1,0:T(8,128)(2,1)S(1)} %get-tuple-element.21.left_ref, bf16[384,1152]{1,0:T(8,128)(2,1)S(1)} %collective-permute-done.left_other_ref, bf16[12,128,128]{2,1,0:T(8,128)(2,1)S(1)} %collective-permute-done.8.staged_ref, f32[28,128,128]{2,1,0:T(8,128)S(1)} %late.1.old_ref), custom_call_target="tpu_custom_call" | custom-call | flops 4194304 | tf_op jit(solution)/shard_map/staged_early/pallas_call | solution.py:434
  26.1 0.0 collective-permute-done.6.late_ref
  26.1 1.2 %multiply.1 = f32[1,23,128,128]{3,2,1,0:T(8,128)} custom-call(bf16[384,1152]{1,0:T(8,128)(2,1)S(1)} %get-tuple-element.21.left_ref, bf16[384,1152]{1,0:T(8,128)(2,1)S(1)} %collective-permute-done.left_other_ref, bf16[4,128,128]{2,1,0:T(8,128)(2,1)S(1)} %collective-permute-done.6.late_ref, ...), custom_call_target="tpu_custom_call", output_to_operand_aliasing={{}: (6, {})} | custom-call | tf_op jit(solution)/shard_map/multiply/pallas_call | solution.py:462
  (3 shorter events, 0.1 us)
Async XLA Ops:
  1.4 8.2 %collective-permute-start = (bf16[384,1152]{1,0:T(8,128)(2,1)S(1)}, bf16[384,1152]{1,0:T(8,128)(2,1)S(1)}, u32[]{:S(2)}, u32[]{:S(2)}) collective-permute-start(bf16[384,1152]{1,0:T(8,128)(2,1)S(1)} %get-tuple-element.21.left_ref), channel_id=1, source_target_pairs={{0,1},{1,0},{2,3},{3,2},{4,5},{5,4},{6,7},{7,6},{8,9},{9,8},{10,11... | collective-permute-start | bytes 2654216 | tf_op jit(solution)/shard_map/ppermute | solution.py:391
  1.9 17.8 %collective-permute-start.4 = (bf16[13,128,128]{2,1,0:T(8,128)(2,1)S(1)}, bf16[13,128,128]{2,1,0:T(8,128)(2,1)S(1)}, u32[]{:S(2)}, u32[]{:S(2)}) collective-permute-start(bf16[13,128,128]{2,1,0:T(8,128)(2,1)S(1)} %get-tuple-element.24), channel_id=1, source_target_pairs={{2,0},{3,1},{0,2},{1,3},{6,4},{7,5},{4,6},{5,7},{10,8},{11,9},{8,1... | collective-permute-start | bytes 1277960 | tf_op jit(solution)/shard_map/ppermute | solution.py:388
  4.4 11.0 %collective-permute-start.5 = (bf16[8,128,128]{2,1,0:T(8,128)(2,1)S(1)}, bf16[8,128,128]{2,1,0:T(8,128)(2,1)S(1)}, u32[]{:S(2)}, u32[]{:S(2)}) collective-permute-start(bf16[8,128,128]{2,1,0:T(8,128)(2,1)S(1)} %get-tuple-element.25), channel_id=1, source_target_pairs={{12,0},{13,1},{6,2},{7,3},{0,4},{1,5},{10,6},{11,7},{4,8},{5,9},{1... | collective-permute-start | bytes 786440 | tf_op jit(solution)/shard_map/ppermute | solution.py:388
  6.0 16.5 %collective-permute-start.1 = (bf16[6,128,128]{2,1,0:T(8,128)(2,1)S(1)}, bf16[6,128,128]{2,1,0:T(8,128)(2,1)S(1)}, u32[]{:S(2)}, u32[]{:S(2)}) collective-permute-start(bf16[6,128,128]{2,1,0:T(8,128)(2,1)S(1)} %get-tuple-element.22), channel_id=1, source_target_pairs={{14,0},{15,1},{4,2},{5,3},{2,4},{3,5},{8,6},{9,7},{6,8},{7,9},{12,... | collective-permute-start | bytes 589832 | tf_op jit(solution)/shard_map/ppermute | solution.py:388
  8.5 14.1 %collective-permute-start.2 = (bf16[5,128,128]{2,1,0:T(8,128)(2,1)S(1)}, bf16[5,128,128]{2,1,0:T(8,128)(2,1)S(1)}, u32[]{:S(2)}, u32[]{:S(2)}) collective-permute-start(bf16[5,128,128]{2,1,0:T(8,128)(2,1)S(1)} %get-tuple-element.23), channel_id=1, source_target_pairs={{4,0},{5,1},{14,2},{15,3},{8,4},{9,5},{2,6},{3,7},{12,8},{13,9},{6... | collective-permute-start | bytes 491528 | tf_op jit(solution)/shard_map/ppermute | solution.py:388
  9.6 12.9 %collective-permute-start.3 = (bf16[1,128,128]{2,1,0:T(8,128)(2,1)S(1)}, bf16[1,128,128]{2,1,0:T(8,128)(2,1)S(1)}, u32[]{:S(2)}, u32[]{:S(2)}) collective-permute-start(bf16[1,128,128]{2,1,0:T(8,128)(2,1)S(1)} %pack_e.1), channel_id=1, source_target_pairs={{10,0},{7,1},{12,2},{9,3},{14,4},{11,5},{0,6},{13,7},{2,8},{15,9},... | collective-permute-start | bytes 98312 | tf_op jit(solution)/shard_map/ppermute | solution.py:388
  19.8 5.7 %collective-permute-start.8 = (bf16[12,128,128]{2,1,0:T(8,128)(2,1)S(1)}, bf16[12,128,128]{2,1,0:T(8,128)(2,1)S(1)}, u32[]{:S(2)}, u32[]{:S(2)}) collective-permute-start(bf16[12,128,128]{2,1,0:T(8,128)(2,1)S(1)} %stage_early.1), channel_id=1, source_target_pairs={{0,1},{1,0},{2,3},{3,2},{4,5},{5,4},{6,7},{7,6},{8,9},{9,8},{10,11... | collective-permute-start | bytes 1179656 | tf_op jit(solution)/shard_map/ppermute | solution.py:391
  22.6 3.5 %collective-permute-start.6 = (bf16[4,128,128]{2,1,0:T(8,128)(2,1)S(1)}, bf16[4,128,128]{2,1,0:T(8,128)(2,1)S(1)}, u32[]{:S(2)}, u32[]{:S(2)}) collective-permute-start(bf16[4,128,128]{2,1,0:T(8,128)(2,1)S(1)} %get-tuple-element.32), channel_id=1, source_target_pairs={{0,1},{1,0},{2,3},{3,2},{4,5},{5,4},{6,7},{7,6},{8,9},{9,8},{10,11... | collective-permute-start | bytes 393224 | tf_op jit(solution)/shard_map/ppermute | solution.py:391
  22.7 3.5 %collective-permute-start.7 = (bf16[4,128,128]{2,1,0:T(8,128)(2,1)S(1)}, bf16[4,128,128]{2,1,0:T(8,128)(2,1)S(1)}, u32[]{:S(2)}, u32[]{:S(2)}) collective-permute-start(bf16[4,128,128]{2,1,0:T(8,128)(2,1)S(1)} %get-tuple-element.33), channel_id=1, source_target_pairs={{0,1},{3,2},{4,5},{7,6},{8,9},{11,10},{12,13},{15,14},{16,17},{19,... | collective-permute-start | bytes 393224 | tf_op jit(solution)/shard_map/ppermute | solution.py:459

commit v19 on v17

--- a/solution.py
+++ b/solution.py
@@ -313,10 +313,11 @@
         for place in here:
             if place % NCOL not in late:
                 store(old_ref, table, out_ref, place, out_sem)
-        add_columns(refs, ("late",), old_ref, made, right, mine, late_pairs)
-        for place in here:
-            if place % NCOL in late:
-                store(made, table, out_ref, place, out_sem)
+        for pair, js in enumerate(late_pairs(mine)):
+            add_columns(refs, ("late",), old_ref, made, right.at[pl.ds(pair, 1)], mine, lambda parity, js=js: [js])
+            for place in here:
+                if place % NCOL in [columns_of(mine).index(j) for j in js]:
+                    store(made, table, out_ref, place, out_sem)
         wait_for(len(here), made, out_ref, out_sem)
 
 

time: 25.6 us -> 25.5 us (level)
  no operation moved by 1% of the time
where the time goes in v19:
time: 25.5 us; the launch traced here: 25.3 us
  starting transfers between devices  9.14 us (36%)
  waiting for transfers between devices  8.63 us (34%)
  Pallas kernels  6.81 us (27%)
  between operations  0.75 us (3%)
    ppermute x5, starting transfers between devices, towards(): return lax.ppermute(message, ('row', 'col'), pairs)  8.47 us
    ppermute x5, waiting for transfers between devices, towards(): return lax.ppermute(message, ('row', 'col'), pairs)  8.14 us
    pallas_call x3, Pallas kernels, added(): pl.pallas_call(kernel, out_shape=blocks(BR * NCOL + 1, jnp.float32), in_s...  2.18 us
    pallas_call x1, Pallas kernels, local(): pl.pallas_call(functools.partial(inner_kernel, nblocks, slots), out_shape...  1.93 us
    pallas_call x1, Pallas kernels, local(): pl.pallas_call(functools.partial(pack_kernel, nblocks, slots), out_shape=...  1.36 us
    pallas_call x1, Pallas kernels, local(): pl.pallas_call(multiply_kernel, out_shape=jax.ShapeDtypeStruct(values.sha...  1.13 us
    ppermute x3, starting transfers between devices, swapped(): return lax.ppermute(block, 'col', [(0, 1), (1, 0)])  0.67 us
  transfers between devices with their start and end apart: 8, of which 4 were waited for; matrix products, arithmetic and copies ran while one was open for 0% of the time, Pallas kernels for 17%

profile of v19, /device:TPU:0, one launch (start us, length us, event | category | flops | bytes accessed | tf_op | source)
XLA Modules:
  0.0 25.3 jit_solution(1667483780920091783)
XLA Ops:
  0.0 1.4 %pack.1 = (bf16[13,128,128]{2,1,0:T(8,128)(2,1)S(1)}, bf16[6,128,128]{2,1,0:T(8,128)(2,1)S(1)}, bf16[8,128,128]{2,1,0:T(8,128)(2,1)S(1)}, bf16[5,128,128]{2,1,0:T(8,128)(2,1)S(1)}, bf16[384,1152]{1,0:T(8,128)(2,1)S(1)}) custom-call(s32[1,23]{1,0:T(1,128)} %rows_ref.3, s32[1,23]{1,0:T(1,128)} %cols_ref.3, bf16[1,23,128,128]{3,2,1,0:T(8,128)(2,1)} %values_ref.1), custom_call_target="tpu_custom_call" | custom-call | tf_op jit(solution)/shard_map/pack/pallas_call | solution.py:349
  1.4 0.5 %collective-permute-start = (bf16[384,1152]{1,0:T(8,128)(2,1)S(1)}, bf16[384,1152]{1,0:T(8,128)(2,1)S(1)}, u32[]{:S(2)}, u32[]{:S(2)}) collective-permute-start(bf16[384,1152]{1,0:T(8,128)(2,1)S(1)} %get-tuple-element.19.left_ref), channel_id=1, source_target_pairs={{0,1},{1,0},{2,3},{3,2},{4,5},{5,4},{6,7},{7,6},{8,9},{9,8},{10,11... | collective-permute-start | bytes 2654216 | tf_op jit(solution)/shard_map/ppermute | solution.py:375
  1.9 2.6 %collective-permute-start.4 = (bf16[13,128,128]{2,1,0:T(8,128)(2,1)S(1)}, bf16[13,128,128]{2,1,0:T(8,128)(2,1)S(1)}, u32[]{:S(2)}, u32[]{:S(2)}) collective-permute-start(bf16[13,128,128]{2,1,0:T(8,128)(2,1)S(1)} %get-tuple-element.22), channel_id=1, source_target_pairs={{2,0},{3,1},{0,2},{1,3},{6,4},{7,5},{4,6},{5,7},{10,8},{11,9},{8,1... | collective-permute-start | bytes 1277960 | tf_op jit(solution)/shard_map/ppermute | solution.py:372
  4.4 1.6 %collective-permute-start.5 = (bf16[8,128,128]{2,1,0:T(8,128)(2,1)S(1)}, bf16[8,128,128]{2,1,0:T(8,128)(2,1)S(1)}, u32[]{:S(2)}, u32[]{:S(2)}) collective-permute-start(bf16[8,128,128]{2,1,0:T(8,128)(2,1)S(1)} %get-tuple-element.23), channel_id=1, source_target_pairs={{12,0},{13,1},{6,2},{7,3},{0,4},{1,5},{10,6},{11,7},{4,8},{5,9},{1... | collective-permute-start | bytes 786440 | tf_op jit(solution)/shard_map/ppermute | solution.py:372
  6.0 2.4 %collective-permute-start.1 = (bf16[6,128,128]{2,1,0:T(8,128)(2,1)S(1)}, bf16[6,128,128]{2,1,0:T(8,128)(2,1)S(1)}, u32[]{:S(2)}, u32[]{:S(2)}) collective-permute-start(bf16[6,128,128]{2,1,0:T(8,128)(2,1)S(1)} %get-tuple-element.20), channel_id=1, source_target_pairs={{14,0},{15,1},{4,2},{5,3},{2,4},{3,5},{8,6},{9,7},{6,8},{7,9},{12,... | collective-permute-start | bytes 589832 | tf_op jit(solution)/shard_map/ppermute | solution.py:372
  8.5 0.4 %collective-permute-start.2 = (bf16[5,128,128]{2,1,0:T(8,128)(2,1)S(1)}, bf16[5,128,128]{2,1,0:T(8,128)(2,1)S(1)}, u32[]{:S(2)}, u32[]{:S(2)}) collective-permute-start(bf16[5,128,128]{2,1,0:T(8,128)(2,1)S(1)} %get-tuple-element.21), channel_id=1, source_target_pairs={{4,0},{5,1},{14,2},{15,3},{8,4},{9,5},{2,6},{3,7},{12,8},{13,9},{6... | collective-permute-start | bytes 491528 | tf_op jit(solution)/shard_map/ppermute | solution.py:372
  9.6 0.0 collective-permute-done.left_other_ref
  9.6 1.4 %collective-permute-start.3 = (bf16[1,128,128]{2,1,0:T(8,128)(2,1)S(1)}, bf16[1,128,128]{2,1,0:T(8,128)(2,1)S(1)}, u32[]{:S(2)}, u32[]{:S(2)}) collective-permute-start(bf16[1,128,128]{2,1,0:T(8,128)(2,1)S(1)} %pack_e.1), channel_id=1, source_target_pairs={{10,0},{7,1},{12,2},{9,3},{14,4},{11,5},{0,6},{13,7},{2,8},{15,9},... | collective-permute-start | bytes 98312 | tf_op jit(solution)/shard_map/ppermute | solution.py:372
  11.1 1.9 %inner.1 = (s32[1,128]{1,0:T(1,128)S(4)}, f32[1,23,128,128]{3,2,1,0:T(8,128)}) custom-call(s32[1,23]{1,0:T(1,128)} %rows_ref.3, s32[1,23]{1,0:T(1,128)} %cols_ref.3, s32[1,1]{1,0:T(1,128)S(6)} %copy.7.counts_ref, bf16[384,1152]{1,0:T(8,128)(2,1)S(1)} %get-tuple-element.19.left_ref, bf16[384,1152]{1,0:T(8,128)(2,1)S(1)} %collective-permute-done.left_other_ref), custom_call_target="tpu_custom_call" | custom-call | flops 427819008 | bytes 1507328 | tf_op jit(solution)/shard_map/inner/pallas_call | solution.py:388
  13.0 2.5 %collective-permute-done.5.c_ref.refs_1_ = bf16[8,128,128]{2,1,0:T(8,128)(2,1)S(1)} collective-permute-done((bf16[8,128,128]{2,1,0:T(8,128)(2,1)S(1)}, bf16[8,128,128]{2,1,0:T(8,128)(2,1)S(1)}, u32[]{:S(2)}, u32[]{:S(2)}) %collective-permute-start.5) | collective-permute-done | bytes 262176 | tf_op jit(solution)/shard_map/ppermute | solution.py:372
  15.5 4.2 %collective-permute-done.4.a_ref.refs_0_ = bf16[13,128,128]{2,1,0:T(8,128)(2,1)S(1)} collective-permute-done((bf16[13,128,128]{2,1,0:T(8,128)(2,1)S(1)}, bf16[13,128,128]{2,1,0:T(8,128)(2,1)S(1)}, u32[]{:S(2)}, u32[]{:S(2)}) %collective-permute-start.4) | collective-permute-done | bytes 426016 | tf_op jit(solution)/shard_map/ppermute | solution.py:372
  19.7 0.2 stage_early.1
  19.8 0.1 collective-permute-start.7
  19.9 1.2 %early.1.old_ref = f32[28,128,128]{2,1,0:T(8,128)S(1)} custom-call(bf16[384,1152]{1,0:T(8,128)(2,1)S(1)} %get-tuple-element.19.left_ref, bf16[384,1152]{1,0:T(8,128)(2,1)S(1)} %collective-permute-done.left_other_ref, bf16[13,128,128]{2,1,0:T(8,128)(2,1)S(1)} %collective-permute-done.4.a_ref.refs_0_, bf16[8,128,128]{2,1,0:T(8,128)(2,1)S(1)} %collective-permute-done.5.c_ref.refs_1_), custom_call_target="tpu_custom_call" | custom-call | flops 4194304 | tf_op jit(solution)/shard_map/early/pallas_call | solution.py:418
  21.1 1.5 %collective-permute-done.2.refs_1_.d_ref = bf16[5,128,128]{2,1,0:T(8,128)(2,1)S(1)} collective-permute-done((bf16[5,128,128]{2,1,0:T(8,128)(2,1)S(1)}, bf16[5,128,128]{2,1,0:T(8,128)(2,1)S(1)}, u32[]{:S(2)}, u32[]{:S(2)}) %collective-permute-start.2) | collective-permute-done | bytes 163872 | tf_op jit(solution)/shard_map/ppermute | solution.py:372
  22.6 0.0 collective-permute-done.1.refs_0_.b_ref
  22.6 0.0 collective-permute-done.3.refs_2_.e_ref
  22.6 0.1 collective-permute-start.6
  22.7 0.5 %late.1.old_ref = f32[28,128,128]{2,1,0:T(8,128)S(1)} custom-call(bf16[384,1152]{1,0:T(8,128)(2,1)S(1)} %get-tuple-element.19.left_ref, bf16[384,1152]{1,0:T(8,128)(2,1)S(1)} %collective-permute-done.left_other_ref, bf16[6,128,128]{2,1,0:T(8,128)(2,1)S(1)} %collective-permute-done.1.refs_0_.b_ref, ...), custom_call_target="tpu_custom_call" | custom-call | flops 16777216000 | tf_op jit(solution)/shard_map/late/pallas_call | solution.py:418
  23.1 0.0 collective-permute-done.7.staged_ref
  23.1 0.6 %staged_early.1.old_ref = f32[28,128,128]{2,1,0:T(8,128)S(1)} custom-call(bf16[384,1152]{1,0:T(8,128)(2,1)S(1)} %get-tuple-element.19.left_ref, bf16[384,1152]{1,0:T(8,128)(2,1)S(1)} %collective-permute-done.left_other_ref, bf16[12,128,128]{2,1,0:T(8,128)(2,1)S(1)} %collective-permute-done.7.staged_ref, f32[28,128,128]{2,1,0:T(8,128)S(1)} %late.1.old_ref), custom_call_target="tpu_custom_call" | custom-call | flops 4194304 | tf_op jit(solution)/shard_map/staged_early/pallas_call | solution.py:418
  23.7 0.5 %collective-permute-done.6.staged_ref = bf16[8,128,128]{2,1,0:T(8,128)(2,1)S(1)} collective-permute-done((bf16[8,128,128]{2,1,0:T(8,128)(2,1)S(1)}, bf16[8,128,128]{2,1,0:T(8,128)(2,1)S(1)}, u32[]{:S(2)}, u32[]{:S(2)}) %collective-permute-start.6) | collective-permute-done | bytes 262176 | tf_op jit(solution)/shard_map/ppermute | solution.py:375
  24.2 1.1 %multiply.1 = f32[1,23,128,128]{3,2,1,0:T(8,128)} custom-call(bf16[384,1152]{1,0:T(8,128)(2,1)S(1)} %get-tuple-element.19.left_ref, bf16[384,1152]{1,0:T(8,128)(2,1)S(1)} %collective-permute-done.left_other_ref, bf16[8,128,128]{2,1,0:T(8,128)(2,1)S(1)} %collective-permute-done.6.staged_ref, ...), custom_call_target="tpu_custom_call", output_to_operand_aliasing={{}: (5, {})} | custom-call | tf_op jit(solution)/shard_map/multiply/pallas_call | solution.py:436
  (2 shorter events, 0.0 us)
Async XLA Ops:
  1.4 8.2 %collective-permute-start = (bf16[384,1152]{1,0:T(8,128)(2,1)S(1)}, bf16[384,1152]{1,0:T(8,128)(2,1)S(1)}, u32[]{:S(2)}, u32[]{:S(2)}) collective-permute-start(bf16[384,1152]{1,0:T(8,128)(2,1)S(1)} %get-tuple-element.19.left_ref), channel_id=1, source_target_pairs={{0,1},{1,0},{2,3},{3,2},{4,5},{5,4},{6,7},{7,6},{8,9},{9,8},{10,11... | collective-permute-start | bytes 2654216 | tf_op jit(solution)/shard_map/ppermute | solution.py:375
  1.9 17.8 %collective-permute-start.4 = (bf16[13,128,128]{2,1,0:T(8,128)(2,1)S(1)}, bf16[13,128,128]{2,1,0:T(8,128)(2,1)S(1)}, u32[]{:S(2)}, u32[]{:S(2)}) collective-permute-start(bf16[13,128,128]{2,1,0:T(8,128)(2,1)S(1)} %get-tuple-element.22), channel_id=1, source_target_pairs={{2,0},{3,1},{0,2},{1,3},{6,4},{7,5},{4,6},{5,7},{10,8},{11,9},{8,1... | collective-permute-start | bytes 1277960 | tf_op jit(solution)/shard_map/ppermute | solution.py:372
  4.4 11.0 %collective-permute-start.5 = (bf16[8,128,128]{2,1,0:T(8,128)(2,1)S(1)}, bf16[8,128,128]{2,1,0:T(8,128)(2,1)S(1)}, u32[]{:S(2)}, u32[]{:S(2)}) collective-permute-start(bf16[8,128,128]{2,1,0:T(8,128)(2,1)S(1)} %get-tuple-element.23), channel_id=1, source_target_pairs={{12,0},{13,1},{6,2},{7,3},{0,4},{1,5},{10,6},{11,7},{4,8},{5,9},{1... | collective-permute-start | bytes 786440 | tf_op jit(solution)/shard_map/ppermute | solution.py:372
  6.0 16.5 %collective-permute-start.1 = (bf16[6,128,128]{2,1,0:T(8,128)(2,1)S(1)}, bf16[6,128,128]{2,1,0:T(8,128)(2,1)S(1)}, u32[]{:S(2)}, u32[]{:S(2)}) collective-permute-start(bf16[6,128,128]{2,1,0:T(8,128)(2,1)S(1)} %get-tuple-element.20), channel_id=1, source_target_pairs={{14,0},{15,1},{4,2},{5,3},{2,4},{3,5},{8,6},{9,7},{6,8},{7,9},{12,... | collective-permute-start | bytes 589832 | tf_op jit(solution)/shard_map/ppermute | solution.py:372
  8.5 14.1 %collective-permute-start.2 = (bf16[5,128,128]{2,1,0:T(8,128)(2,1)S(1)}, bf16[5,128,128]{2,1,0:T(8,128)(2,1)S(1)}, u32[]{:S(2)}, u32[]{:S(2)}) collective-permute-start(bf16[5,128,128]{2,1,0:T(8,128)(2,1)S(1)} %get-tuple-element.21), channel_id=1, source_target_pairs={{4,0},{5,1},{14,2},{15,3},{8,4},{9,5},{2,6},{3,7},{12,8},{13,9},{6... | collective-permute-start | bytes 491528 | tf_op jit(solution)/shard_map/ppermute | solution.py:372
  9.6 12.9 %collective-permute-start.3 = (bf16[1,128,128]{2,1,0:T(8,128)(2,1)S(1)}, bf16[1,128,128]{2,1,0:T(8,128)(2,1)S(1)}, u32[]{:S(2)}, u32[]{:S(2)}) collective-permute-start(bf16[1,128,128]{2,1,0:T(8,128)(2,1)S(1)} %pack_e.1), channel_id=1, source_target_pairs={{10,0},{7,1},{12,2},{9,3},{14,4},{11,5},{0,6},{13,7},{2,8},{15,9},... | collective-permute-start | bytes 98312 | tf_op jit(solution)/shard_map/ppermute | solution.py:372
  19.8 3.3 %collective-permute-start.7 = (bf16[12,128,128]{2,1,0:T(8,128)(2,1)S(1)}, bf16[12,128,128]{2,1,0:T(8,128)(2,1)S(1)}, u32[]{:S(2)}, u32[]{:S(2)}) collective-permute-start(bf16[12,128,128]{2,1,0:T(8,128)(2,1)S(1)} %stage_early.1), channel_id=1, source_target_pairs={{0,1},{1,0},{2,3},{3,2},{4,5},{5,4},{6,7},{7,6},{8,9},{9,8},{10,11... | collective-permute-start | bytes 1179656 | tf_op jit(solution)/shard_map/ppermute | solution.py:375
  22.6 1.6 %collective-permute-start.6 = (bf16[8,128,128]{2,1,0:T(8,128)(2,1)S(1)}, bf16[8,128,128]{2,1,0:T(8,128)(2,1)S(1)}, u32[]{:S(2)}, u32[]{:S(2)}) collective-permute-start(bf16[8,128,128]{2,1,0:T(8,128)(2,1)S(1)} %stage_late.1), channel_id=1, source_target_pairs={{0,1},{1,0},{2,3},{3,2},{4,5},{5,4},{6,7},{7,6},{8,9},{9,8},{10,11... | collective-permute-start | bytes 786440 | tf_op jit(solution)/shard_map/ppermute | solution.py:375
